TPU v7x, 512 devices: a whole 4x4x16 slice. The times are simulated.
512 devices in a mesh: grp: 32 (over z_lo, y), sp: 16 (over x, z_hi, core).
Axes of the slice: x: 4, y: 4, z: 16 (z_hi: 2, z_lo: 8; z = z_hi * 8 + z_lo), core: 2. Of those that a mesh axis runs over, the one named last changes fastest.
Arguments:
- features: bfloat16 [8, 32, 32, 64, 128], P(None, None, 'sp', 'grp'), may hold values from -6 to 6
- weight_fine: bfloat16 [27, 32, 32], replicated, may hold values from -0.21875 to 0.21875
- weight_down: bfloat16 [8, 64, 32], replicated, may hold values from -0.375 to 0.375
- weight_coarse: bfloat16 [27, 64, 64], replicated, may hold values from -0.15625 to 0.15625
- cotangent: bfloat16 [32, 64, 16, 512], P('grp', None, 'sp'), may hold values from -6 to 6
Outputs:
- coarse_out: bfloat16 [32, 64, 16, 512], P('grp', None, 'sp')
- grad_input: bfloat16 [8, 32, 32, 64, 128], P(None, None, 'sp', 'grp')
- grad_fine: float32 [27, 32, 32], replicated
- grad_down: float32 [8, 64, 32], replicated
- grad_coarse: float32 [27, 64, 64], replicated
All inputs are finite; a program needn't handle non-finite values.
Results may differ from a plain program's by a relative error of at most 0.013.
Values may be sent and summed in bfloat16 or wider, within the bound.
No kernel may reach another device: no remote copies, remote signals or barrier semaphores. Data moves between devices by JAX's collectives and lax.ppermute only.
A program may use at most 64 MiB of HBM per device.

v0:
```python
import math

import jax
import jax.numpy as jnp
from jax import lax
from jax.sharding import PartitionSpec as P

QUARTERS = 4


def extended(block, sides, width, periodic):
    for axis, dim in sides:
        count = lax.axis_size(axis)
        forward = [(i, i + 1) for i in range(count - 1)]
        if periodic:
            forward.append((count - 1, 0))
        backward = [(target, source) for source, target in forward]
        low = lax.ppermute(
            lax.slice_in_dim(block, block.shape[dim] - width, None, axis=dim), axis, forward
        )
        high = lax.ppermute(lax.slice_in_dim(block, 0, width, axis=dim), axis, backward)
        block = jnp.concatenate([low, block, high], axis=dim)
    return block


def silu_slope(values):
    sigma = jax.nn.sigmoid(values)
    return sigma * (1.0 + values * (1.0 - sigma))


def tap_offsets(offset_index):
    return (offset_index // 9 - 1, offset_index // 3 % 3 - 1, offset_index % 3 - 1)


def fine_faces(field_volume):
    padded = extended(field_volume, (("grp", 3), ("sp", 2)), 1, False)
    return jnp.pad(padded, ((0, 0), (0, 0), (0, 0), (0, 0), (1, 1)))


def rim_mask(span, lower, upper, dtype):
    place = lax.broadcasted_iota(jnp.int32, (span,), 0)
    return jnp.where(place == 0, lower, jnp.where(place == span - 1, upper, jnp.ones((), dtype)))


def coarse_faces(field_volume):
    padded = extended(field_volume, (("grp", 4), ("sp", 2)), 1, True)
    quarter = (lax.axis_index("grp") - QUARTERS // 2) % QUARTERS
    z_keep = rim_mask(
        padded.shape[4],
        (quarter != 0).astype(padded.dtype),
        (quarter != QUARTERS - 1).astype(padded.dtype),
        padded.dtype,
    )
    brick = lax.axis_index("sp")
    x_keep = rim_mask(
        padded.shape[2],
        (brick != 0).astype(padded.dtype),
        (brick != lax.axis_size("sp") - 1).astype(padded.dtype),
        padded.dtype,
    )
    padded = padded * z_keep
    padded = padded * x_keep[:, None, None]
    return jnp.pad(padded, ((0, 0), (0, 0), (0, 0), (1, 1), (0, 0)))


def make_portion(padded):
    x_cells, y_cells, z_cells = (padded.shape[2] - 2, padded.shape[3] - 2, padded.shape[4] - 2)

    def portion(step_x, step_y, step_z):
        return padded[
            :,
            :,
            1 + step_x : 1 + step_x + x_cells,
            1 + step_y : 1 + step_y + y_cells,
            1 + step_z : 1 + step_z + z_cells,
        ]

    return portion


def convolve(padded, weights, transpose):
    portion = make_portion(padded)
    summed = None
    for offset_index in range(27):
        step_x, step_y, step_z = tap_offsets(offset_index)
        matrix = weights[offset_index]
        if transpose:
            step_x, step_y, step_z = (-step_x, -step_y, -step_z)
            matrix = matrix.T
        term = jnp.einsum(
            "oc,bcxyz->boxyz",
            matrix,
            portion(step_x, step_y, step_z),
            preferred_element_type=jnp.float32,
        )
        summed = term if summed is None else summed + term
    return summed


def gradient(upstream, padded):
    portion = make_portion(padded)
    grads = []
    for offset_index in range(27):
        step_x, step_y, step_z = tap_offsets(offset_index)
        grads.append(
            jnp.einsum(
                "boxyz,bcxyz->oc",
                upstream,
                portion(step_x, step_y, step_z),
                preferred_element_type=jnp.float32,
            )
        )
    return jnp.stack(grads)


def split_pairs(field_volume):
    batch, chans, x_cells, y_cells, z_cells = field_volume.shape
    return field_volume.reshape(batch, chans, x_cells // 2, 2, y_cells // 2, 2, z_cells // 2, 2)


def reduce_resolution(field_volume, reduction_kernel_taps):
    return jnp.einsum(
        "ijloc,bcxiyjzl->boxyz",
        reduction_kernel_taps,
        split_pairs(field_volume),
        preferred_element_type=jnp.float32,
    )


def upsample(upstream, reduction_kernel_taps):
    batch, chans, x_cells, y_cells, z_cells = upstream.shape
    spread = jnp.einsum(
        "ijloc,boxyz->bcxiyjzl", reduction_kernel_taps, upstream, preferred_element_type=jnp.float32
    )
    return spread.reshape(
        batch, reduction_kernel_taps.shape[4], 2 * x_cells, 2 * y_cells, 2 * z_cells
    )


def down_gradient(upstream, field_volume):
    grads = jnp.einsum(
        "boxyz,bcxiyjzl->ijloc",
        upstream,
        split_pairs(field_volume),
        preferred_element_type=jnp.float32,
    )
    return grads.reshape(8, grads.shape[3], grads.shape[4])


def to_blocks(field_volume):
    batch, chans, x_cells, y_cells, z_cells = field_volume.shape
    split = field_volume.reshape(batch, chans, x_cells, y_cells, QUARTERS, z_cells // QUARTERS)
    split = jnp.transpose(split, (0, 4, 1, 2, 3, 5))
    split = split.reshape(batch * QUARTERS, chans, x_cells, y_cells, z_cells // QUARTERS)
    return jnp.roll(split, QUARTERS // 2, axis=0)


def from_blocks(field_volume):
    field_volume = jnp.roll(field_volume, -(QUARTERS // 2), axis=0)
    blocks, chans, x_cells, y_cells, z_part = field_volume.shape
    split = field_volume.reshape(blocks // QUARTERS, QUARTERS, chans, x_cells, y_cells, z_part)
    split = jnp.transpose(split, (0, 2, 3, 4, 1, 5))
    return split.reshape(blocks // QUARTERS, chans, x_cells, y_cells, QUARTERS * z_part)


def local(features, weight_fine, weight_down, weight_coarse, cotangent):
    batch, fine_level_channels, x_cells, y_cells, z_cells = features.shape
    chans_coarse = weight_down.shape[1]
    reduction_kernel_taps = weight_down.reshape(2, 2, 2, chans_coarse, fine_level_channels)
    fine_count = batch * x_cells * lax.axis_size("sp") * y_cells * lax.axis_size("grp") * z_cells
    fine_scale = 1.0 / math.sqrt(fine_count)
    coarse_level_scale = 1.0 / math.sqrt(fine_count // 8)
    padded_input = fine_faces(features)
    pre2 = convolve(padded_input, weight_fine, False)
    act2 = jax.nn.silu(pre2).astype(jnp.bfloat16)
    relocated_features = lax.all_to_all(
        to_blocks(act2), "grp", split_axis=0, concat_axis=3, tiled=True
    )
    third_level_down = reduce_resolution(relocated_features, reduction_kernel_taps).astype(
        jnp.bfloat16
    )
    coarse_shape = third_level_down.shape
    padded_down = coarse_faces(third_level_down)
    pre3 = convolve(padded_down, weight_coarse, False)
    coarse_out = jax.nn.silu(pre3).astype(jnp.bfloat16)
    upstream = cotangent.reshape(coarse_shape).astype(jnp.float32)
    dpre3 = (upstream * silu_slope(pre3)).astype(jnp.bfloat16)
    grad_coarse = gradient(dpre3, padded_down)
    padded_upstream = coarse_faces(dpre3)
    ddown3 = convolve(padded_upstream, weight_coarse, True).astype(jnp.bfloat16)
    grad_down = down_gradient(ddown3, relocated_features)
    dact_moved = upsample(ddown3, reduction_kernel_taps).astype(jnp.bfloat16)
    dact2 = from_blocks(lax.all_to_all(dact_moved, "grp", split_axis=3, concat_axis=0, tiled=True))
    dpre2 = (dact2.astype(jnp.float32) * silu_slope(pre2)).astype(jnp.bfloat16)
    grad_fine = gradient(dpre2, padded_input)
    grad_fine, grad_down, grad_coarse = lax.psum((grad_fine, grad_down, grad_coarse), ("grp", "sp"))
    padded_grad = fine_faces(dpre2)
    grad_input = convolve(padded_grad, weight_fine, True).astype(jnp.bfloat16)
    result_block = coarse_out.reshape(cotangent.shape)
    return (
        result_block,
        grad_input,
        grad_fine * fine_scale,
        grad_down * coarse_level_scale,
        grad_coarse * coarse_level_scale,
    )


def solution(mesh):
    placed = (P(None, None, "sp", "grp", None), P(), P(), P(), P("grp", None, "sp", None))
    return jax.shard_map(
        local,
        mesh=mesh,
        in_specs=placed,
        out_specs=(P("grp", None, "sp", None), P(None, None, "sp", "grp", None), P(), P(), P()),
        check_vma=False,
    )
```

profile of v0, /device:TPU:1, one launch (start us, length us, event | category | flops | bytes accessed | tf_op | source)
XLA Modules:
  0.0 770.7 jit_solution(15242496519451888333)
XLA Ops:
  8.3 4.0 collective-permute-start
  15.0 3.1 collective-permute-done.1
  18.1 17.4 %collective-permute-start.2 = (bf16[8,32,1,4,128]{4,1,3,2,0:T(8,128)(2,1)S(1)}, bf16[8,32,1,4,128]{4,1,3,2,0:T(8,128)(2,1)S(1)}, u32[]{:S(2)}, u32[]{:S(2)}) collective-permute-start(bf16[8,32,1,4,128]{4,1,3,2,0:T(8,128)(2,1)S(1)} %get-tuple-element.35), channel_id=1, source_target_pairs={{0,1},{1,2},{2,3},{3,4},{4,5},{5,6},{6,7},{7,8},{8,9},{9,10},{10,1... | collective-permute-start | bytes 786440 | tf_op jit(solution)/shard_map/ppermute | solution.py:18
  35.6 1.9 collective-permute-start.3
  37.9 15.5 %collective-permute-done.2 = bf16[8,32,1,4,128]{4,1,3,2,0:T(8,128)(2,1)S(1)} collective-permute-done((bf16[8,32,1,4,128]{4,1,3,2,0:T(8,128)(2,1)S(1)}, bf16[8,32,1,4,128]{4,1,3,2,0:T(8,128)(2,1)S(1)}, u32[]{:S(2)}, u32[]{:S(2)}) %collective-permute-start.2) | collective-permute-done | bytes 262176 | tf_op jit(solution)/shard_map/ppermute | solution.py:18
  53.5 1.4 collective-permute-done.3
  64.7 1.6 copy.202
  66.3 1.4 reshape.463
  68.7 1.7 pad_maximum_fusion.1
  70.4 1.4 copy.373
  71.8 3.1 reshape.690
  74.9 14.8 %all-to-all-start = ((bf16[32,2,2048]{2,1,0:T(2,128)(2,1)}), bf16[32,2,2048]{2,1,0:T(2,128)(2,1)S(1)}, u32[]{:S(2)}, u32[]{:S(2)}) async-start(bf16[32,2,2048]{2,1,0:T(2,128)(2,1)} %reshape.690), calls=%async_computation | async-start | bytes 524288 | tf_op jit(solution)/shard_map/all_to_all | solution.py:176
  89.8 13.9 %all-to-all-done = bf16[32,2,2048]{2,1,0:T(2,128)(2,1)S(1)} async-done(((bf16[32,2,2048]{2,1,0:T(2,128)(2,1)}), bf16[32,2,2048]{2,1,0:T(2,128)(2,1)S(1)}, u32[]{:S(2)}, u32[]{:S(2)}) %all-to-all-start) | async-done | bytes 262176 | tf_op jit(solution)/shard_map/all_to_all | solution.py:176
  103.7 1.5 reshape.691
  105.1 2.9 copy.333
  108.0 1.6 fusion.82
  109.7 1.9 collective-permute-start.4
  111.6 12.1 %collective-permute-start.5 = (bf16[1,64,1,32,1]{1,3,4,2,0:T(8,128)(2,1)S(1)}, bf16[1,64,1,32,1]{1,3,4,2,0:T(8,128)(2,1)S(1)}, u32[]{:S(2)}, u32[]{:S(2)}) collective-permute-start(bf16[1,64,1,32,1]{1,3,4,2,0:T(8,128)(2,1)S(1)} %get-tuple-element.50), channel_id=1, source_target_pairs={{16,0},{32,16},{48,32},{64,48},{80,64},{96,80},{112,96},{128,112},... | collective-permute-start | bytes 12296 | tf_op jit(solution)/shard_map/ppermute | solution.py:21
  124.5 4.9 collective-permute-start.6
  129.5 1.9 collective-permute-start.7
  131.4 10.8 %collective-permute-done.6 = bf16[1,64,1,32,18]{1,3,4,2,0:T(8,128)(2,1)S(1)} collective-permute-done((bf16[1,64,1,32,18]{1,3,4,2,0:T(8,128)(2,1)S(1)}, bf16[1,64,1,32,18]{1,3,4,2,0:T(8,128)(2,1)S(1)}, u32[]{:S(2)}, u32[]{:S(2)}) %collective-permute-start.6) | collective-permute-done | bytes 73760 | tf_op jit(solution)/shard_map/ppermute | solution.py:18
  142.2 2.5 collective-permute-done.7
  157.9 1.9 collective-permute-start.8
  159.8 12.6 %collective-permute-start.9 = (bf16[1,64,1,32,1]{1,3,4,2,0:T(8,128)(2,1)S(1)}, bf16[1,64,1,32,1]{1,3,4,2,0:T(8,128)(2,1)S(1)}, u32[]{:S(2)}, u32[]{:S(2)}) collective-permute-start(bf16[1,64,1,32,1]{1,3,4,2,0:T(8,128)(2,1)S(1)} %get-tuple-element.48), channel_id=1, source_target_pairs={{16,0},{32,16},{48,32},{64,48},{80,64},{96,80},{112,96},{128,112},... | collective-permute-start | bytes 12296 | tf_op jit(solution)/shard_map/ppermute | solution.py:21
  173.3 11.2 %collective-permute-start.10 = (bf16[1,64,1,32,18]{1,3,4,2,0:T(8,128)(2,1)S(1)}, bf16[1,64,1,32,18]{1,3,4,2,0:T(8,128)(2,1)S(1)}, u32[]{:S(2)}, u32[]{:S(2)}) collective-permute-start(bf16[1,64,1,32,18]{1,3,4,2,0:T(8,128)(2,1)S(1)} %pad_maximum_fusion.9), channel_id=1, source_target_pairs={{0,1},{1,2},{2,3},{3,4},{4,5},{5,6},{6,7},{7,8},{8,9},{9,10},{10,1... | collective-permute-start | bytes 221192 | tf_op jit(solution)/shard_map/ppermute | solution.py:18
  184.5 1.9 collective-permute-start.11
  186.6 1.3 collective-permute-done.10
  188.0 11.7 %collective-permute-done.11 = bf16[1,64,1,32,18]{1,3,4,2,0:T(8,128)(2,1)S(1)} collective-permute-done((bf16[1,64,1,32,18]{1,3,4,2,0:T(8,128)(2,1)S(1)}, bf16[1,64,1,32,18]{1,3,4,2,0:T(8,128)(2,1)S(1)}, u32[]{:S(2)}, u32[]{:S(2)}) %collective-permute-start.11) | collective-permute-done | bytes 73760 | tf_op jit(solution)/shard_map/ppermute | solution.py:21
  208.0 3.1 reshape.692
  211.0 13.5 %all-to-all-start.1 = ((bf16[32,2,2048]{2,1,0:T(2,128)(2,1)}), bf16[32,2,2048]{2,1,0:T(2,128)(2,1)}, u32[]{:S(2)}, u32[]{:S(2)}) async-start(bf16[32,2,2048]{2,1,0:T(2,128)(2,1)} %reshape.692), calls=%async_computation.1 | async-start | bytes 524288 | tf_op jit(solution)/shard_map/all_to_all | solution.py:193
  225.6 1.6 copy.206
  227.2 1.6 copy.243
  231.2 2.2 fusion.279
  233.5 4.8 all-to-all-done.1
  238.3 2.7 reshape.693
  241.0 2.3 copy.211
  245.7 3.1 copy.213
  248.8 3.0 reshape.527
  251.9 1.4 multiply_convert_fusion
  260.5 1.5 collective-permute-start.12
  264.4 3.5 collective-permute-done.13
  268.0 1.9 collective-permute-start.15
  269.9 12.6 %collective-permute-start.14 = (bf16[8,32,1,4,128]{4,1,3,2,0:T(8,128)(2,1)S(1)}, bf16[8,32,1,4,128]{4,1,3,2,0:T(8,128)(2,1)}, u32[]{:S(2)}, u32[]{:S(2)}) collective-permute-start(bf16[8,32,1,4,128]{4,1,3,2,0:T(8,128)(2,1)S(1)} %get-tuple-element.33), channel_id=1, source_target_pairs={{0,1},{1,2},{2,3},{3,4},{4,5},{5,6},{6,7},{7,8},{8,9},{9,10},{10,1... | collective-permute-start | bytes 786440 | tf_op jit(solution)/shard_map/ppermute | solution.py:18
  283.9 458.8 %all-reduce.7.cloned.1.call-done = (f32[27,32,32]{2,1,0:T(8,128)}, f32[8,64,32]{1,2,0:T(8,128)}, f32[27,64,64]{2,1,0:T(8,128)}) async-done(((f32[27,32,32]{2,1,0:T(8,128)}, f32[8,64,32]{1,2,0:T(8,128)}, f32[27,64,64]{2,1,0:T(8,128)}), (f32[27,32,32]{2,1,0:T(8,128)}, f32[8,64,32]{1,2,0:T(8,128)}, f32[27,64,64]{2,1,0:T(8,128)})) %all-reduce.7.cloned.1.call-update) | async-done | bytes 618512 | tf_op jit(solution)/shard_map/psum | solution.py:196
  742.7 1.8 broadcast_multiply_fusion.1
  744.5 1.6 broadcast_multiply_fusion.2
  746.1 2.2 broadcast_multiply_fusion
  749.0 2.8 select_maximum_fusion
  (250 shorter events, 66.9 us)
Async XLA Ops:
  7.2 100.9 %copy-start = (bf16[8,64,32]{1,2,0:T(8,128)(2,1)S(1)}, bf16[8,64,32]{1,2,0:T(8,128)(2,1)}, u32[]{:S(2)}) copy-start(bf16[8,64,32]{1,2,0:T(8,128)(2,1)} %param.7) | copy-start | bytes 98308
  7.2 7.7 copy-start.6
  7.2 30.3 %copy-start.13 = (bf16[27,32,32]{2,1,0:T(8,128)(2,1)S(1)}, bf16[27,32,32]{2,1,0:T(8,128)(2,1)}, u32[]{:S(2)}) copy-start(bf16[27,32,32]{2,1,0:T(8,128)(2,1)} %param.6) | copy-start | bytes 165892
  8.3 29.5 %copy-start.4 = (bf16[8,32,2,2,128]{4,1,3,2,0:T(8,128)(2,1)}, bf16[8,32,2,2,128]{4,1,3,2,0:T(8,128)(2,1)S(1)}, u32[]{:S(2)}) copy-start(bf16[8,32,2,2,128]{4,1,3,2,0:T(8,128)(2,1)S(1)} %copy.196) | copy-start | bytes 786436
  8.3 6.5 collective-permute-start
  12.4 5.7 collective-permute-start.1
  14.8 22.7 %copy-start.17 = (bf16[8,32,2,1,128]{4,1,3,2,0:T(8,128)(2,1)}, bf16[8,32,2,1,128]{4,1,3,2,0:T(8,128)(2,1)S(1)}, u32[]{:S(2)}) copy-start(bf16[8,32,2,1,128]{4,1,3,2,0:T(8,128)(2,1)S(1)} %collective-permute-done) | copy-start | bytes 393220
  18.1 35.4 %copy-start.15 = (bf16[8,32,2,1,128]{4,1,3,2,0:T(8,128)(2,1)}, bf16[8,32,2,1,128]{4,1,3,2,0:T(8,128)(2,1)S(1)}, u32[]{:S(2)}) copy-start(bf16[8,32,2,1,128]{4,1,3,2,0:T(8,128)(2,1)S(1)} %collective-permute-done.1) | copy-start | bytes 393220
  18.1 35.3 %collective-permute-start.2 = (bf16[8,32,1,4,128]{4,1,3,2,0:T(8,128)(2,1)S(1)}, bf16[8,32,1,4,128]{4,1,3,2,0:T(8,128)(2,1)S(1)}, u32[]{:S(2)}, u32[]{:S(2)}) collective-permute-start(bf16[8,32,1,4,128]{4,1,3,2,0:T(8,128)(2,1)S(1)} %get-tuple-element.35), channel_id=1, source_target_pairs={{0,1},{1,2},{2,3},{3,4},{4,5},{5,6},{6,7},{7,8},{8,9},{9,10},{10,1... | collective-permute-start | bytes 786440 | tf_op jit(solution)/shard_map/ppermute | solution.py:18
  35.6 19.3 %collective-permute-start.3 = (bf16[8,32,1,4,128]{4,1,3,2,0:T(8,128)(2,1)S(1)}, bf16[8,32,1,4,128]{4,1,3,2,0:T(8,128)(2,1)S(1)}, u32[]{:S(2)}, u32[]{:S(2)}) collective-permute-start(bf16[8,32,1,4,128]{4,1,3,2,0:T(8,128)(2,1)S(1)} %get-tuple-element.36), channel_id=1, source_target_pairs={{1,0},{2,1},{3,2},{4,3},{5,4},{6,5},{7,6},{8,7},{9,8},{10,9},{11,1... | collective-permute-start | bytes 786440 | tf_op jit(solution)/shard_map/ppermute | solution.py:21
  53.5 6.3 copy-start.2
  74.9 28.8 %all-to-all-start = ((bf16[32,2,2048]{2,1,0:T(2,128)(2,1)}), bf16[32,2,2048]{2,1,0:T(2,128)(2,1)S(1)}, u32[]{:S(2)}, u32[]{:S(2)}) async-start(bf16[32,2,2048]{2,1,0:T(2,128)(2,1)} %reshape.690), calls=%async_computation | async-start | bytes 524288 | tf_op jit(solution)/shard_map/all_to_all | solution.py:176
  89.8 34.0 %copy-start.22 = (bf16[1,64,1,512]{3,1,2,0:T(8,128)(2,1)S(1)}, bf16[1,64,1,512]{3,1,2,0:T(8,128)(2,1)}, u32[]{:S(2)}) copy-start(bf16[1,64,1,512]{3,1,2,0:T(8,128)(2,1)} %param.9) | copy-start | bytes 196612
  109.7 14.2 %collective-permute-start.4 = (bf16[1,64,1,32,1]{1,3,4,2,0:T(8,128)(2,1)S(1)}, bf16[1,64,1,32,1]{1,3,4,2,0:T(8,128)(2,1)S(1)}, u32[]{:S(2)}, u32[]{:S(2)}) collective-permute-start(bf16[1,64,1,32,1]{1,3,4,2,0:T(8,128)(2,1)S(1)} %get-tuple-element.49), channel_id=1, source_target_pairs={{0,16},{16,32},{32,48},{48,64},{64,80},{80,96},{96,112},{112,128},... | collective-permute-start | bytes 12296 | tf_op jit(solution)/shard_map/ppermute | solution.py:18
  111.6 12.9 %collective-permute-start.5 = (bf16[1,64,1,32,1]{1,3,4,2,0:T(8,128)(2,1)S(1)}, bf16[1,64,1,32,1]{1,3,4,2,0:T(8,128)(2,1)S(1)}, u32[]{:S(2)}, u32[]{:S(2)}) collective-permute-start(bf16[1,64,1,32,1]{1,3,4,2,0:T(8,128)(2,1)S(1)} %get-tuple-element.50), channel_id=1, source_target_pairs={{16,0},{32,16},{48,32},{64,48},{80,64},{96,80},{112,96},{128,112},... | collective-permute-start | bytes 12296 | tf_op jit(solution)/shard_map/ppermute | solution.py:21
  123.9 24.5 %copy-start.10 = (bf16[27,64,64]{2,1,0:T(8,128)(2,1)S(1)}, bf16[27,64,64]{2,1,0:T(8,128)(2,1)}, u32[]{:S(2)}) copy-start(bf16[27,64,64]{2,1,0:T(8,128)(2,1)} %param.8) | copy-start | bytes 663556
  124.5 17.7 %collective-permute-start.6 = (bf16[1,64,1,32,18]{1,3,4,2,0:T(8,128)(2,1)S(1)}, bf16[1,64,1,32,18]{1,3,4,2,0:T(8,128)(2,1)S(1)}, u32[]{:S(2)}, u32[]{:S(2)}) collective-permute-start(bf16[1,64,1,32,18]{1,3,4,2,0:T(8,128)(2,1)S(1)} %pad_maximum_fusion.8), channel_id=1, source_target_pairs={{0,1},{1,2},{2,3},{3,4},{4,5},{5,6},{6,7},{7,8},{8,9},{9,10},{10,1... | collective-permute-start | bytes 221192 | tf_op jit(solution)/shard_map/ppermute | solution.py:18
  129.5 15.2 %collective-permute-start.7 = (bf16[1,64,1,32,18]{1,3,4,2,0:T(8,128)(2,1)S(1)}, bf16[1,64,1,32,18]{1,3,4,2,0:T(8,128)(2,1)S(1)}, u32[]{:S(2)}, u32[]{:S(2)}) collective-permute-start(bf16[1,64,1,32,18]{1,3,4,2,0:T(8,128)(2,1)S(1)} %pad_maximum_fusion.8), channel_id=1, source_target_pairs={{1,0},{2,1},{3,2},{4,3},{5,4},{6,5},{7,6},{8,7},{9,8},{10,9},{11,1... | collective-permute-start | bytes 221192 | tf_op jit(solution)/shard_map/ppermute | solution.py:21
  157.9 14.8 %collective-permute-start.8 = (bf16[1,64,1,32,1]{1,3,4,2,0:T(8,128)(2,1)S(1)}, bf16[1,64,1,32,1]{1,3,4,2,0:T(8,128)(2,1)S(1)}, u32[]{:S(2)}, u32[]{:S(2)}) collective-permute-start(bf16[1,64,1,32,1]{1,3,4,2,0:T(8,128)(2,1)S(1)} %get-tuple-element.47), channel_id=1, source_target_pairs={{0,16},{16,32},{32,48},{48,64},{64,80},{80,96},{96,112},{112,128},... | collective-permute-start | bytes 12296 | tf_op jit(solution)/shard_map/ppermute | solution.py:18
  159.8 13.4 %collective-permute-start.9 = (bf16[1,64,1,32,1]{1,3,4,2,0:T(8,128)(2,1)S(1)}, bf16[1,64,1,32,1]{1,3,4,2,0:T(8,128)(2,1)S(1)}, u32[]{:S(2)}, u32[]{:S(2)}) collective-permute-start(bf16[1,64,1,32,1]{1,3,4,2,0:T(8,128)(2,1)S(1)} %get-tuple-element.48), channel_id=1, source_target_pairs={{16,0},{32,16},{48,32},{64,48},{80,64},{96,80},{112,96},{128,112},... | collective-permute-start | bytes 12296 | tf_op jit(solution)/shard_map/ppermute | solution.py:21
  173.3 14.7 %collective-permute-start.10 = (bf16[1,64,1,32,18]{1,3,4,2,0:T(8,128)(2,1)S(1)}, bf16[1,64,1,32,18]{1,3,4,2,0:T(8,128)(2,1)S(1)}, u32[]{:S(2)}, u32[]{:S(2)}) collective-permute-start(bf16[1,64,1,32,18]{1,3,4,2,0:T(8,128)(2,1)S(1)} %pad_maximum_fusion.9), channel_id=1, source_target_pairs={{0,1},{1,2},{2,3},{3,4},{4,5},{5,6},{6,7},{7,8},{8,9},{9,10},{10,1... | collective-permute-start | bytes 221192 | tf_op jit(solution)/shard_map/ppermute | solution.py:18
  184.5 15.2 %collective-permute-start.11 = (bf16[1,64,1,32,18]{1,3,4,2,0:T(8,128)(2,1)S(1)}, bf16[1,64,1,32,18]{1,3,4,2,0:T(8,128)(2,1)S(1)}, u32[]{:S(2)}, u32[]{:S(2)}) collective-permute-start(bf16[1,64,1,32,18]{1,3,4,2,0:T(8,128)(2,1)S(1)} %pad_maximum_fusion.9), channel_id=1, source_target_pairs={{1,0},{2,1},{3,2},{4,3},{5,4},{6,5},{7,6},{8,7},{9,8},{10,9},{11,1... | collective-permute-start | bytes 221192 | tf_op jit(solution)/shard_map/ppermute | solution.py:21
  186.6 1.4 copy-start.12
  204.6 0.6 copy-start.11
  211.0 27.3 %all-to-all-start.1 = ((bf16[32,2,2048]{2,1,0:T(2,128)(2,1)}), bf16[32,2,2048]{2,1,0:T(2,128)(2,1)}, u32[]{:S(2)}, u32[]{:S(2)}) async-start(bf16[32,2,2048]{2,1,0:T(2,128)(2,1)} %reshape.692), calls=%async_computation.1 | async-start | bytes 524288 | tf_op jit(solution)/shard_map/all_to_all | solution.py:193
  224.5 518.2 %all-reduce.7.cloned.1.call-start = ((), (), s32[]{:S(2)}) async-start(), calls=%async_computation.2 | async-start | bytes 2916352 | tf_op jit(solution)/shard_map/psum | solution.py:196
  251.9 2.4 copy-start.3
  255.0 1.4 copy-start.5
  255.0 1.4 copy-start.18
  255.7 1.4 copy-start.7
  256.2 1.7 copy-start.16
  259.5 3.8 copy-start.14
  260.5 1.5 copy-start.19
  260.5 3.9 collective-permute-start.12
  262.0 5.9 collective-permute-start.13
  268.0 480.3 %collective-permute-start.15 = (bf16[8,32,1,4,128]{4,1,3,2,0:T(8,128)(2,1)S(1)}, bf16[8,32,1,4,128]{4,1,3,2,0:T(8,128)(2,1)S(1)}, u32[]{:S(2)}, u32[]{:S(2)}) collective-permute-start(bf16[8,32,1,4,128]{4,1,3,2,0:T(8,128)(2,1)S(1)} %get-tuple-element.34), channel_id=1, source_target_pairs={{1,0},{2,1},{3,2},{4,3},{5,4},{6,5},{7,6},{8,7},{9,8},{10,9},{11,1... | collective-permute-start | bytes 786440 | tf_op jit(solution)/shard_map/ppermute | solution.py:21
  269.9 479.0 %collective-permute-start.14 = (bf16[8,32,1,4,128]{4,1,3,2,0:T(8,128)(2,1)S(1)}, bf16[8,32,1,4,128]{4,1,3,2,0:T(8,128)(2,1)}, u32[]{:S(2)}, u32[]{:S(2)}) collective-permute-start(bf16[8,32,1,4,128]{4,1,3,2,0:T(8,128)(2,1)S(1)} %get-tuple-element.33), channel_id=1, source_target_pairs={{0,1},{1,2},{2,3},{3,4},{4,5},{5,6},{6,7},{7,8},{8,9},{9,10},{10,1... | collective-permute-start | bytes 786440 | tf_op jit(solution)/shard_map/ppermute | solution.py:18
  748.3 0.7 copy-start.20
  755.0 1.5 copy-start.21
  756.7 1.0 copy-start.8
  756.7 1.2 copy-start.9
  762.0 1.5 copy-start.1
Sparse Core Ops, SparseCore 0:
  263.4 479.2 all-reduce.6
where the time goes:
time: 781 us; the launch traced here: 771 us
  waiting for transfers between devices  528 us (68%)
  starting transfers between devices  119 us (15%)
  matrix products  52.9 us (7%)
  local copies, waits for them, and re-layouts  40.1 us (5%)
  between operations  15.6 us (2%)
  other arithmetic  14.6 us (2%)
    psum x1, waiting for transfers between devices, local(): lax.psum((grad_fine, grad_down, grad_coarse), ('grp', 'sp'))  459 us
    ppermute x8, starting transfers between devices, extended(): lax.ppermute(lax.slice_in_dim(block, block.shape[dim] - width, None, axis...  55.5 us
    ppermute x8, starting transfers between devices, extended(): lax.ppermute(lax.slice_in_dim(block, 0, width, axis=dim), axis, backward)  35 us
    dot_general x108, matrix products, convolve(): jnp.einsum('oc,bcxyz->boxyz', matrix, portion(step_x, step_y, step_z), pr...  34.1 us
    ppermute x8, waiting for transfers between devices, extended(): lax.ppermute(lax.slice_in_dim(block, block.shape[dim] - width, None, axis...  27.7 us
    ppermute x8, waiting for transfers between devices, extended(): lax.ppermute(lax.slice_in_dim(block, 0, width, axis=dim), axis, backward)  23.3 us
    unnamed x56, local copies, waits for them, and re-layouts  16.2 us
  transfers between devices with their start and end apart: 19, of which 13 were waited for; matrix products, arithmetic and copies ran while one was open for 2% of the time, Pallas kernels for 0%

commit v1 on v0

v1 whole, which is shorter than its diff:
```python
import math
from functools import partial

import jax
import jax.numpy as jnp
import numpy as np
from jax import lax
from jax.experimental import pallas as pl
from jax.experimental.pallas import tpu as pltpu
from jax.sharding import PartitionSpec as P

QUARTERS = 4
LANES = 128
STEPS = (-1, 0, 1)
F32 = jnp.float32
BF16 = jnp.bfloat16
INTERPRET = False


def call(kernel, outs, half, *operands):
    spaces = [pltpu.SMEM] + [pltpu.VMEM] * len(operands)
    return pl.pallas_call(
        kernel,
        out_shape=outs,
        in_specs=[pl.BlockSpec(memory_space=space) for space in spaces],
        compiler_params=pltpu.CompilerParams(vmem_limit_bytes=28 * 1024 * 1024),
        interpret=INTERPRET,
    )(half, *operands)


def arrival(block, step_y, across):
    rows, cols = lax.axis_size("grp"), lax.axis_size("sp")
    pairs = []
    for row in range(rows):
        for col in range(cols):
            if 0 <= row + step_y < rows:
                source = (col + cols // 2) % cols if across else col
                pairs.append(((row + step_y) * cols + source, row * cols + col))
    return lax.ppermute(block, ("grp", "sp"), pairs)


def upper_half():
    return lax.axis_index("sp") // (lax.axis_size("sp") // 2)


def reach():
    return min(4, lax.axis_size("sp") // 2)


def joined(own, other):
    low = jnp.concatenate([own, other], axis=0)
    return jnp.where(upper_half() == 0, low, jnp.concatenate([other, own], axis=0))


def nearest(block, count):
    return jnp.where(upper_half() == 0, block[-count:], block[:count])


def fine_pieces(block):
    return [block, arrival(block[:, 1:], -1, False), arrival(block[:, :1], 1, False)]


def coarse_pieces(block):
    return [block, arrival(block, -1, False), arrival(block, 1, False)]


def silu_slope(values, sigma):
    return sigma * (1.0 + values * (1.0 - sigma))


def dot(left, right):
    return lax.dot_general(left, right, (((1,), (0,)), ((), ())), preferred_element_type=F32)


def dot_lanes(left, right):
    return lax.dot_general(left, right, (((1,), (1,)), ((), ())), preferred_element_type=F32)


def shifted(values, step, span):
    if step == 0:
        return values
    place = lax.broadcasted_iota(jnp.int32, values.shape, 1) % span
    width = values.shape[1]
    moved = pltpu.roll(values, (-step) % width, 1)
    return jnp.where(place == (span - 1 if step > 0 else 0), 0.0, moved)


def fold_taps(products, chans, span):
    total = products[chans : 2 * chans]
    total = total + shifted(products[:chans], -1, span)
    return total + shifted(products[2 * chans :], 1, span)


def fine_stack(refs, column, shift=None):
    center, before, after = refs
    cells = center.shape[0]

    def cell(x, y):
        inside = None
        if shift is not None:
            half, skip, count = shift
            inside = half == 1 if x < 0 else half == 0 if x >= count else None
            x = jnp.clip(x + skip * half, 0, cells - 1)
        elif not 0 <= x < cells:
            return jnp.zeros(center.shape[2:], center.dtype)
        value = before[x, 0] if y < 0 else after[x, 0] if y > 1 else center[x, y]
        return value if inside is None else jnp.where(inside, value, jnp.zeros_like(value))

    return jnp.concatenate(
        [
            jnp.concatenate(
                [cell(2 * column + x + a, y + b) for x in (0, 1) for y in (0, 1)], axis=1
            )
            for a in STEPS
            for b in STEPS
        ],
        axis=0,
    )


def coarse_stack(refs):
    tiles = refs[0].shape[1] // LANES
    low = lax.broadcasted_iota(jnp.int32, (refs[0].shape[0], LANES), 1) < LANES // 2
    lined = []
    for ref in (refs[1], refs[0], refs[2]):
        own = [ref[:, tile * LANES : (tile + 1) * LANES] for tile in range(tiles)]
        first = jnp.where(low, own[-1].astype(F32), 0.0)
        last = jnp.where(low, 0.0, own[0].astype(F32))
        first, last = [pltpu.roll(tile, LANES // 2, 1).astype(BF16) for tile in (first, last)]
        lined.append([first, *own, last])
    return jnp.concatenate(
        [jnp.concatenate(lined[b][a : a + tiles], axis=1) for a in range(3) for b in range(3)],
        axis=0,
    )


def own_lanes(half, extent, shape):
    lane = lax.broadcasted_iota(jnp.int32, shape, 1)
    tiles = shape[1] // LANES
    x = lane // LANES + tiles * (lane % LANES // (LANES // 2)) - (2 * tiles - extent) * half
    return (x >= 0) & (x < extent)


def down_kernel(half, *refs):
    pieces, (weights, down_weights, sort, down, sorted_act, slope) = refs[:3], refs[3:]
    columns, chans = pieces[0].shape[0] // 2, pieces[0].shape[2]
    for tile in range(columns // 2):
        acts = []
        for column in (tile, tile + columns // 2):
            products = dot(weights[...], fine_stack(pieces, column))
            parts = []
            for place in range(4):
                pre = fold_taps(products[:, place * LANES : (place + 1) * LANES], chans, LANES)
                sigma = jax.nn.sigmoid(pre)
                slope[column, place * chans : (place + 1) * chans] = silu_slope(pre, sigma)
                parts.append((pre * sigma).astype(BF16))
            acts.append(jnp.concatenate(parts, axis=0))
        parted = dot(jnp.concatenate(acts, axis=1), sort[...]).astype(BF16)
        stacked = jnp.concatenate([parted[:, :LANES], parted[:, LANES:]], axis=0)
        lanes = slice(tile * LANES, (tile + 1) * LANES)
        sorted_act[:, lanes] = stacked
        down[:, lanes] = dot(down_weights[...], stacked).astype(BF16)


def coarse_kernel(half, *refs):
    pieces, (weights, upstream, out, dpre) = refs[:3], refs[3:]
    chans, width = pieces[0].shape
    pre = fold_taps(dot(weights[...], coarse_stack(pieces)), chans, LANES // 2)
    sigma = jax.nn.sigmoid(pre)
    act = pre * sigma
    slope = silu_slope(pre, sigma)
    tiles = width // LANES
    rows = LANES // 4
    for tile in range(tiles):
        lanes = slice(tile * LANES, (tile + 1) * LANES)
        ends = [tile * rows, (tile + tiles) * rows]
        packed = jnp.concatenate([upstream[end : end + rows] for end in ends], axis=0)
        dpre[:, lanes] = (unpacked(packed.astype(F32)) * slope[:, lanes]).astype(BF16)
        both = packed_cells(act[:, lanes]).astype(BF16)
        for member, end in enumerate(ends):
            out[end : end + rows] = both[member * rows : (member + 1) * rows]


def packed_cells(values):
    turned = jnp.concatenate([values, values], axis=0).T.reshape(LANES // 16, 2, 8, LANES)
    low = lax.broadcasted_iota(jnp.int32, (LANES // 16, 8, LANES), 2) < LANES // 2
    return jnp.where(low, turned[:, 0], turned[:, 1]).reshape(LANES // 2, LANES)


def unpacked(values):
    first = values.reshape(LANES // 16, 1, 8, LANES)
    second = pltpu.roll(values, LANES // 2, 1).reshape(LANES // 16, 1, 8, LANES)
    turned = jnp.concatenate([first, second], axis=1).reshape(LANES, LANES).T
    return turned[: LANES // 2]


def pack_kernel(values, out):
    for tile in range(values.shape[1] // LANES):
        part = values[:, tile * LANES : (tile + 1) * LANES].astype(F32)
        out[tile * LANES // 2 : (tile + 1) * LANES // 2] = packed_cells(part).astype(BF16)


def unpack_kernel(values, out):
    for tile in range(out.shape[1] // LANES):
        part = values[tile * LANES // 2 : (tile + 1) * LANES // 2].astype(F32)
        out[:, tile * LANES : (tile + 1) * LANES] = unpacked(part).astype(BF16)


def tap_stack(values, span):
    values = values.astype(F32)
    return jnp.concatenate([shifted(values, -step, span).astype(BF16) for step in STEPS], axis=0)


def store_tiles(ref, base, values):
    rows, cols = values.shape
    for start in range(0, cols, LANES):
        width = min(LANES, cols - start)
        ref[base : base + rows, :width] = values[:, start : start + width].astype(ref.dtype)
        base += rows
    return base


def coarse_grad_kernel(extent, half, *refs):
    pieces, (dpre, grad) = refs[:3], refs[3:]
    grad[...] = jnp.zeros(grad.shape, grad.dtype)
    own = jnp.where(own_lanes(half[0], extent, dpre.shape), dpre[...].astype(F32), 0.0)
    products = dot_lanes(tap_stack(own, LANES // 2), coarse_stack(pieces))
    store_tiles(grad, 0, products)


def back_kernel(extent, half, *refs):
    pieces, feature_pieces = refs[:3], refs[3:6]
    weights, up_weights, unsort, sorted_act, slope, coarse_grad, dpre2, grads = refs[6:]
    chans3 = pieces[0].shape[0]
    columns, chans = feature_pieces[0].shape[0] // 2, feature_pieces[0].shape[2]
    ddown = fold_taps(dot(weights[...], coarse_stack(pieces)), chans3, LANES // 2)
    own_ddown = jnp.where(own_lanes(half[0], extent, ddown.shape), ddown, 0.0).astype(BF16)
    ddown = ddown.astype(BF16)
    spread = dot(up_weights[...], ddown).astype(BF16)
    rows = spread.shape[0] // 2
    total = None
    for tile in range(columns // 2):
        lanes = slice(tile * LANES, (tile + 1) * LANES)
        both = dot(jnp.concatenate([spread[:rows, lanes], spread[rows:, lanes]], axis=1), unsort[...])
        for member in range(2):
            column = tile + member * (columns // 2)
            dpre = both[:, member * LANES : (member + 1) * LANES] * slope[column]
            dpre = dpre.astype(BF16)
            parts = [dpre[place * chans : (place + 1) * chans] for place in range(4)]
            for place in range(4):
                dpre2[2 * column + place // 2, place % 2] = parts[place]
            place = column - (columns - extent) * half[0]
            inside = (place >= 0) & (place < extent)
            parts = [jnp.where(inside, part.astype(F32), 0.0) for part in parts]
            moved = jnp.concatenate([tap_stack(part, LANES) for part in parts], axis=1)
            term = dot_lanes(moved, fine_stack(feature_pieces, column))
            total = term if total is None else total + term
    base = coarse_grad.shape[0]
    grads[:base] = coarse_grad[...]
    grads[base:] = jnp.zeros((grads.shape[0] - base, LANES), grads.dtype)
    base = store_tiles(grads, base, total)
    store_tiles(grads, base, dot_lanes(own_ddown, sorted_act[...]))


def input_kernel(half, *refs):
    pieces, (weights, out) = refs[:3], refs[3:]
    cells, chans = pieces[0].shape[0], pieces[0].shape[2]
    count = out.shape[0]
    for column in range(count // 2):
        stack = fine_stack(pieces, column, (half[0], cells - count, count))
        products = dot(weights[...], stack)
        for place in range(4):
            total = fold_taps(products[:, place * LANES : (place + 1) * LANES], chans, LANES)
            out[2 * column + place // 2, place % 2] = total.astype(BF16)


def tap_matrix(weights):
    taps, outs, ins = weights.shape
    return jnp.transpose(weights.reshape(9, 3, outs, ins), (1, 2, 0, 3)).reshape(3 * outs, 9 * ins)


def reversed_taps(weights):
    return jnp.transpose(weights[::-1], (0, 2, 1))


def sort_matrix():
    table = np.zeros((2 * LANES, 2 * LANES), np.float32)
    for sample in range(2):
        for z in range(LANES):
            table[sample * LANES + z, (z % 2) * LANES + sample * (LANES // 2) + z // 2] = 1.0
    return table


def trade(parts, axis, groups=None):
    return lax.all_to_all(
        parts, axis, split_axis=0, concat_axis=0, axis_index_groups=groups, tiled=True
    )


def share(part, axis, groups=None):
    count = lax.axis_size(axis) if groups is None else len(groups[0])
    return trade(jnp.broadcast_to(part[None], (count, *part.shape)), axis, groups)


def turned(block, across=False):
    rows, cols = lax.axis_size("grp"), lax.axis_size("sp")
    batch, shift = cols // 2, QUARTERS // 2
    pairs = []
    for row in range(rows):
        major, quarter = divmod((row - shift) % rows, QUARTERS)
        for col in range(cols):
            there = (QUARTERS * (col % batch) + quarter + shift) % rows
            side = 1 - col // batch if across else col // batch
            pairs.append((row * cols + col, there * cols + side * batch + major))
    return lax.ppermute(block, ("grp", "sp"), pairs)


def close_groups():
    cols = lax.axis_size("sp")
    return [[col for col in range(cols) if col // 2 % 2 == far] for far in (0, 1)]


def far_groups():
    rows, cols = lax.axis_size("grp"), lax.axis_size("sp")
    return [
        [row * cols + col + far for row in range(rows) for far in (0, 2)]
        for col in range(cols)
        if col // 2 % 2 == 0
    ]


def local(features, weight_fine, weight_down, weight_coarse, cotangent):
    batch, chans, x_cells, y_cells, z_cells = features.shape
    chans3 = weight_down.shape[1]
    rows, cols = lax.axis_size("grp"), lax.axis_size("sp")
    width = batch * z_cells // 2
    extent = batch + reach()
    wider = extent * z_cells // 2
    fine_scale = 1.0 / math.sqrt(batch * x_cells * cols * y_cells * rows * z_cells)
    coarse_scale = 1.0 / math.sqrt(batch * x_cells * cols * y_cells * rows * z_cells // 8)
    shape = jax.ShapeDtypeStruct
    halves = [list(range(batch)), list(range(batch, cols))]
    near = close_groups()
    unit = len(near[0]) * rows * LANES
    grad_rows = -(-(15 * chans3 + 9 * chans + 2 * chans3) * LANES // unit) * unit // LANES
    half = upper_half().astype(jnp.int32).reshape(1)

    sort = jnp.asarray(sort_matrix(), BF16)
    unsort = jnp.asarray(sort_matrix().T, BF16)
    parted = weight_down.reshape(2, 2, 2, chans3, chans)
    down_matrix = jnp.transpose(parted, (3, 2, 0, 1, 4)).reshape(chans3, 8 * chans)

    own = trade(jnp.transpose(features, (0, 2, 3, 1, 4)), "sp", halves)
    own = own.reshape(batch * x_cells, y_cells, chans, LANES)

    block = (rows, width // 2 // rows, LANES)
    cells = pl.pallas_call(
        pack_kernel, out_shape=shape((width // 2, LANES), BF16), interpret=INTERPRET
    )(cotangent.reshape(chans3, width))
    cells = [turned(cells).reshape(block), turned(cells, True).reshape(block)]
    own, *cells = lax.optimization_barrier((own, *cells))
    own = joined(own, arrival(nearest(own, reach() * x_cells), 0, True))
    cells = jnp.roll(trade(jnp.concatenate(cells, axis=1), "grp"), -(QUARTERS // 2), axis=0)
    cells = [part.reshape(width // 2, LANES) for part in jnp.split(cells, 2, axis=1)]
    count = reach() * QUARTERS * block[1]
    other = jnp.where(upper_half() == 0, cells[1][:count], cells[1][-count:])
    upstream = joined(cells[0], other)

    feature_pieces = fine_pieces(own)
    down, sorted_act, slope = call(
        down_kernel,
        (
            shape((chans3, wider), BF16),
            shape((8 * chans, wider), BF16),
            shape((extent, 4 * chans, LANES), F32),
        ),
        half,
        *feature_pieces,
        tap_matrix(weight_fine),
        down_matrix,
        sort,
    )
    down_pieces = coarse_pieces(down)
    coarse, dpre3 = call(
        coarse_kernel,
        (shape(upstream.shape, BF16), shape((chans3, wider), BF16)),
        half,
        *down_pieces,
        tap_matrix(weight_coarse),
        upstream,
    )
    coarse_grad = call(
        partial(coarse_grad_kernel, batch),
        shape((15 * chans3, LANES), BF16),
        half,
        *down_pieces,
        dpre3,
    )
    dpre_pieces = coarse_pieces(dpre3)
    coarse_grad, *dpre_pieces = lax.optimization_barrier((coarse_grad, *dpre_pieces))

    dpre2, grads = call(
        partial(back_kernel, batch),
        (shape(own.shape, BF16), shape((grad_rows, LANES), BF16)),
        half,
        *dpre_pieces,
        *feature_pieces,
        tap_matrix(reversed_taps(weight_coarse)),
        down_matrix.T,
        unsort,
        sorted_act,
        slope,
        coarse_grad,
    )
    spread = fine_pieces(dpre2)
    part = trade(grads.reshape(len(near[0]), -1, LANES), "sp", near)
    part = jnp.sum(part.astype(F32), axis=0).astype(BF16).reshape(rows, -1, LANES)
    gradient = call(
        input_kernel,
        shape((batch * x_cells, *own.shape[1:]), BF16),
        half,
        *spread,
        tap_matrix(reversed_taps(weight_fine)),
    )
    part, gradient = lax.optimization_barrier((part, gradient))
    kept = part.shape[1]
    wide = -(-kept // 8) * 8
    coarse = jnp.where(upper_half() == 0, coarse[: width // 2], coarse[-(width // 2) :])
    coarse = jnp.roll(coarse.reshape(block), QUARTERS // 2, axis=0)
    blank = jnp.zeros((rows, wide - kept, LANES), BF16)
    mixed = trade(jnp.concatenate([part, blank, coarse], axis=1), "grp")
    part = jnp.sum(mixed[:, :wide].astype(F32), axis=0)
    part = share(part, ("grp", "sp"), far_groups()).reshape(rows, 2, wide, LANES)
    grads = (part[:, 0] + part[:, 1])[:, :kept].reshape(rows * kept, LANES)
    grads = share(grads, "sp", near).reshape(grad_rows, LANES)

    grads, gradient = lax.optimization_barrier((grads, gradient))
    gradient = trade(gradient.reshape(batch, x_cells, y_cells, chans, LANES), "sp", halves)
    grad_input = jnp.transpose(gradient, (0, 3, 1, 2, 4))

    result = pl.pallas_call(
        unpack_kernel, out_shape=shape((chans3, width), BF16), interpret=INTERPRET
    )(turned(mixed[:, wide:].reshape(width // 2, LANES)))
    result = result.reshape(cotangent.shape)

    grad_coarse = grads[: 15 * chans3].reshape(5, 3, chans3, 2, chans3)
    grad_coarse = jnp.transpose(grad_coarse, (0, 3, 1, 2, 4)).reshape(30, chans3, chans3)[:27]
    grads = grads[15 * chans3 :]
    grad_fine = grads[: 9 * chans].reshape(3, 3, chans, 4, chans)
    grad_fine = jnp.transpose(grad_fine, (0, 3, 1, 2, 4)).reshape(36, chans, chans)[:27]
    grad_down = grads[9 * chans : 9 * chans + 2 * chans3].reshape(2, chans3, 4, chans)
    grad_down = jnp.transpose(grad_down, (2, 0, 1, 3)).reshape(8, chans3, chans)
    return (
        result,
        grad_input,
        grad_fine * fine_scale,
        grad_down * coarse_scale,
        grad_coarse * coarse_scale,
    )


def solution(mesh):
    placed = (P(None, None, "sp", "grp", None), P(), P(), P(), P("grp", None, "sp", None))
    return jax.shard_map(
        local,
        mesh=mesh,
        in_specs=placed,
        out_specs=(P("grp", None, "sp", None), P(None, None, "sp", "grp", None), P(), P(), P()),
        check_vma=False,
    )
```

time: 781 us -> 238 us (0.30); the launches traced: 771 us -> 237 us
  waiting for transfers between devices: 528 us -> 41.2 us
  blocking collectives: 0 us -> 73.4 us
  matrix products: 52.9 us -> 0 us
  local copies, waits for them, and re-layouts: 40.1 us -> 11.9 us
  starting transfers between devices: 119 us -> 93.8 us
  between operations: 15.6 us -> 1.17 us
  Pallas kernels: 0 us -> 12.1 us
  other arithmetic: 14.6 us -> 2.84 us
    psum x1 -> x0, waiting for transfers between devices: 459 us -> none  [local(): lax.psum((grad_fine, grad_down, grad_coarse), ('grp', 'sp'))]
    all_to_all x0 -> x3, blocking collectives: none -> 73.4 us  [trade(): lax.all_to_all(parts, axis, split_axis=0, concat_axis=0, axis_index_group...]
    dot_general x165 -> x0, matrix products: 52.9 us -> none  [the longest x108 34.1 us: convolve(): jnp.einsum('oc,bcxyz->boxyz', matrix, portion(step_x, step_y, step_z), pr...]
    ppermute x16 -> x12, starting transfers between devices: 90.5 us -> 51.5 us  [the longest x3 27.2 us: turned(): return lax.ppermute(block, ('grp', 'sp'), pairs)]
    all_to_all x2 -> x4, waiting for transfers between devices: 18.7 us -> 0.01 us  [trade(): lax.all_to_all(parts, axis, split_axis=0, concat_axis=0, axis_index_group...]
    all_to_all x2 -> x4, starting transfers between devices: 28.3 us -> 42.4 us  [trade(): lax.all_to_all(parts, axis, split_axis=0, concat_axis=0, axis_index_group...]
    unnamed x56 -> x15, local copies, waits for them, and re-layouts: 16.2 us -> 3.59 us
    pallas_call x0 -> x7, Pallas kernels: none -> 12.1 us  [the longest x5 8.85 us: call(): pl.pallas_call(kernel, out_shape=outs, in_specs=[pl.BlockSpec(memory_spac...]
  transfers between devices with their start and end apart: 19 -> 16, of which waited for: 13 -> 8; matrix products, arithmetic and copies ran while one was open for 2% -> 4% of each run, Pallas kernels for 0% -> 3%
where the time goes in v1:
time: 238 us; the launch traced here: 237 us
  starting transfers between devices  93.8 us (39%)
  blocking collectives  73.4 us (31%)
  waiting for transfers between devices  41.2 us (17%)
  Pallas kernels  12.1 us (5%)
  local copies, waits for them, and re-layouts  11.9 us (5%)
  other arithmetic  2.84 us (1%)
    all_to_all x3, blocking collectives, trade(): lax.all_to_all(parts, axis, split_axis=0, concat_axis=0, axis_index_group...  73.4 us
    all_to_all x4, starting transfers between devices, trade(): lax.all_to_all(parts, axis, split_axis=0, concat_axis=0, axis_index_group...  42.4 us
    ppermute x3, starting transfers between devices, turned(): return lax.ppermute(block, ('grp', 'sp'), pairs)  27.2 us
    ppermute x3, waiting for transfers between devices, turned(): return lax.ppermute(block, ('grp', 'sp'), pairs)  24.8 us
    ppermute x9, starting transfers between devices, arrival(): return lax.ppermute(block, ('grp', 'sp'), pairs)  24.3 us
    ppermute x9, waiting for transfers between devices, arrival(): return lax.ppermute(block, ('grp', 'sp'), pairs)  16.4 us
    pallas_call x5, Pallas kernels, call(): pl.pallas_call(kernel, out_shape=outs, in_specs=[pl.BlockSpec(memory_spac...  8.85 us
  transfers between devices with their start and end apart: 16, of which 8 were waited for; matrix products, arithmetic and copies ran while one was open for 4% of the time, Pallas kernels for 3%

profile of v1, /device:TPU:1, one launch (start us, length us, event | category | flops | bytes accessed | tf_op | source)
XLA Modules:
  0.0 236.6 jit_solution(17484348064911028607)
XLA Ops:
  0.6 17.5 %all-to-all-start = ((bf16[8,2,2,32,128]{4,2,1,3,0:T(2,128)(2,1)}), bf16[8,2,2,32,128]{4,2,1,3,0:T(2,128)(2,1)S(1)}, u32[]{:S(2)}, u32[]{:S(2)}) async-start(bf16[8,2,2,32,128]{4,2,1,3,0:T(2,128)(2,1)} %bitcast.87), calls=%async_computation | async-start | bytes 524288 | tf_op jit(solution)/shard_map/all_to_all | solution.py:295
  18.2 1.6 shard_map.110
  19.7 12.0 %collective-permute-start = (bf16[256,128]{1,0:T(8,128)(2,1)}, bf16[256,128]{1,0:T(8,128)(2,1)S(1)}, u32[]{:S(2)}, u32[]{:S(2)}) collective-permute-start(bf16[256,128]{1,0:T(8,128)(2,1)} %shard_map.110), channel_id=1, source_target_pairs={{0,71},{1,135},{2,199},{3,263},{4,327},{5,391},{6,455},{7,7},{8,79... | collective-permute-start | bytes 196616 | tf_op jit(solution)/shard_map/ppermute | solution.py:315
  31.7 3.2 %collective-permute-start.1 = (bf16[256,128]{1,0:T(8,128)(2,1)}, bf16[256,128]{1,0:T(8,128)(2,1)S(1)}, u32[]{:S(2)}, u32[]{:S(2)}) collective-permute-start(bf16[256,128]{1,0:T(8,128)(2,1)} %shard_map.110), channel_id=1, source_target_pairs={{0,79},{1,143},{2,207},{3,271},{4,335},{5,399},{6,463},{7,15},{8,7... | collective-permute-start | bytes 196616 | tf_op jit(solution)/shard_map/ppermute | solution.py:315
  35.0 6.3 %collective-permute-done = bf16[256,128]{1,0:T(8,128)(2,1)S(1)} collective-permute-done((bf16[256,128]{1,0:T(8,128)(2,1)}, bf16[256,128]{1,0:T(8,128)(2,1)S(1)}, u32[]{:S(2)}, u32[]{:S(2)}) %collective-permute-start) | collective-permute-done | bytes 65568 | tf_op jit(solution)/shard_map/ppermute | solution.py:315
  41.4 4.6 %collective-permute-done.1 = bf16[256,128]{1,0:T(8,128)(2,1)S(1)} collective-permute-done((bf16[256,128]{1,0:T(8,128)(2,1)}, bf16[256,128]{1,0:T(8,128)(2,1)S(1)}, u32[]{:S(2)}, u32[]{:S(2)}) %collective-permute-start.1) | collective-permute-done | bytes 65568 | tf_op jit(solution)/shard_map/ppermute | solution.py:315
  46.0 3.1 %collective-permute-start.2 = (bf16[8,2,32,128]{3,2,1,0:T(8,128)(2,1)S(1)}, bf16[8,2,32,128]{3,2,1,0:T(8,128)(2,1)S(1)}, u32[]{:S(2)}, u32[]{:S(2)}) collective-permute-start(bf16[8,2,32,128]{3,2,1,0:T(8,128)(2,1)S(1)} %slice_select_fusion), channel_id=1, source_target_pairs={{8,0},{9,1},{10,2},{11,3},{12,4},{13,5},{14,6},{15,7},{0,8},{1,9},... | collective-permute-start | bytes 393224 | tf_op jit(solution)/shard_map/ppermute | solution.py:39
  49.2 0.7 pad_maximum_fusion
  49.9 9.7 %all-to-all-start.1 = ((bf16[32,16,128]{2,1,0:T(8,128)(2,1)}), bf16[32,16,128]{2,1,0:T(8,128)(2,1)S(1)}, u32[]{:S(2)}, u32[]{:S(2)}) async-start(bf16[32,16,128]{2,1,0:T(8,128)(2,1)} %pad_maximum_fusion), calls=%async_computation.1 | async-start | bytes 262144 | tf_op jit(solution)/shard_map/all_to_all | solution.py:295
  59.6 0.7 fusion.6
  60.3 3.1 %collective-permute-start.3 = (bf16[24,1,32,128]{3,2,1,0:T(8,128)(2,1)}, bf16[24,1,32,128]{3,2,1,0:T(8,128)(2,1)S(1)}, u32[]{:S(2)}, u32[]{:S(2)}) collective-permute-start(bf16[24,1,32,128]{3,2,1,0:T(8,128)(2,1)} %get-tuple-element.44), channel_id=1, source_target_pairs={{0,16},{1,17},{2,18},{3,19},{4,20},{5,21},{6,22},{7,23},{8,24},{9,... | collective-permute-start | bytes 589832 | tf_op jit(solution)/shard_map/ppermute | solution.py:39
  63.5 1.3 collective-permute-start.4
  65.3 0.7 copy-done.5
  66.1 0.8 rev.6
  66.9 1.2 copy.38
  68.7 0.8 copy-done.3
  69.5 0.4 copy.51
  71.0 0.7 copy-done.1
  71.7 3.0 %shard_map.111 = (bf16[64,768]{1,0:T(8,128)(2,1)S(1)}, bf16[256,768]{1,0:T(8,128)(2,1)S(1)}, f32[12,128,128]{2,1,0:T(8,128)S(1)}) custom-call(s32[1]{0:T(128)} %bitcast.half, bf16[24,2,32,128]{3,2,1,0:T(8,128)(2,1)S(1)} %maximum_select_fusion.refs_0_.refs_3_, bf16[24,1,32,128]{3,2,1,0:T(8,128)(2,1)S(1)} %collective-permute-done.3.refs_1_.refs_4_, ...), custom_call_target="tpu_custom_call" | custom-call | tf_op jit(solution)/shard_map/pallas_call | solution.py:22
  74.8 4.0 %collective-permute-start.5 = (bf16[64,768]{1,0:T(8,128)(2,1)S(1)}, bf16[64,768]{1,0:T(8,128)(2,1)S(1)}, u32[]{:S(2)}, u32[]{:S(2)}) collective-permute-start(bf16[64,768]{1,0:T(8,128)(2,1)S(1)} %get-tuple-element.24.refs_0_), channel_id=1, source_target_pairs={{0,16},{1,17},{2,18},{3,19},{4,20},{5,21},{6,22},{7,23},{8,24},{9,... | collective-permute-start | bytes 294920 | tf_op jit(solution)/shard_map/ppermute | solution.py:39
  78.8 1.3 collective-permute-start.6
  80.4 3.7 %collective-permute-done.6.refs_2_ = bf16[64,768]{1,0:T(8,128)(2,1)S(1)} collective-permute-done((bf16[64,768]{1,0:T(8,128)(2,1)S(1)}, bf16[64,768]{1,0:T(8,128)(2,1)S(1)}, u32[]{:S(2)}, u32[]{:S(2)}) %collective-permute-start.6) | collective-permute-done | bytes 98336 | tf_op jit(solution)/shard_map/ppermute | solution.py:39
  84.1 0.7 shard_map.112
  84.8 3.1 %collective-permute-start.7 = (bf16[64,768]{1,0:T(8,128)(2,1)S(1)}, bf16[64,768]{1,0:T(8,128)(2,1)S(1)}, u32[]{:S(2)}, u32[]{:S(2)}) collective-permute-start(bf16[64,768]{1,0:T(8,128)(2,1)S(1)} %get-tuple-element.28.refs_3_.refs_0_), channel_id=1, source_target_pairs={{0,16},{1,17},{2,18},{3,19},{4,20},{5,21},{6,22},{7,23},{8,24},{9,... | collective-permute-start | bytes 294920 | tf_op jit(solution)/shard_map/ppermute | solution.py:39
  87.9 1.3 collective-permute-start.8
  89.2 0.5 shard_map.113.refs_11_
  89.8 5.0 %collective-permute-done.8.refs_2_ = bf16[64,768]{1,0:T(8,128)(2,1)S(1)} collective-permute-done((bf16[64,768]{1,0:T(8,128)(2,1)S(1)}, bf16[64,768]{1,0:T(8,128)(2,1)S(1)}, u32[]{:S(2)}, u32[]{:S(2)}) %collective-permute-start.8) | collective-permute-done | bytes 98336 | tf_op jit(solution)/shard_map/ppermute | solution.py:39
  94.8 3.8 %shard_map.114 = (bf16[24,2,32,128]{3,2,1,0:T(8,128)(2,1)S(1)}, bf16[1536,128]{1,0:T(8,128)(2,1)}) custom-call(s32[1]{0:T(128)} %bitcast.half, bf16[64,768]{1,0:T(8,128)(2,1)S(1)} %get-tuple-element.28.refs_3_.refs_0_, bf16[64,768]{1,0:T(8,128)(2,1)S(1)} %collective-permute-done.7.refs_1_, bf16[64,768]{1,0:T(8,128)(2,1)S(1)} %collective-permute-done.8.refs_2_, ...), custom_call_target="tpu_custom_call" | custom-call | tf_op jit(solution)/shard_map/pallas_call | solution.py:22
  98.6 10.8 %all-to-all-start.2 = ((bf16[8,192,128]{2,1,0:T(8,128)(2,1)}), bf16[8,192,128]{2,1,0:T(8,128)(2,1)S(1)}, u32[]{:S(2)}, u32[]{:S(2)}) async-start(bf16[8,192,128]{2,1,0:T(8,128)(2,1)} %bitcast.20), calls=%async_computation.2 | async-start | bytes 786432 | tf_op jit(solution)/shard_map/all_to_all | solution.py:295
  109.5 5.8 %collective-permute-start.9 = (bf16[24,1,32,128]{3,2,1,0:T(8,128)(2,1)S(1)}, bf16[24,1,32,128]{3,2,1,0:T(8,128)(2,1)S(1)}, u32[]{:S(2)}, u32[]{:S(2)}) collective-permute-start(bf16[24,1,32,128]{3,2,1,0:T(8,128)(2,1)S(1)} %get-tuple-element.42), channel_id=1, source_target_pairs={{0,16},{1,17},{2,18},{3,19},{4,20},{5,21},{6,22},{7,23},{8,24},{9,... | collective-permute-start | bytes 589832 | tf_op jit(solution)/shard_map/ppermute | solution.py:39
  115.2 1.3 collective-permute-start.10
  116.6 3.0 %collective-permute-done.9.refs_1_ = bf16[24,1,32,128]{3,2,1,0:T(8,128)(2,1)S(1)} collective-permute-done((bf16[24,1,32,128]{3,2,1,0:T(8,128)(2,1)S(1)}, bf16[24,1,32,128]{3,2,1,0:T(8,128)(2,1)S(1)}, u32[]{:S(2)}, u32[]{:S(2)}) %collective-permute-start.9) | collective-permute-done | bytes 196640 | tf_op jit(solution)/shard_map/ppermute | solution.py:39
  119.5 4.4 %collective-permute-done.10.refs_2_ = bf16[24,1,32,128]{3,2,1,0:T(8,128)(2,1)S(1)} collective-permute-done((bf16[24,1,32,128]{3,2,1,0:T(8,128)(2,1)S(1)}, bf16[24,1,32,128]{3,2,1,0:T(8,128)(2,1)S(1)}, u32[]{:S(2)}, u32[]{:S(2)}) %collective-permute-start.10) | collective-permute-done | bytes 196640 | tf_op jit(solution)/shard_map/ppermute | solution.py:39
  123.9 0.8 shard_map.115
  124.9 26.9 %all_to_all.35 = bf16[32,16,128]{2,1,0:T(8,128)(2,1)S(1)} all-to-all(bf16[32,16,128]{2,1,0:T(8,128)(2,1)S(1)} %maximum_maximum_fusion), channel_id=1, replica_groups=mesh['grp'=32,'sp'=16] {'grp'}, dimensions={0} | all-to-all | bytes 262144 | tf_op jit(solution)/shard_map/all_to_all | solution.py:295
  151.9 27.1 %all_to_all.36 = f32[64,8,128]{2,1,0:T(8,128)S(1)} all-to-all(f32[64,8,128]{2,1,0:T(8,128)S(1)} %broadcast_in_dim.17), channel_id=1, replica_groups={{0,2,16,18,32,34,48,50,64,66,80,82,96,98,112,114,128,130,144,146,160,16..., dimensions={0} | all-to-all | bytes 524288 | tf_op jit(solution)/shard_map/all_to_all | solution.py:295
  179.1 19.4 %all_to_all.37 = f32[8,192,128]{2,1,0:T(8,128)S(1)} all-to-all(f32[8,192,128]{2,1,0:T(8,128)S(1)} %broadcast_in_dim.19), channel_id=1, replica_groups={{0,1,4,5,8,9,12,13},{2,3,6,7,10,11,14,15},{16,17,20,21,24,25,28,29},{18..., dimensions={0} | all-to-all | bytes 1572864 | tf_op jit(solution)/shard_map/all_to_all | solution.py:295
  198.5 0.9 copy.44
  199.4 4.4 %all-to-all-start.6 = ((bf16[8,2,2,32,128]{4,2,1,3,0:T(2,128)(2,1)}), bf16[8,2,2,32,128]{4,2,1,3,0:T(2,128)(2,1)S(1)}, u32[]{:S(2)}, u32[]{:S(2)}) async-start(bf16[8,2,2,32,128]{4,2,1,3,0:T(2,128)(2,1)} %copy.44), calls=%async_computation.6 | async-start | bytes 524288 | tf_op jit(solution)/shard_map/all_to_all | solution.py:295
  203.8 12.0 %collective-permute-start.11 = (bf16[256,128]{1,0:T(8,128)(2,1)S(1)}, bf16[256,128]{1,0:T(8,128)(2,1)S(1)}, u32[]{:S(2)}, u32[]{:S(2)}) collective-permute-start(bf16[256,128]{1,0:T(8,128)(2,1)S(1)} %slice_bitcast_fusion), channel_id=1, source_target_pairs={{0,71},{1,135},{2,199},{3,263},{4,327},{5,391},{6,455},{7,7},{8,79... | collective-permute-start | bytes 196616 | tf_op jit(solution)/shard_map/ppermute | solution.py:315
  215.8 13.9 %collective-permute-done.11.values = bf16[256,128]{1,0:T(8,128)(2,1)S(1)} collective-permute-done((bf16[256,128]{1,0:T(8,128)(2,1)S(1)}, bf16[256,128]{1,0:T(8,128)(2,1)S(1)}, u32[]{:S(2)}, u32[]{:S(2)}) %collective-permute-start.11) | collective-permute-done | bytes 65568 | tf_op jit(solution)/shard_map/ppermute | solution.py:315
  229.7 0.6 copy-done.6
  230.3 1.7 shard_map.116
  232.7 0.7 copy.47
  233.4 0.6 reshape.133
  234.1 0.8 slice_multiply_fusion.1
  234.9 1.0 slice_multiply_fusion
  235.9 0.7 copy.54
  (63 shorter events, 3.7 us)
Async XLA Ops:
  0.6 34.3 %all-to-all-start = ((bf16[8,2,2,32,128]{4,2,1,3,0:T(2,128)(2,1)}), bf16[8,2,2,32,128]{4,2,1,3,0:T(2,128)(2,1)S(1)}, u32[]{:S(2)}, u32[]{:S(2)}) async-start(bf16[8,2,2,32,128]{4,2,1,3,0:T(2,128)(2,1)} %bitcast.87), calls=%async_computation | async-start | bytes 524288 | tf_op jit(solution)/shard_map/all_to_all | solution.py:295
  19.7 21.6 %collective-permute-start = (bf16[256,128]{1,0:T(8,128)(2,1)}, bf16[256,128]{1,0:T(8,128)(2,1)S(1)}, u32[]{:S(2)}, u32[]{:S(2)}) collective-permute-start(bf16[256,128]{1,0:T(8,128)(2,1)} %shard_map.110), channel_id=1, source_target_pairs={{0,71},{1,135},{2,199},{3,263},{4,327},{5,391},{6,455},{7,7},{8,79... | collective-permute-start | bytes 196616 | tf_op jit(solution)/shard_map/ppermute | solution.py:315
  31.7 14.2 %collective-permute-start.1 = (bf16[256,128]{1,0:T(8,128)(2,1)}, bf16[256,128]{1,0:T(8,128)(2,1)S(1)}, u32[]{:S(2)}, u32[]{:S(2)}) collective-permute-start(bf16[256,128]{1,0:T(8,128)(2,1)} %shard_map.110), channel_id=1, source_target_pairs={{0,79},{1,143},{2,207},{3,271},{4,335},{5,399},{6,463},{7,15},{8,7... | collective-permute-start | bytes 196616 | tf_op jit(solution)/shard_map/ppermute | solution.py:315
  46.0 13.5 %collective-permute-start.2 = (bf16[8,2,32,128]{3,2,1,0:T(8,128)(2,1)S(1)}, bf16[8,2,32,128]{3,2,1,0:T(8,128)(2,1)S(1)}, u32[]{:S(2)}, u32[]{:S(2)}) collective-permute-start(bf16[8,2,32,128]{3,2,1,0:T(8,128)(2,1)S(1)} %slice_select_fusion), channel_id=1, source_target_pairs={{8,0},{9,1},{10,2},{11,3},{12,4},{13,5},{14,6},{15,7},{0,8},{1,9},... | collective-permute-start | bytes 393224 | tf_op jit(solution)/shard_map/ppermute | solution.py:39
  49.9 30.2 %all-to-all-start.1 = ((bf16[32,16,128]{2,1,0:T(8,128)(2,1)}), bf16[32,16,128]{2,1,0:T(8,128)(2,1)S(1)}, u32[]{:S(2)}, u32[]{:S(2)}) async-start(bf16[32,16,128]{2,1,0:T(8,128)(2,1)} %pad_maximum_fusion), calls=%async_computation.1 | async-start | bytes 262144 | tf_op jit(solution)/shard_map/all_to_all | solution.py:295
  59.6 5.2 %copy-start.4 = (bf16[27,32,32]{2,1,0:T(8,128)(2,1)S(1)}, bf16[27,32,32]{2,1,0:T(8,128)(2,1)}, u32[]{:S(2)}) copy-start(bf16[27,32,32]{2,1,0:T(8,128)(2,1)} %param.8) | copy-start | bytes 165892
  60.3 10.7 %collective-permute-start.3 = (bf16[24,1,32,128]{3,2,1,0:T(8,128)(2,1)}, bf16[24,1,32,128]{3,2,1,0:T(8,128)(2,1)S(1)}, u32[]{:S(2)}, u32[]{:S(2)}) collective-permute-start(bf16[24,1,32,128]{3,2,1,0:T(8,128)(2,1)} %get-tuple-element.44), channel_id=1, source_target_pairs={{0,16},{1,17},{2,18},{3,19},{4,20},{5,21},{6,22},{7,23},{8,24},{9,... | collective-permute-start | bytes 589832 | tf_op jit(solution)/shard_map/ppermute | solution.py:39
  63.5 7.6 %collective-permute-start.4 = (bf16[24,1,32,128]{3,2,1,0:T(8,128)(2,1)S(1)}, bf16[24,1,32,128]{3,2,1,0:T(8,128)(2,1)S(1)}, u32[]{:S(2)}, u32[]{:S(2)}) collective-permute-start(bf16[24,1,32,128]{3,2,1,0:T(8,128)(2,1)S(1)} %get-tuple-element.43), channel_id=1, source_target_pairs={{16,0},{17,1},{18,2},{19,3},{20,4},{21,5},{22,6},{23,7},{24,8},{25... | collective-permute-start | bytes 589832 | tf_op jit(solution)/shard_map/ppermute | solution.py:39
  65.0 1.1 copy-start.2
  65.2 0.8 copy-start.5
  68.5 1.0 copy-start.3
  70.8 0.9 copy-start.1
  74.8 5.6 %collective-permute-start.5 = (bf16[64,768]{1,0:T(8,128)(2,1)S(1)}, bf16[64,768]{1,0:T(8,128)(2,1)S(1)}, u32[]{:S(2)}, u32[]{:S(2)}) collective-permute-start(bf16[64,768]{1,0:T(8,128)(2,1)S(1)} %get-tuple-element.24.refs_0_), channel_id=1, source_target_pairs={{0,16},{1,17},{2,18},{3,19},{4,20},{5,21},{6,22},{7,23},{8,24},{9,... | collective-permute-start | bytes 294920 | tf_op jit(solution)/shard_map/ppermute | solution.py:39
  78.8 5.4 %collective-permute-start.6 = (bf16[64,768]{1,0:T(8,128)(2,1)S(1)}, bf16[64,768]{1,0:T(8,128)(2,1)S(1)}, u32[]{:S(2)}, u32[]{:S(2)}) collective-permute-start(bf16[64,768]{1,0:T(8,128)(2,1)S(1)} %get-tuple-element.24.refs_0_), channel_id=1, source_target_pairs={{16,0},{17,1},{18,2},{19,3},{20,4},{21,5},{22,6},{23,7},{24,8},{25... | collective-permute-start | bytes 294920 | tf_op jit(solution)/shard_map/ppermute | solution.py:39
  84.8 5.0 %collective-permute-start.7 = (bf16[64,768]{1,0:T(8,128)(2,1)S(1)}, bf16[64,768]{1,0:T(8,128)(2,1)S(1)}, u32[]{:S(2)}, u32[]{:S(2)}) collective-permute-start(bf16[64,768]{1,0:T(8,128)(2,1)S(1)} %get-tuple-element.28.refs_3_.refs_0_), channel_id=1, source_target_pairs={{0,16},{1,17},{2,18},{3,19},{4,20},{5,21},{6,22},{7,23},{8,24},{9,... | collective-permute-start | bytes 294920 | tf_op jit(solution)/shard_map/ppermute | solution.py:39
  87.9 6.9 %collective-permute-start.8 = (bf16[64,768]{1,0:T(8,128)(2,1)S(1)}, bf16[64,768]{1,0:T(8,128)(2,1)S(1)}, u32[]{:S(2)}, u32[]{:S(2)}) collective-permute-start(bf16[64,768]{1,0:T(8,128)(2,1)S(1)} %get-tuple-element.28.refs_3_.refs_0_), channel_id=1, source_target_pairs={{16,0},{17,1},{18,2},{19,3},{20,4},{21,5},{22,6},{23,7},{24,8},{25... | collective-permute-start | bytes 294920 | tf_op jit(solution)/shard_map/ppermute | solution.py:39
  89.2 5.6 %copy-start = (bf16[256,256]{1,0:T(8,128)(2,1)S(1)}, bf16[256,256]{1,0:T(8,128)(2,1)}, u32[]{:S(2)}) copy-start(bf16[256,256]{1,0:T(8,128)(2,1)} %constant.46.clone.refs_8_) | copy-start | bytes 393220
  98.6 26.1 %all-to-all-start.2 = ((bf16[8,192,128]{2,1,0:T(8,128)(2,1)}), bf16[8,192,128]{2,1,0:T(8,128)(2,1)S(1)}, u32[]{:S(2)}, u32[]{:S(2)}) async-start(bf16[8,192,128]{2,1,0:T(8,128)(2,1)} %bitcast.20), calls=%async_computation.2 | async-start | bytes 786432 | tf_op jit(solution)/shard_map/all_to_all | solution.py:295
  109.5 10.1 %collective-permute-start.9 = (bf16[24,1,32,128]{3,2,1,0:T(8,128)(2,1)S(1)}, bf16[24,1,32,128]{3,2,1,0:T(8,128)(2,1)S(1)}, u32[]{:S(2)}, u32[]{:S(2)}) collective-permute-start(bf16[24,1,32,128]{3,2,1,0:T(8,128)(2,1)S(1)} %get-tuple-element.42), channel_id=1, source_target_pairs={{0,16},{1,17},{2,18},{3,19},{4,20},{5,21},{6,22},{7,23},{8,24},{9,... | collective-permute-start | bytes 589832 | tf_op jit(solution)/shard_map/ppermute | solution.py:39
  115.2 8.7 %collective-permute-start.10 = (bf16[24,1,32,128]{3,2,1,0:T(8,128)(2,1)S(1)}, bf16[24,1,32,128]{3,2,1,0:T(8,128)(2,1)S(1)}, u32[]{:S(2)}, u32[]{:S(2)}) collective-permute-start(bf16[24,1,32,128]{3,2,1,0:T(8,128)(2,1)S(1)} %get-tuple-element.41), channel_id=1, source_target_pairs={{16,0},{17,1},{18,2},{19,3},{20,4},{21,5},{22,6},{23,7},{24,8},{25... | collective-permute-start | bytes 589832 | tf_op jit(solution)/shard_map/ppermute | solution.py:39
  199.4 36.4 %all-to-all-start.6 = ((bf16[8,2,2,32,128]{4,2,1,3,0:T(2,128)(2,1)}), bf16[8,2,2,32,128]{4,2,1,3,0:T(2,128)(2,1)S(1)}, u32[]{:S(2)}, u32[]{:S(2)}) async-start(bf16[8,2,2,32,128]{4,2,1,3,0:T(2,128)(2,1)} %copy.44), calls=%async_computation.6 | async-start | bytes 524288 | tf_op jit(solution)/shard_map/all_to_all | solution.py:295
  203.8 25.9 %collective-permute-start.11 = (bf16[256,128]{1,0:T(8,128)(2,1)S(1)}, bf16[256,128]{1,0:T(8,128)(2,1)S(1)}, u32[]{:S(2)}, u32[]{:S(2)}) collective-permute-start(bf16[256,128]{1,0:T(8,128)(2,1)S(1)} %slice_bitcast_fusion), channel_id=1, source_target_pairs={{0,71},{1,135},{2,199},{3,263},{4,327},{5,391},{6,455},{7,7},{8,79... | collective-permute-start | bytes 196616 | tf_op jit(solution)/shard_map/ppermute | solution.py:315
  229.7 0.6 copy-start.6

commit v2 on v1

--- a/solution.py
+++ b/solution.py
@@ -222,10 +222,12 @@
 
 def coarse_grad_kernel(extent, half, *refs):
     pieces, (dpre, grad) = refs[:3], refs[3:]
-    grad[...] = jnp.zeros(grad.shape, grad.dtype)
     own = jnp.where(own_lanes(half[0], extent, dpre.shape), dpre[...].astype(F32), 0.0)
     products = dot_lanes(tap_stack(own, LANES // 2), coarse_stack(pieces))
-    store_tiles(grad, 0, products)
+    rows, cols = products.shape
+    base = store_tiles(grad, 0, products[:, : cols - LANES // 2])
+    last = products[:, cols - LANES // 2 :]
+    grad[base:] = jnp.concatenate([last[: rows // 2], last[rows // 2 :]], axis=1).astype(grad.dtype)
 
 
 def back_kernel(extent, half, *refs):
@@ -302,7 +304,7 @@
     return trade(jnp.broadcast_to(part[None], (count, *part.shape)), axis, groups)
 
 
-def turned(block, across=False):
+def turned(block):
     rows, cols = lax.axis_size("grp"), lax.axis_size("sp")
     batch, shift = cols // 2, QUARTERS // 2
     pairs = []
@@ -310,23 +312,85 @@
         major, quarter = divmod((row - shift) % rows, QUARTERS)
         for col in range(cols):
             there = (QUARTERS * (col % batch) + quarter + shift) % rows
-            side = 1 - col // batch if across else col // batch
-            pairs.append((row * cols + col, there * cols + side * batch + major))
+            pairs.append((row * cols + col, there * cols + col // batch * batch + major))
     return lax.ppermute(block, ("grp", "sp"), pairs)
 
 
-def close_groups():
-    cols = lax.axis_size("sp")
-    return [[col for col in range(cols) if col // 2 % 2 == far] for far in (0, 1)]
-
-
-def far_groups():
+def planes():
     rows, cols = lax.axis_size("grp"), lax.axis_size("sp")
     return [
-        [row * cols + col + far for row in range(rows) for far in (0, 2)]
+        [row * cols + col for row in range(start, start + 4) for col in range(cols) if col & 2 == far]
+        for start in range(0, rows, 4)
+        for far in (0, 2)
+    ]
+
+
+def columns():
+    rows, cols = lax.axis_size("grp"), lax.axis_size("sp")
+    return [
+        [row * cols + col + far for row in range(y, rows, 4) for far in (0, 2)]
+        for y in range(4)
         for col in range(cols)
-        if col // 2 % 2 == 0
+        if col & 2 == 0
     ]
+
+
+def late():
+    return (lax.axis_index("grp") % 4 < 2).astype(jnp.int32)
+
+
+def for_plane(cells):
+    lead = cells.shape[0] // 4
+    parts = cells.reshape(lead, 2, 2, QUARTERS, 8, LANES)
+    parts = jnp.roll(jnp.transpose(parts, (3, 0, 2, 1, 4, 5)), QUARTERS // 2, axis=0)
+    blank = jnp.zeros_like(parts)
+    low = upper_half() == 0
+    both = [jnp.where(low, parts, blank), jnp.where(low, blank, parts)]
+    return jnp.concatenate(both, axis=1).reshape(-1, 16, LANES)
+
+
+def for_column(got):
+    lead = lax.axis_size("sp") // 8
+    parts = got.reshape(4, 2, lead, 2, 2, 8, LANES)
+    parts = jnp.where(upper_half() == 0, parts[:, 0], parts[:, 1])
+    parts = jnp.transpose(parts, (1, 2, 3, 0, 4, 5))
+    parts = jnp.stack([parts, jnp.zeros_like(parts)], axis=1).reshape(4 * lead, 2, 32, LANES)
+    steps = 4 * lead
+    shift = 2 * far_side() + late()
+    twice = jnp.concatenate([parts, parts], axis=0)
+    return lax.dynamic_slice_in_dim(twice, steps - shift, steps, axis=0).reshape(-1, 32, LANES)
+
+
+def from_column(got):
+    parts = got.reshape(-1, 2, 32, LANES)
+    steps = parts.shape[0]
+    sample = (lax.axis_index("grp") // 4 - late()) % steps
+    return jnp.where(sample // 2 % 2 == 0, parts[:, 0], parts[:, 1]).reshape(-1, LANES)
+
+
+def far_side():
+    return lax.axis_index("sp") // 2 % 2
+
+
+def far_exchange(parts):
+    near = far_side() == 0
+    kept = jnp.where(near, parts[:, 0], parts[:, 1])
+    sent = jnp.where(near, parts[:, 1], parts[:, 0])
+    got = lax.ppermute(sent, "sp", [(col, col ^ 2) for col in range(lax.axis_size("sp"))])
+    return jnp.stack([jnp.where(near, kept, got), jnp.where(near, got, kept)], axis=1)
+
+
+def near_exchange(parts):
+    cols = lax.axis_size("sp")
+    lead = parts.shape[0]
+    groups = [
+        [start + 4 * far + core for far in range(lead) for core in (0, 1)]
+        for half in range(0, cols, 4 * lead)
+        for start in (half, half + 2)
+    ]
+    rest = parts.shape[3:]
+    parts = jnp.swapaxes(parts, 1, 2).reshape(2 * lead, 2, *rest)
+    return jnp.swapaxes(trade(parts, "sp", groups).reshape(lead, 2, 2, *rest), 1, 2)
 
 
 def local(features, weight_fine, weight_down, weight_coarse, cotangent):
@@ -339,10 +403,9 @@
     fine_scale = 1.0 / math.sqrt(batch * x_cells * cols * y_cells * rows * z_cells)
     coarse_scale = 1.0 / math.sqrt(batch * x_cells * cols * y_cells * rows * z_cells // 8)
     shape = jax.ShapeDtypeStruct
-    halves = [list(range(batch)), list(range(batch, cols))]
-    near = close_groups()
-    unit = len(near[0]) * rows * LANES
-    grad_rows = -(-(15 * chans3 + 9 * chans + 2 * chans3) * LANES // unit) * unit // LANES
+    near = planes()
+    unit = len(near[0]) * 8
+    grad_rows = -(-(27 * chans3 // 2 + 9 * chans + 2 * chans3) // unit) * unit
     half = upper_half().astype(jnp.int32).reshape(1)
 
     sort = jnp.asarray(sort_matrix(), BF16)
@@ -350,6 +413,7 @@
     parted = weight_down.reshape(2, 2, 2, chans3, chans)
     down_matrix = jnp.transpose(parted, (3, 2, 0, 1, 4)).reshape(chans3, 8 * chans)
 
+    halves = [list(range(batch)), list(range(batch, cols))]
     own = trade(jnp.transpose(features, (0, 2, 3, 1, 4)), "sp", halves)
     own = own.reshape(batch * x_cells, y_cells, chans, LANES)
 
@@ -357,14 +421,20 @@
     cells = pl.pallas_call(
         pack_kernel, out_shape=shape((width // 2, LANES), BF16), interpret=INTERPRET
     )(cotangent.reshape(chans3, width))
-    cells = [turned(cells).reshape(block), turned(cells, True).reshape(block)]
-    own, *cells = lax.optimization_barrier((own, *cells))
+    cells = turned(cells).reshape(block)
+    matrices = [
+        tap_matrix(weight_fine),
+        tap_matrix(reversed_taps(weight_fine)),
+        tap_matrix(weight_coarse),
+        tap_matrix(reversed_taps(weight_coarse)),
+        down_matrix,
+        down_matrix.T,
+    ]
+    own, cells, *matrices = lax.optimization_barrier((own, cells, *matrices))
+    fine_matrix, fine_back, coarse_matrix, coarse_back, down_matrix, up_matrix = matrices
     own = joined(own, arrival(nearest(own, reach() * x_cells), 0, True))
-    cells = jnp.roll(trade(jnp.concatenate(cells, axis=1), "grp"), -(QUARTERS // 2), axis=0)
-    cells = [part.reshape(width // 2, LANES) for part in jnp.split(cells, 2, axis=1)]
-    count = reach() * QUARTERS * block[1]
-    other = jnp.where(upper_half() == 0, cells[1][:count], cells[1][-count:])
-    upstream = joined(cells[0], other)
+    cells = jnp.roll(trade(cells, "grp"), -(QUARTERS // 2), axis=0).reshape(width // 2, LANES)
+    upstream = joined(cells, arrival(nearest(cells, reach() * QUARTERS * block[1]), 0, True))
 
     feature_pieces = fine_pieces(own)
     down, sorted_act, slope = call(
@@ -376,7 +446,7 @@
         ),
         half,
         *feature_pieces,
-        tap_matrix(weight_fine),
+        fine_matrix,
         down_matrix,
         sort,
     )
@@ -386,12 +456,12 @@
         (shape(upstream.shape, BF16), shape((chans3, wider), BF16)),
         half,
         *down_pieces,
-        tap_matrix(weight_coarse),
+        coarse_matrix,
         upstream,
     )
     coarse_grad = call(
         partial(coarse_grad_kernel, batch),
-        shape((15 * chans3, LANES), BF16),
+        shape((27 * chans3 // 2, LANES), BF16),
         half,
         *down_pieces,
         dpre3,
@@ -405,47 +475,49 @@
         half,
         *dpre_pieces,
         *feature_pieces,
-        tap_matrix(reversed_taps(weight_coarse)),
-        down_matrix.T,
+        coarse_back,
+        up_matrix,
         unsort,
         sorted_act,
         slope,
         coarse_grad,
     )
-    spread = fine_pieces(dpre2)
-    part = trade(grads.reshape(len(near[0]), -1, LANES), "sp", near)
-    part = jnp.sum(part.astype(F32), axis=0).astype(BF16).reshape(rows, -1, LANES)
+    coarse = jnp.where(upper_half() == 0, coarse[: width // 2], coarse[-(width // 2) :])
+    grads = grads.reshape(len(near[0]), -1, LANES)
+    kept = grads.shape[1]
+    coarse = for_plane(coarse.reshape(batch, QUARTERS, 8, LANES))
+    mixed = trade(jnp.concatenate([grads, coarse], axis=1), ("grp", "sp"), near)
+    part = jnp.sum(mixed[:, :kept].astype(F32), axis=0).astype(BF16)
+    coarse = for_column(mixed[:, kept:])
     gradient = call(
         input_kernel,
         shape((batch * x_cells, *own.shape[1:]), BF16),
         half,
-        *spread,
-        tap_matrix(reversed_taps(weight_fine)),
-    )
-    part, gradient = lax.optimization_barrier((part, gradient))
-    kept = part.shape[1]
-    wide = -(-kept // 8) * 8
-    coarse = jnp.where(upper_half() == 0, coarse[: width // 2], coarse[-(width // 2) :])
-    coarse = jnp.roll(coarse.reshape(block), QUARTERS // 2, axis=0)
-    blank = jnp.zeros((rows, wide - kept, LANES), BF16)
-    mixed = trade(jnp.concatenate([part, blank, coarse], axis=1), "grp")
-    part = jnp.sum(mixed[:, :wide].astype(F32), axis=0)
-    part = share(part, ("grp", "sp"), far_groups()).reshape(rows, 2, wide, LANES)
-    grads = (part[:, 0] + part[:, 1])[:, :kept].reshape(rows * kept, LANES)
-    grads = share(grads, "sp", near).reshape(grad_rows, LANES)
-
+        *fine_pieces(dpre2),
+        fine_back,
+    )
+    part, gradient, coarse = lax.optimization_barrier((part, gradient, coarse))
+    gradient = far_exchange(gradient.reshape(batch // 4, 2, 2, x_cells, y_cells, chans, LANES))
+    part = jnp.broadcast_to(part[None], (coarse.shape[0], *part.shape))
+    mixed = trade(jnp.concatenate([part, coarse], axis=1), ("grp", "sp"), columns())
+    part = jnp.sum(mixed[:, :kept].astype(F32), axis=0)
+    coarse = from_column(mixed[:, kept:])
+    grads = share(part, ("grp", "sp"), near).reshape(grad_rows, LANES)
     grads, gradient = lax.optimization_barrier((grads, gradient))
-    gradient = trade(gradient.reshape(batch, x_cells, y_cells, chans, LANES), "sp", halves)
+    gradient = near_exchange(gradient).reshape(batch, x_cells, y_cells, chans, LANES)
     grad_input = jnp.transpose(gradient, (0, 3, 1, 2, 4))
 
     result = pl.pallas_call(
         unpack_kernel, out_shape=shape((chans3, width), BF16), interpret=INTERPRET
-    )(turned(mixed[:, wide:].reshape(width // 2, LANES)))
+    )(coarse)
     result = result.reshape(cotangent.shape)
 
-    grad_coarse = grads[: 15 * chans3].reshape(5, 3, chans3, 2, chans3)
-    grad_coarse = jnp.transpose(grad_coarse, (0, 3, 1, 2, 4)).reshape(30, chans3, chans3)[:27]
-    grads = grads[15 * chans3 :]
+    grad_coarse = grads[: 12 * chans3].reshape(4, 3, chans3, 2, chans3)
+    grad_coarse = jnp.transpose(grad_coarse, (0, 3, 1, 2, 4)).reshape(24, chans3, chans3)
+    last = grads[12 * chans3 : 27 * chans3 // 2].reshape(-1, 2, chans3)
+    last = jnp.swapaxes(last, 0, 1).reshape(3, chans3, chans3)
+    grad_coarse = jnp.concatenate([grad_coarse, last], axis=0)
+    grads = grads[27 * chans3 // 2 :]
     grad_fine = grads[: 9 * chans].reshape(3, 3, chans, 4, chans)
     grad_fine = jnp.transpose(grad_fine, (0, 3, 1, 2, 4)).reshape(36, chans, chans)[:27]
     grad_down = grads[9 * chans : 9 * chans + 2 * chans3].reshape(2, chans3, 4, chans)

time: 238 us -> 193 us (0.81)
  blocking collectives: 73.4 us -> 0 us
  starting transfers between devices: 93.8 us -> 122 us
  waiting for transfers between devices: 41.2 us -> 44.1 us
  local copies, waits for them, and re-layouts: 11.9 us -> 9.11 us
    all_to_all x3 -> x0, blocking collectives: 73.4 us -> none  [trade(): lax.all_to_all(parts, axis, split_axis=0, concat_axis=0, axis_index_group...]
    all_to_all x4 -> x6, starting transfers between devices: 42.4 us -> 74.1 us  [trade(): lax.all_to_all(parts, axis, split_axis=0, concat_axis=0, axis_index_group...]
    all_to_all x4 -> x6, waiting for transfers between devices: 0.01 us -> 24.2 us  [trade(): lax.all_to_all(parts, axis, split_axis=0, concat_axis=0, axis_index_group...]
    ppermute x3 -> x1, waiting for transfers between devices: 24.8 us -> 5.85 us  [turned(): return lax.ppermute(block, ('grp', 'sp'), pairs)]
    ppermute x3 -> x1, starting transfers between devices: 27.2 us -> 12 us  [turned(): return lax.ppermute(block, ('grp', 'sp'), pairs)]
    ppermute x0 -> x1, starting transfers between devices: none -> 12 us  [far_exchange(): lax.ppermute(sent, 'sp', [(col, col ^ 2) for col in range(lax.axis_size('...]
    ppermute x9 -> x10, waiting for transfers between devices: 16.4 us -> 14 us  [arrival(): return lax.ppermute(block, ('grp', 'sp'), pairs)]
    ppermute x9 -> x10, starting transfers between devices: 24.3 us -> 23.8 us  [arrival(): return lax.ppermute(block, ('grp', 'sp'), pairs)]
  transfers between devices with their start and end apart: 16 -> 18, of which waited for: 8 -> 9; matrix products, arithmetic and copies ran while one was open for 4% -> 4% of each run, Pallas kernels for 3% -> 4%
where the time goes in v2:
time: 193 us; the launch traced here: 192 us
  starting transfers between devices  122 us (63%)
  waiting for transfers between devices  44.1 us (23%)
  Pallas kernels  11.5 us (6%)
  local copies, waits for them, and re-layouts  9.11 us (5%)
  other arithmetic  4.42 us (2%)
    all_to_all x6, starting transfers between devices, trade(): lax.all_to_all(parts, axis, split_axis=0, concat_axis=0, axis_index_group...  74.1 us
    all_to_all x6, waiting for transfers between devices, trade(): lax.all_to_all(parts, axis, split_axis=0, concat_axis=0, axis_index_group...  24.2 us
    ppermute x10, starting transfers between devices, arrival(): return lax.ppermute(block, ('grp', 'sp'), pairs)  23.8 us
    ppermute x10, waiting for transfers between devices, arrival(): return lax.ppermute(block, ('grp', 'sp'), pairs)  14 us
    ppermute x1, starting transfers between devices, turned(): return lax.ppermute(block, ('grp', 'sp'), pairs)  12 us
    ppermute x1, starting transfers between devices, far_exchange(): lax.ppermute(sent, 'sp', [(col, col ^ 2) for col in range(lax.axis_size('...  12 us
    pallas_call x5, Pallas kernels, call(): pl.pallas_call(kernel, out_shape=outs, in_specs=[pl.BlockSpec(memory_spac...  8.2 us
    ppermute x1, waiting for transfers between devices, turned(): return lax.ppermute(block, ('grp', 'sp'), pairs)  5.85 us
  transfers between devices with their start and end apart: 18, of which 9 were waited for; matrix products, arithmetic and copies ran while one was open for 4% of the time, Pallas kernels for 4%

profile of v2, /device:TPU:1, one launch (start us, length us, event | category | flops | bytes accessed | tf_op | source)
XLA Modules:
  0.0 192.4 jit_solution(318294265823327493)
XLA Ops:
  0.6 17.7 %all-to-all-start = ((bf16[8,2,2,32,128]{4,2,1,3,0:T(2,128)(2,1)}), bf16[8,2,2,32,128]{4,2,1,3,0:T(2,128)(2,1)S(1)}, u32[]{:S(2)}, u32[]{:S(2)}) async-start(bf16[8,2,2,32,128]{4,2,1,3,0:T(2,128)(2,1)} %bitcast.146), calls=%async_computation | async-start | bytes 524288 | tf_op jit(solution)/shard_map/all_to_all | solution.py:297
  18.3 1.6 shard_map.110
  19.9 12.0 %collective-permute-start = (bf16[256,128]{1,0:T(8,128)(2,1)}, bf16[256,128]{1,0:T(8,128)(2,1)}, u32[]{:S(2)}, u32[]{:S(2)}) collective-permute-start(bf16[256,128]{1,0:T(8,128)(2,1)} %shard_map.110), channel_id=1, source_target_pairs={{0,71},{1,135},{2,199},{3,263},{4,327},{5,391},{6,455},{7,7},{8,79... | collective-permute-start | bytes 196616 | tf_op jit(solution)/shard_map/ppermute | solution.py:316
  32.0 0.4 copy.73
  32.4 0.4 reshape.143
  32.8 1.2 copy.46
  34.0 0.4 reshape.141
  34.4 0.6 copy-done.3
  35.7 5.9 %collective-permute-done = bf16[256,128]{1,0:T(8,128)(2,1)} collective-permute-done((bf16[256,128]{1,0:T(8,128)(2,1)}, bf16[256,128]{1,0:T(8,128)(2,1)}, u32[]{:S(2)}, u32[]{:S(2)}) %collective-permute-start) | collective-permute-done | bytes 65568 | tf_op jit(solution)/shard_map/ppermute | solution.py:316
  41.6 4.4 %collective-permute-start.1 = (bf16[8,2,32,128]{3,2,1,0:T(8,128)(2,1)S(1)}, bf16[8,2,32,128]{3,2,1,0:T(8,128)(2,1)S(1)}, u32[]{:S(2)}, u32[]{:S(2)}) collective-permute-start(bf16[8,2,32,128]{3,2,1,0:T(8,128)(2,1)S(1)} %slice_select_fusion), channel_id=1, source_target_pairs={{8,0},{9,1},{10,2},{11,3},{12,4},{13,5},{14,6},{15,7},{0,8},{1,9},... | collective-permute-start | bytes 393224 | tf_op jit(solution)/shard_map/ppermute | solution.py:39
  46.0 9.6 %all-to-all-start.1 = ((bf16[32,8,128]{2,1,0:T(8,128)(2,1)}), bf16[32,8,128]{2,1,0:T(8,128)(2,1)S(1)}, u32[]{:S(2)}, u32[]{:S(2)}) async-start(bf16[32,8,128]{2,1,0:T(8,128)(2,1)} %bitcast.4), calls=%async_computation.1 | async-start | bytes 131072 | tf_op jit(solution)/shard_map/all_to_all | solution.py:297
  56.2 3.1 %collective-permute-start.2 = (bf16[24,1,32,128]{3,2,1,0:T(8,128)(2,1)S(1)}, bf16[24,1,32,128]{3,2,1,0:T(8,128)(2,1)S(1)}, u32[]{:S(2)}, u32[]{:S(2)}) collective-permute-start(bf16[24,1,32,128]{3,2,1,0:T(8,128)(2,1)S(1)} %get-tuple-element.63), channel_id=1, source_target_pairs={{0,16},{1,17},{2,18},{3,19},{4,20},{5,21},{6,22},{7,23},{8,24},{9,... | collective-permute-start | bytes 589832 | tf_op jit(solution)/shard_map/ppermute | solution.py:39
  59.4 1.3 collective-permute-start.3
  60.7 6.7 %all-to-all-done.1 = bf16[32,8,128]{2,1,0:T(8,128)(2,1)S(1)} async-done(((bf16[32,8,128]{2,1,0:T(8,128)(2,1)}), bf16[32,8,128]{2,1,0:T(8,128)(2,1)S(1)}, u32[]{:S(2)}, u32[]{:S(2)}) %all-to-all-start.1) | async-done | bytes 65568 | tf_op jit(solution)/shard_map/all_to_all | solution.py:297
  67.4 2.6 %collective-permute-start.6 = (bf16[128,128]{1,0:T(8,128)(2,1)S(1)}, bf16[128,128]{1,0:T(8,128)(2,1)S(1)}, u32[]{:S(2)}, u32[]{:S(2)}) collective-permute-start(bf16[128,128]{1,0:T(8,128)(2,1)S(1)} %fusion.7), channel_id=1, source_target_pairs={{8,0},{9,1},{10,2},{11,3},{12,4},{13,5},{14,6},{15,7},{0,8},{1,9},... | collective-permute-start | bytes 98312 | tf_op jit(solution)/shard_map/ppermute | solution.py:39
  70.0 3.0 %shard_map.111 = (bf16[64,768]{1,0:T(8,128)(2,1)S(1)}, bf16[256,768]{1,0:T(8,128)(2,1)S(1)}, f32[12,128,128]{2,1,0:T(8,128)S(1)}) custom-call(s32[1]{0:T(128)} %bitcast.half, bf16[24,2,32,128]{3,2,1,0:T(8,128)(2,1)S(1)} %maximum_select_fusion.refs_0_.refs_3_, bf16[24,1,32,128]{3,2,1,0:T(8,128)(2,1)S(1)} %collective-permute-done.2.refs_1_.refs_4_, ...), custom_call_target="tpu_custom_call" | custom-call | tf_op jit(solution)/shard_map/pallas_call | solution.py:22
  73.1 2.2 %collective-permute-start.4 = (bf16[64,768]{1,0:T(8,128)(2,1)S(1)}, bf16[64,768]{1,0:T(8,128)(2,1)S(1)}, u32[]{:S(2)}, u32[]{:S(2)}) collective-permute-start(bf16[64,768]{1,0:T(8,128)(2,1)S(1)} %get-tuple-element.32.refs_0_), channel_id=1, source_target_pairs={{0,16},{1,17},{2,18},{3,19},{4,20},{5,21},{6,22},{7,23},{8,24},{9,... | collective-permute-start | bytes 294920 | tf_op jit(solution)/shard_map/ppermute | solution.py:39
  75.3 1.3 collective-permute-start.5
  76.9 3.7 %collective-permute-done.5.refs_2_ = bf16[64,768]{1,0:T(8,128)(2,1)S(1)} collective-permute-done((bf16[64,768]{1,0:T(8,128)(2,1)S(1)}, bf16[64,768]{1,0:T(8,128)(2,1)S(1)}, u32[]{:S(2)}, u32[]{:S(2)}) %collective-permute-start.5) | collective-permute-done | bytes 98336 | tf_op jit(solution)/shard_map/ppermute | solution.py:39
  80.6 0.7 shard_map.112
  81.3 2.4 %collective-permute-start.7 = (bf16[64,768]{1,0:T(8,128)(2,1)S(1)}, bf16[64,768]{1,0:T(8,128)(2,1)S(1)}, u32[]{:S(2)}, u32[]{:S(2)}) collective-permute-start(bf16[64,768]{1,0:T(8,128)(2,1)S(1)} %get-tuple-element.36.refs_3_.refs_0_), channel_id=1, source_target_pairs={{0,16},{1,17},{2,18},{3,19},{4,20},{5,21},{6,22},{7,23},{8,24},{9,... | collective-permute-start | bytes 294920 | tf_op jit(solution)/shard_map/ppermute | solution.py:39
  83.6 1.3 collective-permute-start.8
  85.1 0.6 shard_map.113.refs_11_
  85.7 3.3 %collective-permute-done.8.refs_2_ = bf16[64,768]{1,0:T(8,128)(2,1)S(1)} collective-permute-done((bf16[64,768]{1,0:T(8,128)(2,1)S(1)}, bf16[64,768]{1,0:T(8,128)(2,1)S(1)}, u32[]{:S(2)}, u32[]{:S(2)}) %collective-permute-start.8) | collective-permute-done | bytes 98336 | tf_op jit(solution)/shard_map/ppermute | solution.py:39
  89.0 3.1 %shard_map.114 = (bf16[24,2,32,128]{3,2,1,0:T(8,128)(2,1)S(1)}, bf16[1280,128]{1,0:T(8,128)(2,1)S(1)}) custom-call(s32[1]{0:T(128)} %bitcast.half, bf16[64,768]{1,0:T(8,128)(2,1)S(1)} %get-tuple-element.36.refs_3_.refs_0_, bf16[64,768]{1,0:T(8,128)(2,1)S(1)} %collective-permute-done.7.refs_1_, bf16[64,768]{1,0:T(8,128)(2,1)S(1)} %collective-permute-done.8.refs_2_, ...), custom_call_target="tpu_custom_call" | custom-call | tf_op jit(solution)/shard_map/pallas_call | solution.py:22
  92.1 0.8 pad_maximum_fusion
  92.9 16.4 %all-to-all-start.2 = ((bf16[32,56,128]{2,1,0:T(8,128)(2,1)}), bf16[32,56,128]{2,1,0:T(8,128)(2,1)S(1)}, u32[]{:S(2)}, u32[]{:S(2)}) async-start(bf16[32,56,128]{2,1,0:T(8,128)(2,1)} %pad_maximum_fusion), calls=%async_computation.2 | async-start | bytes 917504 | tf_op jit(solution)/shard_map/all_to_all | solution.py:297
  109.3 1.3 collective-permute-start.10
  110.6 4.0 %collective-permute-start.9 = (bf16[24,1,32,128]{3,2,1,0:T(8,128)(2,1)S(1)}, bf16[24,1,32,128]{3,2,1,0:T(8,128)(2,1)S(1)}, u32[]{:S(2)}, u32[]{:S(2)}) collective-permute-start(bf16[24,1,32,128]{3,2,1,0:T(8,128)(2,1)S(1)} %get-tuple-element.61), channel_id=1, source_target_pairs={{0,16},{1,17},{2,18},{3,19},{4,20},{5,21},{6,22},{7,23},{8,24},{9,... | collective-permute-start | bytes 589832 | tf_op jit(solution)/shard_map/ppermute | solution.py:39
  114.8 6.6 %collective-permute-done.10.refs_2_ = bf16[24,1,32,128]{3,2,1,0:T(8,128)(2,1)S(1)} collective-permute-done((bf16[24,1,32,128]{3,2,1,0:T(8,128)(2,1)S(1)}, bf16[24,1,32,128]{3,2,1,0:T(8,128)(2,1)S(1)}, u32[]{:S(2)}, u32[]{:S(2)}) %collective-permute-start.10) | collective-permute-done | bytes 196640 | tf_op jit(solution)/shard_map/ppermute | solution.py:39
  121.4 0.8 shard_map.115
  122.5 0.7 pad_maximum_fusion.1
  123.2 12.0 %all-to-all-start.3 = ((bf16[16,72,128]{2,1,0:T(8,128)(2,1)}), bf16[16,72,128]{2,1,0:T(8,128)(2,1)S(1)}, u32[]{:S(2)}, u32[]{:S(2)}) async-start(bf16[16,72,128]{2,1,0:T(8,128)(2,1)} %pad_maximum_fusion.1), calls=%async_computation.3 | async-start | bytes 589824 | tf_op jit(solution)/shard_map/all_to_all | solution.py:297
  135.3 12.0 %collective-permute-start.11 = (bf16[2,2,2,2,32,128]{5,4,3,2,1,0:T(8,128)(2,1)S(1)}, bf16[2,2,2,2,32,128]{5,4,3,2,1,0:T(8,128)(2,1)S(1)}, u32[]{:S(2)}, u32[]{:S(2)}) collective-permute-start(bf16[2,2,2,2,32,128]{5,4,3,2,1,0:T(8,128)(2,1)S(1)} %fusion), channel_id=1, source_target_pairs={{0,2},{1,3},{2,0},{3,1},{4,6},{5,7},{6,4},{7,5},{8,10},{9,11},{10,... | collective-permute-start | bytes 393224 | tf_op jit(solution)/shard_map/ppermute | solution.py:379
  147.3 4.7 %all-to-all-done.3 = bf16[16,72,128]{2,1,0:T(8,128)(2,1)S(1)} async-done(((bf16[16,72,128]{2,1,0:T(8,128)(2,1)}), bf16[16,72,128]{2,1,0:T(8,128)(2,1)S(1)}, u32[]{:S(2)}, u32[]{:S(2)}) %all-to-all-start.3) | async-done | bytes 294944 | tf_op jit(solution)/shard_map/all_to_all | solution.py:297
  152.0 0.9 broadcast_in_dim.8
  152.9 14.6 %all-to-all-start.4 = ((f32[32,40,128]{2,1,0:T(8,128)}), f32[32,40,128]{2,1,0:T(8,128)S(1)}, u32[]{:S(2)}, u32[]{:S(2)}) async-start(f32[32,40,128]{2,1,0:T(8,128)} %broadcast_in_dim.8), calls=%async_computation.4 | async-start | bytes 1310720 | tf_op jit(solution)/shard_map/all_to_all | solution.py:297
  167.7 0.6 slice_select_fusion.1
  168.3 1.7 shard_map.116
  170.1 10.4 %all-to-all-done.4 = f32[32,40,128]{2,1,0:T(8,128)S(1)} async-done(((f32[32,40,128]{2,1,0:T(8,128)}), f32[32,40,128]{2,1,0:T(8,128)S(1)}, u32[]{:S(2)}, u32[]{:S(2)}) %all-to-all-start.4) | async-done | bytes 655392 | tf_op jit(solution)/shard_map/all_to_all | solution.py:297
  180.5 0.5 reshape.161
  181.7 0.7 copy.60
  182.4 3.9 %all-to-all-start.5 = ((bf16[4,2,2,2,32,128]{5,4,3,2,1,0:T(8,128)(2,1)}), bf16[4,2,2,2,32,128]{5,4,3,2,1,0:T(8,128)(2,1)S(1)}, u32[]{:S(2)}, u32[]{:S(2)}) async-start(bf16[4,2,2,2,32,128]{5,4,3,2,1,0:T(8,128)(2,1)} %bitcast.46), calls=%async_computation.5 | async-start | bytes 524288 | tf_op jit(solution)/shard_map/all_to_all | solution.py:297
  186.5 0.7 copy.64
  187.2 1.0 maximum_multiply_fusion
  188.2 0.8 slice_multiply_fusion
  189.0 2.5 %all-to-all-done.5 = bf16[4,2,2,2,32,128]{5,4,3,2,1,0:T(8,128)(2,1)S(1)} async-done(((bf16[4,2,2,2,32,128]{5,4,3,2,1,0:T(8,128)(2,1)}), bf16[4,2,2,2,32,128]{5,4,3,2,1,0:T(8,128)(2,1)S(1)}, u32[]{:S(2)}, u32[]{:S(2)}) %all-to-all-start.5) | async-done | bytes 262176 | tf_op jit(solution)/shard_map/all_to_all | solution.py:297
  191.5 0.9 copy.68
  (70 shorter events, 3.3 us)
Async XLA Ops:
  0.6 31.3 %copy-start.2 = (bf16[27,64,64]{2,1,0:T(8,128)(2,1)S(1)}, bf16[27,64,64]{2,1,0:T(8,128)(2,1)}, u32[]{:S(2)}) copy-start(bf16[27,64,64]{2,1,0:T(8,128)(2,1)} %param.10) | copy-start | bytes 663556
  0.6 35.0 %all-to-all-start = ((bf16[8,2,2,32,128]{4,2,1,3,0:T(2,128)(2,1)}), bf16[8,2,2,32,128]{4,2,1,3,0:T(2,128)(2,1)S(1)}, u32[]{:S(2)}, u32[]{:S(2)}) async-start(bf16[8,2,2,32,128]{4,2,1,3,0:T(2,128)(2,1)} %bitcast.146), calls=%async_computation | async-start | bytes 524288 | tf_op jit(solution)/shard_map/all_to_all | solution.py:297
  18.3 13.6 %copy-start.4 = (bf16[8,64,32]{1,2,0:T(8,128)(2,1)S(1)}, bf16[8,64,32]{1,2,0:T(8,128)(2,1)}, u32[]{:S(2)}) copy-start(bf16[8,64,32]{1,2,0:T(8,128)(2,1)} %param.9) | copy-start | bytes 98308
  19.9 21.7 %collective-permute-start = (bf16[256,128]{1,0:T(8,128)(2,1)}, bf16[256,128]{1,0:T(8,128)(2,1)}, u32[]{:S(2)}, u32[]{:S(2)}) collective-permute-start(bf16[256,128]{1,0:T(8,128)(2,1)} %shard_map.110), channel_id=1, source_target_pairs={{0,71},{1,135},{2,199},{3,263},{4,327},{5,391},{6,455},{7,7},{8,79... | collective-permute-start | bytes 196616 | tf_op jit(solution)/shard_map/ppermute | solution.py:316
  34.0 0.9 copy-start.3
  41.6 14.5 %collective-permute-start.1 = (bf16[8,2,32,128]{3,2,1,0:T(8,128)(2,1)S(1)}, bf16[8,2,32,128]{3,2,1,0:T(8,128)(2,1)S(1)}, u32[]{:S(2)}, u32[]{:S(2)}) collective-permute-start(bf16[8,2,32,128]{3,2,1,0:T(8,128)(2,1)S(1)} %slice_select_fusion), channel_id=1, source_target_pairs={{8,0},{9,1},{10,2},{11,3},{12,4},{13,5},{14,6},{15,7},{0,8},{1,9},... | collective-permute-start | bytes 393224 | tf_op jit(solution)/shard_map/ppermute | solution.py:39
  46.0 21.4 %all-to-all-start.1 = ((bf16[32,8,128]{2,1,0:T(8,128)(2,1)}), bf16[32,8,128]{2,1,0:T(8,128)(2,1)S(1)}, u32[]{:S(2)}, u32[]{:S(2)}) async-start(bf16[32,8,128]{2,1,0:T(8,128)(2,1)} %bitcast.4), calls=%async_computation.1 | async-start | bytes 131072 | tf_op jit(solution)/shard_map/all_to_all | solution.py:297
  56.2 13.8 %collective-permute-start.2 = (bf16[24,1,32,128]{3,2,1,0:T(8,128)(2,1)S(1)}, bf16[24,1,32,128]{3,2,1,0:T(8,128)(2,1)S(1)}, u32[]{:S(2)}, u32[]{:S(2)}) collective-permute-start(bf16[24,1,32,128]{3,2,1,0:T(8,128)(2,1)S(1)} %get-tuple-element.63), channel_id=1, source_target_pairs={{0,16},{1,17},{2,18},{3,19},{4,20},{5,21},{6,22},{7,23},{8,24},{9,... | collective-permute-start | bytes 589832 | tf_op jit(solution)/shard_map/ppermute | solution.py:39
  59.4 10.6 %collective-permute-start.3 = (bf16[24,1,32,128]{3,2,1,0:T(8,128)(2,1)S(1)}, bf16[24,1,32,128]{3,2,1,0:T(8,128)(2,1)S(1)}, u32[]{:S(2)}, u32[]{:S(2)}) collective-permute-start(bf16[24,1,32,128]{3,2,1,0:T(8,128)(2,1)S(1)} %get-tuple-element.62), channel_id=1, source_target_pairs={{16,0},{17,1},{18,2},{19,3},{20,4},{21,5},{22,6},{23,7},{24,8},{25... | collective-permute-start | bytes 589832 | tf_op jit(solution)/shard_map/ppermute | solution.py:39
  67.4 2.6 %copy-start.1 = (bf16[256,256]{1,0:T(8,128)(2,1)S(1)}, bf16[256,256]{1,0:T(8,128)(2,1)}, u32[]{:S(2)}) copy-start(bf16[256,256]{1,0:T(8,128)(2,1)} %constant.119.clone.refs_5_) | copy-start | bytes 393220
  67.4 9.2 %collective-permute-start.6 = (bf16[128,128]{1,0:T(8,128)(2,1)S(1)}, bf16[128,128]{1,0:T(8,128)(2,1)S(1)}, u32[]{:S(2)}, u32[]{:S(2)}) collective-permute-start(bf16[128,128]{1,0:T(8,128)(2,1)S(1)} %fusion.7), channel_id=1, source_target_pairs={{8,0},{9,1},{10,2},{11,3},{12,4},{13,5},{14,6},{15,7},{0,8},{1,9},... | collective-permute-start | bytes 98312 | tf_op jit(solution)/shard_map/ppermute | solution.py:39
  73.1 3.8 %collective-permute-start.4 = (bf16[64,768]{1,0:T(8,128)(2,1)S(1)}, bf16[64,768]{1,0:T(8,128)(2,1)S(1)}, u32[]{:S(2)}, u32[]{:S(2)}) collective-permute-start(bf16[64,768]{1,0:T(8,128)(2,1)S(1)} %get-tuple-element.32.refs_0_), channel_id=1, source_target_pairs={{0,16},{1,17},{2,18},{3,19},{4,20},{5,21},{6,22},{7,23},{8,24},{9,... | collective-permute-start | bytes 294920 | tf_op jit(solution)/shard_map/ppermute | solution.py:39
  75.3 5.4 %collective-permute-start.5 = (bf16[64,768]{1,0:T(8,128)(2,1)S(1)}, bf16[64,768]{1,0:T(8,128)(2,1)S(1)}, u32[]{:S(2)}, u32[]{:S(2)}) collective-permute-start(bf16[64,768]{1,0:T(8,128)(2,1)S(1)} %get-tuple-element.32.refs_0_), channel_id=1, source_target_pairs={{16,0},{17,1},{18,2},{19,3},{20,4},{21,5},{22,6},{23,7},{24,8},{25... | collective-permute-start | bytes 294920 | tf_op jit(solution)/shard_map/ppermute | solution.py:39
  81.3 4.4 %collective-permute-start.7 = (bf16[64,768]{1,0:T(8,128)(2,1)S(1)}, bf16[64,768]{1,0:T(8,128)(2,1)S(1)}, u32[]{:S(2)}, u32[]{:S(2)}) collective-permute-start(bf16[64,768]{1,0:T(8,128)(2,1)S(1)} %get-tuple-element.36.refs_3_.refs_0_), channel_id=1, source_target_pairs={{0,16},{1,17},{2,18},{3,19},{4,20},{5,21},{6,22},{7,23},{8,24},{9,... | collective-permute-start | bytes 294920 | tf_op jit(solution)/shard_map/ppermute | solution.py:39
  83.6 5.4 %collective-permute-start.8 = (bf16[64,768]{1,0:T(8,128)(2,1)S(1)}, bf16[64,768]{1,0:T(8,128)(2,1)S(1)}, u32[]{:S(2)}, u32[]{:S(2)}) collective-permute-start(bf16[64,768]{1,0:T(8,128)(2,1)S(1)} %get-tuple-element.36.refs_3_.refs_0_), channel_id=1, source_target_pairs={{16,0},{17,1},{18,2},{19,3},{20,4},{21,5},{22,6},{23,7},{24,8},{25... | collective-permute-start | bytes 294920 | tf_op jit(solution)/shard_map/ppermute | solution.py:39
  85.1 4.0 %copy-start = (bf16[256,256]{1,0:T(8,128)(2,1)S(1)}, bf16[256,256]{1,0:T(8,128)(2,1)}, u32[]{:S(2)}) copy-start(bf16[256,256]{1,0:T(8,128)(2,1)} %constant.120.clone.refs_8_) | copy-start | bytes 393220
  92.9 29.3 %all-to-all-start.2 = ((bf16[32,56,128]{2,1,0:T(8,128)(2,1)}), bf16[32,56,128]{2,1,0:T(8,128)(2,1)S(1)}, u32[]{:S(2)}, u32[]{:S(2)}) async-start(bf16[32,56,128]{2,1,0:T(8,128)(2,1)} %pad_maximum_fusion), calls=%async_computation.2 | async-start | bytes 917504 | tf_op jit(solution)/shard_map/all_to_all | solution.py:297
  109.3 12.1 %collective-permute-start.10 = (bf16[24,1,32,128]{3,2,1,0:T(8,128)(2,1)S(1)}, bf16[24,1,32,128]{3,2,1,0:T(8,128)(2,1)S(1)}, u32[]{:S(2)}, u32[]{:S(2)}) collective-permute-start(bf16[24,1,32,128]{3,2,1,0:T(8,128)(2,1)S(1)} %get-tuple-element.60), channel_id=1, source_target_pairs={{16,0},{17,1},{18,2},{19,3},{20,4},{21,5},{22,6},{23,7},{24,8},{25... | collective-permute-start | bytes 589832 | tf_op jit(solution)/shard_map/ppermute | solution.py:39
  110.6 10.8 %collective-permute-start.9 = (bf16[24,1,32,128]{3,2,1,0:T(8,128)(2,1)S(1)}, bf16[24,1,32,128]{3,2,1,0:T(8,128)(2,1)S(1)}, u32[]{:S(2)}, u32[]{:S(2)}) collective-permute-start(bf16[24,1,32,128]{3,2,1,0:T(8,128)(2,1)S(1)} %get-tuple-element.61), channel_id=1, source_target_pairs={{0,16},{1,17},{2,18},{3,19},{4,20},{5,21},{6,22},{7,23},{8,24},{9,... | collective-permute-start | bytes 589832 | tf_op jit(solution)/shard_map/ppermute | solution.py:39
  123.2 28.8 %all-to-all-start.3 = ((bf16[16,72,128]{2,1,0:T(8,128)(2,1)}), bf16[16,72,128]{2,1,0:T(8,128)(2,1)S(1)}, u32[]{:S(2)}, u32[]{:S(2)}) async-start(bf16[16,72,128]{2,1,0:T(8,128)(2,1)} %pad_maximum_fusion.1), calls=%async_computation.3 | async-start | bytes 589824 | tf_op jit(solution)/shard_map/all_to_all | solution.py:297
  135.3 32.3 %collective-permute-start.11 = (bf16[2,2,2,2,32,128]{5,4,3,2,1,0:T(8,128)(2,1)S(1)}, bf16[2,2,2,2,32,128]{5,4,3,2,1,0:T(8,128)(2,1)S(1)}, u32[]{:S(2)}, u32[]{:S(2)}) collective-permute-start(bf16[2,2,2,2,32,128]{5,4,3,2,1,0:T(8,128)(2,1)S(1)} %fusion), channel_id=1, source_target_pairs={{0,2},{1,3},{2,0},{3,1},{4,6},{5,7},{6,4},{7,5},{8,10},{9,11},{10,... | collective-permute-start | bytes 393224 | tf_op jit(solution)/shard_map/ppermute | solution.py:379
  152.9 27.5 %all-to-all-start.4 = ((f32[32,40,128]{2,1,0:T(8,128)}), f32[32,40,128]{2,1,0:T(8,128)S(1)}, u32[]{:S(2)}, u32[]{:S(2)}) async-start(f32[32,40,128]{2,1,0:T(8,128)} %broadcast_in_dim.8), calls=%async_computation.4 | async-start | bytes 1310720 | tf_op jit(solution)/shard_map/all_to_all | solution.py:297
  182.4 9.1 %all-to-all-start.5 = ((bf16[4,2,2,2,32,128]{5,4,3,2,1,0:T(8,128)(2,1)}), bf16[4,2,2,2,32,128]{5,4,3,2,1,0:T(8,128)(2,1)S(1)}, u32[]{:S(2)}, u32[]{:S(2)}) async-start(bf16[4,2,2,2,32,128]{5,4,3,2,1,0:T(8,128)(2,1)} %bitcast.46), calls=%async_computation.5 | async-start | bytes 524288 | tf_op jit(solution)/shard_map/all_to_all | solution.py:297

commit v3 on v2

--- a/solution.py
+++ b/solution.py
@@ -377,20 +377,30 @@
     kept = jnp.where(near, parts[:, 0], parts[:, 1])
     sent = jnp.where(near, parts[:, 1], parts[:, 0])
     got = lax.ppermute(sent, "sp", [(col, col ^ 2) for col in range(lax.axis_size("sp"))])
-    return jnp.stack([jnp.where(near, kept, got), jnp.where(near, got, kept)], axis=1)
+    return jnp.stack([jnp.where(near, kept, got), jnp.where(near, got, kept)], axis=2)
+
+
+def matched(parts, far, core):
+    if parts.shape[0] > 1:
+        parts = jnp.where(far == 0, parts, parts[::-1])
+    return jnp.where(core == 0, parts, parts[:, ::-1])
 
 
 def near_exchange(parts):
-    cols = lax.axis_size("sp")
-    lead = parts.shape[0]
-    groups = [
-        [start + 4 * far + core for far in range(lead) for core in (0, 1)]
-        for half in range(0, cols, 4 * lead)
-        for start in (half, half + 2)
+    cols, lead = lax.axis_size("sp"), parts.shape[0]
+    place = lax.axis_index("sp")
+    far, core = place // 4 % lead, place % 2
+    parts = matched(parts, far, core)
+    got = [
+        [
+            parts[x, c]
+            if x == c == 0
+            else lax.ppermute(parts[x, c], "sp", [(col, col ^ (4 * x + c)) for col in range(cols)])
+            for c in (0, 1)
+        ]
+        for x in range(lead)
     ]
-    rest = parts.shape[3:]
-    parts = jnp.swapaxes(parts, 1, 2).reshape(2 * lead, 2, *rest)
-    return jnp.swapaxes(trade(parts, "sp", groups).reshape(lead, 2, 2, *rest), 1, 2)
+    return matched(jnp.stack([jnp.stack(row) for row in got]), far, core)
 
 
 def local(features, weight_fine, weight_down, weight_coarse, cotangent):
@@ -420,8 +430,8 @@
     block = (rows, width // 2 // rows, LANES)
     cells = pl.pallas_call(
         pack_kernel, out_shape=shape((width // 2, LANES), BF16), interpret=INTERPRET
-    )(cotangent.reshape(chans3, width))
-    cells = turned(cells).reshape(block)
+    )(turned(cotangent.reshape(chans3, width)))
+    cells = cells.reshape(block)
     matrices = [
         tap_matrix(weight_fine),
         tap_matrix(reversed_taps(weight_fine)),
@@ -500,12 +510,12 @@
     gradient = far_exchange(gradient.reshape(batch // 4, 2, 2, x_cells, y_cells, chans, LANES))
     part = jnp.broadcast_to(part[None], (coarse.shape[0], *part.shape))
     mixed = trade(jnp.concatenate([part, coarse], axis=1), ("grp", "sp"), columns())
-    part = jnp.sum(mixed[:, :kept].astype(F32), axis=0)
+    part = jnp.sum(mixed[:, :kept].astype(F32), axis=0).astype(BF16)
     coarse = from_column(mixed[:, kept:])
-    grads = share(part, ("grp", "sp"), near).reshape(grad_rows, LANES)
+    grads = share(part, ("grp", "sp"), near).reshape(grad_rows, LANES).astype(F32)
+    gradient = near_exchange(gradient)
     grads, gradient = lax.optimization_barrier((grads, gradient))
-    gradient = near_exchange(gradient).reshape(batch, x_cells, y_cells, chans, LANES)
-    grad_input = jnp.transpose(gradient, (0, 3, 1, 2, 4))
+    grad_input = jnp.transpose(gradient, (0, 2, 1, 5, 3, 4, 6)).reshape(features.shape)
 
     result = pl.pallas_call(
         unpack_kernel, out_shape=shape((chans3, width), BF16), interpret=INTERPRET

time: 193 us -> 191 us (0.990)
  starting transfers between devices: 122 us -> 114 us
  waiting for transfers between devices: 44.1 us -> 47.2 us
  local copies, waits for them, and re-layouts: 9.11 us -> 11.1 us
    all_to_all x6 -> x5, starting transfers between devices: 74.1 us -> 64.5 us  [trade(): lax.all_to_all(parts, axis, split_axis=0, concat_axis=0, axis_index_group...]
    ppermute x0 -> x3, starting transfers between devices: none -> 9.44 us  [near_exchange(): lax.ppermute(parts[x, c], 'sp', [(col, col ^ 4 * x + c) for col in range(...]
    ppermute x1, starting transfers between devices: 12 us -> 4.4 us  [far_exchange(): lax.ppermute(sent, 'sp', [(col, col ^ 2) for col in range(lax.axis_size('...]
    ppermute x0 -> x3, waiting for transfers between devices: none -> 3.79 us  [near_exchange(): lax.ppermute(parts[x, c], 'sp', [(col, col ^ 4 * x + c) for col in range(...]
    all_to_all x6 -> x5, waiting for transfers between devices: 24.2 us -> 22 us  [trade(): lax.all_to_all(parts, axis, split_axis=0, concat_axis=0, axis_index_group...]
  transfers between devices with their start and end apart: 18 -> 20, of which waited for: 9 -> 10; matrix products, arithmetic and copies ran while one was open for 4% -> 3% of each run, Pallas kernels for 4% -> 4%
where the time goes in v3:
time: 191 us; the launch traced here: 190 us
  starting transfers between devices  114 us (60%)
  waiting for transfers between devices  47.2 us (25%)
  Pallas kernels  11.5 us (6%)
  local copies, waits for them, and re-layouts  11.1 us (6%)
  other arithmetic  4.8 us (3%)
    all_to_all x5, starting transfers between devices, trade(): lax.all_to_all(parts, axis, split_axis=0, concat_axis=0, axis_index_group...  64.5 us
    ppermute x10, starting transfers between devices, arrival(): return lax.ppermute(block, ('grp', 'sp'), pairs)  23.8 us
    all_to_all x5, waiting for transfers between devices, trade(): lax.all_to_all(parts, axis, split_axis=0, concat_axis=0, axis_index_group...  22 us
    ppermute x10, waiting for transfers between devices, arrival(): return lax.ppermute(block, ('grp', 'sp'), pairs)  14 us
    ppermute x1, starting transfers between devices, turned(): return lax.ppermute(block, ('grp', 'sp'), pairs)  12 us
    ppermute x3, starting transfers between devices, near_exchange(): lax.ppermute(parts[x, c], 'sp', [(col, col ^ 4 * x + c) for col in range(...  9.44 us
    pallas_call x5, Pallas kernels, call(): pl.pallas_call(kernel, out_shape=outs, in_specs=[pl.BlockSpec(memory_spac...  8.21 us
    ppermute x1, waiting for transfers between devices, turned(): return lax.ppermute(block, ('grp', 'sp'), pairs)  7.45 us
  transfers between devices with their start and end apart: 20, of which 10 were waited for; matrix products, arithmetic and copies ran while one was open for 3% of the time, Pallas kernels for 4%

profile of v3, /device:TPU:1, one launch (start us, length us, event | category | flops | bytes accessed | tf_op | source)
XLA Modules:
  0.0 190.2 jit_solution(15840673456198717511)
XLA Ops:
  0.7 17.7 %all-to-all-start = ((bf16[8,2,2,32,128]{4,2,1,3,0:T(2,128)(2,1)}), bf16[8,2,2,32,128]{4,2,1,3,0:T(2,128)(2,1)S(1)}, u32[]{:S(2)}, u32[]{:S(2)}) async-start(bf16[8,2,2,32,128]{4,2,1,3,0:T(2,128)(2,1)} %bitcast.157), calls=%async_computation | async-start | bytes 524288 | tf_op jit(solution)/shard_map/all_to_all | solution.py:297
  18.3 12.0 %collective-permute-start = (bf16[64,512]{1,0:T(8,128)(2,1)}, bf16[64,512]{1,0:T(8,128)(2,1)S(1)}, u32[]{:S(2)}, u32[]{:S(2)}) collective-permute-start(bf16[64,512]{1,0:T(8,128)(2,1)} %bitcast.165), channel_id=1, source_target_pairs={{0,71},{1,135},{2,199},{3,263},{4,327},{5,391},{6,455},{7,7},{8,79... | collective-permute-start | bytes 196616 | tf_op jit(solution)/shard_map/ppermute | solution.py:316
  31.2 1.2 copy.57
  34.1 7.4 %collective-permute-done.values = bf16[64,512]{1,0:T(8,128)(2,1)S(1)} collective-permute-done((bf16[64,512]{1,0:T(8,128)(2,1)}, bf16[64,512]{1,0:T(8,128)(2,1)S(1)}, u32[]{:S(2)}, u32[]{:S(2)}) %collective-permute-start) | collective-permute-done | bytes 65568 | tf_op jit(solution)/shard_map/ppermute | solution.py:316
  41.5 0.6 copy-done.6
  42.2 1.6 shard_map.110
  43.8 4.4 %collective-permute-start.1 = (bf16[8,2,32,128]{3,2,1,0:T(8,128)(2,1)S(1)}, bf16[8,2,32,128]{3,2,1,0:T(8,128)(2,1)S(1)}, u32[]{:S(2)}, u32[]{:S(2)}) collective-permute-start(bf16[8,2,32,128]{3,2,1,0:T(8,128)(2,1)S(1)} %slice_select_fusion), channel_id=1, source_target_pairs={{8,0},{9,1},{10,2},{11,3},{12,4},{13,5},{14,6},{15,7},{0,8},{1,9},... | collective-permute-start | bytes 393224 | tf_op jit(solution)/shard_map/ppermute | solution.py:39
  48.2 9.5 %all-to-all-start.1 = ((bf16[32,8,128]{2,1,0:T(8,128)(2,1)}), bf16[32,8,128]{2,1,0:T(8,128)(2,1)S(1)}, u32[]{:S(2)}, u32[]{:S(2)}) async-start(bf16[32,8,128]{2,1,0:T(8,128)(2,1)} %bitcast.4), calls=%async_computation.1 | async-start | bytes 131072 | tf_op jit(solution)/shard_map/all_to_all | solution.py:297
  58.4 3.1 %collective-permute-start.2 = (bf16[24,1,32,128]{3,2,1,0:T(8,128)(2,1)S(1)}, bf16[24,1,32,128]{3,2,1,0:T(8,128)(2,1)S(1)}, u32[]{:S(2)}, u32[]{:S(2)}) collective-permute-start(bf16[24,1,32,128]{3,2,1,0:T(8,128)(2,1)S(1)} %get-tuple-element.58), channel_id=1, source_target_pairs={{0,16},{1,17},{2,18},{3,19},{4,20},{5,21},{6,22},{7,23},{8,24},{9,... | collective-permute-start | bytes 589832 | tf_op jit(solution)/shard_map/ppermute | solution.py:39
  61.6 1.3 collective-permute-start.3
  62.9 6.7 %all-to-all-done.1 = bf16[32,8,128]{2,1,0:T(8,128)(2,1)S(1)} async-done(((bf16[32,8,128]{2,1,0:T(8,128)(2,1)}), bf16[32,8,128]{2,1,0:T(8,128)(2,1)S(1)}, u32[]{:S(2)}, u32[]{:S(2)}) %all-to-all-start.1) | async-done | bytes 65568 | tf_op jit(solution)/shard_map/all_to_all | solution.py:297
  69.6 2.6 %collective-permute-start.6 = (bf16[128,128]{1,0:T(8,128)(2,1)S(1)}, bf16[128,128]{1,0:T(8,128)(2,1)S(1)}, u32[]{:S(2)}, u32[]{:S(2)}) collective-permute-start(bf16[128,128]{1,0:T(8,128)(2,1)S(1)} %fusion.7), channel_id=1, source_target_pairs={{8,0},{9,1},{10,2},{11,3},{12,4},{13,5},{14,6},{15,7},{0,8},{1,9},... | collective-permute-start | bytes 98312 | tf_op jit(solution)/shard_map/ppermute | solution.py:39
  72.2 3.0 %shard_map.111 = (bf16[64,768]{1,0:T(8,128)(2,1)S(1)}, bf16[256,768]{1,0:T(8,128)(2,1)S(1)}, f32[12,128,128]{2,1,0:T(8,128)S(1)}) custom-call(s32[1]{0:T(128)} %bitcast.half, bf16[24,2,32,128]{3,2,1,0:T(8,128)(2,1)S(1)} %maximum_select_fusion.refs_0_.refs_3_, bf16[24,1,32,128]{3,2,1,0:T(8,128)(2,1)S(1)} %collective-permute-done.2.refs_1_.refs_4_, ...), custom_call_target="tpu_custom_call" | custom-call | tf_op jit(solution)/shard_map/pallas_call | solution.py:22
  75.2 2.2 %collective-permute-start.4 = (bf16[64,768]{1,0:T(8,128)(2,1)S(1)}, bf16[64,768]{1,0:T(8,128)(2,1)S(1)}, u32[]{:S(2)}, u32[]{:S(2)}) collective-permute-start(bf16[64,768]{1,0:T(8,128)(2,1)S(1)} %get-tuple-element.32.refs_0_), channel_id=1, source_target_pairs={{0,16},{1,17},{2,18},{3,19},{4,20},{5,21},{6,22},{7,23},{8,24},{9,... | collective-permute-start | bytes 294920 | tf_op jit(solution)/shard_map/ppermute | solution.py:39
  77.4 1.3 collective-permute-start.5
  79.1 3.7 %collective-permute-done.5.refs_2_ = bf16[64,768]{1,0:T(8,128)(2,1)S(1)} collective-permute-done((bf16[64,768]{1,0:T(8,128)(2,1)S(1)}, bf16[64,768]{1,0:T(8,128)(2,1)S(1)}, u32[]{:S(2)}, u32[]{:S(2)}) %collective-permute-start.5) | collective-permute-done | bytes 98336 | tf_op jit(solution)/shard_map/ppermute | solution.py:39
  82.8 0.7 shard_map.112
  83.5 2.4 %collective-permute-start.7 = (bf16[64,768]{1,0:T(8,128)(2,1)S(1)}, bf16[64,768]{1,0:T(8,128)(2,1)S(1)}, u32[]{:S(2)}, u32[]{:S(2)}) collective-permute-start(bf16[64,768]{1,0:T(8,128)(2,1)S(1)} %get-tuple-element.36.refs_3_.refs_0_), channel_id=1, source_target_pairs={{0,16},{1,17},{2,18},{3,19},{4,20},{5,21},{6,22},{7,23},{8,24},{9,... | collective-permute-start | bytes 294920 | tf_op jit(solution)/shard_map/ppermute | solution.py:39
  85.8 1.3 collective-permute-start.8
  87.2 0.6 shard_map.113.refs_11_
  87.8 3.3 %collective-permute-done.8.refs_2_ = bf16[64,768]{1,0:T(8,128)(2,1)S(1)} collective-permute-done((bf16[64,768]{1,0:T(8,128)(2,1)S(1)}, bf16[64,768]{1,0:T(8,128)(2,1)S(1)}, u32[]{:S(2)}, u32[]{:S(2)}) %collective-permute-start.8) | collective-permute-done | bytes 98336 | tf_op jit(solution)/shard_map/ppermute | solution.py:39
  91.2 3.1 %shard_map.114 = (bf16[24,2,32,128]{3,2,1,0:T(8,128)(2,1)S(1)}, bf16[1280,128]{1,0:T(8,128)(2,1)S(1)}) custom-call(s32[1]{0:T(128)} %bitcast.half, bf16[64,768]{1,0:T(8,128)(2,1)S(1)} %get-tuple-element.36.refs_3_.refs_0_, bf16[64,768]{1,0:T(8,128)(2,1)S(1)} %collective-permute-done.7.refs_1_, bf16[64,768]{1,0:T(8,128)(2,1)S(1)} %collective-permute-done.8.refs_2_, ...), custom_call_target="tpu_custom_call" | custom-call | tf_op jit(solution)/shard_map/pallas_call | solution.py:22
  94.3 0.8 pad_maximum_fusion
  95.1 16.3 %all-to-all-start.2 = ((bf16[32,56,128]{2,1,0:T(8,128)(2,1)}), bf16[32,56,128]{2,1,0:T(8,128)(2,1)S(1)}, u32[]{:S(2)}, u32[]{:S(2)}) async-start(bf16[32,56,128]{2,1,0:T(8,128)(2,1)} %pad_maximum_fusion), calls=%async_computation.2 | async-start | bytes 917504 | tf_op jit(solution)/shard_map/all_to_all | solution.py:297
  111.5 1.3 collective-permute-start.10
  112.8 4.0 %collective-permute-start.9 = (bf16[24,1,32,128]{3,2,1,0:T(8,128)(2,1)S(1)}, bf16[24,1,32,128]{3,2,1,0:T(8,128)(2,1)S(1)}, u32[]{:S(2)}, u32[]{:S(2)}) collective-permute-start(bf16[24,1,32,128]{3,2,1,0:T(8,128)(2,1)S(1)} %get-tuple-element.56), channel_id=1, source_target_pairs={{0,16},{1,17},{2,18},{3,19},{4,20},{5,21},{6,22},{7,23},{8,24},{9,... | collective-permute-start | bytes 589832 | tf_op jit(solution)/shard_map/ppermute | solution.py:39
  117.0 6.6 %collective-permute-done.10.refs_2_ = bf16[24,1,32,128]{3,2,1,0:T(8,128)(2,1)S(1)} collective-permute-done((bf16[24,1,32,128]{3,2,1,0:T(8,128)(2,1)S(1)}, bf16[24,1,32,128]{3,2,1,0:T(8,128)(2,1)S(1)}, u32[]{:S(2)}, u32[]{:S(2)}) %collective-permute-start.10) | collective-permute-done | bytes 196640 | tf_op jit(solution)/shard_map/ppermute | solution.py:39
  123.6 0.8 shard_map.115
  124.7 4.4 %collective-permute-start.11 = (bf16[2,2,2,2,32,128]{5,4,3,2,1,0:T(8,128)(2,1)S(1)}, bf16[2,2,2,2,32,128]{5,4,3,2,1,0:T(8,128)(2,1)S(1)}, u32[]{:S(2)}, u32[]{:S(2)}) collective-permute-start(bf16[2,2,2,2,32,128]{5,4,3,2,1,0:T(8,128)(2,1)S(1)} %fusion), channel_id=1, source_target_pairs={{0,2},{1,3},{2,0},{3,1},{4,6},{5,7},{6,4},{7,5},{8,10},{9,11},{10,... | collective-permute-start | bytes 393224 | tf_op jit(solution)/shard_map/ppermute | solution.py:379
  129.1 0.7 pad_maximum_fusion.1
  129.9 14.6 %all-to-all-start.3 = ((bf16[16,72,128]{2,1,0:T(8,128)(2,1)}), bf16[16,72,128]{2,1,0:T(8,128)(2,1)S(1)}, u32[]{:S(2)}, u32[]{:S(2)}) async-start(bf16[16,72,128]{2,1,0:T(8,128)(2,1)} %pad_maximum_fusion.1), calls=%async_computation.3 | async-start | bytes 589824 | tf_op jit(solution)/shard_map/all_to_all | solution.py:297
  144.8 4.0 %collective-permute-start.12 = (bf16[2,2,2,32,128]{4,3,2,1,0:T(8,128)(2,1)S(1)}, bf16[2,2,2,32,128]{4,3,2,1,0:T(8,128)(2,1)S(1)}, u32[]{:S(2)}, u32[]{:S(2)}) collective-permute-start(bf16[2,2,2,32,128]{4,3,2,1,0:T(8,128)(2,1)S(1)} %get-tuple-element.60), channel_id=1, source_target_pairs={{0,1},{1,0},{2,3},{3,2},{4,5},{5,4},{6,7},{7,6},{8,9},{9,8},{10,11... | collective-permute-start | bytes 196616 | tf_op jit(solution)/shard_map/ppermute | solution.py:398
  148.8 3.1 %collective-permute-start.13 = (bf16[2,2,2,32,128]{4,3,2,1,0:T(8,128)(2,1)S(1)}, bf16[2,2,2,32,128]{4,3,2,1,0:T(8,128)(2,1)S(1)}, u32[]{:S(2)}, u32[]{:S(2)}) collective-permute-start(bf16[2,2,2,32,128]{4,3,2,1,0:T(8,128)(2,1)S(1)} %get-tuple-element.62), channel_id=1, source_target_pairs={{0,4},{1,5},{2,6},{3,7},{4,0},{5,1},{6,2},{7,3},{8,12},{9,13},{10,... | collective-permute-start | bytes 196616 | tf_op jit(solution)/shard_map/ppermute | solution.py:398
  151.9 2.4 %collective-permute-start.14 = (bf16[2,2,2,32,128]{4,3,2,1,0:T(8,128)(2,1)S(1)}, bf16[2,2,2,32,128]{4,3,2,1,0:T(8,128)(2,1)S(1)}, u32[]{:S(2)}, u32[]{:S(2)}) collective-permute-start(bf16[2,2,2,32,128]{4,3,2,1,0:T(8,128)(2,1)S(1)} %get-tuple-element.61), channel_id=1, source_target_pairs={{0,5},{1,4},{2,7},{3,6},{4,1},{5,0},{6,3},{7,2},{8,13},{9,12},{10,... | collective-permute-start | bytes 196616 | tf_op jit(solution)/shard_map/ppermute | solution.py:398
  154.4 3.7 %collective-permute-done.14 = bf16[2,2,2,32,128]{4,3,2,1,0:T(8,128)(2,1)S(1)} collective-permute-done((bf16[2,2,2,32,128]{4,3,2,1,0:T(8,128)(2,1)S(1)}, bf16[2,2,2,32,128]{4,3,2,1,0:T(8,128)(2,1)S(1)}, u32[]{:S(2)}, u32[]{:S(2)}) %collective-permute-start.14) | collective-permute-done | bytes 65568 | tf_op jit(solution)/shard_map/ppermute | solution.py:398
  158.2 8.2 %all-to-all-done.3 = bf16[16,72,128]{2,1,0:T(8,128)(2,1)S(1)} async-done(((bf16[16,72,128]{2,1,0:T(8,128)(2,1)}), bf16[16,72,128]{2,1,0:T(8,128)(2,1)S(1)}, u32[]{:S(2)}, u32[]{:S(2)}) %all-to-all-start.3) | async-done | bytes 294944 | tf_op jit(solution)/shard_map/all_to_all | solution.py:297
  166.4 0.8 broadcast_in_dim.8
  167.2 6.3 %all-to-all-start.4 = ((bf16[32,40,128]{2,1,0:T(8,128)(2,1)}), bf16[32,40,128]{2,1,0:T(8,128)(2,1)S(1)}, u32[]{:S(2)}, u32[]{:S(2)}) async-start(bf16[32,40,128]{2,1,0:T(8,128)(2,1)} %broadcast_in_dim.8), calls=%async_computation.4 | async-start | bytes 655360 | tf_op jit(solution)/shard_map/all_to_all | solution.py:297
  173.6 0.6 slice_select_fusion.1
  174.3 1.7 shard_map.116
  176.0 7.1 %all-to-all-done.4 = bf16[32,40,128]{2,1,0:T(8,128)(2,1)S(1)} async-done(((bf16[32,40,128]{2,1,0:T(8,128)(2,1)}), bf16[32,40,128]{2,1,0:T(8,128)(2,1)S(1)}, u32[]{:S(2)}, u32[]{:S(2)}) %all-to-all-start.4) | async-done | bytes 327712 | tf_op jit(solution)/shard_map/all_to_all | solution.py:297
  183.2 0.8 copy-done.2
  184.6 0.7 slice-done
  185.5 0.7 slice-done.1
  186.5 0.8 slice_multiply_fusion
  187.6 0.7 copy.79
  188.3 0.9 copy.76
  189.2 1.0 maximum_multiply_fusion
  (87 shorter events, 5.9 us)
Async XLA Ops:
  0.6 29.7 %copy-start.3 = (bf16[27,64,64]{2,1,0:T(8,128)(2,1)S(1)}, bf16[27,64,64]{2,1,0:T(8,128)(2,1)}, u32[]{:S(2)}) copy-start(bf16[27,64,64]{2,1,0:T(8,128)(2,1)} %param.10) | copy-start | bytes 663556
  0.6 29.7 %copy-start.5 = (bf16[8,64,32]{1,2,0:T(8,128)(2,1)S(1)}, bf16[8,64,32]{1,2,0:T(8,128)(2,1)}, u32[]{:S(2)}) copy-start(bf16[8,64,32]{1,2,0:T(8,128)(2,1)} %param.9) | copy-start | bytes 98308
  0.7 43.1 %all-to-all-start = ((bf16[8,2,2,32,128]{4,2,1,3,0:T(2,128)(2,1)}), bf16[8,2,2,32,128]{4,2,1,3,0:T(2,128)(2,1)S(1)}, u32[]{:S(2)}, u32[]{:S(2)}) async-start(bf16[8,2,2,32,128]{4,2,1,3,0:T(2,128)(2,1)} %bitcast.157), calls=%async_computation | async-start | bytes 524288 | tf_op jit(solution)/shard_map/all_to_all | solution.py:297
  18.3 23.2 %collective-permute-start = (bf16[64,512]{1,0:T(8,128)(2,1)}, bf16[64,512]{1,0:T(8,128)(2,1)S(1)}, u32[]{:S(2)}, u32[]{:S(2)}) collective-permute-start(bf16[64,512]{1,0:T(8,128)(2,1)} %bitcast.165), channel_id=1, source_target_pairs={{0,71},{1,135},{2,199},{3,263},{4,327},{5,391},{6,455},{7,7},{8,79... | collective-permute-start | bytes 196616 | tf_op jit(solution)/shard_map/ppermute | solution.py:316
  32.4 0.9 copy-start.4
  41.5 0.6 copy-start.6
  43.8 14.5 %collective-permute-start.1 = (bf16[8,2,32,128]{3,2,1,0:T(8,128)(2,1)S(1)}, bf16[8,2,32,128]{3,2,1,0:T(8,128)(2,1)S(1)}, u32[]{:S(2)}, u32[]{:S(2)}) collective-permute-start(bf16[8,2,32,128]{3,2,1,0:T(8,128)(2,1)S(1)} %slice_select_fusion), channel_id=1, source_target_pairs={{8,0},{9,1},{10,2},{11,3},{12,4},{13,5},{14,6},{15,7},{0,8},{1,9},... | collective-permute-start | bytes 393224 | tf_op jit(solution)/shard_map/ppermute | solution.py:39
  48.2 21.4 %all-to-all-start.1 = ((bf16[32,8,128]{2,1,0:T(8,128)(2,1)}), bf16[32,8,128]{2,1,0:T(8,128)(2,1)S(1)}, u32[]{:S(2)}, u32[]{:S(2)}) async-start(bf16[32,8,128]{2,1,0:T(8,128)(2,1)} %bitcast.4), calls=%async_computation.1 | async-start | bytes 131072 | tf_op jit(solution)/shard_map/all_to_all | solution.py:297
  58.4 13.8 %collective-permute-start.2 = (bf16[24,1,32,128]{3,2,1,0:T(8,128)(2,1)S(1)}, bf16[24,1,32,128]{3,2,1,0:T(8,128)(2,1)S(1)}, u32[]{:S(2)}, u32[]{:S(2)}) collective-permute-start(bf16[24,1,32,128]{3,2,1,0:T(8,128)(2,1)S(1)} %get-tuple-element.58), channel_id=1, source_target_pairs={{0,16},{1,17},{2,18},{3,19},{4,20},{5,21},{6,22},{7,23},{8,24},{9,... | collective-permute-start | bytes 589832 | tf_op jit(solution)/shard_map/ppermute | solution.py:39
  61.6 10.6 %collective-permute-start.3 = (bf16[24,1,32,128]{3,2,1,0:T(8,128)(2,1)S(1)}, bf16[24,1,32,128]{3,2,1,0:T(8,128)(2,1)S(1)}, u32[]{:S(2)}, u32[]{:S(2)}) collective-permute-start(bf16[24,1,32,128]{3,2,1,0:T(8,128)(2,1)S(1)} %get-tuple-element.57), channel_id=1, source_target_pairs={{16,0},{17,1},{18,2},{19,3},{20,4},{21,5},{22,6},{23,7},{24,8},{25... | collective-permute-start | bytes 589832 | tf_op jit(solution)/shard_map/ppermute | solution.py:39
  69.6 2.6 %copy-start.1 = (bf16[256,256]{1,0:T(8,128)(2,1)S(1)}, bf16[256,256]{1,0:T(8,128)(2,1)}, u32[]{:S(2)}) copy-start(bf16[256,256]{1,0:T(8,128)(2,1)} %constant.134.clone.refs_5_) | copy-start | bytes 393220
  69.6 9.1 %collective-permute-start.6 = (bf16[128,128]{1,0:T(8,128)(2,1)S(1)}, bf16[128,128]{1,0:T(8,128)(2,1)S(1)}, u32[]{:S(2)}, u32[]{:S(2)}) collective-permute-start(bf16[128,128]{1,0:T(8,128)(2,1)S(1)} %fusion.7), channel_id=1, source_target_pairs={{8,0},{9,1},{10,2},{11,3},{12,4},{13,5},{14,6},{15,7},{0,8},{1,9},... | collective-permute-start | bytes 98312 | tf_op jit(solution)/shard_map/ppermute | solution.py:39
  75.2 3.8 %collective-permute-start.4 = (bf16[64,768]{1,0:T(8,128)(2,1)S(1)}, bf16[64,768]{1,0:T(8,128)(2,1)S(1)}, u32[]{:S(2)}, u32[]{:S(2)}) collective-permute-start(bf16[64,768]{1,0:T(8,128)(2,1)S(1)} %get-tuple-element.32.refs_0_), channel_id=1, source_target_pairs={{0,16},{1,17},{2,18},{3,19},{4,20},{5,21},{6,22},{7,23},{8,24},{9,... | collective-permute-start | bytes 294920 | tf_op jit(solution)/shard_map/ppermute | solution.py:39
  77.4 5.4 %collective-permute-start.5 = (bf16[64,768]{1,0:T(8,128)(2,1)S(1)}, bf16[64,768]{1,0:T(8,128)(2,1)S(1)}, u32[]{:S(2)}, u32[]{:S(2)}) collective-permute-start(bf16[64,768]{1,0:T(8,128)(2,1)S(1)} %get-tuple-element.32.refs_0_), channel_id=1, source_target_pairs={{16,0},{17,1},{18,2},{19,3},{20,4},{21,5},{22,6},{23,7},{24,8},{25... | collective-permute-start | bytes 294920 | tf_op jit(solution)/shard_map/ppermute | solution.py:39
  83.5 4.4 %collective-permute-start.7 = (bf16[64,768]{1,0:T(8,128)(2,1)S(1)}, bf16[64,768]{1,0:T(8,128)(2,1)S(1)}, u32[]{:S(2)}, u32[]{:S(2)}) collective-permute-start(bf16[64,768]{1,0:T(8,128)(2,1)S(1)} %get-tuple-element.36.refs_3_.refs_0_), channel_id=1, source_target_pairs={{0,16},{1,17},{2,18},{3,19},{4,20},{5,21},{6,22},{7,23},{8,24},{9,... | collective-permute-start | bytes 294920 | tf_op jit(solution)/shard_map/ppermute | solution.py:39
  85.8 5.4 %collective-permute-start.8 = (bf16[64,768]{1,0:T(8,128)(2,1)S(1)}, bf16[64,768]{1,0:T(8,128)(2,1)S(1)}, u32[]{:S(2)}, u32[]{:S(2)}) collective-permute-start(bf16[64,768]{1,0:T(8,128)(2,1)S(1)} %get-tuple-element.36.refs_3_.refs_0_), channel_id=1, source_target_pairs={{16,0},{17,1},{18,2},{19,3},{20,4},{21,5},{22,6},{23,7},{24,8},{25... | collective-permute-start | bytes 294920 | tf_op jit(solution)/shard_map/ppermute | solution.py:39
  87.2 4.0 %copy-start = (bf16[256,256]{1,0:T(8,128)(2,1)S(1)}, bf16[256,256]{1,0:T(8,128)(2,1)}, u32[]{:S(2)}) copy-start(bf16[256,256]{1,0:T(8,128)(2,1)} %constant.135.clone.refs_8_) | copy-start | bytes 393220
  95.1 29.3 %all-to-all-start.2 = ((bf16[32,56,128]{2,1,0:T(8,128)(2,1)}), bf16[32,56,128]{2,1,0:T(8,128)(2,1)S(1)}, u32[]{:S(2)}, u32[]{:S(2)}) async-start(bf16[32,56,128]{2,1,0:T(8,128)(2,1)} %pad_maximum_fusion), calls=%async_computation.2 | async-start | bytes 917504 | tf_op jit(solution)/shard_map/all_to_all | solution.py:297
  111.5 12.1 %collective-permute-start.10 = (bf16[24,1,32,128]{3,2,1,0:T(8,128)(2,1)S(1)}, bf16[24,1,32,128]{3,2,1,0:T(8,128)(2,1)S(1)}, u32[]{:S(2)}, u32[]{:S(2)}) collective-permute-start(bf16[24,1,32,128]{3,2,1,0:T(8,128)(2,1)S(1)} %get-tuple-element.55), channel_id=1, source_target_pairs={{16,0},{17,1},{18,2},{19,3},{20,4},{21,5},{22,6},{23,7},{24,8},{25... | collective-permute-start | bytes 589832 | tf_op jit(solution)/shard_map/ppermute | solution.py:39
  112.8 10.8 %collective-permute-start.9 = (bf16[24,1,32,128]{3,2,1,0:T(8,128)(2,1)S(1)}, bf16[24,1,32,128]{3,2,1,0:T(8,128)(2,1)S(1)}, u32[]{:S(2)}, u32[]{:S(2)}) collective-permute-start(bf16[24,1,32,128]{3,2,1,0:T(8,128)(2,1)S(1)} %get-tuple-element.56), channel_id=1, source_target_pairs={{0,16},{1,17},{2,18},{3,19},{4,20},{5,21},{6,22},{7,23},{8,24},{9,... | collective-permute-start | bytes 589832 | tf_op jit(solution)/shard_map/ppermute | solution.py:39
  124.7 19.8 %collective-permute-start.11 = (bf16[2,2,2,2,32,128]{5,4,3,2,1,0:T(8,128)(2,1)S(1)}, bf16[2,2,2,2,32,128]{5,4,3,2,1,0:T(8,128)(2,1)S(1)}, u32[]{:S(2)}, u32[]{:S(2)}) collective-permute-start(bf16[2,2,2,2,32,128]{5,4,3,2,1,0:T(8,128)(2,1)S(1)} %fusion), channel_id=1, source_target_pairs={{0,2},{1,3},{2,0},{3,1},{4,6},{5,7},{6,4},{7,5},{8,10},{9,11},{10,... | collective-permute-start | bytes 393224 | tf_op jit(solution)/shard_map/ppermute | solution.py:379
  129.9 36.5 %all-to-all-start.3 = ((bf16[16,72,128]{2,1,0:T(8,128)(2,1)}), bf16[16,72,128]{2,1,0:T(8,128)(2,1)S(1)}, u32[]{:S(2)}, u32[]{:S(2)}) async-start(bf16[16,72,128]{2,1,0:T(8,128)(2,1)} %pad_maximum_fusion.1), calls=%async_computation.3 | async-start | bytes 589824 | tf_op jit(solution)/shard_map/all_to_all | solution.py:297
  144.8 9.5 %collective-permute-start.12 = (bf16[2,2,2,32,128]{4,3,2,1,0:T(8,128)(2,1)S(1)}, bf16[2,2,2,32,128]{4,3,2,1,0:T(8,128)(2,1)S(1)}, u32[]{:S(2)}, u32[]{:S(2)}) collective-permute-start(bf16[2,2,2,32,128]{4,3,2,1,0:T(8,128)(2,1)S(1)} %get-tuple-element.60), channel_id=1, source_target_pairs={{0,1},{1,0},{2,3},{3,2},{4,5},{5,4},{6,7},{7,6},{8,9},{9,8},{10,11... | collective-permute-start | bytes 196616 | tf_op jit(solution)/shard_map/ppermute | solution.py:398
  148.8 5.6 %collective-permute-start.13 = (bf16[2,2,2,32,128]{4,3,2,1,0:T(8,128)(2,1)S(1)}, bf16[2,2,2,32,128]{4,3,2,1,0:T(8,128)(2,1)S(1)}, u32[]{:S(2)}, u32[]{:S(2)}) collective-permute-start(bf16[2,2,2,32,128]{4,3,2,1,0:T(8,128)(2,1)S(1)} %get-tuple-element.62), channel_id=1, source_target_pairs={{0,4},{1,5},{2,6},{3,7},{4,0},{5,1},{6,2},{7,3},{8,12},{9,13},{10,... | collective-permute-start | bytes 196616 | tf_op jit(solution)/shard_map/ppermute | solution.py:398
  151.9 6.2 %collective-permute-start.14 = (bf16[2,2,2,32,128]{4,3,2,1,0:T(8,128)(2,1)S(1)}, bf16[2,2,2,32,128]{4,3,2,1,0:T(8,128)(2,1)S(1)}, u32[]{:S(2)}, u32[]{:S(2)}) collective-permute-start(bf16[2,2,2,32,128]{4,3,2,1,0:T(8,128)(2,1)S(1)} %get-tuple-element.61), channel_id=1, source_target_pairs={{0,5},{1,4},{2,7},{3,6},{4,1},{5,0},{6,3},{7,2},{8,13},{9,12},{10,... | collective-permute-start | bytes 196616 | tf_op jit(solution)/shard_map/ppermute | solution.py:398
  167.2 15.9 %all-to-all-start.4 = ((bf16[32,40,128]{2,1,0:T(8,128)(2,1)}), bf16[32,40,128]{2,1,0:T(8,128)(2,1)S(1)}, u32[]{:S(2)}, u32[]{:S(2)}) async-start(bf16[32,40,128]{2,1,0:T(8,128)(2,1)} %broadcast_in_dim.8), calls=%async_computation.4 | async-start | bytes 655360 | tf_op jit(solution)/shard_map/all_to_all | solution.py:297
  183.1 0.8 copy-start.2
  184.5 0.8 slice-start
  185.3 0.9 slice-start.1

commit v4 on v3

--- a/solution.py
+++ b/solution.py
@@ -261,7 +261,11 @@
     grads[:base] = coarse_grad[...]
     grads[base:] = jnp.zeros((grads.shape[0] - base, LANES), grads.dtype)
     base = store_tiles(grads, base, total)
-    store_tiles(grads, base, dot_lanes(own_ddown, sorted_act[...]))
+    grad_down = dot_lanes(sorted_act[...], own_ddown)
+    rows = grad_down.shape[0] // 2
+    grads[base : base + rows] = jnp.concatenate(
+        [grad_down[:rows], grad_down[rows:]], axis=1
+    ).astype(grads.dtype)
 
 
 def input_kernel(half, *refs):
@@ -276,6 +280,36 @@
             out[2 * column + place // 2, place % 2] = total.astype(BF16)
 
 
+def assemble_kernel(fine_scale, coarse_scale, rows, fine, down, coarse):
+    def pieces(start, count, width, scale):
+        tile = rows[start : start + count].astype(F32) * scale
+        return [
+            (tile if lane == 0 else pltpu.roll(tile, LANES - lane, 1))[:, :width]
+            for lane in range(0, LANES, width)
+        ]
+
+    chans, chans3 = fine.shape[1], coarse.shape[1]
+    for tile in range(4):
+        for h, part in enumerate(pieces(3 * tile * chans3, 3 * chans3, chans3, coarse_scale)):
+            for c in range(3):
+                coarse[6 * tile + 3 * h + c] = part[c * chans3 : (c + 1) * chans3]
+    base = 12 * chans3
+    low, high = pieces(base, 3 * chans3 // 2, chans3, coarse_scale)
+    coarse[24] = low[:chans3]
+    coarse[25] = jnp.concatenate([low[chans3:], high[: chans3 // 2]], axis=0)
+    coarse[26] = high[chans3 // 2 :]
+    base += 3 * chans3 // 2
+    for tile in range(3):
+        for h, part in enumerate(pieces(base, 3 * chans, chans, fine_scale)):
+            for c in range(3):
+                if 4 * tile + h < 9:
+                    fine[3 * (4 * tile + h) + c] = part[c * chans : (c + 1) * chans]
+        base += 3 * chans
+    for last, part in enumerate(pieces(base, 4 * chans, chans3, coarse_scale)):
+        for first in range(4):
+            down[2 * first + last] = part[first * chans : (first + 1) * chans]
+
+
 def tap_matrix(weights):
     taps, outs, ins = weights.shape
     return jnp.transpose(weights.reshape(9, 3, outs, ins), (1, 2, 0, 3)).reshape(3 * outs, 9 * ins)
@@ -366,6 +400,10 @@
     steps = parts.shape[0]
     sample = (lax.axis_index("grp") // 4 - late()) % steps
     return jnp.where(sample // 2 % 2 == 0, parts[:, 0], parts[:, 1]).reshape(-1, LANES)
+
+
+def after(value, *others):
+    return lax.optimization_barrier((value, *others))[0]
 
 
 def far_side():
@@ -440,7 +478,8 @@
         down_matrix,
         down_matrix.T,
     ]
-    own, cells, *matrices = lax.optimization_barrier((own, cells, *matrices))
+    own, *matrices = lax.optimization_barrier((own, *matrices))
+    cells = after(cells, own)
     fine_matrix, fine_back, coarse_matrix, coarse_back, down_matrix, up_matrix = matrices
     own = joined(own, arrival(nearest(own, reach() * x_cells), 0, True))
     cells = jnp.roll(trade(cells, "grp"), -(QUARTERS // 2), axis=0).reshape(width // 2, LANES)
@@ -506,13 +545,14 @@
         *fine_pieces(dpre2),
         fine_back,
     )
-    part, gradient, coarse = lax.optimization_barrier((part, gradient, coarse))
+    part, coarse = after(part, gradient), after(coarse, gradient)
     gradient = far_exchange(gradient.reshape(batch // 4, 2, 2, x_cells, y_cells, chans, LANES))
     part = jnp.broadcast_to(part[None], (coarse.shape[0], *part.shape))
     mixed = trade(jnp.concatenate([part, coarse], axis=1), ("grp", "sp"), columns())
     part = jnp.sum(mixed[:, :kept].astype(F32), axis=0).astype(BF16)
     coarse = from_column(mixed[:, kept:])
-    grads = share(part, ("grp", "sp"), near).reshape(grad_rows, LANES).astype(F32)
+    gradient = after(gradient, part)
+    grads = share(part, ("grp", "sp"), near).reshape(grad_rows, LANES)
     gradient = near_exchange(gradient)
     grads, gradient = lax.optimization_barrier((grads, gradient))
     grad_input = jnp.transpose(gradient, (0, 2, 1, 5, 3, 4, 6)).reshape(features.shape)
@@ -522,23 +562,16 @@
     )(coarse)
     result = result.reshape(cotangent.shape)
 
-    grad_coarse = grads[: 12 * chans3].reshape(4, 3, chans3, 2, chans3)
-    grad_coarse = jnp.transpose(grad_coarse, (0, 3, 1, 2, 4)).reshape(24, chans3, chans3)
-    last = grads[12 * chans3 : 27 * chans3 // 2].reshape(-1, 2, chans3)
-    last = jnp.swapaxes(last, 0, 1).reshape(3, chans3, chans3)
-    grad_coarse = jnp.concatenate([grad_coarse, last], axis=0)
-    grads = grads[27 * chans3 // 2 :]
-    grad_fine = grads[: 9 * chans].reshape(3, 3, chans, 4, chans)
-    grad_fine = jnp.transpose(grad_fine, (0, 3, 1, 2, 4)).reshape(36, chans, chans)[:27]
-    grad_down = grads[9 * chans : 9 * chans + 2 * chans3].reshape(2, chans3, 4, chans)
-    grad_down = jnp.transpose(grad_down, (2, 0, 1, 3)).reshape(8, chans3, chans)
-    return (
-        result,
-        grad_input,
-        grad_fine * fine_scale,
-        grad_down * coarse_scale,
-        grad_coarse * coarse_scale,
-    )
+    grad_fine, grad_down, grad_coarse = pl.pallas_call(
+        partial(assemble_kernel, fine_scale, coarse_scale),
+        out_shape=(
+            shape(weight_fine.shape, F32),
+            shape((8, chans, chans3), F32),
+            shape(weight_coarse.shape, F32),
+        ),
+        interpret=INTERPRET,
+    )(grads)
+    return result, grad_input, grad_fine, jnp.swapaxes(grad_down, 1, 2), grad_coarse
 
 
 def solution(mesh):

time: 191 us -> 210 us (1.099)
  waiting for transfers between devices: 47.2 us -> 67.4 us
  local copies, waits for them, and re-layouts: 11.1 us -> 7.6 us
  Pallas kernels: 11.5 us -> 13.9 us
    ppermute x1, waiting for transfers between devices: 0.01 us -> 19.3 us  [far_exchange(): lax.ppermute(sent, 'sp', [(col, col ^ 2) for col in range(lax.axis_size('...]
    ppermute x1, starting transfers between devices: 12 us -> 3.53 us  [turned(): return lax.ppermute(block, ('grp', 'sp'), pairs)]
    ppermute x1, starting transfers between devices: 4.4 us -> 12 us  [far_exchange(): lax.ppermute(sent, 'sp', [(col, col ^ 2) for col in range(lax.axis_size('...]
    ppermute x3, waiting for transfers between devices: 3.79 us -> 0.01 us  [near_exchange(): lax.ppermute(parts[x, c], 'sp', [(col, col ^ 4 * x + c) for col in range(...]
    ppermute x1, waiting for transfers between devices: 7.45 us -> 9.98 us  [turned(): return lax.ppermute(block, ('grp', 'sp'), pairs)]
    pallas_call x0 -> x1, Pallas kernels: none -> 2.33 us  [local(): pl.pallas_call(partial(assemble_kernel, fine_scale, coarse_scale), out_sh...]
    ppermute x3, starting transfers between devices: 9.44 us -> 11.8 us  [near_exchange(): lax.ppermute(parts[x, c], 'sp', [(col, col ^ 4 * x + c) for col in range(...]
    all_to_all x5, waiting for transfers between devices: 22 us -> 24.1 us  [trade(): lax.all_to_all(parts, axis, split_axis=0, concat_axis=0, axis_index_group...]
  transfers between devices with their start and end apart: 20 -> 20, of which waited for: 10 -> 9; matrix products, arithmetic and copies ran while one was open for 3% -> 3% of each run, Pallas kernels for 4% -> 4%
where the time goes in v4:
time: 210 us; the launch traced here: 209 us
  starting transfers between devices  116 us (55%)
  waiting for transfers between devices  67.4 us (32%)
  Pallas kernels  13.9 us (7%)
  local copies, waits for them, and re-layouts  7.6 us (4%)
  other arithmetic  2.9 us (1%)
    all_to_all x5, starting transfers between devices, trade(): lax.all_to_all(parts, axis, split_axis=0, concat_axis=0, axis_index_group...  64.5 us
    all_to_all x5, waiting for transfers between devices, trade(): lax.all_to_all(parts, axis, split_axis=0, concat_axis=0, axis_index_group...  24.1 us
    ppermute x10, starting transfers between devices, arrival(): return lax.ppermute(block, ('grp', 'sp'), pairs)  23.9 us
    ppermute x1, waiting for transfers between devices, far_exchange(): lax.ppermute(sent, 'sp', [(col, col ^ 2) for col in range(lax.axis_size('...  19.3 us
    ppermute x10, waiting for transfers between devices, arrival(): return lax.ppermute(block, ('grp', 'sp'), pairs)  14 us
    ppermute x1, starting transfers between devices, far_exchange(): lax.ppermute(sent, 'sp', [(col, col ^ 2) for col in range(lax.axis_size('...  12 us
    ppermute x3, starting transfers between devices, near_exchange(): lax.ppermute(parts[x, c], 'sp', [(col, col ^ 4 * x + c) for col in range(...  11.8 us
    ppermute x1, waiting for transfers between devices, turned(): return lax.ppermute(block, ('grp', 'sp'), pairs)  9.98 us
  transfers between devices with their start and end apart: 20, of which 9 were waited for; matrix products, arithmetic and copies ran while one was open for 3% of the time, Pallas kernels for 4%

profile of v4, /device:TPU:1, one launch (start us, length us, event | category | flops | bytes accessed | tf_op | source)
XLA Modules:
  0.0 208.8 jit_solution(11146018308421507880)
XLA Ops:
  0.7 17.7 %all-to-all-start = ((bf16[8,2,2,32,128]{4,2,1,3,0:T(2,128)(2,1)}), bf16[8,2,2,32,128]{4,2,1,3,0:T(2,128)(2,1)S(1)}, u32[]{:S(2)}, u32[]{:S(2)}) async-start(bf16[8,2,2,32,128]{4,2,1,3,0:T(2,128)(2,1)} %bitcast.138), calls=%async_computation | async-start | bytes 524288 | tf_op jit(solution)/shard_map/all_to_all | solution.py:331
  18.4 0.4 copy.82
  18.8 0.4 reshape.111
  19.1 1.2 copy.55
  20.4 0.4 reshape.109
  20.7 0.6 copy-done.4
  22.0 10.6 %all-to-all-done = bf16[8,2,2,32,128]{4,2,1,3,0:T(2,128)(2,1)S(1)} async-done(((bf16[8,2,2,32,128]{4,2,1,3,0:T(2,128)(2,1)}), bf16[8,2,2,32,128]{4,2,1,3,0:T(2,128)(2,1)S(1)}, u32[]{:S(2)}, u32[]{:S(2)}) %all-to-all-start) | async-done | bytes 262176 | tf_op jit(solution)/shard_map/all_to_all | solution.py:331
  32.7 4.4 %collective-permute-start = (bf16[8,2,32,128]{3,2,1,0:T(8,128)(2,1)S(1)}, bf16[8,2,32,128]{3,2,1,0:T(8,128)(2,1)S(1)}, u32[]{:S(2)}, u32[]{:S(2)}) collective-permute-start(bf16[8,2,32,128]{3,2,1,0:T(8,128)(2,1)S(1)} %slice_select_fusion), channel_id=1, source_target_pairs={{8,0},{9,1},{10,2},{11,3},{12,4},{13,5},{14,6},{15,7},{0,8},{1,9},... | collective-permute-start | bytes 393224 | tf_op jit(solution)/shard_map/ppermute | solution.py:39
  37.1 3.5 %collective-permute-start.5 = (bf16[64,512]{1,0:T(8,128)(2,1)S(1)}, bf16[64,512]{1,0:T(8,128)(2,1)S(1)}, u32[]{:S(2)}, u32[]{:S(2)}) collective-permute-start(bf16[64,512]{1,0:T(8,128)(2,1)S(1)} %bitcast.147), channel_id=1, source_target_pairs={{0,71},{1,135},{2,199},{3,263},{4,327},{5,391},{6,455},{7,7},{8,79... | collective-permute-start | bytes 196616 | tf_op jit(solution)/shard_map/ppermute | solution.py:350
  40.6 10.0 %collective-permute-done.5.values = bf16[64,512]{1,0:T(8,128)(2,1)S(1)} collective-permute-done((bf16[64,512]{1,0:T(8,128)(2,1)S(1)}, bf16[64,512]{1,0:T(8,128)(2,1)S(1)}, u32[]{:S(2)}, u32[]{:S(2)}) %collective-permute-start.5) | collective-permute-done | bytes 65568 | tf_op jit(solution)/shard_map/ppermute | solution.py:350
  50.6 0.6 copy-done.6
  51.2 1.6 shard_map.111
  52.8 11.7 %all-to-all-start.1 = ((bf16[32,8,128]{2,1,0:T(8,128)(2,1)}), bf16[32,8,128]{2,1,0:T(8,128)(2,1)S(1)}, u32[]{:S(2)}, u32[]{:S(2)}) async-start(bf16[32,8,128]{2,1,0:T(8,128)(2,1)} %bitcast.140), calls=%async_computation.1 | async-start | bytes 131072 | tf_op jit(solution)/shard_map/all_to_all | solution.py:331
  65.2 3.1 %collective-permute-start.1 = (bf16[24,1,32,128]{3,2,1,0:T(8,128)(2,1)S(1)}, bf16[24,1,32,128]{3,2,1,0:T(8,128)(2,1)S(1)}, u32[]{:S(2)}, u32[]{:S(2)}) collective-permute-start(bf16[24,1,32,128]{3,2,1,0:T(8,128)(2,1)S(1)} %get-tuple-element.64), channel_id=1, source_target_pairs={{0,16},{1,17},{2,18},{3,19},{4,20},{5,21},{6,22},{7,23},{8,24},{9,... | collective-permute-start | bytes 589832 | tf_op jit(solution)/shard_map/ppermute | solution.py:39
  68.4 1.3 collective-permute-start.2
  69.7 6.6 %all-to-all-done.1 = bf16[32,8,128]{2,1,0:T(8,128)(2,1)S(1)} async-done(((bf16[32,8,128]{2,1,0:T(8,128)(2,1)}), bf16[32,8,128]{2,1,0:T(8,128)(2,1)S(1)}, u32[]{:S(2)}, u32[]{:S(2)}) %all-to-all-start.1) | async-done | bytes 65568 | tf_op jit(solution)/shard_map/all_to_all | solution.py:331
  76.3 2.6 %collective-permute-start.6 = (bf16[128,128]{1,0:T(8,128)(2,1)S(1)}, bf16[128,128]{1,0:T(8,128)(2,1)S(1)}, u32[]{:S(2)}, u32[]{:S(2)}) collective-permute-start(bf16[128,128]{1,0:T(8,128)(2,1)S(1)} %fusion.7), channel_id=1, source_target_pairs={{8,0},{9,1},{10,2},{11,3},{12,4},{13,5},{14,6},{15,7},{0,8},{1,9},... | collective-permute-start | bytes 98312 | tf_op jit(solution)/shard_map/ppermute | solution.py:39
  78.9 3.0 %shard_map.110 = (bf16[64,768]{1,0:T(8,128)(2,1)S(1)}, bf16[256,768]{1,0:T(8,128)(2,1)S(1)}, f32[12,128,128]{2,1,0:T(8,128)S(1)}) custom-call(s32[1]{0:T(128)} %bitcast.half, bf16[24,2,32,128]{3,2,1,0:T(8,128)(2,1)S(1)} %maximum_select_fusion.refs_0_.refs_3_, bf16[24,1,32,128]{3,2,1,0:T(8,128)(2,1)S(1)} %collective-permute-done.1.refs_1_.refs_4_, ...), custom_call_target="tpu_custom_call" | custom-call | tf_op jit(solution)/shard_map/pallas_call | solution.py:22
  82.0 2.2 %collective-permute-start.3 = (bf16[64,768]{1,0:T(8,128)(2,1)S(1)}, bf16[64,768]{1,0:T(8,128)(2,1)S(1)}, u32[]{:S(2)}, u32[]{:S(2)}) collective-permute-start(bf16[64,768]{1,0:T(8,128)(2,1)S(1)} %get-tuple-element.35.refs_0_), channel_id=1, source_target_pairs={{0,16},{1,17},{2,18},{3,19},{4,20},{5,21},{6,22},{7,23},{8,24},{9,... | collective-permute-start | bytes 294920 | tf_op jit(solution)/shard_map/ppermute | solution.py:39
  84.2 1.3 collective-permute-start.4
  85.8 3.7 %collective-permute-done.4.refs_2_ = bf16[64,768]{1,0:T(8,128)(2,1)S(1)} collective-permute-done((bf16[64,768]{1,0:T(8,128)(2,1)S(1)}, bf16[64,768]{1,0:T(8,128)(2,1)S(1)}, u32[]{:S(2)}, u32[]{:S(2)}) %collective-permute-start.4) | collective-permute-done | bytes 98336 | tf_op jit(solution)/shard_map/ppermute | solution.py:39
  89.5 0.7 shard_map.112
  90.2 2.4 %collective-permute-start.7 = (bf16[64,768]{1,0:T(8,128)(2,1)S(1)}, bf16[64,768]{1,0:T(8,128)(2,1)S(1)}, u32[]{:S(2)}, u32[]{:S(2)}) collective-permute-start(bf16[64,768]{1,0:T(8,128)(2,1)S(1)} %get-tuple-element.39.refs_3_.refs_0_), channel_id=1, source_target_pairs={{0,16},{1,17},{2,18},{3,19},{4,20},{5,21},{6,22},{7,23},{8,24},{9,... | collective-permute-start | bytes 294920 | tf_op jit(solution)/shard_map/ppermute | solution.py:39
  92.6 1.3 collective-permute-start.8
  94.1 0.6 shard_map.113.refs_11_
  94.7 3.3 %collective-permute-done.8.refs_2_ = bf16[64,768]{1,0:T(8,128)(2,1)S(1)} collective-permute-done((bf16[64,768]{1,0:T(8,128)(2,1)S(1)}, bf16[64,768]{1,0:T(8,128)(2,1)S(1)}, u32[]{:S(2)}, u32[]{:S(2)}) %collective-permute-start.8) | collective-permute-done | bytes 98336 | tf_op jit(solution)/shard_map/ppermute | solution.py:39
  98.0 3.2 %shard_map.114 = (bf16[24,2,32,128]{3,2,1,0:T(8,128)(2,1)S(1)}, bf16[1280,128]{1,0:T(8,128)(2,1)S(1)}) custom-call(s32[1]{0:T(128)} %bitcast.half, bf16[64,768]{1,0:T(8,128)(2,1)S(1)} %get-tuple-element.39.refs_3_.refs_0_, bf16[64,768]{1,0:T(8,128)(2,1)S(1)} %collective-permute-done.7.refs_1_, bf16[64,768]{1,0:T(8,128)(2,1)S(1)} %collective-permute-done.8.refs_2_, ...), custom_call_target="tpu_custom_call" | custom-call | tf_op jit(solution)/shard_map/pallas_call | solution.py:22
  101.2 0.8 pad_maximum_fusion
  102.0 18.5 %all-to-all-start.2 = ((bf16[32,56,128]{2,1,0:T(8,128)(2,1)}), bf16[32,56,128]{2,1,0:T(8,128)(2,1)S(1)}, u32[]{:S(2)}, u32[]{:S(2)}) async-start(bf16[32,56,128]{2,1,0:T(8,128)(2,1)} %pad_maximum_fusion), calls=%async_computation.2 | async-start | bytes 917504 | tf_op jit(solution)/shard_map/all_to_all | solution.py:331
  120.5 1.3 collective-permute-start.10
  121.8 4.0 %collective-permute-start.9 = (bf16[24,1,32,128]{3,2,1,0:T(8,128)(2,1)S(1)}, bf16[24,1,32,128]{3,2,1,0:T(8,128)(2,1)S(1)}, u32[]{:S(2)}, u32[]{:S(2)}) collective-permute-start(bf16[24,1,32,128]{3,2,1,0:T(8,128)(2,1)S(1)} %get-tuple-element.62), channel_id=1, source_target_pairs={{0,16},{1,17},{2,18},{3,19},{4,20},{5,21},{6,22},{7,23},{8,24},{9,... | collective-permute-start | bytes 589832 | tf_op jit(solution)/shard_map/ppermute | solution.py:39
  126.0 6.6 %collective-permute-done.10.refs_2_ = bf16[24,1,32,128]{3,2,1,0:T(8,128)(2,1)S(1)} collective-permute-done((bf16[24,1,32,128]{3,2,1,0:T(8,128)(2,1)S(1)}, bf16[24,1,32,128]{3,2,1,0:T(8,128)(2,1)S(1)}, u32[]{:S(2)}, u32[]{:S(2)}) %collective-permute-start.10) | collective-permute-done | bytes 196640 | tf_op jit(solution)/shard_map/ppermute | solution.py:39
  132.6 0.8 shard_map.115
  133.7 0.7 pad_maximum_fusion.1
  134.4 12.0 %all-to-all-start.3 = ((bf16[16,72,128]{2,1,0:T(8,128)(2,1)}), bf16[16,72,128]{2,1,0:T(8,128)(2,1)S(1)}, u32[]{:S(2)}, u32[]{:S(2)}) async-start(bf16[16,72,128]{2,1,0:T(8,128)(2,1)} %pad_maximum_fusion.1), calls=%async_computation.3 | async-start | bytes 589824 | tf_op jit(solution)/shard_map/all_to_all | solution.py:331
  146.5 12.0 %collective-permute-start.11 = (bf16[2,2,2,2,32,128]{5,4,3,2,1,0:T(8,128)(2,1)S(1)}, bf16[2,2,2,2,32,128]{5,4,3,2,1,0:T(8,128)(2,1)S(1)}, u32[]{:S(2)}, u32[]{:S(2)}) collective-permute-start(bf16[2,2,2,2,32,128]{5,4,3,2,1,0:T(8,128)(2,1)S(1)} %fusion), channel_id=1, source_target_pairs={{0,2},{1,3},{2,0},{3,1},{4,6},{5,7},{6,4},{7,5},{8,10},{9,11},{10,... | collective-permute-start | bytes 393224 | tf_op jit(solution)/shard_map/ppermute | solution.py:417
  158.6 19.3 %collective-permute-done.11 = bf16[2,2,2,2,32,128]{5,4,3,2,1,0:T(8,128)(2,1)S(1)} collective-permute-done((bf16[2,2,2,2,32,128]{5,4,3,2,1,0:T(8,128)(2,1)S(1)}, bf16[2,2,2,2,32,128]{5,4,3,2,1,0:T(8,128)(2,1)S(1)}, u32[]{:S(2)}, u32[]{:S(2)}) %collective-permute-start.11) | collective-permute-done | bytes 131104 | tf_op jit(solution)/shard_map/ppermute | solution.py:417
  178.1 6.3 %collective-permute-start.12 = (bf16[2,2,2,32,128]{4,3,2,1,0:T(8,128)(2,1)S(1)}, bf16[2,2,2,32,128]{4,3,2,1,0:T(8,128)(2,1)S(1)}, u32[]{:S(2)}, u32[]{:S(2)}) collective-permute-start(bf16[2,2,2,32,128]{4,3,2,1,0:T(8,128)(2,1)S(1)} %get-tuple-element.66), channel_id=1, source_target_pairs={{0,1},{1,0},{2,3},{3,2},{4,5},{5,4},{6,7},{7,6},{8,9},{9,8},{10,11... | collective-permute-start | bytes 196616 | tf_op jit(solution)/shard_map/ppermute | solution.py:436
  184.4 3.1 %collective-permute-start.13 = (bf16[2,2,2,32,128]{4,3,2,1,0:T(8,128)(2,1)S(1)}, bf16[2,2,2,32,128]{4,3,2,1,0:T(8,128)(2,1)S(1)}, u32[]{:S(2)}, u32[]{:S(2)}) collective-permute-start(bf16[2,2,2,32,128]{4,3,2,1,0:T(8,128)(2,1)S(1)} %get-tuple-element.68), channel_id=1, source_target_pairs={{0,4},{1,5},{2,6},{3,7},{4,0},{5,1},{6,2},{7,3},{8,12},{9,13},{10,... | collective-permute-start | bytes 196616 | tf_op jit(solution)/shard_map/ppermute | solution.py:436
  187.6 2.4 %collective-permute-start.14 = (bf16[2,2,2,32,128]{4,3,2,1,0:T(8,128)(2,1)S(1)}, bf16[2,2,2,32,128]{4,3,2,1,0:T(8,128)(2,1)S(1)}, u32[]{:S(2)}, u32[]{:S(2)}) collective-permute-start(bf16[2,2,2,32,128]{4,3,2,1,0:T(8,128)(2,1)S(1)} %get-tuple-element.67), channel_id=1, source_target_pairs={{0,5},{1,4},{2,7},{3,6},{4,1},{5,0},{6,3},{7,2},{8,13},{9,12},{10,... | collective-permute-start | bytes 196616 | tf_op jit(solution)/shard_map/ppermute | solution.py:436
  189.9 0.8 broadcast_in_dim.8
  190.7 4.6 %all-to-all-start.4 = ((bf16[32,40,128]{2,1,0:T(8,128)(2,1)}), bf16[32,40,128]{2,1,0:T(8,128)(2,1)S(1)}, u32[]{:S(2)}, u32[]{:S(2)}) async-start(bf16[32,40,128]{2,1,0:T(8,128)(2,1)} %broadcast_in_dim.8), calls=%async_computation.4 | async-start | bytes 655360 | tf_op jit(solution)/shard_map/all_to_all | solution.py:331
  195.4 0.6 slice_select_fusion.1
  196.0 1.7 shard_map.116
  197.9 6.9 %all-to-all-done.4 = bf16[32,40,128]{2,1,0:T(8,128)(2,1)S(1)} async-done(((bf16[32,40,128]{2,1,0:T(8,128)(2,1)}), bf16[32,40,128]{2,1,0:T(8,128)(2,1)S(1)}, u32[]{:S(2)}, u32[]{:S(2)}) %all-to-all-start.4) | async-done | bytes 327712 | tf_op jit(solution)/shard_map/all_to_all | solution.py:331
  204.9 0.7 copy-done.3
  205.6 2.3 %shard_map.117 = (f32[27,32,32]{2,1,0:T(8,128)}, f32[8,32,64]{2,1,0:T(8,128)}, f32[27,64,64]{2,1,0:T(8,128)}) custom-call(bf16[1280,128]{1,0:T(8,128)(2,1)} %bitcast.125), custom_call_target="tpu_custom_call" | custom-call | tf_op jit(solution)/shard_map/pallas_call | solution.py:565
  207.9 0.9 copy.74
  (72 shorter events, 2.7 us)
Async XLA Ops:
  0.6 17.7 %copy-start.2 = (bf16[27,64,64]{2,1,0:T(8,128)(2,1)S(1)}, bf16[27,64,64]{2,1,0:T(8,128)(2,1)}, u32[]{:S(2)}) copy-start(bf16[27,64,64]{2,1,0:T(8,128)(2,1)} %param.10) | copy-start | bytes 663556
  0.6 17.7 %copy-start.5 = (bf16[8,64,32]{1,2,0:T(8,128)(2,1)S(1)}, bf16[8,64,32]{1,2,0:T(8,128)(2,1)}, u32[]{:S(2)}) copy-start(bf16[8,64,32]{1,2,0:T(8,128)(2,1)} %param.9) | copy-start | bytes 98308
  0.7 32.0 %all-to-all-start = ((bf16[8,2,2,32,128]{4,2,1,3,0:T(2,128)(2,1)}), bf16[8,2,2,32,128]{4,2,1,3,0:T(2,128)(2,1)S(1)}, u32[]{:S(2)}, u32[]{:S(2)}) async-start(bf16[8,2,2,32,128]{4,2,1,3,0:T(2,128)(2,1)} %bitcast.138), calls=%async_computation | async-start | bytes 524288 | tf_op jit(solution)/shard_map/all_to_all | solution.py:331
  20.4 0.9 copy-start.4
  32.7 4.4 %copy-start.7 = (bf16[1,64,1,512]{3,1,2,0:T(8,128)(2,1)S(1)}, bf16[1,64,1,512]{3,1,2,0:T(8,128)(2,1)}, u32[]{:S(2)}) copy-start(bf16[1,64,1,512]{3,1,2,0:T(8,128)(2,1)} %param.11) | copy-start | bytes 196612
  32.7 32.4 %collective-permute-start = (bf16[8,2,32,128]{3,2,1,0:T(8,128)(2,1)S(1)}, bf16[8,2,32,128]{3,2,1,0:T(8,128)(2,1)S(1)}, u32[]{:S(2)}, u32[]{:S(2)}) collective-permute-start(bf16[8,2,32,128]{3,2,1,0:T(8,128)(2,1)S(1)} %slice_select_fusion), channel_id=1, source_target_pairs={{8,0},{9,1},{10,2},{11,3},{12,4},{13,5},{14,6},{15,7},{0,8},{1,9},... | collective-permute-start | bytes 393224 | tf_op jit(solution)/shard_map/ppermute | solution.py:39
  37.1 13.5 %collective-permute-start.5 = (bf16[64,512]{1,0:T(8,128)(2,1)S(1)}, bf16[64,512]{1,0:T(8,128)(2,1)S(1)}, u32[]{:S(2)}, u32[]{:S(2)}) collective-permute-start(bf16[64,512]{1,0:T(8,128)(2,1)S(1)} %bitcast.147), channel_id=1, source_target_pairs={{0,71},{1,135},{2,199},{3,263},{4,327},{5,391},{6,455},{7,7},{8,79... | collective-permute-start | bytes 196616 | tf_op jit(solution)/shard_map/ppermute | solution.py:350
  50.6 0.6 copy-start.6
  52.8 23.5 %all-to-all-start.1 = ((bf16[32,8,128]{2,1,0:T(8,128)(2,1)}), bf16[32,8,128]{2,1,0:T(8,128)(2,1)S(1)}, u32[]{:S(2)}, u32[]{:S(2)}) async-start(bf16[32,8,128]{2,1,0:T(8,128)(2,1)} %bitcast.140), calls=%async_computation.1 | async-start | bytes 131072 | tf_op jit(solution)/shard_map/all_to_all | solution.py:331
  65.2 13.7 %collective-permute-start.1 = (bf16[24,1,32,128]{3,2,1,0:T(8,128)(2,1)S(1)}, bf16[24,1,32,128]{3,2,1,0:T(8,128)(2,1)S(1)}, u32[]{:S(2)}, u32[]{:S(2)}) collective-permute-start(bf16[24,1,32,128]{3,2,1,0:T(8,128)(2,1)S(1)} %get-tuple-element.64), channel_id=1, source_target_pairs={{0,16},{1,17},{2,18},{3,19},{4,20},{5,21},{6,22},{7,23},{8,24},{9,... | collective-permute-start | bytes 589832 | tf_op jit(solution)/shard_map/ppermute | solution.py:39
  68.4 10.5 %collective-permute-start.2 = (bf16[24,1,32,128]{3,2,1,0:T(8,128)(2,1)S(1)}, bf16[24,1,32,128]{3,2,1,0:T(8,128)(2,1)S(1)}, u32[]{:S(2)}, u32[]{:S(2)}) collective-permute-start(bf16[24,1,32,128]{3,2,1,0:T(8,128)(2,1)S(1)} %get-tuple-element.63), channel_id=1, source_target_pairs={{16,0},{17,1},{18,2},{19,3},{20,4},{21,5},{22,6},{23,7},{24,8},{25... | collective-permute-start | bytes 589832 | tf_op jit(solution)/shard_map/ppermute | solution.py:39
  76.3 2.6 %copy-start.1 = (bf16[256,256]{1,0:T(8,128)(2,1)S(1)}, bf16[256,256]{1,0:T(8,128)(2,1)}, u32[]{:S(2)}) copy-start(bf16[256,256]{1,0:T(8,128)(2,1)} %constant.129.clone.refs_5_) | copy-start | bytes 393220
  76.3 9.2 %collective-permute-start.6 = (bf16[128,128]{1,0:T(8,128)(2,1)S(1)}, bf16[128,128]{1,0:T(8,128)(2,1)S(1)}, u32[]{:S(2)}, u32[]{:S(2)}) collective-permute-start(bf16[128,128]{1,0:T(8,128)(2,1)S(1)} %fusion.7), channel_id=1, source_target_pairs={{8,0},{9,1},{10,2},{11,3},{12,4},{13,5},{14,6},{15,7},{0,8},{1,9},... | collective-permute-start | bytes 98312 | tf_op jit(solution)/shard_map/ppermute | solution.py:39
  82.0 3.8 %collective-permute-start.3 = (bf16[64,768]{1,0:T(8,128)(2,1)S(1)}, bf16[64,768]{1,0:T(8,128)(2,1)S(1)}, u32[]{:S(2)}, u32[]{:S(2)}) collective-permute-start(bf16[64,768]{1,0:T(8,128)(2,1)S(1)} %get-tuple-element.35.refs_0_), channel_id=1, source_target_pairs={{0,16},{1,17},{2,18},{3,19},{4,20},{5,21},{6,22},{7,23},{8,24},{9,... | collective-permute-start | bytes 294920 | tf_op jit(solution)/shard_map/ppermute | solution.py:39
  84.2 5.4 %collective-permute-start.4 = (bf16[64,768]{1,0:T(8,128)(2,1)S(1)}, bf16[64,768]{1,0:T(8,128)(2,1)S(1)}, u32[]{:S(2)}, u32[]{:S(2)}) collective-permute-start(bf16[64,768]{1,0:T(8,128)(2,1)S(1)} %get-tuple-element.35.refs_0_), channel_id=1, source_target_pairs={{16,0},{17,1},{18,2},{19,3},{20,4},{21,5},{22,6},{23,7},{24,8},{25... | collective-permute-start | bytes 294920 | tf_op jit(solution)/shard_map/ppermute | solution.py:39
  90.2 4.5 %collective-permute-start.7 = (bf16[64,768]{1,0:T(8,128)(2,1)S(1)}, bf16[64,768]{1,0:T(8,128)(2,1)S(1)}, u32[]{:S(2)}, u32[]{:S(2)}) collective-permute-start(bf16[64,768]{1,0:T(8,128)(2,1)S(1)} %get-tuple-element.39.refs_3_.refs_0_), channel_id=1, source_target_pairs={{0,16},{1,17},{2,18},{3,19},{4,20},{5,21},{6,22},{7,23},{8,24},{9,... | collective-permute-start | bytes 294920 | tf_op jit(solution)/shard_map/ppermute | solution.py:39
  92.6 5.4 %collective-permute-start.8 = (bf16[64,768]{1,0:T(8,128)(2,1)S(1)}, bf16[64,768]{1,0:T(8,128)(2,1)S(1)}, u32[]{:S(2)}, u32[]{:S(2)}) collective-permute-start(bf16[64,768]{1,0:T(8,128)(2,1)S(1)} %get-tuple-element.39.refs_3_.refs_0_), channel_id=1, source_target_pairs={{16,0},{17,1},{18,2},{19,3},{20,4},{21,5},{22,6},{23,7},{24,8},{25... | collective-permute-start | bytes 294920 | tf_op jit(solution)/shard_map/ppermute | solution.py:39
  94.1 4.0 %copy-start = (bf16[256,256]{1,0:T(8,128)(2,1)S(1)}, bf16[256,256]{1,0:T(8,128)(2,1)}, u32[]{:S(2)}) copy-start(bf16[256,256]{1,0:T(8,128)(2,1)} %constant.130.clone.refs_8_) | copy-start | bytes 393220
  102.0 31.4 %all-to-all-start.2 = ((bf16[32,56,128]{2,1,0:T(8,128)(2,1)}), bf16[32,56,128]{2,1,0:T(8,128)(2,1)S(1)}, u32[]{:S(2)}, u32[]{:S(2)}) async-start(bf16[32,56,128]{2,1,0:T(8,128)(2,1)} %pad_maximum_fusion), calls=%async_computation.2 | async-start | bytes 917504 | tf_op jit(solution)/shard_map/all_to_all | solution.py:331
  120.5 12.1 %collective-permute-start.10 = (bf16[24,1,32,128]{3,2,1,0:T(8,128)(2,1)S(1)}, bf16[24,1,32,128]{3,2,1,0:T(8,128)(2,1)S(1)}, u32[]{:S(2)}, u32[]{:S(2)}) collective-permute-start(bf16[24,1,32,128]{3,2,1,0:T(8,128)(2,1)S(1)} %get-tuple-element.61), channel_id=1, source_target_pairs={{16,0},{17,1},{18,2},{19,3},{20,4},{21,5},{22,6},{23,7},{24,8},{25... | collective-permute-start | bytes 589832 | tf_op jit(solution)/shard_map/ppermute | solution.py:39
  121.8 10.8 %collective-permute-start.9 = (bf16[24,1,32,128]{3,2,1,0:T(8,128)(2,1)S(1)}, bf16[24,1,32,128]{3,2,1,0:T(8,128)(2,1)S(1)}, u32[]{:S(2)}, u32[]{:S(2)}) collective-permute-start(bf16[24,1,32,128]{3,2,1,0:T(8,128)(2,1)S(1)} %get-tuple-element.62), channel_id=1, source_target_pairs={{0,16},{1,17},{2,18},{3,19},{4,20},{5,21},{6,22},{7,23},{8,24},{9,... | collective-permute-start | bytes 589832 | tf_op jit(solution)/shard_map/ppermute | solution.py:39
  134.4 43.5 %all-to-all-start.3 = ((bf16[16,72,128]{2,1,0:T(8,128)(2,1)}), bf16[16,72,128]{2,1,0:T(8,128)(2,1)S(1)}, u32[]{:S(2)}, u32[]{:S(2)}) async-start(bf16[16,72,128]{2,1,0:T(8,128)(2,1)} %pad_maximum_fusion.1), calls=%async_computation.3 | async-start | bytes 589824 | tf_op jit(solution)/shard_map/all_to_all | solution.py:331
  146.5 31.4 %collective-permute-start.11 = (bf16[2,2,2,2,32,128]{5,4,3,2,1,0:T(8,128)(2,1)S(1)}, bf16[2,2,2,2,32,128]{5,4,3,2,1,0:T(8,128)(2,1)S(1)}, u32[]{:S(2)}, u32[]{:S(2)}) collective-permute-start(bf16[2,2,2,2,32,128]{5,4,3,2,1,0:T(8,128)(2,1)S(1)} %fusion), channel_id=1, source_target_pairs={{0,2},{1,3},{2,0},{3,1},{4,6},{5,7},{6,4},{7,5},{8,10},{9,11},{10,... | collective-permute-start | bytes 393224 | tf_op jit(solution)/shard_map/ppermute | solution.py:417
  178.1 19.6 %collective-permute-start.12 = (bf16[2,2,2,32,128]{4,3,2,1,0:T(8,128)(2,1)S(1)}, bf16[2,2,2,32,128]{4,3,2,1,0:T(8,128)(2,1)S(1)}, u32[]{:S(2)}, u32[]{:S(2)}) collective-permute-start(bf16[2,2,2,32,128]{4,3,2,1,0:T(8,128)(2,1)S(1)} %get-tuple-element.66), channel_id=1, source_target_pairs={{0,1},{1,0},{2,3},{3,2},{4,5},{5,4},{6,7},{7,6},{8,9},{9,8},{10,11... | collective-permute-start | bytes 196616 | tf_op jit(solution)/shard_map/ppermute | solution.py:436
  184.4 13.3 %collective-permute-start.13 = (bf16[2,2,2,32,128]{4,3,2,1,0:T(8,128)(2,1)S(1)}, bf16[2,2,2,32,128]{4,3,2,1,0:T(8,128)(2,1)S(1)}, u32[]{:S(2)}, u32[]{:S(2)}) collective-permute-start(bf16[2,2,2,32,128]{4,3,2,1,0:T(8,128)(2,1)S(1)} %get-tuple-element.68), channel_id=1, source_target_pairs={{0,4},{1,5},{2,6},{3,7},{4,0},{5,1},{6,2},{7,3},{8,12},{9,13},{10,... | collective-permute-start | bytes 196616 | tf_op jit(solution)/shard_map/ppermute | solution.py:436
  187.6 10.2 %collective-permute-start.14 = (bf16[2,2,2,32,128]{4,3,2,1,0:T(8,128)(2,1)S(1)}, bf16[2,2,2,32,128]{4,3,2,1,0:T(8,128)(2,1)S(1)}, u32[]{:S(2)}, u32[]{:S(2)}) collective-permute-start(bf16[2,2,2,32,128]{4,3,2,1,0:T(8,128)(2,1)S(1)} %get-tuple-element.67), channel_id=1, source_target_pairs={{0,5},{1,4},{2,7},{3,6},{4,1},{5,0},{6,3},{7,2},{8,13},{9,12},{10,... | collective-permute-start | bytes 196616 | tf_op jit(solution)/shard_map/ppermute | solution.py:436
  190.7 14.2 %all-to-all-start.4 = ((bf16[32,40,128]{2,1,0:T(8,128)(2,1)}), bf16[32,40,128]{2,1,0:T(8,128)(2,1)S(1)}, u32[]{:S(2)}, u32[]{:S(2)}) async-start(bf16[32,40,128]{2,1,0:T(8,128)(2,1)} %broadcast_in_dim.8), calls=%async_computation.4 | async-start | bytes 655360 | tf_op jit(solution)/shard_map/all_to_all | solution.py:331
  204.9 0.7 copy-start.3

commit v5 on v4

--- a/solution.py
+++ b/solution.py
@@ -402,10 +402,6 @@
     return jnp.where(sample // 2 % 2 == 0, parts[:, 0], parts[:, 1]).reshape(-1, LANES)
 
 
-def after(value, *others):
-    return lax.optimization_barrier((value, *others))[0]
-
-
 def far_side():
     return lax.axis_index("sp") // 2 % 2
 
@@ -418,27 +414,14 @@
     return jnp.stack([jnp.where(near, kept, got), jnp.where(near, got, kept)], axis=2)
 
 
-def matched(parts, far, core):
-    if parts.shape[0] > 1:
-        parts = jnp.where(far == 0, parts, parts[::-1])
-    return jnp.where(core == 0, parts, parts[:, ::-1])
-
-
 def near_exchange(parts):
     cols, lead = lax.axis_size("sp"), parts.shape[0]
-    place = lax.axis_index("sp")
-    far, core = place // 4 % lead, place % 2
-    parts = matched(parts, far, core)
-    got = [
-        [
-            parts[x, c]
-            if x == c == 0
-            else lax.ppermute(parts[x, c], "sp", [(col, col ^ (4 * x + c)) for col in range(cols)])
-            for c in (0, 1)
-        ]
-        for x in range(lead)
+    groups = [
+        [start + 4 * far + core for far in range(lead) for core in (0, 1)]
+        for half in range(0, cols, 4 * lead)
+        for start in (half, half + 2)
     ]
-    return matched(jnp.stack([jnp.stack(row) for row in got]), far, core)
+    return trade(parts.reshape(2 * lead, *parts.shape[2:]), "sp", groups).reshape(parts.shape)
 
 
 def local(features, weight_fine, weight_down, weight_coarse, cotangent):
@@ -468,8 +451,8 @@
     block = (rows, width // 2 // rows, LANES)
     cells = pl.pallas_call(
         pack_kernel, out_shape=shape((width // 2, LANES), BF16), interpret=INTERPRET
-    )(turned(cotangent.reshape(chans3, width)))
-    cells = cells.reshape(block)
+    )(cotangent.reshape(chans3, width))
+    cells = turned(cells).reshape(block)
     matrices = [
         tap_matrix(weight_fine),
         tap_matrix(reversed_taps(weight_fine)),
@@ -478,8 +461,7 @@
         down_matrix,
         down_matrix.T,
     ]
-    own, *matrices = lax.optimization_barrier((own, *matrices))
-    cells = after(cells, own)
+    own, cells, *matrices = lax.optimization_barrier((own, cells, *matrices))
     fine_matrix, fine_back, coarse_matrix, coarse_back, down_matrix, up_matrix = matrices
     own = joined(own, arrival(nearest(own, reach() * x_cells), 0, True))
     cells = jnp.roll(trade(cells, "grp"), -(QUARTERS // 2), axis=0).reshape(width // 2, LANES)
@@ -545,16 +527,15 @@
         *fine_pieces(dpre2),
         fine_back,
     )
-    part, coarse = after(part, gradient), after(coarse, gradient)
+    part, gradient, coarse = lax.optimization_barrier((part, gradient, coarse))
     gradient = far_exchange(gradient.reshape(batch // 4, 2, 2, x_cells, y_cells, chans, LANES))
     part = jnp.broadcast_to(part[None], (coarse.shape[0], *part.shape))
     mixed = trade(jnp.concatenate([part, coarse], axis=1), ("grp", "sp"), columns())
     part = jnp.sum(mixed[:, :kept].astype(F32), axis=0).astype(BF16)
     coarse = from_column(mixed[:, kept:])
-    gradient = after(gradient, part)
     grads = share(part, ("grp", "sp"), near).reshape(grad_rows, LANES)
+    grads, gradient = lax.optimization_barrier((grads, gradient))
     gradient = near_exchange(gradient)
-    grads, gradient = lax.optimization_barrier((grads, gradient))
     grad_input = jnp.transpose(gradient, (0, 2, 1, 5, 3, 4, 6)).reshape(features.shape)
 
     result = pl.pallas_call(

time: 210 us -> 189 us (0.900)
  waiting for transfers between devices: 67.4 us -> 41.1 us
  starting transfers between devices: 116 us -> 122 us
    ppermute x1, waiting for transfers between devices: 19.3 us -> 0.01 us  [far_exchange(): lax.ppermute(sent, 'sp', [(col, col ^ 2) for col in range(lax.axis_size('...]
    ppermute x3 -> x0, starting transfers between devices: 11.8 us -> none  [near_exchange(): lax.ppermute(parts[x, c], 'sp', [(col, col ^ 4 * x + c) for col in range(...]
    all_to_all x5 -> x6, starting transfers between devices: 64.5 us -> 74.1 us  [trade(): lax.all_to_all(parts, axis, split_axis=0, concat_axis=0, axis_index_group...]
    ppermute x1, starting transfers between devices: 3.53 us -> 12 us  [turned(): return lax.ppermute(block, ('grp', 'sp'), pairs)]
    ppermute x1, waiting for transfers between devices: 9.98 us -> 5.86 us  [turned(): return lax.ppermute(block, ('grp', 'sp'), pairs)]
    all_to_all x5 -> x6, waiting for transfers between devices: 24.1 us -> 21.2 us  [trade(): lax.all_to_all(parts, axis, split_axis=0, concat_axis=0, axis_index_group...]
  transfers between devices with their start and end apart: 20 -> 18, of which waited for: 9 -> 9; matrix products, arithmetic and copies ran while one was open for 3% -> 3% of each run, Pallas kernels for 4% -> 5%
where the time goes in v5:
time: 189 us; the launch traced here: 188 us
  starting transfers between devices  122 us (65%)
  waiting for transfers between devices  41.1 us (22%)
  Pallas kernels  13.9 us (7%)
  local copies, waits for them, and re-layouts  7.08 us (4%)
  other arithmetic  2.6 us (1%)
    all_to_all x6, starting transfers between devices, trade(): lax.all_to_all(parts, axis, split_axis=0, concat_axis=0, axis_index_group...  74.1 us
    ppermute x10, starting transfers between devices, arrival(): return lax.ppermute(block, ('grp', 'sp'), pairs)  23.8 us
    all_to_all x6, waiting for transfers between devices, trade(): lax.all_to_all(parts, axis, split_axis=0, concat_axis=0, axis_index_group...  21.2 us
    ppermute x10, waiting for transfers between devices, arrival(): return lax.ppermute(block, ('grp', 'sp'), pairs)  14 us
    ppermute x1, starting transfers between devices, turned(): return lax.ppermute(block, ('grp', 'sp'), pairs)  12 us
    ppermute x1, starting transfers between devices, far_exchange(): lax.ppermute(sent, 'sp', [(col, col ^ 2) for col in range(lax.axis_size('...  12 us
    pallas_call x5, Pallas kernels, call(): pl.pallas_call(kernel, out_shape=outs, in_specs=[pl.BlockSpec(memory_spac...  8.26 us
    ppermute x1, waiting for transfers between devices, turned(): return lax.ppermute(block, ('grp', 'sp'), pairs)  5.86 us
  transfers between devices with their start and end apart: 18, of which 9 were waited for; matrix products, arithmetic and copies ran while one was open for 3% of the time, Pallas kernels for 5%

profile of v5, /device:TPU:1, one launch (start us, length us, event | category | flops | bytes accessed | tf_op | source)
XLA Modules:
  0.0 187.8 jit_solution(11417655954865169575)
XLA Ops:
  0.6 17.7 %all-to-all-start = ((bf16[8,2,2,32,128]{4,2,1,3,0:T(2,128)(2,1)}), bf16[8,2,2,32,128]{4,2,1,3,0:T(2,128)(2,1)S(1)}, u32[]{:S(2)}, u32[]{:S(2)}) async-start(bf16[8,2,2,32,128]{4,2,1,3,0:T(2,128)(2,1)} %bitcast.121), calls=%async_computation | async-start | bytes 524288 | tf_op jit(solution)/shard_map/all_to_all | solution.py:331
  18.3 1.6 shard_map.110
  19.9 12.0 %collective-permute-start = (bf16[256,128]{1,0:T(8,128)(2,1)}, bf16[256,128]{1,0:T(8,128)(2,1)}, u32[]{:S(2)}, u32[]{:S(2)}) collective-permute-start(bf16[256,128]{1,0:T(8,128)(2,1)} %shard_map.110), channel_id=1, source_target_pairs={{0,71},{1,135},{2,199},{3,263},{4,327},{5,391},{6,455},{7,7},{8,79... | collective-permute-start | bytes 196616 | tf_op jit(solution)/shard_map/ppermute | solution.py:350
  32.0 0.4 copy.65
  32.4 0.4 reshape.119
  32.8 1.2 copy.44
  34.0 0.4 reshape.117
  34.4 0.6 copy-done.5
  35.3 0.2 copy.42
  35.7 5.9 %collective-permute-done = bf16[256,128]{1,0:T(8,128)(2,1)} collective-permute-done((bf16[256,128]{1,0:T(8,128)(2,1)}, bf16[256,128]{1,0:T(8,128)(2,1)}, u32[]{:S(2)}, u32[]{:S(2)}) %collective-permute-start) | collective-permute-done | bytes 65568 | tf_op jit(solution)/shard_map/ppermute | solution.py:350
  41.6 4.4 %collective-permute-start.1 = (bf16[8,2,32,128]{3,2,1,0:T(8,128)(2,1)S(1)}, bf16[8,2,32,128]{3,2,1,0:T(8,128)(2,1)S(1)}, u32[]{:S(2)}, u32[]{:S(2)}) collective-permute-start(bf16[8,2,32,128]{3,2,1,0:T(8,128)(2,1)S(1)} %slice_select_fusion), channel_id=1, source_target_pairs={{8,0},{9,1},{10,2},{11,3},{12,4},{13,5},{14,6},{15,7},{0,8},{1,9},... | collective-permute-start | bytes 393224 | tf_op jit(solution)/shard_map/ppermute | solution.py:39
  46.0 9.6 %all-to-all-start.1 = ((bf16[32,8,128]{2,1,0:T(8,128)(2,1)}), bf16[32,8,128]{2,1,0:T(8,128)(2,1)S(1)}, u32[]{:S(2)}, u32[]{:S(2)}) async-start(bf16[32,8,128]{2,1,0:T(8,128)(2,1)} %bitcast.4), calls=%async_computation.1 | async-start | bytes 131072 | tf_op jit(solution)/shard_map/all_to_all | solution.py:331
  56.0 0.2 copy.50.refs_6_
  56.2 3.1 %collective-permute-start.2 = (bf16[24,1,32,128]{3,2,1,0:T(8,128)(2,1)S(1)}, bf16[24,1,32,128]{3,2,1,0:T(8,128)(2,1)S(1)}, u32[]{:S(2)}, u32[]{:S(2)}) collective-permute-start(bf16[24,1,32,128]{3,2,1,0:T(8,128)(2,1)S(1)} %get-tuple-element.69), channel_id=1, source_target_pairs={{0,16},{1,17},{2,18},{3,19},{4,20},{5,21},{6,22},{7,23},{8,24},{9,... | collective-permute-start | bytes 589832 | tf_op jit(solution)/shard_map/ppermute | solution.py:39
  59.4 1.3 collective-permute-start.3
  60.7 6.7 %all-to-all-done.1 = bf16[32,8,128]{2,1,0:T(8,128)(2,1)S(1)} async-done(((bf16[32,8,128]{2,1,0:T(8,128)(2,1)}), bf16[32,8,128]{2,1,0:T(8,128)(2,1)S(1)}, u32[]{:S(2)}, u32[]{:S(2)}) %all-to-all-start.1) | async-done | bytes 65568 | tf_op jit(solution)/shard_map/all_to_all | solution.py:331
  67.4 2.6 %collective-permute-start.6 = (bf16[128,128]{1,0:T(8,128)(2,1)S(1)}, bf16[128,128]{1,0:T(8,128)(2,1)S(1)}, u32[]{:S(2)}, u32[]{:S(2)}) collective-permute-start(bf16[128,128]{1,0:T(8,128)(2,1)S(1)} %fusion.7), channel_id=1, source_target_pairs={{8,0},{9,1},{10,2},{11,3},{12,4},{13,5},{14,6},{15,7},{0,8},{1,9},... | collective-permute-start | bytes 98312 | tf_op jit(solution)/shard_map/ppermute | solution.py:39
  70.0 3.0 %shard_map.111 = (bf16[64,768]{1,0:T(8,128)(2,1)S(1)}, bf16[256,768]{1,0:T(8,128)(2,1)S(1)}, f32[12,128,128]{2,1,0:T(8,128)S(1)}) custom-call(s32[1]{0:T(128)} %bitcast.half, bf16[24,2,32,128]{3,2,1,0:T(8,128)(2,1)S(1)} %maximum_select_fusion.refs_0_.refs_3_, bf16[24,1,32,128]{3,2,1,0:T(8,128)(2,1)S(1)} %collective-permute-done.2.refs_1_.refs_4_, ...), custom_call_target="tpu_custom_call" | custom-call | tf_op jit(solution)/shard_map/pallas_call | solution.py:22
  73.1 2.2 %collective-permute-start.4 = (bf16[64,768]{1,0:T(8,128)(2,1)S(1)}, bf16[64,768]{1,0:T(8,128)(2,1)S(1)}, u32[]{:S(2)}, u32[]{:S(2)}) collective-permute-start(bf16[64,768]{1,0:T(8,128)(2,1)S(1)} %get-tuple-element.35.refs_0_), channel_id=1, source_target_pairs={{0,16},{1,17},{2,18},{3,19},{4,20},{5,21},{6,22},{7,23},{8,24},{9,... | collective-permute-start | bytes 294920 | tf_op jit(solution)/shard_map/ppermute | solution.py:39
  75.3 1.3 collective-permute-start.5
  76.6 0.3 collective-permute-done.4.refs_1_
  76.9 3.7 %collective-permute-done.5.refs_2_ = bf16[64,768]{1,0:T(8,128)(2,1)S(1)} collective-permute-done((bf16[64,768]{1,0:T(8,128)(2,1)S(1)}, bf16[64,768]{1,0:T(8,128)(2,1)S(1)}, u32[]{:S(2)}, u32[]{:S(2)}) %collective-permute-start.5) | collective-permute-done | bytes 98336 | tf_op jit(solution)/shard_map/ppermute | solution.py:39
  80.6 0.7 shard_map.112
  81.3 2.4 %collective-permute-start.7 = (bf16[64,768]{1,0:T(8,128)(2,1)S(1)}, bf16[64,768]{1,0:T(8,128)(2,1)S(1)}, u32[]{:S(2)}, u32[]{:S(2)}) collective-permute-start(bf16[64,768]{1,0:T(8,128)(2,1)S(1)} %get-tuple-element.39.refs_3_.refs_0_), channel_id=1, source_target_pairs={{0,16},{1,17},{2,18},{3,19},{4,20},{5,21},{6,22},{7,23},{8,24},{9,... | collective-permute-start | bytes 294920 | tf_op jit(solution)/shard_map/ppermute | solution.py:39
  83.6 1.3 collective-permute-start.8
  85.1 0.6 shard_map.113.refs_11_
  85.7 3.3 %collective-permute-done.8.refs_2_ = bf16[64,768]{1,0:T(8,128)(2,1)S(1)} collective-permute-done((bf16[64,768]{1,0:T(8,128)(2,1)S(1)}, bf16[64,768]{1,0:T(8,128)(2,1)S(1)}, u32[]{:S(2)}, u32[]{:S(2)}) %collective-permute-start.8) | collective-permute-done | bytes 98336 | tf_op jit(solution)/shard_map/ppermute | solution.py:39
  89.0 3.2 %shard_map.114 = (bf16[24,2,32,128]{3,2,1,0:T(8,128)(2,1)S(1)}, bf16[1280,128]{1,0:T(8,128)(2,1)S(1)}) custom-call(s32[1]{0:T(128)} %bitcast.half, bf16[64,768]{1,0:T(8,128)(2,1)S(1)} %get-tuple-element.39.refs_3_.refs_0_, bf16[64,768]{1,0:T(8,128)(2,1)S(1)} %collective-permute-done.7.refs_1_, bf16[64,768]{1,0:T(8,128)(2,1)S(1)} %collective-permute-done.8.refs_2_, ...), custom_call_target="tpu_custom_call" | custom-call | tf_op jit(solution)/shard_map/pallas_call | solution.py:22
  92.2 0.8 pad_maximum_fusion
  93.0 16.4 %all-to-all-start.2 = ((bf16[32,56,128]{2,1,0:T(8,128)(2,1)}), bf16[32,56,128]{2,1,0:T(8,128)(2,1)S(1)}, u32[]{:S(2)}, u32[]{:S(2)}) async-start(bf16[32,56,128]{2,1,0:T(8,128)(2,1)} %pad_maximum_fusion), calls=%async_computation.2 | async-start | bytes 917504 | tf_op jit(solution)/shard_map/all_to_all | solution.py:331
  109.4 1.3 collective-permute-start.10
  110.7 4.0 %collective-permute-start.9 = (bf16[24,1,32,128]{3,2,1,0:T(8,128)(2,1)S(1)}, bf16[24,1,32,128]{3,2,1,0:T(8,128)(2,1)S(1)}, u32[]{:S(2)}, u32[]{:S(2)}) collective-permute-start(bf16[24,1,32,128]{3,2,1,0:T(8,128)(2,1)S(1)} %get-tuple-element.67), channel_id=1, source_target_pairs={{0,16},{1,17},{2,18},{3,19},{4,20},{5,21},{6,22},{7,23},{8,24},{9,... | collective-permute-start | bytes 589832 | tf_op jit(solution)/shard_map/ppermute | solution.py:39
  114.9 6.6 %collective-permute-done.10.refs_2_ = bf16[24,1,32,128]{3,2,1,0:T(8,128)(2,1)S(1)} collective-permute-done((bf16[24,1,32,128]{3,2,1,0:T(8,128)(2,1)S(1)}, bf16[24,1,32,128]{3,2,1,0:T(8,128)(2,1)S(1)}, u32[]{:S(2)}, u32[]{:S(2)}) %collective-permute-start.10) | collective-permute-done | bytes 196640 | tf_op jit(solution)/shard_map/ppermute | solution.py:39
  121.5 0.8 shard_map.115
  122.6 0.7 pad_maximum_fusion.1
  123.3 12.0 %all-to-all-start.3 = ((bf16[16,72,128]{2,1,0:T(8,128)(2,1)}), bf16[16,72,128]{2,1,0:T(8,128)(2,1)S(1)}, u32[]{:S(2)}, u32[]{:S(2)}) async-start(bf16[16,72,128]{2,1,0:T(8,128)(2,1)} %pad_maximum_fusion.1), calls=%async_computation.3 | async-start | bytes 589824 | tf_op jit(solution)/shard_map/all_to_all | solution.py:331
  135.4 12.0 %collective-permute-start.11 = (bf16[2,2,2,2,32,128]{5,4,3,2,1,0:T(8,128)(2,1)S(1)}, bf16[2,2,2,2,32,128]{5,4,3,2,1,0:T(8,128)(2,1)S(1)}, u32[]{:S(2)}, u32[]{:S(2)}) collective-permute-start(bf16[2,2,2,2,32,128]{5,4,3,2,1,0:T(8,128)(2,1)S(1)} %fusion), channel_id=1, source_target_pairs={{0,2},{1,3},{2,0},{3,1},{4,6},{5,7},{6,4},{7,5},{8,10},{9,11},{10,... | collective-permute-start | bytes 393224 | tf_op jit(solution)/shard_map/ppermute | solution.py:413
  147.4 4.6 %all-to-all-done.3 = bf16[16,72,128]{2,1,0:T(8,128)(2,1)S(1)} async-done(((bf16[16,72,128]{2,1,0:T(8,128)(2,1)}), bf16[16,72,128]{2,1,0:T(8,128)(2,1)S(1)}, u32[]{:S(2)}, u32[]{:S(2)}) %all-to-all-start.3) | async-done | bytes 294944 | tf_op jit(solution)/shard_map/all_to_all | solution.py:331
  152.1 0.8 broadcast_in_dim.8
  152.9 14.6 %all-to-all-start.4 = ((bf16[32,40,128]{2,1,0:T(8,128)(2,1)}), bf16[32,40,128]{2,1,0:T(8,128)(2,1)S(1)}, u32[]{:S(2)}, u32[]{:S(2)}) async-start(bf16[32,40,128]{2,1,0:T(8,128)(2,1)} %broadcast_in_dim.8), calls=%async_computation.4 | async-start | bytes 655360 | tf_op jit(solution)/shard_map/all_to_all | solution.py:331
  167.6 9.4 %all-to-all-done.4 = bf16[32,40,128]{2,1,0:T(8,128)(2,1)S(1)} async-done(((bf16[32,40,128]{2,1,0:T(8,128)(2,1)}), bf16[32,40,128]{2,1,0:T(8,128)(2,1)S(1)}, u32[]{:S(2)}, u32[]{:S(2)}) %all-to-all-start.4) | async-done | bytes 327712 | tf_op jit(solution)/shard_map/all_to_all | solution.py:331
  177.1 0.8 copy.58
  177.9 3.8 %all-to-all-start.5 = ((bf16[4,2,2,2,32,128]{5,4,3,2,1,0:T(8,128)(2,1)}), bf16[4,2,2,2,32,128]{5,4,3,2,1,0:T(8,128)(2,1)S(1)}, u32[]{:S(2)}, u32[]{:S(2)}) async-start(bf16[4,2,2,2,32,128]{5,4,3,2,1,0:T(8,128)(2,1)} %bitcast.45), calls=%async_computation.5 | async-start | bytes 524288 | tf_op jit(solution)/shard_map/all_to_all | solution.py:331
  181.7 0.6 slice_select_fusion.1
  182.3 1.7 shard_map.116
  184.0 2.3 %shard_map.117 = (f32[27,32,32]{2,1,0:T(8,128)}, f32[8,32,64]{2,1,0:T(8,128)}, f32[27,64,64]{2,1,0:T(8,128)}) custom-call(bf16[1280,128]{1,0:T(8,128)(2,1)} %bitcast.107), custom_call_target="tpu_custom_call" | custom-call | tf_op jit(solution)/shard_map/pallas_call | solution.py:546
  186.4 0.5 all-to-all-done.5
  186.9 0.9 copy.60
  (61 shorter events, 1.8 us)
Async XLA Ops:
  0.6 31.3 %copy-start.2 = (bf16[27,64,64]{2,1,0:T(8,128)(2,1)S(1)}, bf16[27,64,64]{2,1,0:T(8,128)(2,1)}, u32[]{:S(2)}) copy-start(bf16[27,64,64]{2,1,0:T(8,128)(2,1)} %param.10) | copy-start | bytes 663556
  0.6 35.0 %all-to-all-start = ((bf16[8,2,2,32,128]{4,2,1,3,0:T(2,128)(2,1)}), bf16[8,2,2,32,128]{4,2,1,3,0:T(2,128)(2,1)S(1)}, u32[]{:S(2)}, u32[]{:S(2)}) async-start(bf16[8,2,2,32,128]{4,2,1,3,0:T(2,128)(2,1)} %bitcast.121), calls=%async_computation | async-start | bytes 524288 | tf_op jit(solution)/shard_map/all_to_all | solution.py:331
  18.3 13.6 %copy-start.6 = (bf16[8,64,32]{1,2,0:T(8,128)(2,1)S(1)}, bf16[8,64,32]{1,2,0:T(8,128)(2,1)}, u32[]{:S(2)}) copy-start(bf16[8,64,32]{1,2,0:T(8,128)(2,1)} %param.9) | copy-start | bytes 98308
  19.9 21.7 %collective-permute-start = (bf16[256,128]{1,0:T(8,128)(2,1)}, bf16[256,128]{1,0:T(8,128)(2,1)}, u32[]{:S(2)}, u32[]{:S(2)}) collective-permute-start(bf16[256,128]{1,0:T(8,128)(2,1)} %shard_map.110), channel_id=1, source_target_pairs={{0,71},{1,135},{2,199},{3,263},{4,327},{5,391},{6,455},{7,7},{8,79... | collective-permute-start | bytes 196616 | tf_op jit(solution)/shard_map/ppermute | solution.py:350
  34.0 0.9 copy-start.5
  41.6 14.5 %collective-permute-start.1 = (bf16[8,2,32,128]{3,2,1,0:T(8,128)(2,1)S(1)}, bf16[8,2,32,128]{3,2,1,0:T(8,128)(2,1)S(1)}, u32[]{:S(2)}, u32[]{:S(2)}) collective-permute-start(bf16[8,2,32,128]{3,2,1,0:T(8,128)(2,1)S(1)} %slice_select_fusion), channel_id=1, source_target_pairs={{8,0},{9,1},{10,2},{11,3},{12,4},{13,5},{14,6},{15,7},{0,8},{1,9},... | collective-permute-start | bytes 393224 | tf_op jit(solution)/shard_map/ppermute | solution.py:39
  46.0 21.4 %all-to-all-start.1 = ((bf16[32,8,128]{2,1,0:T(8,128)(2,1)}), bf16[32,8,128]{2,1,0:T(8,128)(2,1)S(1)}, u32[]{:S(2)}, u32[]{:S(2)}) async-start(bf16[32,8,128]{2,1,0:T(8,128)(2,1)} %bitcast.4), calls=%async_computation.1 | async-start | bytes 131072 | tf_op jit(solution)/shard_map/all_to_all | solution.py:331
  56.2 13.8 %collective-permute-start.2 = (bf16[24,1,32,128]{3,2,1,0:T(8,128)(2,1)S(1)}, bf16[24,1,32,128]{3,2,1,0:T(8,128)(2,1)S(1)}, u32[]{:S(2)}, u32[]{:S(2)}) collective-permute-start(bf16[24,1,32,128]{3,2,1,0:T(8,128)(2,1)S(1)} %get-tuple-element.69), channel_id=1, source_target_pairs={{0,16},{1,17},{2,18},{3,19},{4,20},{5,21},{6,22},{7,23},{8,24},{9,... | collective-permute-start | bytes 589832 | tf_op jit(solution)/shard_map/ppermute | solution.py:39
  59.4 10.6 %collective-permute-start.3 = (bf16[24,1,32,128]{3,2,1,0:T(8,128)(2,1)S(1)}, bf16[24,1,32,128]{3,2,1,0:T(8,128)(2,1)S(1)}, u32[]{:S(2)}, u32[]{:S(2)}) collective-permute-start(bf16[24,1,32,128]{3,2,1,0:T(8,128)(2,1)S(1)} %get-tuple-element.68), channel_id=1, source_target_pairs={{16,0},{17,1},{18,2},{19,3},{20,4},{21,5},{22,6},{23,7},{24,8},{25... | collective-permute-start | bytes 589832 | tf_op jit(solution)/shard_map/ppermute | solution.py:39
  67.4 2.6 %copy-start.1 = (bf16[256,256]{1,0:T(8,128)(2,1)S(1)}, bf16[256,256]{1,0:T(8,128)(2,1)}, u32[]{:S(2)}) copy-start(bf16[256,256]{1,0:T(8,128)(2,1)} %constant.114.clone.refs_5_) | copy-start | bytes 393220
  67.4 9.1 %collective-permute-start.6 = (bf16[128,128]{1,0:T(8,128)(2,1)S(1)}, bf16[128,128]{1,0:T(8,128)(2,1)S(1)}, u32[]{:S(2)}, u32[]{:S(2)}) collective-permute-start(bf16[128,128]{1,0:T(8,128)(2,1)S(1)} %fusion.7), channel_id=1, source_target_pairs={{8,0},{9,1},{10,2},{11,3},{12,4},{13,5},{14,6},{15,7},{0,8},{1,9},... | collective-permute-start | bytes 98312 | tf_op jit(solution)/shard_map/ppermute | solution.py:39
  73.1 3.8 %collective-permute-start.4 = (bf16[64,768]{1,0:T(8,128)(2,1)S(1)}, bf16[64,768]{1,0:T(8,128)(2,1)S(1)}, u32[]{:S(2)}, u32[]{:S(2)}) collective-permute-start(bf16[64,768]{1,0:T(8,128)(2,1)S(1)} %get-tuple-element.35.refs_0_), channel_id=1, source_target_pairs={{0,16},{1,17},{2,18},{3,19},{4,20},{5,21},{6,22},{7,23},{8,24},{9,... | collective-permute-start | bytes 294920 | tf_op jit(solution)/shard_map/ppermute | solution.py:39
  75.3 5.4 %collective-permute-start.5 = (bf16[64,768]{1,0:T(8,128)(2,1)S(1)}, bf16[64,768]{1,0:T(8,128)(2,1)S(1)}, u32[]{:S(2)}, u32[]{:S(2)}) collective-permute-start(bf16[64,768]{1,0:T(8,128)(2,1)S(1)} %get-tuple-element.35.refs_0_), channel_id=1, source_target_pairs={{16,0},{17,1},{18,2},{19,3},{20,4},{21,5},{22,6},{23,7},{24,8},{25... | collective-permute-start | bytes 294920 | tf_op jit(solution)/shard_map/ppermute | solution.py:39
  81.3 4.4 %collective-permute-start.7 = (bf16[64,768]{1,0:T(8,128)(2,1)S(1)}, bf16[64,768]{1,0:T(8,128)(2,1)S(1)}, u32[]{:S(2)}, u32[]{:S(2)}) collective-permute-start(bf16[64,768]{1,0:T(8,128)(2,1)S(1)} %get-tuple-element.39.refs_3_.refs_0_), channel_id=1, source_target_pairs={{0,16},{1,17},{2,18},{3,19},{4,20},{5,21},{6,22},{7,23},{8,24},{9,... | collective-permute-start | bytes 294920 | tf_op jit(solution)/shard_map/ppermute | solution.py:39
  83.6 5.4 %collective-permute-start.8 = (bf16[64,768]{1,0:T(8,128)(2,1)S(1)}, bf16[64,768]{1,0:T(8,128)(2,1)S(1)}, u32[]{:S(2)}, u32[]{:S(2)}) collective-permute-start(bf16[64,768]{1,0:T(8,128)(2,1)S(1)} %get-tuple-element.39.refs_3_.refs_0_), channel_id=1, source_target_pairs={{16,0},{17,1},{18,2},{19,3},{20,4},{21,5},{22,6},{23,7},{24,8},{25... | collective-permute-start | bytes 294920 | tf_op jit(solution)/shard_map/ppermute | solution.py:39
  85.1 4.0 %copy-start = (bf16[256,256]{1,0:T(8,128)(2,1)S(1)}, bf16[256,256]{1,0:T(8,128)(2,1)}, u32[]{:S(2)}) copy-start(bf16[256,256]{1,0:T(8,128)(2,1)} %constant.115.clone.refs_8_) | copy-start | bytes 393220
  93.0 29.3 %all-to-all-start.2 = ((bf16[32,56,128]{2,1,0:T(8,128)(2,1)}), bf16[32,56,128]{2,1,0:T(8,128)(2,1)S(1)}, u32[]{:S(2)}, u32[]{:S(2)}) async-start(bf16[32,56,128]{2,1,0:T(8,128)(2,1)} %pad_maximum_fusion), calls=%async_computation.2 | async-start | bytes 917504 | tf_op jit(solution)/shard_map/all_to_all | solution.py:331
  109.4 12.1 %collective-permute-start.10 = (bf16[24,1,32,128]{3,2,1,0:T(8,128)(2,1)S(1)}, bf16[24,1,32,128]{3,2,1,0:T(8,128)(2,1)S(1)}, u32[]{:S(2)}, u32[]{:S(2)}) collective-permute-start(bf16[24,1,32,128]{3,2,1,0:T(8,128)(2,1)S(1)} %get-tuple-element.66), channel_id=1, source_target_pairs={{16,0},{17,1},{18,2},{19,3},{20,4},{21,5},{22,6},{23,7},{24,8},{25... | collective-permute-start | bytes 589832 | tf_op jit(solution)/shard_map/ppermute | solution.py:39
  110.7 10.8 %collective-permute-start.9 = (bf16[24,1,32,128]{3,2,1,0:T(8,128)(2,1)S(1)}, bf16[24,1,32,128]{3,2,1,0:T(8,128)(2,1)S(1)}, u32[]{:S(2)}, u32[]{:S(2)}) collective-permute-start(bf16[24,1,32,128]{3,2,1,0:T(8,128)(2,1)S(1)} %get-tuple-element.67), channel_id=1, source_target_pairs={{0,16},{1,17},{2,18},{3,19},{4,20},{5,21},{6,22},{7,23},{8,24},{9,... | collective-permute-start | bytes 589832 | tf_op jit(solution)/shard_map/ppermute | solution.py:39
  123.3 28.7 %all-to-all-start.3 = ((bf16[16,72,128]{2,1,0:T(8,128)(2,1)}), bf16[16,72,128]{2,1,0:T(8,128)(2,1)S(1)}, u32[]{:S(2)}, u32[]{:S(2)}) async-start(bf16[16,72,128]{2,1,0:T(8,128)(2,1)} %pad_maximum_fusion.1), calls=%async_computation.3 | async-start | bytes 589824 | tf_op jit(solution)/shard_map/all_to_all | solution.py:331
  135.4 32.2 %collective-permute-start.11 = (bf16[2,2,2,2,32,128]{5,4,3,2,1,0:T(8,128)(2,1)S(1)}, bf16[2,2,2,2,32,128]{5,4,3,2,1,0:T(8,128)(2,1)S(1)}, u32[]{:S(2)}, u32[]{:S(2)}) collective-permute-start(bf16[2,2,2,2,32,128]{5,4,3,2,1,0:T(8,128)(2,1)S(1)} %fusion), channel_id=1, source_target_pairs={{0,2},{1,3},{2,0},{3,1},{4,6},{5,7},{6,4},{7,5},{8,10},{9,11},{10,... | collective-permute-start | bytes 393224 | tf_op jit(solution)/shard_map/ppermute | solution.py:413
  152.0 15.6 %copy-start.4 = (bf16[16,72,128]{2,1,0:T(8,128)(2,1)}, bf16[16,72,128]{2,1,0:T(8,128)(2,1)S(1)}, u32[]{:S(2)}) copy-start(bf16[16,72,128]{2,1,0:T(8,128)(2,1)S(1)} %all-to-all-done.3) | copy-start | bytes 884740
  152.9 24.2 %all-to-all-start.4 = ((bf16[32,40,128]{2,1,0:T(8,128)(2,1)}), bf16[32,40,128]{2,1,0:T(8,128)(2,1)S(1)}, u32[]{:S(2)}, u32[]{:S(2)}) async-start(bf16[32,40,128]{2,1,0:T(8,128)(2,1)} %broadcast_in_dim.8), calls=%async_computation.4 | async-start | bytes 655360 | tf_op jit(solution)/shard_map/all_to_all | solution.py:331
  177.0 0.8 copy-start.3
  177.8 3.9 %slice-start = ((bf16[16,72,128]{2,1,0:T(8,128)(2,1)}), bf16[16,32,128]{2,1,0:T(8,128)(2,1)S(1)}, s32[]{:S(2)}) async-start(bf16[16,72,128]{2,1,0:T(8,128)(2,1)} %copy-done.4), calls=%async_computation.6 | async-start | bytes 262144 | tf_op jit(solution)/shard_map/slice | solution.py:535
  177.9 9.0 %all-to-all-start.5 = ((bf16[4,2,2,2,32,128]{5,4,3,2,1,0:T(8,128)(2,1)}), bf16[4,2,2,2,32,128]{5,4,3,2,1,0:T(8,128)(2,1)S(1)}, u32[]{:S(2)}, u32[]{:S(2)}) async-start(bf16[4,2,2,2,32,128]{5,4,3,2,1,0:T(8,128)(2,1)} %bitcast.45), calls=%async_computation.5 | async-start | bytes 524288 | tf_op jit(solution)/shard_map/all_to_all | solution.py:331

commit v6 on v4

--- a/solution.py
+++ b/solution.py
@@ -402,10 +402,6 @@
     return jnp.where(sample // 2 % 2 == 0, parts[:, 0], parts[:, 1]).reshape(-1, LANES)
 
 
-def after(value, *others):
-    return lax.optimization_barrier((value, *others))[0]
-
-
 def far_side():
     return lax.axis_index("sp") // 2 % 2
 
@@ -468,8 +464,8 @@
     block = (rows, width // 2 // rows, LANES)
     cells = pl.pallas_call(
         pack_kernel, out_shape=shape((width // 2, LANES), BF16), interpret=INTERPRET
-    )(turned(cotangent.reshape(chans3, width)))
-    cells = cells.reshape(block)
+    )(cotangent.reshape(chans3, width))
+    cells = turned(cells).reshape(block)
     matrices = [
         tap_matrix(weight_fine),
         tap_matrix(reversed_taps(weight_fine)),
@@ -478,8 +474,7 @@
         down_matrix,
         down_matrix.T,
     ]
-    own, *matrices = lax.optimization_barrier((own, *matrices))
-    cells = after(cells, own)
+    own, cells, *matrices = lax.optimization_barrier((own, cells, *matrices))
     fine_matrix, fine_back, coarse_matrix, coarse_back, down_matrix, up_matrix = matrices
     own = joined(own, arrival(nearest(own, reach() * x_cells), 0, True))
     cells = jnp.roll(trade(cells, "grp"), -(QUARTERS // 2), axis=0).reshape(width // 2, LANES)
@@ -532,6 +527,8 @@
         coarse_grad,
     )
     coarse = jnp.where(upper_half() == 0, coarse[: width // 2], coarse[-(width // 2) :])
+    spread = fine_pieces(dpre2)
+    grads, *spread[1:] = lax.optimization_barrier((grads, *spread[1:]))
     grads = grads.reshape(len(near[0]), -1, LANES)
     kept = grads.shape[1]
     coarse = for_plane(coarse.reshape(batch, QUARTERS, 8, LANES))
@@ -542,16 +539,15 @@
         input_kernel,
         shape((batch * x_cells, *own.shape[1:]), BF16),
         half,
-        *fine_pieces(dpre2),
+        *spread,
         fine_back,
     )
-    part, coarse = after(part, gradient), after(coarse, gradient)
+    part, gradient, coarse = lax.optimization_barrier((part, gradient, coarse))
     gradient = far_exchange(gradient.reshape(batch // 4, 2, 2, x_cells, y_cells, chans, LANES))
     part = jnp.broadcast_to(part[None], (coarse.shape[0], *part.shape))
     mixed = trade(jnp.concatenate([part, coarse], axis=1), ("grp", "sp"), columns())
     part = jnp.sum(mixed[:, :kept].astype(F32), axis=0).astype(BF16)
     coarse = from_column(mixed[:, kept:])
-    gradient = after(gradient, part)
     grads = share(part, ("grp", "sp"), near).reshape(grad_rows, LANES)
     gradient = near_exchange(gradient)
     grads, gradient = lax.optimization_barrier((grads, gradient))

time: 210 us -> 193 us (0.919)
  waiting for transfers between devices: 67.4 us -> 51.2 us
    ppermute x1, waiting for transfers between devices: 19.3 us -> 0.01 us  [far_exchange(): lax.ppermute(sent, 'sp', [(col, col ^ 2) for col in range(lax.axis_size('...]
    ppermute x1, starting transfers between devices: 3.53 us -> 12 us  [turned(): return lax.ppermute(block, ('grp', 'sp'), pairs)]
    all_to_all x5, waiting for transfers between devices: 24.1 us -> 32.5 us  [trade(): lax.all_to_all(parts, axis, split_axis=0, concat_axis=0, axis_index_group...]
    ppermute x1, starting transfers between devices: 12 us -> 4.47 us  [far_exchange(): lax.ppermute(sent, 'sp', [(col, col ^ 2) for col in range(lax.axis_size('...]
    ppermute x1, waiting for transfers between devices: 9.98 us -> 5.85 us  [turned(): return lax.ppermute(block, ('grp', 'sp'), pairs)]
    ppermute x10, waiting for transfers between devices: 14 us -> 9.95 us  [arrival(): return lax.ppermute(block, ('grp', 'sp'), pairs)]
    ppermute x3, starting transfers between devices: 11.8 us -> 8.33 us  [near_exchange(): lax.ppermute(parts[x, c], 'sp', [(col, col ^ 4 * x + c) for col in range(...]
    ppermute x3, waiting for transfers between devices: 0.01 us -> 2.91 us  [near_exchange(): lax.ppermute(parts[x, c], 'sp', [(col, col ^ 4 * x + c) for col in range(...]
  transfers between devices with their start and end apart: 20 -> 20, of which waited for: 9 -> 12; matrix products, arithmetic and copies ran while one was open for 3% -> 3% of each run, Pallas kernels for 4% -> 4%
where the time goes in v6:
time: 193 us; the launch traced here: 192 us
  starting transfers between devices  116 us (60%)
  waiting for transfers between devices  51.2 us (27%)
  Pallas kernels  13.9 us (7%)
  local copies, waits for them, and re-layouts  6.97 us (4%)
  other arithmetic  2.9 us (2%)
    all_to_all x5, starting transfers between devices, trade(): lax.all_to_all(parts, axis, split_axis=0, concat_axis=0, axis_index_group...  65.1 us
    all_to_all x5, waiting for transfers between devices, trade(): lax.all_to_all(parts, axis, split_axis=0, concat_axis=0, axis_index_group...  32.5 us
    ppermute x10, starting transfers between devices, arrival(): return lax.ppermute(block, ('grp', 'sp'), pairs)  25.8 us
    ppermute x1, starting transfers between devices, turned(): return lax.ppermute(block, ('grp', 'sp'), pairs)  12 us
    ppermute x10, waiting for transfers between devices, arrival(): return lax.ppermute(block, ('grp', 'sp'), pairs)  9.95 us
    ppermute x3, starting transfers between devices, near_exchange(): lax.ppermute(parts[x, c], 'sp', [(col, col ^ 4 * x + c) for col in range(...  8.33 us
    pallas_call x5, Pallas kernels, call(): pl.pallas_call(kernel, out_shape=outs, in_specs=[pl.BlockSpec(memory_spac...  8.26 us
    ppermute x1, waiting for transfers between devices, turned(): return lax.ppermute(block, ('grp', 'sp'), pairs)  5.85 us
  transfers between devices with their start and end apart: 20, of which 12 were waited for; matrix products, arithmetic and copies ran while one was open for 3% of the time, Pallas kernels for 4%

profile of v6, /device:TPU:1, one launch (start us, length us, event | category | flops | bytes accessed | tf_op | source)
XLA Modules:
  0.0 192.1 jit_solution(3624301347385601988)
XLA Ops:
  0.6 17.7 %all-to-all-start = ((bf16[8,2,2,32,128]{4,2,1,3,0:T(2,128)(2,1)}), bf16[8,2,2,32,128]{4,2,1,3,0:T(2,128)(2,1)S(1)}, u32[]{:S(2)}, u32[]{:S(2)}) async-start(bf16[8,2,2,32,128]{4,2,1,3,0:T(2,128)(2,1)} %bitcast.138), calls=%async_computation | async-start | bytes 524288 | tf_op jit(solution)/shard_map/all_to_all | solution.py:331
  18.3 1.6 shard_map.110
  19.9 12.0 %collective-permute-start = (bf16[256,128]{1,0:T(8,128)(2,1)}, bf16[256,128]{1,0:T(8,128)(2,1)}, u32[]{:S(2)}, u32[]{:S(2)}) collective-permute-start(bf16[256,128]{1,0:T(8,128)(2,1)} %shard_map.110), channel_id=1, source_target_pairs={{0,71},{1,135},{2,199},{3,263},{4,327},{5,391},{6,455},{7,7},{8,79... | collective-permute-start | bytes 196616 | tf_op jit(solution)/shard_map/ppermute | solution.py:350
  32.0 0.4 copy.82
  32.4 0.4 reshape.113
  32.8 1.2 copy.55
  34.4 0.6 copy-done.4
  35.7 5.9 %collective-permute-done = bf16[256,128]{1,0:T(8,128)(2,1)} collective-permute-done((bf16[256,128]{1,0:T(8,128)(2,1)}, bf16[256,128]{1,0:T(8,128)(2,1)}, u32[]{:S(2)}, u32[]{:S(2)}) %collective-permute-start) | collective-permute-done | bytes 65568 | tf_op jit(solution)/shard_map/ppermute | solution.py:350
  41.6 4.4 %collective-permute-start.1 = (bf16[8,2,32,128]{3,2,1,0:T(8,128)(2,1)S(1)}, bf16[8,2,32,128]{3,2,1,0:T(8,128)(2,1)S(1)}, u32[]{:S(2)}, u32[]{:S(2)}) collective-permute-start(bf16[8,2,32,128]{3,2,1,0:T(8,128)(2,1)S(1)} %slice_select_fusion), channel_id=1, source_target_pairs={{8,0},{9,1},{10,2},{11,3},{12,4},{13,5},{14,6},{15,7},{0,8},{1,9},... | collective-permute-start | bytes 393224 | tf_op jit(solution)/shard_map/ppermute | solution.py:39
  46.0 9.6 %all-to-all-start.1 = ((bf16[32,8,128]{2,1,0:T(8,128)(2,1)}), bf16[32,8,128]{2,1,0:T(8,128)(2,1)S(1)}, u32[]{:S(2)}, u32[]{:S(2)}) async-start(bf16[32,8,128]{2,1,0:T(8,128)(2,1)} %bitcast.4), calls=%async_computation.1 | async-start | bytes 131072 | tf_op jit(solution)/shard_map/all_to_all | solution.py:331
  56.2 3.1 %collective-permute-start.2 = (bf16[24,1,32,128]{3,2,1,0:T(8,128)(2,1)S(1)}, bf16[24,1,32,128]{3,2,1,0:T(8,128)(2,1)S(1)}, u32[]{:S(2)}, u32[]{:S(2)}) collective-permute-start(bf16[24,1,32,128]{3,2,1,0:T(8,128)(2,1)S(1)} %get-tuple-element.70), channel_id=1, source_target_pairs={{0,16},{1,17},{2,18},{3,19},{4,20},{5,21},{6,22},{7,23},{8,24},{9,... | collective-permute-start | bytes 589832 | tf_op jit(solution)/shard_map/ppermute | solution.py:39
  59.4 1.3 collective-permute-start.3
  60.7 6.7 %all-to-all-done.1 = bf16[32,8,128]{2,1,0:T(8,128)(2,1)S(1)} async-done(((bf16[32,8,128]{2,1,0:T(8,128)(2,1)}), bf16[32,8,128]{2,1,0:T(8,128)(2,1)S(1)}, u32[]{:S(2)}, u32[]{:S(2)}) %all-to-all-start.1) | async-done | bytes 65568 | tf_op jit(solution)/shard_map/all_to_all | solution.py:331
  67.4 2.6 %collective-permute-start.6 = (bf16[128,128]{1,0:T(8,128)(2,1)S(1)}, bf16[128,128]{1,0:T(8,128)(2,1)S(1)}, u32[]{:S(2)}, u32[]{:S(2)}) collective-permute-start(bf16[128,128]{1,0:T(8,128)(2,1)S(1)} %fusion.7), channel_id=1, source_target_pairs={{8,0},{9,1},{10,2},{11,3},{12,4},{13,5},{14,6},{15,7},{0,8},{1,9},... | collective-permute-start | bytes 98312 | tf_op jit(solution)/shard_map/ppermute | solution.py:39
  70.0 3.0 %shard_map.111 = (bf16[64,768]{1,0:T(8,128)(2,1)S(1)}, bf16[256,768]{1,0:T(8,128)(2,1)S(1)}, f32[12,128,128]{2,1,0:T(8,128)S(1)}) custom-call(s32[1]{0:T(128)} %bitcast.half, bf16[24,2,32,128]{3,2,1,0:T(8,128)(2,1)S(1)} %maximum_select_fusion.refs_0_.refs_3_, bf16[24,1,32,128]{3,2,1,0:T(8,128)(2,1)S(1)} %collective-permute-done.2.refs_1_.refs_4_, ...), custom_call_target="tpu_custom_call" | custom-call | tf_op jit(solution)/shard_map/pallas_call | solution.py:22
  73.1 2.2 %collective-permute-start.4 = (bf16[64,768]{1,0:T(8,128)(2,1)S(1)}, bf16[64,768]{1,0:T(8,128)(2,1)S(1)}, u32[]{:S(2)}, u32[]{:S(2)}) collective-permute-start(bf16[64,768]{1,0:T(8,128)(2,1)S(1)} %get-tuple-element.38.refs_0_), channel_id=1, source_target_pairs={{0,16},{1,17},{2,18},{3,19},{4,20},{5,21},{6,22},{7,23},{8,24},{9,... | collective-permute-start | bytes 294920 | tf_op jit(solution)/shard_map/ppermute | solution.py:39
  75.3 1.3 collective-permute-start.5
  76.9 3.7 %collective-permute-done.5.refs_2_ = bf16[64,768]{1,0:T(8,128)(2,1)S(1)} collective-permute-done((bf16[64,768]{1,0:T(8,128)(2,1)S(1)}, bf16[64,768]{1,0:T(8,128)(2,1)S(1)}, u32[]{:S(2)}, u32[]{:S(2)}) %collective-permute-start.5) | collective-permute-done | bytes 98336 | tf_op jit(solution)/shard_map/ppermute | solution.py:39
  80.6 0.7 shard_map.112
  81.3 2.4 %collective-permute-start.7 = (bf16[64,768]{1,0:T(8,128)(2,1)S(1)}, bf16[64,768]{1,0:T(8,128)(2,1)S(1)}, u32[]{:S(2)}, u32[]{:S(2)}) collective-permute-start(bf16[64,768]{1,0:T(8,128)(2,1)S(1)} %get-tuple-element.42.refs_3_.refs_0_), channel_id=1, source_target_pairs={{0,16},{1,17},{2,18},{3,19},{4,20},{5,21},{6,22},{7,23},{8,24},{9,... | collective-permute-start | bytes 294920 | tf_op jit(solution)/shard_map/ppermute | solution.py:39
  83.6 1.3 collective-permute-start.8
  85.0 0.6 shard_map.113.refs_11_
  85.6 3.4 %collective-permute-done.8.refs_2_ = bf16[64,768]{1,0:T(8,128)(2,1)S(1)} collective-permute-done((bf16[64,768]{1,0:T(8,128)(2,1)S(1)}, bf16[64,768]{1,0:T(8,128)(2,1)S(1)}, u32[]{:S(2)}, u32[]{:S(2)}) %collective-permute-start.8) | collective-permute-done | bytes 98336 | tf_op jit(solution)/shard_map/ppermute | solution.py:39
  89.0 3.2 %shard_map.114 = (bf16[24,2,32,128]{3,2,1,0:T(8,128)(2,1)S(1)}, bf16[1280,128]{1,0:T(8,128)(2,1)S(1)}) custom-call(s32[1]{0:T(128)} %bitcast.half, bf16[64,768]{1,0:T(8,128)(2,1)S(1)} %get-tuple-element.42.refs_3_.refs_0_, bf16[64,768]{1,0:T(8,128)(2,1)S(1)} %collective-permute-done.7.refs_1_, bf16[64,768]{1,0:T(8,128)(2,1)S(1)} %collective-permute-done.8.refs_2_, ...), custom_call_target="tpu_custom_call" | custom-call | tf_op jit(solution)/shard_map/pallas_call | solution.py:22
  92.2 1.3 collective-permute-start.10
  93.5 6.1 %collective-permute-start.9 = (bf16[24,1,32,128]{3,2,1,0:T(8,128)(2,1)S(1)}, bf16[24,1,32,128]{3,2,1,0:T(8,128)(2,1)S(1)}, u32[]{:S(2)}, u32[]{:S(2)}) collective-permute-start(bf16[24,1,32,128]{3,2,1,0:T(8,128)(2,1)S(1)} %get-tuple-element.68), channel_id=1, source_target_pairs={{0,16},{1,17},{2,18},{3,19},{4,20},{5,21},{6,22},{7,23},{8,24},{9,... | collective-permute-start | bytes 589832 | tf_op jit(solution)/shard_map/ppermute | solution.py:39
  99.7 1.0 collective-permute-done.10.refs_2_
  100.7 1.5 collective-permute-done.9.refs_1_
  102.2 0.8 pad_maximum_fusion
  103.0 17.5 %all-to-all-start.2 = ((bf16[32,56,128]{2,1,0:T(8,128)(2,1)}), bf16[32,56,128]{2,1,0:T(8,128)(2,1)S(1)}, u32[]{:S(2)}, u32[]{:S(2)}) async-start(bf16[32,56,128]{2,1,0:T(8,128)(2,1)} %pad_maximum_fusion), calls=%async_computation.2 | async-start | bytes 917504 | tf_op jit(solution)/shard_map/all_to_all | solution.py:331
  120.7 0.8 shard_map.115
  121.5 9.9 %all-to-all-done.2 = bf16[32,56,128]{2,1,0:T(8,128)(2,1)S(1)} async-done(((bf16[32,56,128]{2,1,0:T(8,128)(2,1)}), bf16[32,56,128]{2,1,0:T(8,128)(2,1)S(1)}, u32[]{:S(2)}, u32[]{:S(2)}) %all-to-all-start.2) | async-done | bytes 458784 | tf_op jit(solution)/shard_map/all_to_all | solution.py:331
  131.6 4.5 %collective-permute-start.11 = (bf16[2,2,2,2,32,128]{5,4,3,2,1,0:T(8,128)(2,1)S(1)}, bf16[2,2,2,2,32,128]{5,4,3,2,1,0:T(8,128)(2,1)S(1)}, u32[]{:S(2)}, u32[]{:S(2)}) collective-permute-start(bf16[2,2,2,2,32,128]{5,4,3,2,1,0:T(8,128)(2,1)S(1)} %fusion), channel_id=1, source_target_pairs={{0,2},{1,3},{2,0},{3,1},{4,6},{5,7},{6,4},{7,5},{8,10},{9,11},{10,... | collective-permute-start | bytes 393224 | tf_op jit(solution)/shard_map/ppermute | solution.py:413
  136.2 0.7 pad_maximum_fusion.1
  136.9 13.5 %all-to-all-start.3 = ((bf16[16,72,128]{2,1,0:T(8,128)(2,1)}), bf16[16,72,128]{2,1,0:T(8,128)(2,1)S(1)}, u32[]{:S(2)}, u32[]{:S(2)}) async-start(bf16[16,72,128]{2,1,0:T(8,128)(2,1)} %pad_maximum_fusion.1), calls=%async_computation.3 | async-start | bytes 589824 | tf_op jit(solution)/shard_map/all_to_all | solution.py:331
  150.6 2.9 %collective-permute-start.12 = (bf16[2,2,2,32,128]{4,3,2,1,0:T(8,128)(2,1)S(1)}, bf16[2,2,2,32,128]{4,3,2,1,0:T(8,128)(2,1)S(1)}, u32[]{:S(2)}, u32[]{:S(2)}) collective-permute-start(bf16[2,2,2,32,128]{4,3,2,1,0:T(8,128)(2,1)S(1)} %get-tuple-element.72), channel_id=1, source_target_pairs={{0,1},{1,0},{2,3},{3,2},{4,5},{5,4},{6,7},{7,6},{8,9},{9,8},{10,11... | collective-permute-start | bytes 196616 | tf_op jit(solution)/shard_map/ppermute | solution.py:432
  153.6 2.2 %collective-permute-start.13 = (bf16[2,2,2,32,128]{4,3,2,1,0:T(8,128)(2,1)S(1)}, bf16[2,2,2,32,128]{4,3,2,1,0:T(8,128)(2,1)S(1)}, u32[]{:S(2)}, u32[]{:S(2)}) collective-permute-start(bf16[2,2,2,32,128]{4,3,2,1,0:T(8,128)(2,1)S(1)} %get-tuple-element.74), channel_id=1, source_target_pairs={{0,4},{1,5},{2,6},{3,7},{4,0},{5,1},{6,2},{7,3},{8,12},{9,13},{10,... | collective-permute-start | bytes 196616 | tf_op jit(solution)/shard_map/ppermute | solution.py:432
  155.8 3.2 %collective-permute-start.14 = (bf16[2,2,2,32,128]{4,3,2,1,0:T(8,128)(2,1)S(1)}, bf16[2,2,2,32,128]{4,3,2,1,0:T(8,128)(2,1)S(1)}, u32[]{:S(2)}, u32[]{:S(2)}) collective-permute-start(bf16[2,2,2,32,128]{4,3,2,1,0:T(8,128)(2,1)S(1)} %get-tuple-element.73), channel_id=1, source_target_pairs={{0,5},{1,4},{2,7},{3,6},{4,1},{5,0},{6,3},{7,2},{8,13},{9,12},{10,... | collective-permute-start | bytes 196616 | tf_op jit(solution)/shard_map/ppermute | solution.py:432
  159.2 2.8 %collective-permute-done.14 = bf16[2,2,2,32,128]{4,3,2,1,0:T(8,128)(2,1)S(1)} collective-permute-done((bf16[2,2,2,32,128]{4,3,2,1,0:T(8,128)(2,1)S(1)}, bf16[2,2,2,32,128]{4,3,2,1,0:T(8,128)(2,1)S(1)}, u32[]{:S(2)}, u32[]{:S(2)}) %collective-permute-start.14) | collective-permute-done | bytes 65568 | tf_op jit(solution)/shard_map/ppermute | solution.py:432
  162.1 8.8 %all-to-all-done.3 = bf16[16,72,128]{2,1,0:T(8,128)(2,1)S(1)} async-done(((bf16[16,72,128]{2,1,0:T(8,128)(2,1)}), bf16[16,72,128]{2,1,0:T(8,128)(2,1)S(1)}, u32[]{:S(2)}, u32[]{:S(2)}) %all-to-all-start.3) | async-done | bytes 294944 | tf_op jit(solution)/shard_map/all_to_all | solution.py:331
  170.9 0.8 broadcast_in_dim.8
  171.7 6.9 %all-to-all-start.4 = ((bf16[32,40,128]{2,1,0:T(8,128)(2,1)}), bf16[32,40,128]{2,1,0:T(8,128)(2,1)S(1)}, u32[]{:S(2)}, u32[]{:S(2)}) async-start(bf16[32,40,128]{2,1,0:T(8,128)(2,1)} %broadcast_in_dim.8), calls=%async_computation.4 | async-start | bytes 655360 | tf_op jit(solution)/shard_map/all_to_all | solution.py:331
  178.7 0.6 slice_select_fusion.1
  179.4 1.7 shard_map.116
  181.1 7.1 %all-to-all-done.4 = bf16[32,40,128]{2,1,0:T(8,128)(2,1)S(1)} async-done(((bf16[32,40,128]{2,1,0:T(8,128)(2,1)}), bf16[32,40,128]{2,1,0:T(8,128)(2,1)S(1)}, u32[]{:S(2)}, u32[]{:S(2)}) %all-to-all-start.4) | async-done | bytes 327712 | tf_op jit(solution)/shard_map/all_to_all | solution.py:331
  188.2 0.7 copy-done.3
  188.9 2.3 %shard_map.117 = (f32[27,32,32]{2,1,0:T(8,128)}, f32[8,32,64]{2,1,0:T(8,128)}, f32[27,64,64]{2,1,0:T(8,128)}) custom-call(bf16[1280,128]{1,0:T(8,128)(2,1)} %bitcast.125), custom_call_target="tpu_custom_call" | custom-call | tf_op jit(solution)/shard_map/pallas_call | solution.py:561
  191.2 0.9 copy.74
  (68 shorter events, 3.1 us)
Async XLA Ops:
  0.6 31.3 %copy-start.2 = (bf16[27,64,64]{2,1,0:T(8,128)(2,1)S(1)}, bf16[27,64,64]{2,1,0:T(8,128)(2,1)}, u32[]{:S(2)}) copy-start(bf16[27,64,64]{2,1,0:T(8,128)(2,1)} %param.10) | copy-start | bytes 663556
  0.6 35.0 %all-to-all-start = ((bf16[8,2,2,32,128]{4,2,1,3,0:T(2,128)(2,1)}), bf16[8,2,2,32,128]{4,2,1,3,0:T(2,128)(2,1)S(1)}, u32[]{:S(2)}, u32[]{:S(2)}) async-start(bf16[8,2,2,32,128]{4,2,1,3,0:T(2,128)(2,1)} %bitcast.138), calls=%async_computation | async-start | bytes 524288 | tf_op jit(solution)/shard_map/all_to_all | solution.py:331
  18.3 13.6 %copy-start.5 = (bf16[8,64,32]{1,2,0:T(8,128)(2,1)S(1)}, bf16[8,64,32]{1,2,0:T(8,128)(2,1)}, u32[]{:S(2)}) copy-start(bf16[8,64,32]{1,2,0:T(8,128)(2,1)} %param.9) | copy-start | bytes 98308
  19.9 21.7 %collective-permute-start = (bf16[256,128]{1,0:T(8,128)(2,1)}, bf16[256,128]{1,0:T(8,128)(2,1)}, u32[]{:S(2)}, u32[]{:S(2)}) collective-permute-start(bf16[256,128]{1,0:T(8,128)(2,1)} %shard_map.110), channel_id=1, source_target_pairs={{0,71},{1,135},{2,199},{3,263},{4,327},{5,391},{6,455},{7,7},{8,79... | collective-permute-start | bytes 196616 | tf_op jit(solution)/shard_map/ppermute | solution.py:350
  34.0 0.9 copy-start.4
  41.6 14.5 %collective-permute-start.1 = (bf16[8,2,32,128]{3,2,1,0:T(8,128)(2,1)S(1)}, bf16[8,2,32,128]{3,2,1,0:T(8,128)(2,1)S(1)}, u32[]{:S(2)}, u32[]{:S(2)}) collective-permute-start(bf16[8,2,32,128]{3,2,1,0:T(8,128)(2,1)S(1)} %slice_select_fusion), channel_id=1, source_target_pairs={{8,0},{9,1},{10,2},{11,3},{12,4},{13,5},{14,6},{15,7},{0,8},{1,9},... | collective-permute-start | bytes 393224 | tf_op jit(solution)/shard_map/ppermute | solution.py:39
  46.0 21.4 %all-to-all-start.1 = ((bf16[32,8,128]{2,1,0:T(8,128)(2,1)}), bf16[32,8,128]{2,1,0:T(8,128)(2,1)S(1)}, u32[]{:S(2)}, u32[]{:S(2)}) async-start(bf16[32,8,128]{2,1,0:T(8,128)(2,1)} %bitcast.4), calls=%async_computation.1 | async-start | bytes 131072 | tf_op jit(solution)/shard_map/all_to_all | solution.py:331
  56.2 13.8 %collective-permute-start.2 = (bf16[24,1,32,128]{3,2,1,0:T(8,128)(2,1)S(1)}, bf16[24,1,32,128]{3,2,1,0:T(8,128)(2,1)S(1)}, u32[]{:S(2)}, u32[]{:S(2)}) collective-permute-start(bf16[24,1,32,128]{3,2,1,0:T(8,128)(2,1)S(1)} %get-tuple-element.70), channel_id=1, source_target_pairs={{0,16},{1,17},{2,18},{3,19},{4,20},{5,21},{6,22},{7,23},{8,24},{9,... | collective-permute-start | bytes 589832 | tf_op jit(solution)/shard_map/ppermute | solution.py:39
  59.4 10.6 %collective-permute-start.3 = (bf16[24,1,32,128]{3,2,1,0:T(8,128)(2,1)S(1)}, bf16[24,1,32,128]{3,2,1,0:T(8,128)(2,1)S(1)}, u32[]{:S(2)}, u32[]{:S(2)}) collective-permute-start(bf16[24,1,32,128]{3,2,1,0:T(8,128)(2,1)S(1)} %get-tuple-element.69), channel_id=1, source_target_pairs={{16,0},{17,1},{18,2},{19,3},{20,4},{21,5},{22,6},{23,7},{24,8},{25... | collective-permute-start | bytes 589832 | tf_op jit(solution)/shard_map/ppermute | solution.py:39
  67.4 2.6 %copy-start.1 = (bf16[256,256]{1,0:T(8,128)(2,1)S(1)}, bf16[256,256]{1,0:T(8,128)(2,1)}, u32[]{:S(2)}) copy-start(bf16[256,256]{1,0:T(8,128)(2,1)} %constant.129.clone.refs_5_) | copy-start | bytes 393220
  67.4 9.1 %collective-permute-start.6 = (bf16[128,128]{1,0:T(8,128)(2,1)S(1)}, bf16[128,128]{1,0:T(8,128)(2,1)S(1)}, u32[]{:S(2)}, u32[]{:S(2)}) collective-permute-start(bf16[128,128]{1,0:T(8,128)(2,1)S(1)} %fusion.7), channel_id=1, source_target_pairs={{8,0},{9,1},{10,2},{11,3},{12,4},{13,5},{14,6},{15,7},{0,8},{1,9},... | collective-permute-start | bytes 98312 | tf_op jit(solution)/shard_map/ppermute | solution.py:39
  73.1 3.8 %collective-permute-start.4 = (bf16[64,768]{1,0:T(8,128)(2,1)S(1)}, bf16[64,768]{1,0:T(8,128)(2,1)S(1)}, u32[]{:S(2)}, u32[]{:S(2)}) collective-permute-start(bf16[64,768]{1,0:T(8,128)(2,1)S(1)} %get-tuple-element.38.refs_0_), channel_id=1, source_target_pairs={{0,16},{1,17},{2,18},{3,19},{4,20},{5,21},{6,22},{7,23},{8,24},{9,... | collective-permute-start | bytes 294920 | tf_op jit(solution)/shard_map/ppermute | solution.py:39
  75.3 5.4 %collective-permute-start.5 = (bf16[64,768]{1,0:T(8,128)(2,1)S(1)}, bf16[64,768]{1,0:T(8,128)(2,1)S(1)}, u32[]{:S(2)}, u32[]{:S(2)}) collective-permute-start(bf16[64,768]{1,0:T(8,128)(2,1)S(1)} %get-tuple-element.38.refs_0_), channel_id=1, source_target_pairs={{16,0},{17,1},{18,2},{19,3},{20,4},{21,5},{22,6},{23,7},{24,8},{25... | collective-permute-start | bytes 294920 | tf_op jit(solution)/shard_map/ppermute | solution.py:39
  81.3 4.3 %collective-permute-start.7 = (bf16[64,768]{1,0:T(8,128)(2,1)S(1)}, bf16[64,768]{1,0:T(8,128)(2,1)S(1)}, u32[]{:S(2)}, u32[]{:S(2)}) collective-permute-start(bf16[64,768]{1,0:T(8,128)(2,1)S(1)} %get-tuple-element.42.refs_3_.refs_0_), channel_id=1, source_target_pairs={{0,16},{1,17},{2,18},{3,19},{4,20},{5,21},{6,22},{7,23},{8,24},{9,... | collective-permute-start | bytes 294920 | tf_op jit(solution)/shard_map/ppermute | solution.py:39
  83.6 5.4 %collective-permute-start.8 = (bf16[64,768]{1,0:T(8,128)(2,1)S(1)}, bf16[64,768]{1,0:T(8,128)(2,1)S(1)}, u32[]{:S(2)}, u32[]{:S(2)}) collective-permute-start(bf16[64,768]{1,0:T(8,128)(2,1)S(1)} %get-tuple-element.42.refs_3_.refs_0_), channel_id=1, source_target_pairs={{16,0},{17,1},{18,2},{19,3},{20,4},{21,5},{22,6},{23,7},{24,8},{25... | collective-permute-start | bytes 294920 | tf_op jit(solution)/shard_map/ppermute | solution.py:39
  85.0 4.0 %copy-start = (bf16[256,256]{1,0:T(8,128)(2,1)S(1)}, bf16[256,256]{1,0:T(8,128)(2,1)}, u32[]{:S(2)}) copy-start(bf16[256,256]{1,0:T(8,128)(2,1)} %constant.130.clone.refs_8_) | copy-start | bytes 393220
  92.2 8.5 %collective-permute-start.10 = (bf16[24,1,32,128]{3,2,1,0:T(8,128)(2,1)S(1)}, bf16[24,1,32,128]{3,2,1,0:T(8,128)(2,1)S(1)}, u32[]{:S(2)}, u32[]{:S(2)}) collective-permute-start(bf16[24,1,32,128]{3,2,1,0:T(8,128)(2,1)S(1)} %get-tuple-element.67), channel_id=1, source_target_pairs={{16,0},{17,1},{18,2},{19,3},{20,4},{21,5},{22,6},{23,7},{24,8},{25... | collective-permute-start | bytes 589832 | tf_op jit(solution)/shard_map/ppermute | solution.py:39
  93.5 8.7 %collective-permute-start.9 = (bf16[24,1,32,128]{3,2,1,0:T(8,128)(2,1)S(1)}, bf16[24,1,32,128]{3,2,1,0:T(8,128)(2,1)S(1)}, u32[]{:S(2)}, u32[]{:S(2)}) collective-permute-start(bf16[24,1,32,128]{3,2,1,0:T(8,128)(2,1)S(1)} %get-tuple-element.68), channel_id=1, source_target_pairs={{0,16},{1,17},{2,18},{3,19},{4,20},{5,21},{6,22},{7,23},{8,24},{9,... | collective-permute-start | bytes 589832 | tf_op jit(solution)/shard_map/ppermute | solution.py:39
  103.0 28.4 %all-to-all-start.2 = ((bf16[32,56,128]{2,1,0:T(8,128)(2,1)}), bf16[32,56,128]{2,1,0:T(8,128)(2,1)S(1)}, u32[]{:S(2)}, u32[]{:S(2)}) async-start(bf16[32,56,128]{2,1,0:T(8,128)(2,1)} %pad_maximum_fusion), calls=%async_computation.2 | async-start | bytes 917504 | tf_op jit(solution)/shard_map/all_to_all | solution.py:331
  131.6 18.8 %collective-permute-start.11 = (bf16[2,2,2,2,32,128]{5,4,3,2,1,0:T(8,128)(2,1)S(1)}, bf16[2,2,2,2,32,128]{5,4,3,2,1,0:T(8,128)(2,1)S(1)}, u32[]{:S(2)}, u32[]{:S(2)}) collective-permute-start(bf16[2,2,2,2,32,128]{5,4,3,2,1,0:T(8,128)(2,1)S(1)} %fusion), channel_id=1, source_target_pairs={{0,2},{1,3},{2,0},{3,1},{4,6},{5,7},{6,4},{7,5},{8,10},{9,11},{10,... | collective-permute-start | bytes 393224 | tf_op jit(solution)/shard_map/ppermute | solution.py:413
  136.9 34.0 %all-to-all-start.3 = ((bf16[16,72,128]{2,1,0:T(8,128)(2,1)}), bf16[16,72,128]{2,1,0:T(8,128)(2,1)S(1)}, u32[]{:S(2)}, u32[]{:S(2)}) async-start(bf16[16,72,128]{2,1,0:T(8,128)(2,1)} %pad_maximum_fusion.1), calls=%async_computation.3 | async-start | bytes 589824 | tf_op jit(solution)/shard_map/all_to_all | solution.py:331
  150.6 8.4 %collective-permute-start.12 = (bf16[2,2,2,32,128]{4,3,2,1,0:T(8,128)(2,1)S(1)}, bf16[2,2,2,32,128]{4,3,2,1,0:T(8,128)(2,1)S(1)}, u32[]{:S(2)}, u32[]{:S(2)}) collective-permute-start(bf16[2,2,2,32,128]{4,3,2,1,0:T(8,128)(2,1)S(1)} %get-tuple-element.72), channel_id=1, source_target_pairs={{0,1},{1,0},{2,3},{3,2},{4,5},{5,4},{6,7},{7,6},{8,9},{9,8},{10,11... | collective-permute-start | bytes 196616 | tf_op jit(solution)/shard_map/ppermute | solution.py:432
  153.6 5.6 %collective-permute-start.13 = (bf16[2,2,2,32,128]{4,3,2,1,0:T(8,128)(2,1)S(1)}, bf16[2,2,2,32,128]{4,3,2,1,0:T(8,128)(2,1)S(1)}, u32[]{:S(2)}, u32[]{:S(2)}) collective-permute-start(bf16[2,2,2,32,128]{4,3,2,1,0:T(8,128)(2,1)S(1)} %get-tuple-element.74), channel_id=1, source_target_pairs={{0,4},{1,5},{2,6},{3,7},{4,0},{5,1},{6,2},{7,3},{8,12},{9,13},{10,... | collective-permute-start | bytes 196616 | tf_op jit(solution)/shard_map/ppermute | solution.py:432
  155.8 6.2 %collective-permute-start.14 = (bf16[2,2,2,32,128]{4,3,2,1,0:T(8,128)(2,1)S(1)}, bf16[2,2,2,32,128]{4,3,2,1,0:T(8,128)(2,1)S(1)}, u32[]{:S(2)}, u32[]{:S(2)}) collective-permute-start(bf16[2,2,2,32,128]{4,3,2,1,0:T(8,128)(2,1)S(1)} %get-tuple-element.73), channel_id=1, source_target_pairs={{0,5},{1,4},{2,7},{3,6},{4,1},{5,0},{6,3},{7,2},{8,13},{9,12},{10,... | collective-permute-start | bytes 196616 | tf_op jit(solution)/shard_map/ppermute | solution.py:432
  171.7 16.5 %all-to-all-start.4 = ((bf16[32,40,128]{2,1,0:T(8,128)(2,1)}), bf16[32,40,128]{2,1,0:T(8,128)(2,1)S(1)}, u32[]{:S(2)}, u32[]{:S(2)}) async-start(bf16[32,40,128]{2,1,0:T(8,128)(2,1)} %broadcast_in_dim.8), calls=%async_computation.4 | async-start | bytes 655360 | tf_op jit(solution)/shard_map/all_to_all | solution.py:331
  188.2 0.7 copy-start.3

commit v7 on v5

--- a/solution.py
+++ b/solution.py
@@ -402,6 +402,10 @@
     return jnp.where(sample // 2 % 2 == 0, parts[:, 0], parts[:, 1]).reshape(-1, LANES)
 
 
+def following(value, other):
+    return lax.optimization_barrier((value, other))[0]
+
+
 def far_side():
     return lax.axis_index("sp") // 2 % 2
 
@@ -465,7 +469,6 @@
     fine_matrix, fine_back, coarse_matrix, coarse_back, down_matrix, up_matrix = matrices
     own = joined(own, arrival(nearest(own, reach() * x_cells), 0, True))
     cells = jnp.roll(trade(cells, "grp"), -(QUARTERS // 2), axis=0).reshape(width // 2, LANES)
-    upstream = joined(cells, arrival(nearest(cells, reach() * QUARTERS * block[1]), 0, True))
 
     feature_pieces = fine_pieces(own)
     down, sorted_act, slope = call(
@@ -481,6 +484,8 @@
         down_matrix,
         sort,
     )
+    cells = following(cells, down)
+    upstream = joined(cells, arrival(nearest(cells, reach() * QUARTERS * block[1]), 0, True))
     down_pieces = coarse_pieces(down)
     coarse, dpre3 = call(
         coarse_kernel,
@@ -528,11 +533,12 @@
         fine_back,
     )
     part, gradient, coarse = lax.optimization_barrier((part, gradient, coarse))
-    gradient = far_exchange(gradient.reshape(batch // 4, 2, 2, x_cells, y_cells, chans, LANES))
     part = jnp.broadcast_to(part[None], (coarse.shape[0], *part.shape))
     mixed = trade(jnp.concatenate([part, coarse], axis=1), ("grp", "sp"), columns())
     part = jnp.sum(mixed[:, :kept].astype(F32), axis=0).astype(BF16)
     coarse = from_column(mixed[:, kept:])
+    gradient = following(gradient, part)
+    gradient = far_exchange(gradient.reshape(batch // 4, 2, 2, x_cells, y_cells, chans, LANES))
     grads = share(part, ("grp", "sp"), near).reshape(grad_rows, LANES)
     grads, gradient = lax.optimization_barrier((grads, gradient))
     gradient = near_exchange(gradient)

time: 189 us -> 191 us (1.011)
  waiting for transfers between devices: 41.1 us -> 53.8 us
  starting transfers between devices: 122 us -> 111 us
    all_to_all x6, waiting for transfers between devices: 21.2 us -> 28.9 us  [trade(): lax.all_to_all(parts, axis, split_axis=0, concat_axis=0, axis_index_group...]
    all_to_all x6, starting transfers between devices: 74.1 us -> 66.6 us  [trade(): lax.all_to_all(parts, axis, split_axis=0, concat_axis=0, axis_index_group...]
    ppermute x1, waiting for transfers between devices: 0.01 us -> 4.88 us  [far_exchange(): lax.ppermute(sent, 'sp', [(col, col ^ 2) for col in range(lax.axis_size('...]
    ppermute x1, starting transfers between devices: 12 us -> 7.66 us  [far_exchange(): lax.ppermute(sent, 'sp', [(col, col ^ 2) for col in range(lax.axis_size('...]
  transfers between devices with their start and end apart: 18 -> 18, of which waited for: 9 -> 10; matrix products, arithmetic and copies ran while one was open for 3% -> 3% of each run, Pallas kernels for 5% -> 4%
where the time goes in v7:
time: 191 us; the launch traced here: 190 us
  starting transfers between devices  111 us (58%)
  waiting for transfers between devices  53.8 us (28%)
  Pallas kernels  13.9 us (7%)
  local copies, waits for them, and re-layouts  7.05 us (4%)
  other arithmetic  2.59 us (1%)
    all_to_all x6, starting transfers between devices, trade(): lax.all_to_all(parts, axis, split_axis=0, concat_axis=0, axis_index_group...  66.6 us
    all_to_all x6, waiting for transfers between devices, trade(): lax.all_to_all(parts, axis, split_axis=0, concat_axis=0, axis_index_group...  28.9 us
    ppermute x10, starting transfers between devices, arrival(): return lax.ppermute(block, ('grp', 'sp'), pairs)  25.2 us
    ppermute x10, waiting for transfers between devices, arrival(): return lax.ppermute(block, ('grp', 'sp'), pairs)  14.2 us
    ppermute x1, starting transfers between devices, turned(): return lax.ppermute(block, ('grp', 'sp'), pairs)  12 us
    pallas_call x5, Pallas kernels, call(): pl.pallas_call(kernel, out_shape=outs, in_specs=[pl.BlockSpec(memory_spac...  8.26 us
    ppermute x1, starting transfers between devices, far_exchange(): lax.ppermute(sent, 'sp', [(col, col ^ 2) for col in range(lax.axis_size('...  7.66 us
    ppermute x1, waiting for transfers between devices, turned(): return lax.ppermute(block, ('grp', 'sp'), pairs)  5.87 us
  transfers between devices with their start and end apart: 18, of which 10 were waited for; matrix products, arithmetic and copies ran while one was open for 3% of the time, Pallas kernels for 4%

profile of v7, /device:TPU:1, one launch (start us, length us, event | category | flops | bytes accessed | tf_op | source)
XLA Modules:
  0.0 190.1 jit_solution(5937705298544155004)
XLA Ops:
  0.6 17.7 %all-to-all-start = ((bf16[8,2,2,32,128]{4,2,1,3,0:T(2,128)(2,1)}), bf16[8,2,2,32,128]{4,2,1,3,0:T(2,128)(2,1)S(1)}, u32[]{:S(2)}, u32[]{:S(2)}) async-start(bf16[8,2,2,32,128]{4,2,1,3,0:T(2,128)(2,1)} %bitcast.119), calls=%async_computation | async-start | bytes 524288 | tf_op jit(solution)/shard_map/all_to_all | solution.py:331
  18.3 1.6 shard_map.110
  19.9 12.0 %collective-permute-start = (bf16[256,128]{1,0:T(8,128)(2,1)}, bf16[256,128]{1,0:T(8,128)(2,1)}, u32[]{:S(2)}, u32[]{:S(2)}) collective-permute-start(bf16[256,128]{1,0:T(8,128)(2,1)} %shard_map.110), channel_id=1, source_target_pairs={{0,71},{1,135},{2,199},{3,263},{4,327},{5,391},{6,455},{7,7},{8,79... | collective-permute-start | bytes 196616 | tf_op jit(solution)/shard_map/ppermute | solution.py:350
  32.0 0.4 copy.65
  32.4 0.4 reshape.115
  32.8 1.2 copy.44
  34.0 0.4 reshape.113
  34.4 0.6 copy-done.5
  35.3 0.2 copy.42
  35.7 5.9 %collective-permute-done = bf16[256,128]{1,0:T(8,128)(2,1)} collective-permute-done((bf16[256,128]{1,0:T(8,128)(2,1)}, bf16[256,128]{1,0:T(8,128)(2,1)}, u32[]{:S(2)}, u32[]{:S(2)}) %collective-permute-start) | collective-permute-done | bytes 65568 | tf_op jit(solution)/shard_map/ppermute | solution.py:350
  41.6 4.4 %collective-permute-start.1 = (bf16[8,2,32,128]{3,2,1,0:T(8,128)(2,1)S(1)}, bf16[8,2,32,128]{3,2,1,0:T(8,128)(2,1)S(1)}, u32[]{:S(2)}, u32[]{:S(2)}) collective-permute-start(bf16[8,2,32,128]{3,2,1,0:T(8,128)(2,1)S(1)} %slice_select_fusion), channel_id=1, source_target_pairs={{8,0},{9,1},{10,2},{11,3},{12,4},{13,5},{14,6},{15,7},{0,8},{1,9},... | collective-permute-start | bytes 393224 | tf_op jit(solution)/shard_map/ppermute | solution.py:39
  46.0 9.6 %all-to-all-start.1 = ((bf16[32,8,128]{2,1,0:T(8,128)(2,1)}), bf16[32,8,128]{2,1,0:T(8,128)(2,1)S(1)}, u32[]{:S(2)}, u32[]{:S(2)}) async-start(bf16[32,8,128]{2,1,0:T(8,128)(2,1)} %bitcast.4), calls=%async_computation.1 | async-start | bytes 131072 | tf_op jit(solution)/shard_map/all_to_all | solution.py:331
  55.7 3.1 %collective-permute-start.2 = (bf16[24,1,32,128]{3,2,1,0:T(8,128)(2,1)S(1)}, bf16[24,1,32,128]{3,2,1,0:T(8,128)(2,1)S(1)}, u32[]{:S(2)}, u32[]{:S(2)}) collective-permute-start(bf16[24,1,32,128]{3,2,1,0:T(8,128)(2,1)S(1)} %get-tuple-element.73), channel_id=1, source_target_pairs={{0,16},{1,17},{2,18},{3,19},{4,20},{5,21},{6,22},{7,23},{8,24},{9,... | collective-permute-start | bytes 589832 | tf_op jit(solution)/shard_map/ppermute | solution.py:39
  58.8 1.3 collective-permute-start.3
  60.4 7.0 %all-to-all-done.1 = bf16[32,8,128]{2,1,0:T(8,128)(2,1)S(1)} async-done(((bf16[32,8,128]{2,1,0:T(8,128)(2,1)}), bf16[32,8,128]{2,1,0:T(8,128)(2,1)S(1)}, u32[]{:S(2)}, u32[]{:S(2)}) %all-to-all-start.1) | async-done | bytes 65568 | tf_op jit(solution)/shard_map/all_to_all | solution.py:331
  67.4 3.0 %shard_map.111 = (bf16[64,768]{1,0:T(8,128)(2,1)S(1)}, bf16[256,768]{1,0:T(8,128)(2,1)S(1)}, f32[12,128,128]{2,1,0:T(8,128)S(1)}) custom-call(s32[1]{0:T(128)} %bitcast.half, bf16[24,2,32,128]{3,2,1,0:T(8,128)(2,1)S(1)} %maximum_select_fusion.refs_0_.refs_3_, bf16[24,1,32,128]{3,2,1,0:T(8,128)(2,1)S(1)} %collective-permute-done.2.refs_1_.refs_4_, ...), custom_call_target="tpu_custom_call" | custom-call | tf_op jit(solution)/shard_map/pallas_call | solution.py:22
  70.5 2.4 %collective-permute-start.6 = (bf16[128,128]{1,0:T(8,128)(2,1)S(1)}, bf16[128,128]{1,0:T(8,128)(2,1)S(1)}, u32[]{:S(2)}, u32[]{:S(2)}) collective-permute-start(bf16[128,128]{1,0:T(8,128)(2,1)S(1)} %slice_select_fusion.4), channel_id=1, source_target_pairs={{8,0},{9,1},{10,2},{11,3},{12,4},{13,5},{14,6},{15,7},{0,8},{1,9},... | collective-permute-start | bytes 98312 | tf_op jit(solution)/shard_map/ppermute | solution.py:39
  73.3 2.1 %collective-permute-start.4 = (bf16[64,768]{1,0:T(8,128)(2,1)S(1)}, bf16[64,768]{1,0:T(8,128)(2,1)S(1)}, u32[]{:S(2)}, u32[]{:S(2)}) collective-permute-start(bf16[64,768]{1,0:T(8,128)(2,1)S(1)} %get-tuple-element.37.refs_0_), channel_id=1, source_target_pairs={{0,16},{1,17},{2,18},{3,19},{4,20},{5,21},{6,22},{7,23},{8,24},{9,... | collective-permute-start | bytes 294920 | tf_op jit(solution)/shard_map/ppermute | solution.py:39
  75.5 1.3 collective-permute-start.5
  76.8 0.3 collective-permute-done.4.refs_1_
  77.1 3.9 %collective-permute-done.5.refs_2_ = bf16[64,768]{1,0:T(8,128)(2,1)S(1)} collective-permute-done((bf16[64,768]{1,0:T(8,128)(2,1)S(1)}, bf16[64,768]{1,0:T(8,128)(2,1)S(1)}, u32[]{:S(2)}, u32[]{:S(2)}) %collective-permute-start.5) | collective-permute-done | bytes 98336 | tf_op jit(solution)/shard_map/ppermute | solution.py:39
  81.0 0.7 shard_map.112
  81.7 4.0 %collective-permute-start.7 = (bf16[64,768]{1,0:T(8,128)(2,1)S(1)}, bf16[64,768]{1,0:T(8,128)(2,1)S(1)}, u32[]{:S(2)}, u32[]{:S(2)}) collective-permute-start(bf16[64,768]{1,0:T(8,128)(2,1)S(1)} %get-tuple-element.42.refs_3_.refs_0_), channel_id=1, source_target_pairs={{0,16},{1,17},{2,18},{3,19},{4,20},{5,21},{6,22},{7,23},{8,24},{9,... | collective-permute-start | bytes 294920 | tf_op jit(solution)/shard_map/ppermute | solution.py:39
  85.6 1.3 collective-permute-start.8
  87.1 0.6 shard_map.113.refs_11_
  87.7 3.3 %collective-permute-done.8.refs_2_ = bf16[64,768]{1,0:T(8,128)(2,1)S(1)} collective-permute-done((bf16[64,768]{1,0:T(8,128)(2,1)S(1)}, bf16[64,768]{1,0:T(8,128)(2,1)S(1)}, u32[]{:S(2)}, u32[]{:S(2)}) %collective-permute-start.8) | collective-permute-done | bytes 98336 | tf_op jit(solution)/shard_map/ppermute | solution.py:39
  91.0 3.2 %shard_map.114 = (bf16[24,2,32,128]{3,2,1,0:T(8,128)(2,1)S(1)}, bf16[1280,128]{1,0:T(8,128)(2,1)S(1)}) custom-call(s32[1]{0:T(128)} %bitcast.half, bf16[64,768]{1,0:T(8,128)(2,1)S(1)} %get-tuple-element.42.refs_3_.refs_0_, bf16[64,768]{1,0:T(8,128)(2,1)S(1)} %collective-permute-done.7.refs_1_, bf16[64,768]{1,0:T(8,128)(2,1)S(1)} %collective-permute-done.8.refs_2_, ...), custom_call_target="tpu_custom_call" | custom-call | tf_op jit(solution)/shard_map/pallas_call | solution.py:22
  94.2 0.8 pad_maximum_fusion
  95.0 14.8 %all-to-all-start.2 = ((bf16[32,56,128]{2,1,0:T(8,128)(2,1)}), bf16[32,56,128]{2,1,0:T(8,128)(2,1)S(1)}, u32[]{:S(2)}, u32[]{:S(2)}) async-start(bf16[32,56,128]{2,1,0:T(8,128)(2,1)} %pad_maximum_fusion), calls=%async_computation.2 | async-start | bytes 917504 | tf_op jit(solution)/shard_map/all_to_all | solution.py:331
  109.8 1.3 collective-permute-start.10
  111.1 4.0 %collective-permute-start.9 = (bf16[24,1,32,128]{3,2,1,0:T(8,128)(2,1)S(1)}, bf16[24,1,32,128]{3,2,1,0:T(8,128)(2,1)S(1)}, u32[]{:S(2)}, u32[]{:S(2)}) collective-permute-start(bf16[24,1,32,128]{3,2,1,0:T(8,128)(2,1)S(1)} %get-tuple-element.71), channel_id=1, source_target_pairs={{0,16},{1,17},{2,18},{3,19},{4,20},{5,21},{6,22},{7,23},{8,24},{9,... | collective-permute-start | bytes 589832 | tf_op jit(solution)/shard_map/ppermute | solution.py:39
  115.3 6.6 %collective-permute-done.10.refs_2_ = bf16[24,1,32,128]{3,2,1,0:T(8,128)(2,1)S(1)} collective-permute-done((bf16[24,1,32,128]{3,2,1,0:T(8,128)(2,1)S(1)}, bf16[24,1,32,128]{3,2,1,0:T(8,128)(2,1)S(1)}, u32[]{:S(2)}, u32[]{:S(2)}) %collective-permute-start.10) | collective-permute-done | bytes 196640 | tf_op jit(solution)/shard_map/ppermute | solution.py:39
  121.9 0.8 shard_map.115
  123.0 0.7 pad_maximum_fusion.1
  123.7 14.8 %all-to-all-start.3 = ((bf16[16,72,128]{2,1,0:T(8,128)(2,1)}), bf16[16,72,128]{2,1,0:T(8,128)(2,1)S(1)}, u32[]{:S(2)}, u32[]{:S(2)}) async-start(bf16[16,72,128]{2,1,0:T(8,128)(2,1)} %pad_maximum_fusion.1), calls=%async_computation.3 | async-start | bytes 589824 | tf_op jit(solution)/shard_map/all_to_all | solution.py:331
  138.5 16.7 %all-to-all-done.3 = bf16[16,72,128]{2,1,0:T(8,128)(2,1)S(1)} async-done(((bf16[16,72,128]{2,1,0:T(8,128)(2,1)}), bf16[16,72,128]{2,1,0:T(8,128)(2,1)S(1)}, u32[]{:S(2)}, u32[]{:S(2)}) %all-to-all-start.3) | async-done | bytes 294944 | tf_op jit(solution)/shard_map/all_to_all | solution.py:331
  155.3 7.7 %collective-permute-start.11 = (bf16[2,2,2,2,32,128]{5,4,3,2,1,0:T(8,128)(2,1)S(1)}, bf16[2,2,2,2,32,128]{5,4,3,2,1,0:T(8,128)(2,1)S(1)}, u32[]{:S(2)}, u32[]{:S(2)}) collective-permute-start(bf16[2,2,2,2,32,128]{5,4,3,2,1,0:T(8,128)(2,1)S(1)} %fusion), channel_id=1, source_target_pairs={{0,2},{1,3},{2,0},{3,1},{4,6},{5,7},{6,4},{7,5},{8,10},{9,11},{10,... | collective-permute-start | bytes 393224 | tf_op jit(solution)/shard_map/ppermute | solution.py:417
  163.0 0.8 broadcast_in_dim.8
  163.8 5.8 %all-to-all-start.4 = ((bf16[32,40,128]{2,1,0:T(8,128)(2,1)}), bf16[32,40,128]{2,1,0:T(8,128)(2,1)S(1)}, u32[]{:S(2)}, u32[]{:S(2)}) async-start(bf16[32,40,128]{2,1,0:T(8,128)(2,1)} %broadcast_in_dim.8), calls=%async_computation.4 | async-start | bytes 655360 | tf_op jit(solution)/shard_map/all_to_all | solution.py:331
  169.6 4.9 %collective-permute-done.11 = bf16[2,2,2,2,32,128]{5,4,3,2,1,0:T(8,128)(2,1)S(1)} collective-permute-done((bf16[2,2,2,2,32,128]{5,4,3,2,1,0:T(8,128)(2,1)S(1)}, bf16[2,2,2,2,32,128]{5,4,3,2,1,0:T(8,128)(2,1)S(1)}, u32[]{:S(2)}, u32[]{:S(2)}) %collective-permute-start.11) | collective-permute-done | bytes 131104 | tf_op jit(solution)/shard_map/ppermute | solution.py:417
  174.5 4.6 %all-to-all-done.4 = bf16[32,40,128]{2,1,0:T(8,128)(2,1)S(1)} async-done(((bf16[32,40,128]{2,1,0:T(8,128)(2,1)}), bf16[32,40,128]{2,1,0:T(8,128)(2,1)S(1)}, u32[]{:S(2)}, u32[]{:S(2)}) %all-to-all-start.4) | async-done | bytes 327712 | tf_op jit(solution)/shard_map/all_to_all | solution.py:331
  179.2 0.8 copy.58
  180.0 4.0 %all-to-all-start.5 = ((bf16[4,2,2,2,32,128]{5,4,3,2,1,0:T(8,128)(2,1)}), bf16[4,2,2,2,32,128]{5,4,3,2,1,0:T(8,128)(2,1)S(1)}, u32[]{:S(2)}, u32[]{:S(2)}) async-start(bf16[4,2,2,2,32,128]{5,4,3,2,1,0:T(8,128)(2,1)} %bitcast.44), calls=%async_computation.5 | async-start | bytes 524288 | tf_op jit(solution)/shard_map/all_to_all | solution.py:331
  184.0 0.6 slice_select_fusion.1
  184.6 1.7 shard_map.116
  186.3 2.3 %shard_map.117 = (f32[27,32,32]{2,1,0:T(8,128)}, f32[8,32,64]{2,1,0:T(8,128)}, f32[27,64,64]{2,1,0:T(8,128)}) custom-call(bf16[1280,128]{1,0:T(8,128)(2,1)} %bitcast.105), custom_call_target="tpu_custom_call" | custom-call | tf_op jit(solution)/shard_map/pallas_call | solution.py:552
  188.7 0.5 all-to-all-done.5
  189.2 0.9 copy.60
  (61 shorter events, 1.9 us)
Async XLA Ops:
  0.6 31.3 %copy-start.2 = (bf16[27,64,64]{2,1,0:T(8,128)(2,1)S(1)}, bf16[27,64,64]{2,1,0:T(8,128)(2,1)}, u32[]{:S(2)}) copy-start(bf16[27,64,64]{2,1,0:T(8,128)(2,1)} %param.10) | copy-start | bytes 663556
  0.6 35.0 %all-to-all-start = ((bf16[8,2,2,32,128]{4,2,1,3,0:T(2,128)(2,1)}), bf16[8,2,2,32,128]{4,2,1,3,0:T(2,128)(2,1)S(1)}, u32[]{:S(2)}, u32[]{:S(2)}) async-start(bf16[8,2,2,32,128]{4,2,1,3,0:T(2,128)(2,1)} %bitcast.119), calls=%async_computation | async-start | bytes 524288 | tf_op jit(solution)/shard_map/all_to_all | solution.py:331
  18.3 13.6 %copy-start.6 = (bf16[8,64,32]{1,2,0:T(8,128)(2,1)S(1)}, bf16[8,64,32]{1,2,0:T(8,128)(2,1)}, u32[]{:S(2)}) copy-start(bf16[8,64,32]{1,2,0:T(8,128)(2,1)} %param.9) | copy-start | bytes 98308
  19.9 21.7 %collective-permute-start = (bf16[256,128]{1,0:T(8,128)(2,1)}, bf16[256,128]{1,0:T(8,128)(2,1)}, u32[]{:S(2)}, u32[]{:S(2)}) collective-permute-start(bf16[256,128]{1,0:T(8,128)(2,1)} %shard_map.110), channel_id=1, source_target_pairs={{0,71},{1,135},{2,199},{3,263},{4,327},{5,391},{6,455},{7,7},{8,79... | collective-permute-start | bytes 196616 | tf_op jit(solution)/shard_map/ppermute | solution.py:350
  34.0 0.9 copy-start.5
  41.6 13.9 %collective-permute-start.1 = (bf16[8,2,32,128]{3,2,1,0:T(8,128)(2,1)S(1)}, bf16[8,2,32,128]{3,2,1,0:T(8,128)(2,1)S(1)}, u32[]{:S(2)}, u32[]{:S(2)}) collective-permute-start(bf16[8,2,32,128]{3,2,1,0:T(8,128)(2,1)S(1)} %slice_select_fusion), channel_id=1, source_target_pairs={{8,0},{9,1},{10,2},{11,3},{12,4},{13,5},{14,6},{15,7},{0,8},{1,9},... | collective-permute-start | bytes 393224 | tf_op jit(solution)/shard_map/ppermute | solution.py:39
  46.0 21.4 %all-to-all-start.1 = ((bf16[32,8,128]{2,1,0:T(8,128)(2,1)}), bf16[32,8,128]{2,1,0:T(8,128)(2,1)S(1)}, u32[]{:S(2)}, u32[]{:S(2)}) async-start(bf16[32,8,128]{2,1,0:T(8,128)(2,1)} %bitcast.4), calls=%async_computation.1 | async-start | bytes 131072 | tf_op jit(solution)/shard_map/all_to_all | solution.py:331
  55.7 11.7 %collective-permute-start.2 = (bf16[24,1,32,128]{3,2,1,0:T(8,128)(2,1)S(1)}, bf16[24,1,32,128]{3,2,1,0:T(8,128)(2,1)S(1)}, u32[]{:S(2)}, u32[]{:S(2)}) collective-permute-start(bf16[24,1,32,128]{3,2,1,0:T(8,128)(2,1)S(1)} %get-tuple-element.73), channel_id=1, source_target_pairs={{0,16},{1,17},{2,18},{3,19},{4,20},{5,21},{6,22},{7,23},{8,24},{9,... | collective-permute-start | bytes 589832 | tf_op jit(solution)/shard_map/ppermute | solution.py:39
  58.8 8.6 %collective-permute-start.3 = (bf16[24,1,32,128]{3,2,1,0:T(8,128)(2,1)S(1)}, bf16[24,1,32,128]{3,2,1,0:T(8,128)(2,1)S(1)}, u32[]{:S(2)}, u32[]{:S(2)}) collective-permute-start(bf16[24,1,32,128]{3,2,1,0:T(8,128)(2,1)S(1)} %get-tuple-element.72), channel_id=1, source_target_pairs={{16,0},{17,1},{18,2},{19,3},{20,4},{21,5},{22,6},{23,7},{24,8},{25... | collective-permute-start | bytes 589832 | tf_op jit(solution)/shard_map/ppermute | solution.py:39
  60.3 7.1 %copy-start.1 = (bf16[256,256]{1,0:T(8,128)(2,1)S(1)}, bf16[256,256]{1,0:T(8,128)(2,1)}, u32[]{:S(2)}) copy-start(bf16[256,256]{1,0:T(8,128)(2,1)} %constant.114.clone.refs_5_) | copy-start | bytes 393220
  70.5 6.3 %collective-permute-start.6 = (bf16[128,128]{1,0:T(8,128)(2,1)S(1)}, bf16[128,128]{1,0:T(8,128)(2,1)S(1)}, u32[]{:S(2)}, u32[]{:S(2)}) collective-permute-start(bf16[128,128]{1,0:T(8,128)(2,1)S(1)} %slice_select_fusion.4), channel_id=1, source_target_pairs={{8,0},{9,1},{10,2},{11,3},{12,4},{13,5},{14,6},{15,7},{0,8},{1,9},... | collective-permute-start | bytes 98312 | tf_op jit(solution)/shard_map/ppermute | solution.py:39
  73.3 3.8 %collective-permute-start.4 = (bf16[64,768]{1,0:T(8,128)(2,1)S(1)}, bf16[64,768]{1,0:T(8,128)(2,1)S(1)}, u32[]{:S(2)}, u32[]{:S(2)}) collective-permute-start(bf16[64,768]{1,0:T(8,128)(2,1)S(1)} %get-tuple-element.37.refs_0_), channel_id=1, source_target_pairs={{0,16},{1,17},{2,18},{3,19},{4,20},{5,21},{6,22},{7,23},{8,24},{9,... | collective-permute-start | bytes 294920 | tf_op jit(solution)/shard_map/ppermute | solution.py:39
  75.5 5.6 %collective-permute-start.5 = (bf16[64,768]{1,0:T(8,128)(2,1)S(1)}, bf16[64,768]{1,0:T(8,128)(2,1)S(1)}, u32[]{:S(2)}, u32[]{:S(2)}) collective-permute-start(bf16[64,768]{1,0:T(8,128)(2,1)S(1)} %get-tuple-element.37.refs_0_), channel_id=1, source_target_pairs={{16,0},{17,1},{18,2},{19,3},{20,4},{21,5},{22,6},{23,7},{24,8},{25... | collective-permute-start | bytes 294920 | tf_op jit(solution)/shard_map/ppermute | solution.py:39
  81.7 6.0 %collective-permute-start.7 = (bf16[64,768]{1,0:T(8,128)(2,1)S(1)}, bf16[64,768]{1,0:T(8,128)(2,1)S(1)}, u32[]{:S(2)}, u32[]{:S(2)}) collective-permute-start(bf16[64,768]{1,0:T(8,128)(2,1)S(1)} %get-tuple-element.42.refs_3_.refs_0_), channel_id=1, source_target_pairs={{0,16},{1,17},{2,18},{3,19},{4,20},{5,21},{6,22},{7,23},{8,24},{9,... | collective-permute-start | bytes 294920 | tf_op jit(solution)/shard_map/ppermute | solution.py:39
  85.6 5.4 %collective-permute-start.8 = (bf16[64,768]{1,0:T(8,128)(2,1)S(1)}, bf16[64,768]{1,0:T(8,128)(2,1)S(1)}, u32[]{:S(2)}, u32[]{:S(2)}) collective-permute-start(bf16[64,768]{1,0:T(8,128)(2,1)S(1)} %get-tuple-element.42.refs_3_.refs_0_), channel_id=1, source_target_pairs={{16,0},{17,1},{18,2},{19,3},{20,4},{21,5},{22,6},{23,7},{24,8},{25... | collective-permute-start | bytes 294920 | tf_op jit(solution)/shard_map/ppermute | solution.py:39
  87.1 4.0 %copy-start = (bf16[256,256]{1,0:T(8,128)(2,1)S(1)}, bf16[256,256]{1,0:T(8,128)(2,1)}, u32[]{:S(2)}) copy-start(bf16[256,256]{1,0:T(8,128)(2,1)} %constant.115.clone.refs_8_) | copy-start | bytes 393220
  95.0 27.7 %all-to-all-start.2 = ((bf16[32,56,128]{2,1,0:T(8,128)(2,1)}), bf16[32,56,128]{2,1,0:T(8,128)(2,1)S(1)}, u32[]{:S(2)}, u32[]{:S(2)}) async-start(bf16[32,56,128]{2,1,0:T(8,128)(2,1)} %pad_maximum_fusion), calls=%async_computation.2 | async-start | bytes 917504 | tf_op jit(solution)/shard_map/all_to_all | solution.py:331
  109.8 12.1 %collective-permute-start.10 = (bf16[24,1,32,128]{3,2,1,0:T(8,128)(2,1)S(1)}, bf16[24,1,32,128]{3,2,1,0:T(8,128)(2,1)S(1)}, u32[]{:S(2)}, u32[]{:S(2)}) collective-permute-start(bf16[24,1,32,128]{3,2,1,0:T(8,128)(2,1)S(1)} %get-tuple-element.70), channel_id=1, source_target_pairs={{16,0},{17,1},{18,2},{19,3},{20,4},{21,5},{22,6},{23,7},{24,8},{25... | collective-permute-start | bytes 589832 | tf_op jit(solution)/shard_map/ppermute | solution.py:39
  111.1 10.8 %collective-permute-start.9 = (bf16[24,1,32,128]{3,2,1,0:T(8,128)(2,1)S(1)}, bf16[24,1,32,128]{3,2,1,0:T(8,128)(2,1)S(1)}, u32[]{:S(2)}, u32[]{:S(2)}) collective-permute-start(bf16[24,1,32,128]{3,2,1,0:T(8,128)(2,1)S(1)} %get-tuple-element.71), channel_id=1, source_target_pairs={{0,16},{1,17},{2,18},{3,19},{4,20},{5,21},{6,22},{7,23},{8,24},{9,... | collective-permute-start | bytes 589832 | tf_op jit(solution)/shard_map/ppermute | solution.py:39
  123.7 31.5 %all-to-all-start.3 = ((bf16[16,72,128]{2,1,0:T(8,128)(2,1)}), bf16[16,72,128]{2,1,0:T(8,128)(2,1)S(1)}, u32[]{:S(2)}, u32[]{:S(2)}) async-start(bf16[16,72,128]{2,1,0:T(8,128)(2,1)} %pad_maximum_fusion.1), calls=%async_computation.3 | async-start | bytes 589824 | tf_op jit(solution)/shard_map/all_to_all | solution.py:331
  155.2 14.4 %copy-start.4 = (bf16[16,72,128]{2,1,0:T(8,128)(2,1)}, bf16[16,72,128]{2,1,0:T(8,128)(2,1)S(1)}, u32[]{:S(2)}) copy-start(bf16[16,72,128]{2,1,0:T(8,128)(2,1)S(1)} %all-to-all-done.3) | copy-start | bytes 884740
  155.3 19.2 %collective-permute-start.11 = (bf16[2,2,2,2,32,128]{5,4,3,2,1,0:T(8,128)(2,1)S(1)}, bf16[2,2,2,2,32,128]{5,4,3,2,1,0:T(8,128)(2,1)S(1)}, u32[]{:S(2)}, u32[]{:S(2)}) collective-permute-start(bf16[2,2,2,2,32,128]{5,4,3,2,1,0:T(8,128)(2,1)S(1)} %fusion), channel_id=1, source_target_pairs={{0,2},{1,3},{2,0},{3,1},{4,6},{5,7},{6,4},{7,5},{8,10},{9,11},{10,... | collective-permute-start | bytes 393224 | tf_op jit(solution)/shard_map/ppermute | solution.py:417
  163.8 15.4 %all-to-all-start.4 = ((bf16[32,40,128]{2,1,0:T(8,128)(2,1)}), bf16[32,40,128]{2,1,0:T(8,128)(2,1)S(1)}, u32[]{:S(2)}, u32[]{:S(2)}) async-start(bf16[32,40,128]{2,1,0:T(8,128)(2,1)} %broadcast_in_dim.8), calls=%async_computation.4 | async-start | bytes 655360 | tf_op jit(solution)/shard_map/all_to_all | solution.py:331
  179.2 0.8 copy-start.3
  180.0 4.0 %slice-start = ((bf16[16,72,128]{2,1,0:T(8,128)(2,1)}), bf16[16,32,128]{2,1,0:T(8,128)(2,1)S(1)}, s32[]{:S(2)}) async-start(bf16[16,72,128]{2,1,0:T(8,128)(2,1)} %copy-done.4), calls=%async_computation.6 | async-start | bytes 262144 | tf_op jit(solution)/shard_map/slice | solution.py:539
  180.0 9.1 %all-to-all-start.5 = ((bf16[4,2,2,2,32,128]{5,4,3,2,1,0:T(8,128)(2,1)}), bf16[4,2,2,2,32,128]{5,4,3,2,1,0:T(8,128)(2,1)S(1)}, u32[]{:S(2)}, u32[]{:S(2)}) async-start(bf16[4,2,2,2,32,128]{5,4,3,2,1,0:T(8,128)(2,1)} %bitcast.44), calls=%async_computation.5 | async-start | bytes 524288 | tf_op jit(solution)/shard_map/all_to_all | solution.py:331

commit v8 on v6

--- a/solution.py
+++ b/solution.py
@@ -406,14 +406,6 @@
     return lax.axis_index("sp") // 2 % 2
 
 
-def far_exchange(parts):
-    near = far_side() == 0
-    kept = jnp.where(near, parts[:, 0], parts[:, 1])
-    sent = jnp.where(near, parts[:, 1], parts[:, 0])
-    got = lax.ppermute(sent, "sp", [(col, col ^ 2) for col in range(lax.axis_size("sp"))])
-    return jnp.stack([jnp.where(near, kept, got), jnp.where(near, got, kept)], axis=2)
-
-
 def matched(parts, far, core):
     if parts.shape[0] > 1:
         parts = jnp.where(far == 0, parts, parts[::-1])
@@ -435,6 +427,14 @@
         for x in range(lead)
     ]
     return matched(jnp.stack([jnp.stack(row) for row in got]), far, core)
+
+
+def far_exchange(parts):
+    near = far_side() == 0
+    kept = jnp.where(near, parts[:, :, 0], parts[:, :, 1])
+    sent = jnp.where(near, parts[:, :, 1], parts[:, :, 0])
+    got = lax.ppermute(sent, "sp", [(col, col ^ 2) for col in range(lax.axis_size("sp"))])
+    return jnp.stack([jnp.where(near, kept, got), jnp.where(near, got, kept)], axis=2)
 
 
 def local(features, weight_fine, weight_down, weight_coarse, cotangent):
@@ -527,14 +527,14 @@
         coarse_grad,
     )
     coarse = jnp.where(upper_half() == 0, coarse[: width // 2], coarse[-(width // 2) :])
-    spread = fine_pieces(dpre2)
-    grads, *spread[1:] = lax.optimization_barrier((grads, *spread[1:]))
     grads = grads.reshape(len(near[0]), -1, LANES)
     kept = grads.shape[1]
     coarse = for_plane(coarse.reshape(batch, QUARTERS, 8, LANES))
     mixed = trade(jnp.concatenate([grads, coarse], axis=1), ("grp", "sp"), near)
     part = jnp.sum(mixed[:, :kept].astype(F32), axis=0).astype(BF16)
     coarse = for_column(mixed[:, kept:])
+    spread = fine_pieces(dpre2)
+    part, coarse, *spread[1:] = lax.optimization_barrier((part, coarse, *spread[1:]))
     gradient = call(
         input_kernel,
         shape((batch * x_cells, *own.shape[1:]), BF16),
@@ -542,14 +542,13 @@
         *spread,
         fine_back,
     )
-    part, gradient, coarse = lax.optimization_barrier((part, gradient, coarse))
-    gradient = far_exchange(gradient.reshape(batch // 4, 2, 2, x_cells, y_cells, chans, LANES))
+    gradient = gradient.reshape(batch // 4, 2, 2, x_cells, y_cells, chans, LANES)
+    gradient = far_exchange(near_exchange(jnp.swapaxes(gradient, 1, 2)))
     part = jnp.broadcast_to(part[None], (coarse.shape[0], *part.shape))
     mixed = trade(jnp.concatenate([part, coarse], axis=1), ("grp", "sp"), columns())
     part = jnp.sum(mixed[:, :kept].astype(F32), axis=0).astype(BF16)
     coarse = from_column(mixed[:, kept:])
     grads = share(part, ("grp", "sp"), near).reshape(grad_rows, LANES)
-    gradient = near_exchange(gradient)
     grads, gradient = lax.optimization_barrier((grads, gradient))
     grad_input = jnp.transpose(gradient, (0, 2, 1, 5, 3, 4, 6)).reshape(features.shape)
 

time: 193 us -> 200 us (1.036)
  waiting for transfers between devices: 51.2 us -> 56.1 us
  starting transfers between devices: 116 us -> 118 us
    ppermute x1, waiting for transfers between devices: 0.01 us -> 22.5 us  [far_exchange(): lax.ppermute(sent, 'sp', [(col, col ^ 2) for col in range(lax.axis_size('...]
    all_to_all x5, waiting for transfers between devices: 32.5 us -> 19.1 us  [trade(): lax.all_to_all(parts, axis, split_axis=0, concat_axis=0, axis_index_group...]
    ppermute x1, starting transfers between devices: 4.47 us -> 12 us  [far_exchange(): lax.ppermute(sent, 'sp', [(col, col ^ 2) for col in range(lax.axis_size('...]
    all_to_all x5, starting transfers between devices: 65.1 us -> 61.9 us  [trade(): lax.all_to_all(parts, axis, split_axis=0, concat_axis=0, axis_index_group...]
    ppermute x3, waiting for transfers between devices: 2.91 us -> 0.01 us  [near_exchange(): lax.ppermute(parts[x, c], 'sp', [(col, col ^ 4 * x + c) for col in range(...]
    ppermute x10, starting transfers between devices: 25.8 us -> 23.8 us  [arrival(): return lax.ppermute(block, ('grp', 'sp'), pairs)]
  transfers between devices with their start and end apart: 20 -> 20, of which waited for: 12 -> 9; matrix products, arithmetic and copies ran while one was open for 3% -> 3% of each run, Pallas kernels for 4% -> 3%
where the time goes in v8:
time: 200 us; the launch traced here: 199 us
  starting transfers between devices  118 us (59%)
  waiting for transfers between devices  56.1 us (28%)
  Pallas kernels  13.9 us (7%)
  local copies, waits for them, and re-layouts  6.97 us (3%)
  other arithmetic  2.9 us (1%)
    all_to_all x5, starting transfers between devices, trade(): lax.all_to_all(parts, axis, split_axis=0, concat_axis=0, axis_index_group...  61.9 us
    ppermute x10, starting transfers between devices, arrival(): return lax.ppermute(block, ('grp', 'sp'), pairs)  23.8 us
    ppermute x1, waiting for transfers between devices, far_exchange(): lax.ppermute(sent, 'sp', [(col, col ^ 2) for col in range(lax.axis_size('...  22.5 us
    all_to_all x5, waiting for transfers between devices, trade(): lax.all_to_all(parts, axis, split_axis=0, concat_axis=0, axis_index_group...  19.1 us
    ppermute x1, starting transfers between devices, turned(): return lax.ppermute(block, ('grp', 'sp'), pairs)  12 us
    ppermute x1, starting transfers between devices, far_exchange(): lax.ppermute(sent, 'sp', [(col, col ^ 2) for col in range(lax.axis_size('...  12 us
    ppermute x10, waiting for transfers between devices, arrival(): return lax.ppermute(block, ('grp', 'sp'), pairs)  8.62 us
    pallas_call x5, Pallas kernels, call(): pl.pallas_call(kernel, out_shape=outs, in_specs=[pl.BlockSpec(memory_spac...  8.25 us
  transfers between devices with their start and end apart: 20, of which 9 were waited for; matrix products, arithmetic and copies ran while one was open for 3% of the time, Pallas kernels for 3%

profile of v8, /device:TPU:1, one launch (start us, length us, event | category | flops | bytes accessed | tf_op | source)
XLA Modules:
  0.0 198.9 jit_solution(16560929873174238737)
XLA Ops:
  0.6 17.7 %all-to-all-start = ((bf16[8,2,2,32,128]{4,2,1,3,0:T(2,128)(2,1)}), bf16[8,2,2,32,128]{4,2,1,3,0:T(2,128)(2,1)S(1)}, u32[]{:S(2)}, u32[]{:S(2)}) async-start(bf16[8,2,2,32,128]{4,2,1,3,0:T(2,128)(2,1)} %bitcast.139), calls=%async_computation | async-start | bytes 524288 | tf_op jit(solution)/shard_map/all_to_all | solution.py:331
  18.3 1.6 shard_map.110
  19.9 12.0 %collective-permute-start = (bf16[256,128]{1,0:T(8,128)(2,1)}, bf16[256,128]{1,0:T(8,128)(2,1)}, u32[]{:S(2)}, u32[]{:S(2)}) collective-permute-start(bf16[256,128]{1,0:T(8,128)(2,1)} %shard_map.110), channel_id=1, source_target_pairs={{0,71},{1,135},{2,199},{3,263},{4,327},{5,391},{6,455},{7,7},{8,79... | collective-permute-start | bytes 196616 | tf_op jit(solution)/shard_map/ppermute | solution.py:350
  32.0 0.4 copy.82
  32.4 0.4 reshape.113
  32.8 1.2 copy.55
  34.0 0.4 reshape.111
  34.4 0.6 copy-done.4
  35.7 5.9 %collective-permute-done = bf16[256,128]{1,0:T(8,128)(2,1)} collective-permute-done((bf16[256,128]{1,0:T(8,128)(2,1)}, bf16[256,128]{1,0:T(8,128)(2,1)}, u32[]{:S(2)}, u32[]{:S(2)}) %collective-permute-start) | collective-permute-done | bytes 65568 | tf_op jit(solution)/shard_map/ppermute | solution.py:350
  41.6 4.4 %collective-permute-start.1 = (bf16[8,2,32,128]{3,2,1,0:T(8,128)(2,1)S(1)}, bf16[8,2,32,128]{3,2,1,0:T(8,128)(2,1)S(1)}, u32[]{:S(2)}, u32[]{:S(2)}) collective-permute-start(bf16[8,2,32,128]{3,2,1,0:T(8,128)(2,1)S(1)} %slice_select_fusion), channel_id=1, source_target_pairs={{8,0},{9,1},{10,2},{11,3},{12,4},{13,5},{14,6},{15,7},{0,8},{1,9},... | collective-permute-start | bytes 393224 | tf_op jit(solution)/shard_map/ppermute | solution.py:39
  46.0 9.6 %all-to-all-start.1 = ((bf16[32,8,128]{2,1,0:T(8,128)(2,1)}), bf16[32,8,128]{2,1,0:T(8,128)(2,1)S(1)}, u32[]{:S(2)}, u32[]{:S(2)}) async-start(bf16[32,8,128]{2,1,0:T(8,128)(2,1)} %bitcast.4), calls=%async_computation.1 | async-start | bytes 131072 | tf_op jit(solution)/shard_map/all_to_all | solution.py:331
  56.2 3.1 %collective-permute-start.2 = (bf16[24,1,32,128]{3,2,1,0:T(8,128)(2,1)S(1)}, bf16[24,1,32,128]{3,2,1,0:T(8,128)(2,1)S(1)}, u32[]{:S(2)}, u32[]{:S(2)}) collective-permute-start(bf16[24,1,32,128]{3,2,1,0:T(8,128)(2,1)S(1)} %get-tuple-element.66), channel_id=1, source_target_pairs={{0,16},{1,17},{2,18},{3,19},{4,20},{5,21},{6,22},{7,23},{8,24},{9,... | collective-permute-start | bytes 589832 | tf_op jit(solution)/shard_map/ppermute | solution.py:39
  59.4 1.3 collective-permute-start.3
  60.7 6.7 %all-to-all-done.1 = bf16[32,8,128]{2,1,0:T(8,128)(2,1)S(1)} async-done(((bf16[32,8,128]{2,1,0:T(8,128)(2,1)}), bf16[32,8,128]{2,1,0:T(8,128)(2,1)S(1)}, u32[]{:S(2)}, u32[]{:S(2)}) %all-to-all-start.1) | async-done | bytes 65568 | tf_op jit(solution)/shard_map/all_to_all | solution.py:331
  67.4 2.6 %collective-permute-start.6 = (bf16[128,128]{1,0:T(8,128)(2,1)S(1)}, bf16[128,128]{1,0:T(8,128)(2,1)S(1)}, u32[]{:S(2)}, u32[]{:S(2)}) collective-permute-start(bf16[128,128]{1,0:T(8,128)(2,1)S(1)} %fusion.7), channel_id=1, source_target_pairs={{8,0},{9,1},{10,2},{11,3},{12,4},{13,5},{14,6},{15,7},{0,8},{1,9},... | collective-permute-start | bytes 98312 | tf_op jit(solution)/shard_map/ppermute | solution.py:39
  70.0 3.0 %shard_map.111 = (bf16[64,768]{1,0:T(8,128)(2,1)S(1)}, bf16[256,768]{1,0:T(8,128)(2,1)S(1)}, f32[12,128,128]{2,1,0:T(8,128)S(1)}) custom-call(s32[1]{0:T(128)} %bitcast.half, bf16[24,2,32,128]{3,2,1,0:T(8,128)(2,1)S(1)} %maximum_select_fusion.refs_0_.refs_3_, bf16[24,1,32,128]{3,2,1,0:T(8,128)(2,1)S(1)} %collective-permute-done.2.refs_1_.refs_4_, ...), custom_call_target="tpu_custom_call" | custom-call | tf_op jit(solution)/shard_map/pallas_call | solution.py:22
  73.1 2.2 %collective-permute-start.4 = (bf16[64,768]{1,0:T(8,128)(2,1)S(1)}, bf16[64,768]{1,0:T(8,128)(2,1)S(1)}, u32[]{:S(2)}, u32[]{:S(2)}) collective-permute-start(bf16[64,768]{1,0:T(8,128)(2,1)S(1)} %get-tuple-element.36.refs_0_), channel_id=1, source_target_pairs={{0,16},{1,17},{2,18},{3,19},{4,20},{5,21},{6,22},{7,23},{8,24},{9,... | collective-permute-start | bytes 294920 | tf_op jit(solution)/shard_map/ppermute | solution.py:39
  75.3 1.3 collective-permute-start.5
  76.6 0.3 collective-permute-done.4.refs_1_
  76.9 3.7 %collective-permute-done.5.refs_2_ = bf16[64,768]{1,0:T(8,128)(2,1)S(1)} collective-permute-done((bf16[64,768]{1,0:T(8,128)(2,1)S(1)}, bf16[64,768]{1,0:T(8,128)(2,1)S(1)}, u32[]{:S(2)}, u32[]{:S(2)}) %collective-permute-start.5) | collective-permute-done | bytes 98336 | tf_op jit(solution)/shard_map/ppermute | solution.py:39
  80.6 0.7 shard_map.112
  81.3 2.4 %collective-permute-start.7 = (bf16[64,768]{1,0:T(8,128)(2,1)S(1)}, bf16[64,768]{1,0:T(8,128)(2,1)S(1)}, u32[]{:S(2)}, u32[]{:S(2)}) collective-permute-start(bf16[64,768]{1,0:T(8,128)(2,1)S(1)} %get-tuple-element.40.refs_3_.refs_0_), channel_id=1, source_target_pairs={{0,16},{1,17},{2,18},{3,19},{4,20},{5,21},{6,22},{7,23},{8,24},{9,... | collective-permute-start | bytes 294920 | tf_op jit(solution)/shard_map/ppermute | solution.py:39
  83.6 1.3 collective-permute-start.8
  85.1 0.6 shard_map.113.refs_11_
  85.7 3.3 %collective-permute-done.8.refs_2_ = bf16[64,768]{1,0:T(8,128)(2,1)S(1)} collective-permute-done((bf16[64,768]{1,0:T(8,128)(2,1)S(1)}, bf16[64,768]{1,0:T(8,128)(2,1)S(1)}, u32[]{:S(2)}, u32[]{:S(2)}) %collective-permute-start.8) | collective-permute-done | bytes 98336 | tf_op jit(solution)/shard_map/ppermute | solution.py:39
  89.0 3.2 %shard_map.114 = (bf16[24,2,32,128]{3,2,1,0:T(8,128)(2,1)S(1)}, bf16[1280,128]{1,0:T(8,128)(2,1)S(1)}) custom-call(s32[1]{0:T(128)} %bitcast.half, bf16[64,768]{1,0:T(8,128)(2,1)S(1)} %get-tuple-element.40.refs_3_.refs_0_, bf16[64,768]{1,0:T(8,128)(2,1)S(1)} %collective-permute-done.7.refs_1_, bf16[64,768]{1,0:T(8,128)(2,1)S(1)} %collective-permute-done.8.refs_2_, ...), custom_call_target="tpu_custom_call" | custom-call | tf_op jit(solution)/shard_map/pallas_call | solution.py:22
  92.2 0.8 pad_maximum_fusion
  93.0 16.3 %all-to-all-start.2 = ((bf16[32,56,128]{2,1,0:T(8,128)(2,1)}), bf16[32,56,128]{2,1,0:T(8,128)(2,1)S(1)}, u32[]{:S(2)}, u32[]{:S(2)}) async-start(bf16[32,56,128]{2,1,0:T(8,128)(2,1)} %pad_maximum_fusion), calls=%async_computation.2 | async-start | bytes 917504 | tf_op jit(solution)/shard_map/all_to_all | solution.py:331
  109.6 1.3 collective-permute-start.10
  110.9 4.0 %collective-permute-start.9 = (bf16[24,1,32,128]{3,2,1,0:T(8,128)(2,1)S(1)}, bf16[24,1,32,128]{3,2,1,0:T(8,128)(2,1)S(1)}, u32[]{:S(2)}, u32[]{:S(2)}) collective-permute-start(bf16[24,1,32,128]{3,2,1,0:T(8,128)(2,1)S(1)} %get-tuple-element.64), channel_id=1, source_target_pairs={{0,16},{1,17},{2,18},{3,19},{4,20},{5,21},{6,22},{7,23},{8,24},{9,... | collective-permute-start | bytes 589832 | tf_op jit(solution)/shard_map/ppermute | solution.py:39
  114.9 5.3 %all-to-all-done.2 = bf16[32,56,128]{2,1,0:T(8,128)(2,1)S(1)} async-done(((bf16[32,56,128]{2,1,0:T(8,128)(2,1)}), bf16[32,56,128]{2,1,0:T(8,128)(2,1)S(1)}, u32[]{:S(2)}, u32[]{:S(2)}) %all-to-all-start.2) | async-done | bytes 458784 | tf_op jit(solution)/shard_map/all_to_all | solution.py:331
  120.4 1.3 collective-permute-done.10.refs_2_
  121.7 0.8 shard_map.116
  122.7 2.5 %collective-permute-start.11 = (bf16[2,2,2,32,128]{4,3,2,1,0:T(8,128)(2,1)S(1)}, bf16[2,2,2,32,128]{4,3,2,1,0:T(8,128)(2,1)S(1)}, u32[]{:S(2)}, u32[]{:S(2)}) collective-permute-start(bf16[2,2,2,32,128]{4,3,2,1,0:T(8,128)(2,1)S(1)} %get-tuple-element.68), channel_id=1, source_target_pairs={{0,1},{1,0},{2,3},{3,2},{4,5},{5,4},{6,7},{7,6},{8,9},{9,8},{10,11... | collective-permute-start | bytes 196616 | tf_op jit(solution)/shard_map/ppermute | solution.py:424
  125.2 2.4 %collective-permute-start.12 = (bf16[2,2,2,32,128]{4,3,2,1,0:T(8,128)(2,1)S(1)}, bf16[2,2,2,32,128]{4,3,2,1,0:T(8,128)(2,1)S(1)}, u32[]{:S(2)}, u32[]{:S(2)}) collective-permute-start(bf16[2,2,2,32,128]{4,3,2,1,0:T(8,128)(2,1)S(1)} %get-tuple-element.70), channel_id=1, source_target_pairs={{0,4},{1,5},{2,6},{3,7},{4,0},{5,1},{6,2},{7,3},{8,12},{9,13},{10,... | collective-permute-start | bytes 196616 | tf_op jit(solution)/shard_map/ppermute | solution.py:424
  127.6 3.0 %collective-permute-start.13 = (bf16[2,2,2,32,128]{4,3,2,1,0:T(8,128)(2,1)S(1)}, bf16[2,2,2,32,128]{4,3,2,1,0:T(8,128)(2,1)S(1)}, u32[]{:S(2)}, u32[]{:S(2)}) collective-permute-start(bf16[2,2,2,32,128]{4,3,2,1,0:T(8,128)(2,1)S(1)} %get-tuple-element.69), channel_id=1, source_target_pairs={{0,5},{1,4},{2,7},{3,6},{4,1},{5,0},{6,3},{7,2},{8,13},{9,12},{10,... | collective-permute-start | bytes 196616 | tf_op jit(solution)/shard_map/ppermute | solution.py:424
  130.7 0.7 pad_maximum_fusion.1
  131.4 12.9 %all-to-all-start.3 = ((bf16[16,72,128]{2,1,0:T(8,128)(2,1)}), bf16[16,72,128]{2,1,0:T(8,128)(2,1)S(1)}, u32[]{:S(2)}, u32[]{:S(2)}) async-start(bf16[16,72,128]{2,1,0:T(8,128)(2,1)} %pad_maximum_fusion.1), calls=%async_computation.3 | async-start | bytes 589824 | tf_op jit(solution)/shard_map/all_to_all | solution.py:331
  144.6 12.0 %collective-permute-start.14 = (bf16[2,2,2,2,32,128]{5,4,3,2,1,0:T(8,128)(2,1)S(1)}, bf16[2,2,2,2,32,128]{5,4,3,2,1,0:T(8,128)(2,1)S(1)}, u32[]{:S(2)}, u32[]{:S(2)}) collective-permute-start(bf16[2,2,2,2,32,128]{5,4,3,2,1,0:T(8,128)(2,1)S(1)} %fusion), channel_id=1, source_target_pairs={{0,2},{1,3},{2,0},{3,1},{4,6},{5,7},{6,4},{7,5},{8,10},{9,11},{10,... | collective-permute-start | bytes 393224 | tf_op jit(solution)/shard_map/ppermute | solution.py:436
  156.7 22.5 %collective-permute-done.14 = bf16[2,2,2,2,32,128]{5,4,3,2,1,0:T(8,128)(2,1)S(1)} collective-permute-done((bf16[2,2,2,2,32,128]{5,4,3,2,1,0:T(8,128)(2,1)S(1)}, bf16[2,2,2,2,32,128]{5,4,3,2,1,0:T(8,128)(2,1)S(1)}, u32[]{:S(2)}, u32[]{:S(2)}) %collective-permute-start.14) | collective-permute-done | bytes 131104 | tf_op jit(solution)/shard_map/ppermute | solution.py:436
  179.3 0.8 broadcast_in_dim.8
  180.0 5.4 %all-to-all-start.4 = ((bf16[32,40,128]{2,1,0:T(8,128)(2,1)}), bf16[32,40,128]{2,1,0:T(8,128)(2,1)S(1)}, u32[]{:S(2)}, u32[]{:S(2)}) async-start(bf16[32,40,128]{2,1,0:T(8,128)(2,1)} %broadcast_in_dim.8), calls=%async_computation.4 | async-start | bytes 655360 | tf_op jit(solution)/shard_map/all_to_all | solution.py:331
  185.5 0.6 slice_select_fusion.1
  186.1 1.7 shard_map.115
  187.8 7.1 %all-to-all-done.4 = bf16[32,40,128]{2,1,0:T(8,128)(2,1)S(1)} async-done(((bf16[32,40,128]{2,1,0:T(8,128)(2,1)}), bf16[32,40,128]{2,1,0:T(8,128)(2,1)S(1)}, u32[]{:S(2)}, u32[]{:S(2)}) %all-to-all-start.4) | async-done | bytes 327712 | tf_op jit(solution)/shard_map/all_to_all | solution.py:331
  195.0 0.7 copy-done.3
  195.7 2.3 %shard_map.117 = (f32[27,32,32]{2,1,0:T(8,128)}, f32[8,32,64]{2,1,0:T(8,128)}, f32[27,64,64]{2,1,0:T(8,128)}) custom-call(bf16[1280,128]{1,0:T(8,128)(2,1)} %bitcast.126), custom_call_target="tpu_custom_call" | custom-call | tf_op jit(solution)/shard_map/pallas_call | solution.py:560
  198.0 0.9 copy.74
  (68 shorter events, 2.4 us)
Async XLA Ops:
  0.6 31.3 %copy-start.2 = (bf16[27,64,64]{2,1,0:T(8,128)(2,1)S(1)}, bf16[27,64,64]{2,1,0:T(8,128)(2,1)}, u32[]{:S(2)}) copy-start(bf16[27,64,64]{2,1,0:T(8,128)(2,1)} %param.10) | copy-start | bytes 663556
  0.6 35.0 %all-to-all-start = ((bf16[8,2,2,32,128]{4,2,1,3,0:T(2,128)(2,1)}), bf16[8,2,2,32,128]{4,2,1,3,0:T(2,128)(2,1)S(1)}, u32[]{:S(2)}, u32[]{:S(2)}) async-start(bf16[8,2,2,32,128]{4,2,1,3,0:T(2,128)(2,1)} %bitcast.139), calls=%async_computation | async-start | bytes 524288 | tf_op jit(solution)/shard_map/all_to_all | solution.py:331
  18.3 13.6 %copy-start.5 = (bf16[8,64,32]{1,2,0:T(8,128)(2,1)S(1)}, bf16[8,64,32]{1,2,0:T(8,128)(2,1)}, u32[]{:S(2)}) copy-start(bf16[8,64,32]{1,2,0:T(8,128)(2,1)} %param.9) | copy-start | bytes 98308
  19.9 21.7 %collective-permute-start = (bf16[256,128]{1,0:T(8,128)(2,1)}, bf16[256,128]{1,0:T(8,128)(2,1)}, u32[]{:S(2)}, u32[]{:S(2)}) collective-permute-start(bf16[256,128]{1,0:T(8,128)(2,1)} %shard_map.110), channel_id=1, source_target_pairs={{0,71},{1,135},{2,199},{3,263},{4,327},{5,391},{6,455},{7,7},{8,79... | collective-permute-start | bytes 196616 | tf_op jit(solution)/shard_map/ppermute | solution.py:350
  34.0 0.9 copy-start.4
  41.6 14.5 %collective-permute-start.1 = (bf16[8,2,32,128]{3,2,1,0:T(8,128)(2,1)S(1)}, bf16[8,2,32,128]{3,2,1,0:T(8,128)(2,1)S(1)}, u32[]{:S(2)}, u32[]{:S(2)}) collective-permute-start(bf16[8,2,32,128]{3,2,1,0:T(8,128)(2,1)S(1)} %slice_select_fusion), channel_id=1, source_target_pairs={{8,0},{9,1},{10,2},{11,3},{12,4},{13,5},{14,6},{15,7},{0,8},{1,9},... | collective-permute-start | bytes 393224 | tf_op jit(solution)/shard_map/ppermute | solution.py:39
  46.0 21.4 %all-to-all-start.1 = ((bf16[32,8,128]{2,1,0:T(8,128)(2,1)}), bf16[32,8,128]{2,1,0:T(8,128)(2,1)S(1)}, u32[]{:S(2)}, u32[]{:S(2)}) async-start(bf16[32,8,128]{2,1,0:T(8,128)(2,1)} %bitcast.4), calls=%async_computation.1 | async-start | bytes 131072 | tf_op jit(solution)/shard_map/all_to_all | solution.py:331
  56.2 13.8 %collective-permute-start.2 = (bf16[24,1,32,128]{3,2,1,0:T(8,128)(2,1)S(1)}, bf16[24,1,32,128]{3,2,1,0:T(8,128)(2,1)S(1)}, u32[]{:S(2)}, u32[]{:S(2)}) collective-permute-start(bf16[24,1,32,128]{3,2,1,0:T(8,128)(2,1)S(1)} %get-tuple-element.66), channel_id=1, source_target_pairs={{0,16},{1,17},{2,18},{3,19},{4,20},{5,21},{6,22},{7,23},{8,24},{9,... | collective-permute-start | bytes 589832 | tf_op jit(solution)/shard_map/ppermute | solution.py:39
  59.4 10.6 %collective-permute-start.3 = (bf16[24,1,32,128]{3,2,1,0:T(8,128)(2,1)S(1)}, bf16[24,1,32,128]{3,2,1,0:T(8,128)(2,1)S(1)}, u32[]{:S(2)}, u32[]{:S(2)}) collective-permute-start(bf16[24,1,32,128]{3,2,1,0:T(8,128)(2,1)S(1)} %get-tuple-element.65), channel_id=1, source_target_pairs={{16,0},{17,1},{18,2},{19,3},{20,4},{21,5},{22,6},{23,7},{24,8},{25... | collective-permute-start | bytes 589832 | tf_op jit(solution)/shard_map/ppermute | solution.py:39
  67.4 2.6 %copy-start.1 = (bf16[256,256]{1,0:T(8,128)(2,1)S(1)}, bf16[256,256]{1,0:T(8,128)(2,1)}, u32[]{:S(2)}) copy-start(bf16[256,256]{1,0:T(8,128)(2,1)} %constant.129.clone.refs_5_) | copy-start | bytes 393220
  67.4 9.1 %collective-permute-start.6 = (bf16[128,128]{1,0:T(8,128)(2,1)S(1)}, bf16[128,128]{1,0:T(8,128)(2,1)S(1)}, u32[]{:S(2)}, u32[]{:S(2)}) collective-permute-start(bf16[128,128]{1,0:T(8,128)(2,1)S(1)} %fusion.7), channel_id=1, source_target_pairs={{8,0},{9,1},{10,2},{11,3},{12,4},{13,5},{14,6},{15,7},{0,8},{1,9},... | collective-permute-start | bytes 98312 | tf_op jit(solution)/shard_map/ppermute | solution.py:39
  73.1 3.8 %collective-permute-start.4 = (bf16[64,768]{1,0:T(8,128)(2,1)S(1)}, bf16[64,768]{1,0:T(8,128)(2,1)S(1)}, u32[]{:S(2)}, u32[]{:S(2)}) collective-permute-start(bf16[64,768]{1,0:T(8,128)(2,1)S(1)} %get-tuple-element.36.refs_0_), channel_id=1, source_target_pairs={{0,16},{1,17},{2,18},{3,19},{4,20},{5,21},{6,22},{7,23},{8,24},{9,... | collective-permute-start | bytes 294920 | tf_op jit(solution)/shard_map/ppermute | solution.py:39
  75.3 5.4 %collective-permute-start.5 = (bf16[64,768]{1,0:T(8,128)(2,1)S(1)}, bf16[64,768]{1,0:T(8,128)(2,1)S(1)}, u32[]{:S(2)}, u32[]{:S(2)}) collective-permute-start(bf16[64,768]{1,0:T(8,128)(2,1)S(1)} %get-tuple-element.36.refs_0_), channel_id=1, source_target_pairs={{16,0},{17,1},{18,2},{19,3},{20,4},{21,5},{22,6},{23,7},{24,8},{25... | collective-permute-start | bytes 294920 | tf_op jit(solution)/shard_map/ppermute | solution.py:39
  81.3 4.4 %collective-permute-start.7 = (bf16[64,768]{1,0:T(8,128)(2,1)S(1)}, bf16[64,768]{1,0:T(8,128)(2,1)S(1)}, u32[]{:S(2)}, u32[]{:S(2)}) collective-permute-start(bf16[64,768]{1,0:T(8,128)(2,1)S(1)} %get-tuple-element.40.refs_3_.refs_0_), channel_id=1, source_target_pairs={{0,16},{1,17},{2,18},{3,19},{4,20},{5,21},{6,22},{7,23},{8,24},{9,... | collective-permute-start | bytes 294920 | tf_op jit(solution)/shard_map/ppermute | solution.py:39
  83.6 5.4 %collective-permute-start.8 = (bf16[64,768]{1,0:T(8,128)(2,1)S(1)}, bf16[64,768]{1,0:T(8,128)(2,1)S(1)}, u32[]{:S(2)}, u32[]{:S(2)}) collective-permute-start(bf16[64,768]{1,0:T(8,128)(2,1)S(1)} %get-tuple-element.40.refs_3_.refs_0_), channel_id=1, source_target_pairs={{16,0},{17,1},{18,2},{19,3},{20,4},{21,5},{22,6},{23,7},{24,8},{25... | collective-permute-start | bytes 294920 | tf_op jit(solution)/shard_map/ppermute | solution.py:39
  85.0 4.0 %copy-start = (bf16[256,256]{1,0:T(8,128)(2,1)S(1)}, bf16[256,256]{1,0:T(8,128)(2,1)}, u32[]{:S(2)}) copy-start(bf16[256,256]{1,0:T(8,128)(2,1)} %constant.130.clone.refs_8_) | copy-start | bytes 393220
  93.0 27.2 %all-to-all-start.2 = ((bf16[32,56,128]{2,1,0:T(8,128)(2,1)}), bf16[32,56,128]{2,1,0:T(8,128)(2,1)S(1)}, u32[]{:S(2)}, u32[]{:S(2)}) async-start(bf16[32,56,128]{2,1,0:T(8,128)(2,1)} %pad_maximum_fusion), calls=%async_computation.2 | async-start | bytes 917504 | tf_op jit(solution)/shard_map/all_to_all | solution.py:331
  109.6 12.1 %collective-permute-start.10 = (bf16[24,1,32,128]{3,2,1,0:T(8,128)(2,1)S(1)}, bf16[24,1,32,128]{3,2,1,0:T(8,128)(2,1)S(1)}, u32[]{:S(2)}, u32[]{:S(2)}) collective-permute-start(bf16[24,1,32,128]{3,2,1,0:T(8,128)(2,1)S(1)} %get-tuple-element.63), channel_id=1, source_target_pairs={{16,0},{17,1},{18,2},{19,3},{20,4},{21,5},{22,6},{23,7},{24,8},{25... | collective-permute-start | bytes 589832 | tf_op jit(solution)/shard_map/ppermute | solution.py:39
  110.9 10.8 %collective-permute-start.9 = (bf16[24,1,32,128]{3,2,1,0:T(8,128)(2,1)S(1)}, bf16[24,1,32,128]{3,2,1,0:T(8,128)(2,1)S(1)}, u32[]{:S(2)}, u32[]{:S(2)}) collective-permute-start(bf16[24,1,32,128]{3,2,1,0:T(8,128)(2,1)S(1)} %get-tuple-element.64), channel_id=1, source_target_pairs={{0,16},{1,17},{2,18},{3,19},{4,20},{5,21},{6,22},{7,23},{8,24},{9,... | collective-permute-start | bytes 589832 | tf_op jit(solution)/shard_map/ppermute | solution.py:39
  122.7 21.7 %collective-permute-start.11 = (bf16[2,2,2,32,128]{4,3,2,1,0:T(8,128)(2,1)S(1)}, bf16[2,2,2,32,128]{4,3,2,1,0:T(8,128)(2,1)S(1)}, u32[]{:S(2)}, u32[]{:S(2)}) collective-permute-start(bf16[2,2,2,32,128]{4,3,2,1,0:T(8,128)(2,1)S(1)} %get-tuple-element.68), channel_id=1, source_target_pairs={{0,1},{1,0},{2,3},{3,2},{4,5},{5,4},{6,7},{7,6},{8,9},{9,8},{10,11... | collective-permute-start | bytes 196616 | tf_op jit(solution)/shard_map/ppermute | solution.py:424
  125.2 19.2 %collective-permute-start.12 = (bf16[2,2,2,32,128]{4,3,2,1,0:T(8,128)(2,1)S(1)}, bf16[2,2,2,32,128]{4,3,2,1,0:T(8,128)(2,1)S(1)}, u32[]{:S(2)}, u32[]{:S(2)}) collective-permute-start(bf16[2,2,2,32,128]{4,3,2,1,0:T(8,128)(2,1)S(1)} %get-tuple-element.70), channel_id=1, source_target_pairs={{0,4},{1,5},{2,6},{3,7},{4,0},{5,1},{6,2},{7,3},{8,12},{9,13},{10,... | collective-permute-start | bytes 196616 | tf_op jit(solution)/shard_map/ppermute | solution.py:424
  127.6 16.8 %collective-permute-start.13 = (bf16[2,2,2,32,128]{4,3,2,1,0:T(8,128)(2,1)S(1)}, bf16[2,2,2,32,128]{4,3,2,1,0:T(8,128)(2,1)S(1)}, u32[]{:S(2)}, u32[]{:S(2)}) collective-permute-start(bf16[2,2,2,32,128]{4,3,2,1,0:T(8,128)(2,1)S(1)} %get-tuple-element.69), channel_id=1, source_target_pairs={{0,5},{1,4},{2,7},{3,6},{4,1},{5,0},{6,3},{7,2},{8,13},{9,12},{10,... | collective-permute-start | bytes 196616 | tf_op jit(solution)/shard_map/ppermute | solution.py:424
  131.4 47.8 %all-to-all-start.3 = ((bf16[16,72,128]{2,1,0:T(8,128)(2,1)}), bf16[16,72,128]{2,1,0:T(8,128)(2,1)S(1)}, u32[]{:S(2)}, u32[]{:S(2)}) async-start(bf16[16,72,128]{2,1,0:T(8,128)(2,1)} %pad_maximum_fusion.1), calls=%async_computation.3 | async-start | bytes 589824 | tf_op jit(solution)/shard_map/all_to_all | solution.py:331
  144.6 34.6 %collective-permute-start.14 = (bf16[2,2,2,2,32,128]{5,4,3,2,1,0:T(8,128)(2,1)S(1)}, bf16[2,2,2,2,32,128]{5,4,3,2,1,0:T(8,128)(2,1)S(1)}, u32[]{:S(2)}, u32[]{:S(2)}) collective-permute-start(bf16[2,2,2,2,32,128]{5,4,3,2,1,0:T(8,128)(2,1)S(1)} %fusion), channel_id=1, source_target_pairs={{0,2},{1,3},{2,0},{3,1},{4,6},{5,7},{6,4},{7,5},{8,10},{9,11},{10,... | collective-permute-start | bytes 393224 | tf_op jit(solution)/shard_map/ppermute | solution.py:436
  180.0 14.9 %all-to-all-start.4 = ((bf16[32,40,128]{2,1,0:T(8,128)(2,1)}), bf16[32,40,128]{2,1,0:T(8,128)(2,1)S(1)}, u32[]{:S(2)}, u32[]{:S(2)}) async-start(bf16[32,40,128]{2,1,0:T(8,128)(2,1)} %broadcast_in_dim.8), calls=%async_computation.4 | async-start | bytes 655360 | tf_op jit(solution)/shard_map/all_to_all | solution.py:331
  195.0 0.7 copy-start.3

commit v9 on v5

--- a/solution.py
+++ b/solution.py
@@ -60,6 +60,11 @@
     return [block, arrival(block[:, 1:], -1, False), arrival(block[:, :1], 1, False)]
 
 
+def last_pieces(block, count):
+    there = jnp.where(upper_half() == 0, block[: count + 1], block[-(count + 1) :])
+    return [block, arrival(there[:, 1:], -1, False), arrival(there[:, :1], 1, False)]
+
+
 def coarse_pieces(block):
     return [block, arrival(block, -1, False), arrival(block, 1, False)]
 
@@ -100,10 +105,14 @@
         if shift is not None:
             half, skip, count = shift
             inside = half == 1 if x < 0 else half == 0 if x >= count else None
+            lag = 0 if before.shape[0] == cells else skip - 1
+            beside = jnp.clip(x + (skip - lag) * half, 0, before.shape[0] - 1)
             x = jnp.clip(x + skip * half, 0, cells - 1)
         elif not 0 <= x < cells:
             return jnp.zeros(center.shape[2:], center.dtype)
-        value = before[x, 0] if y < 0 else after[x, 0] if y > 1 else center[x, y]
+        else:
+            beside = x
+        value = before[beside, 0] if y < 0 else after[beside, 0] if y > 1 else center[x, y]
         return value if inside is None else jnp.where(inside, value, jnp.zeros_like(value))
 
     return jnp.concatenate(
@@ -240,7 +249,6 @@
     ddown = ddown.astype(BF16)
     spread = dot(up_weights[...], ddown).astype(BF16)
     rows = spread.shape[0] // 2
-    total = None
     for tile in range(columns // 2):
         lanes = slice(tile * LANES, (tile + 1) * LANES)
         both = dot(jnp.concatenate([spread[:rows, lanes], spread[rows:, lanes]], axis=1), unsort[...])
@@ -251,12 +259,15 @@
             parts = [dpre[place * chans : (place + 1) * chans] for place in range(4)]
             for place in range(4):
                 dpre2[2 * column + place // 2, place % 2] = parts[place]
-            place = column - (columns - extent) * half[0]
-            inside = (place >= 0) & (place < extent)
-            parts = [jnp.where(inside, part.astype(F32), 0.0) for part in parts]
-            moved = jnp.concatenate([tap_stack(part, LANES) for part in parts], axis=1)
-            term = dot_lanes(moved, fine_stack(feature_pieces, column))
-            total = term if total is None else total + term
+    total = None
+    skip = columns - extent
+    for place in range(extent):
+        column = place + skip * half[0]
+        parts = [dpre2[2 * column + x, y] for x in (0, 1) for y in (0, 1)]
+        moved = jnp.concatenate([tap_stack(part, LANES) for part in parts], axis=1)
+        stack = fine_stack(feature_pieces, place, (half[0], 2 * skip, 2 * extent))
+        term = dot_lanes(moved, stack)
+        total = term if total is None else total + term
     base = coarse_grad.shape[0]
     grads[:base] = coarse_grad[...]
     grads[base:] = jnp.zeros((grads.shape[0] - base, LANES), grads.dtype)
@@ -524,7 +535,7 @@
         input_kernel,
         shape((batch * x_cells, *own.shape[1:]), BF16),
         half,
-        *fine_pieces(dpre2),
+        *last_pieces(dpre2, batch * x_cells),
         fine_back,
     )
     part, gradient, coarse = lax.optimization_barrier((part, gradient, coarse))

time: 189 us -> 187 us (0.989)
  no operation moved by 1% of the time
where the time goes in v9:
time: 187 us; the launch traced here: 186 us
  starting transfers between devices  122 us (65%)
  waiting for transfers between devices  39.9 us (21%)
  Pallas kernels  13.1 us (7%)
  local copies, waits for them, and re-layouts  7.07 us (4%)
  other arithmetic  2.62 us (1%)
    all_to_all x6, starting transfers between devices, trade(): lax.all_to_all(parts, axis, split_axis=0, concat_axis=0, axis_index_group...  74 us
    ppermute x10, starting transfers between devices, arrival(): return lax.ppermute(block, ('grp', 'sp'), pairs)  23.8 us
    all_to_all x6, waiting for transfers between devices, trade(): lax.all_to_all(parts, axis, split_axis=0, concat_axis=0, axis_index_group...  21.2 us
    ppermute x10, waiting for transfers between devices, arrival(): return lax.ppermute(block, ('grp', 'sp'), pairs)  12.8 us
    ppermute x1, starting transfers between devices, turned(): return lax.ppermute(block, ('grp', 'sp'), pairs)  12 us
    ppermute x1, starting transfers between devices, far_exchange(): lax.ppermute(sent, 'sp', [(col, col ^ 2) for col in range(lax.axis_size('...  12 us
    pallas_call x5, Pallas kernels, call(): pl.pallas_call(kernel, out_shape=outs, in_specs=[pl.BlockSpec(memory_spac...  7.44 us
    ppermute x1, waiting for transfers between devices, turned(): return lax.ppermute(block, ('grp', 'sp'), pairs)  5.86 us
  transfers between devices with their start and end apart: 18, of which 9 were waited for; matrix products, arithmetic and copies ran while one was open for 3% of the time, Pallas kernels for 5%

profile of v9, /device:TPU:1, one launch (start us, length us, event | category | flops | bytes accessed | tf_op | source)
XLA Modules:
  0.0 185.8 jit_solution(16016841738333141315)
XLA Ops:
  0.6 17.7 %all-to-all-start = ((bf16[8,2,2,32,128]{4,2,1,3,0:T(2,128)(2,1)}), bf16[8,2,2,32,128]{4,2,1,3,0:T(2,128)(2,1)S(1)}, u32[]{:S(2)}, u32[]{:S(2)}) async-start(bf16[8,2,2,32,128]{4,2,1,3,0:T(2,128)(2,1)} %bitcast.121), calls=%async_computation | async-start | bytes 524288 | tf_op jit(solution)/shard_map/all_to_all | solution.py:342
  18.3 1.6 shard_map.110
  19.9 12.0 %collective-permute-start = (bf16[256,128]{1,0:T(8,128)(2,1)}, bf16[256,128]{1,0:T(8,128)(2,1)}, u32[]{:S(2)}, u32[]{:S(2)}) collective-permute-start(bf16[256,128]{1,0:T(8,128)(2,1)} %shard_map.110), channel_id=1, source_target_pairs={{0,71},{1,135},{2,199},{3,263},{4,327},{5,391},{6,455},{7,7},{8,79... | collective-permute-start | bytes 196616 | tf_op jit(solution)/shard_map/ppermute | solution.py:361
  32.0 0.4 copy.65
  32.4 0.4 reshape.119
  32.8 1.2 copy.44
  34.0 0.4 reshape.117
  34.4 0.6 copy-done.5
  35.3 0.2 copy.42
  35.7 5.9 %collective-permute-done = bf16[256,128]{1,0:T(8,128)(2,1)} collective-permute-done((bf16[256,128]{1,0:T(8,128)(2,1)}, bf16[256,128]{1,0:T(8,128)(2,1)}, u32[]{:S(2)}, u32[]{:S(2)}) %collective-permute-start) | collective-permute-done | bytes 65568 | tf_op jit(solution)/shard_map/ppermute | solution.py:361
  41.6 4.4 %collective-permute-start.1 = (bf16[8,2,32,128]{3,2,1,0:T(8,128)(2,1)S(1)}, bf16[8,2,32,128]{3,2,1,0:T(8,128)(2,1)S(1)}, u32[]{:S(2)}, u32[]{:S(2)}) collective-permute-start(bf16[8,2,32,128]{3,2,1,0:T(8,128)(2,1)S(1)} %slice_select_fusion.1), channel_id=1, source_target_pairs={{8,0},{9,1},{10,2},{11,3},{12,4},{13,5},{14,6},{15,7},{0,8},{1,9},... | collective-permute-start | bytes 393224 | tf_op jit(solution)/shard_map/ppermute | solution.py:39
  46.0 9.6 %all-to-all-start.1 = ((bf16[32,8,128]{2,1,0:T(8,128)(2,1)}), bf16[32,8,128]{2,1,0:T(8,128)(2,1)S(1)}, u32[]{:S(2)}, u32[]{:S(2)}) async-start(bf16[32,8,128]{2,1,0:T(8,128)(2,1)} %bitcast.4), calls=%async_computation.1 | async-start | bytes 131072 | tf_op jit(solution)/shard_map/all_to_all | solution.py:342
  56.0 0.2 copy.50.refs_6_
  56.2 3.1 %collective-permute-start.2 = (bf16[24,1,32,128]{3,2,1,0:T(8,128)(2,1)S(1)}, bf16[24,1,32,128]{3,2,1,0:T(8,128)(2,1)S(1)}, u32[]{:S(2)}, u32[]{:S(2)}) collective-permute-start(bf16[24,1,32,128]{3,2,1,0:T(8,128)(2,1)S(1)} %get-tuple-element.67), channel_id=1, source_target_pairs={{0,16},{1,17},{2,18},{3,19},{4,20},{5,21},{6,22},{7,23},{8,24},{9,... | collective-permute-start | bytes 589832 | tf_op jit(solution)/shard_map/ppermute | solution.py:39
  59.4 1.3 collective-permute-start.3
  60.7 6.7 %all-to-all-done.1 = bf16[32,8,128]{2,1,0:T(8,128)(2,1)S(1)} async-done(((bf16[32,8,128]{2,1,0:T(8,128)(2,1)}), bf16[32,8,128]{2,1,0:T(8,128)(2,1)S(1)}, u32[]{:S(2)}, u32[]{:S(2)}) %all-to-all-start.1) | async-done | bytes 65568 | tf_op jit(solution)/shard_map/all_to_all | solution.py:342
  67.4 2.6 %collective-permute-start.6 = (bf16[128,128]{1,0:T(8,128)(2,1)S(1)}, bf16[128,128]{1,0:T(8,128)(2,1)S(1)}, u32[]{:S(2)}, u32[]{:S(2)}) collective-permute-start(bf16[128,128]{1,0:T(8,128)(2,1)S(1)} %fusion.7), channel_id=1, source_target_pairs={{8,0},{9,1},{10,2},{11,3},{12,4},{13,5},{14,6},{15,7},{0,8},{1,9},... | collective-permute-start | bytes 98312 | tf_op jit(solution)/shard_map/ppermute | solution.py:39
  70.0 3.0 %shard_map.111 = (bf16[64,768]{1,0:T(8,128)(2,1)S(1)}, bf16[256,768]{1,0:T(8,128)(2,1)S(1)}, f32[12,128,128]{2,1,0:T(8,128)S(1)}) custom-call(s32[1]{0:T(128)} %bitcast.half, bf16[24,2,32,128]{3,2,1,0:T(8,128)(2,1)S(1)} %maximum_select_fusion.refs_0_.refs_3_, bf16[24,1,32,128]{3,2,1,0:T(8,128)(2,1)S(1)} %collective-permute-done.2.refs_1_.refs_4_, ...), custom_call_target="tpu_custom_call" | custom-call | tf_op jit(solution)/shard_map/pallas_call | solution.py:22
  73.1 2.2 %collective-permute-start.4 = (bf16[64,768]{1,0:T(8,128)(2,1)S(1)}, bf16[64,768]{1,0:T(8,128)(2,1)S(1)}, u32[]{:S(2)}, u32[]{:S(2)}) collective-permute-start(bf16[64,768]{1,0:T(8,128)(2,1)S(1)} %get-tuple-element.35.refs_0_), channel_id=1, source_target_pairs={{0,16},{1,17},{2,18},{3,19},{4,20},{5,21},{6,22},{7,23},{8,24},{9,... | collective-permute-start | bytes 294920 | tf_op jit(solution)/shard_map/ppermute | solution.py:39
  75.3 1.3 collective-permute-start.5
  76.6 0.3 collective-permute-done.4.refs_1_
  76.9 3.7 %collective-permute-done.5.refs_2_ = bf16[64,768]{1,0:T(8,128)(2,1)S(1)} collective-permute-done((bf16[64,768]{1,0:T(8,128)(2,1)S(1)}, bf16[64,768]{1,0:T(8,128)(2,1)S(1)}, u32[]{:S(2)}, u32[]{:S(2)}) %collective-permute-start.5) | collective-permute-done | bytes 98336 | tf_op jit(solution)/shard_map/ppermute | solution.py:39
  80.6 0.7 shard_map.112
  81.3 2.4 %collective-permute-start.7 = (bf16[64,768]{1,0:T(8,128)(2,1)S(1)}, bf16[64,768]{1,0:T(8,128)(2,1)S(1)}, u32[]{:S(2)}, u32[]{:S(2)}) collective-permute-start(bf16[64,768]{1,0:T(8,128)(2,1)S(1)} %get-tuple-element.39.refs_3_.refs_0_), channel_id=1, source_target_pairs={{0,16},{1,17},{2,18},{3,19},{4,20},{5,21},{6,22},{7,23},{8,24},{9,... | collective-permute-start | bytes 294920 | tf_op jit(solution)/shard_map/ppermute | solution.py:39
  83.6 1.3 collective-permute-start.8
  85.1 0.6 shard_map.113.refs_11_
  85.7 3.3 %collective-permute-done.8.refs_2_ = bf16[64,768]{1,0:T(8,128)(2,1)S(1)} collective-permute-done((bf16[64,768]{1,0:T(8,128)(2,1)S(1)}, bf16[64,768]{1,0:T(8,128)(2,1)S(1)}, u32[]{:S(2)}, u32[]{:S(2)}) %collective-permute-start.8) | collective-permute-done | bytes 98336 | tf_op jit(solution)/shard_map/ppermute | solution.py:39
  89.0 2.4 %shard_map.114 = (bf16[24,2,32,128]{3,2,1,0:T(8,128)(2,1)S(1)}, bf16[1280,128]{1,0:T(8,128)(2,1)S(1)}) custom-call(s32[1]{0:T(128)} %bitcast.half, bf16[64,768]{1,0:T(8,128)(2,1)S(1)} %get-tuple-element.39.refs_3_.refs_0_, bf16[64,768]{1,0:T(8,128)(2,1)S(1)} %collective-permute-done.7.refs_1_, bf16[64,768]{1,0:T(8,128)(2,1)S(1)} %collective-permute-done.8.refs_2_, ...), custom_call_target="tpu_custom_call" | custom-call | tf_op jit(solution)/shard_map/pallas_call | solution.py:22
  91.4 0.8 pad_maximum_fusion
  92.2 16.3 %all-to-all-start.2 = ((bf16[32,56,128]{2,1,0:T(8,128)(2,1)}), bf16[32,56,128]{2,1,0:T(8,128)(2,1)S(1)}, u32[]{:S(2)}, u32[]{:S(2)}) async-start(bf16[32,56,128]{2,1,0:T(8,128)(2,1)} %pad_maximum_fusion), calls=%async_computation.2 | async-start | bytes 917504 | tf_op jit(solution)/shard_map/all_to_all | solution.py:342
  108.6 1.3 collective-permute-start.10
  109.9 4.0 %collective-permute-start.9 = (bf16[17,1,32,128]{3,2,1,0:T(8,128)(2,1)S(1)}, bf16[17,1,32,128]{3,2,1,0:T(8,128)(2,1)S(1)}, u32[]{:S(2)}, u32[]{:S(2)}) collective-permute-start(bf16[17,1,32,128]{3,2,1,0:T(8,128)(2,1)S(1)} %get-tuple-element.69), channel_id=1, source_target_pairs={{0,16},{1,17},{2,18},{3,19},{4,20},{5,21},{6,22},{7,23},{8,24},{9,... | collective-permute-start | bytes 417800 | tf_op jit(solution)/shard_map/ppermute | solution.py:39
  114.1 5.4 %collective-permute-done.10.refs_2_ = bf16[17,1,32,128]{3,2,1,0:T(8,128)(2,1)S(1)} collective-permute-done((bf16[17,1,32,128]{3,2,1,0:T(8,128)(2,1)S(1)}, bf16[17,1,32,128]{3,2,1,0:T(8,128)(2,1)S(1)}, u32[]{:S(2)}, u32[]{:S(2)}) %collective-permute-start.10) | collective-permute-done | bytes 139296 | tf_op jit(solution)/shard_map/ppermute | solution.py:39
  119.5 0.8 shard_map.115
  120.5 0.7 pad_maximum_fusion.1
  121.3 12.0 %all-to-all-start.3 = ((bf16[16,72,128]{2,1,0:T(8,128)(2,1)}), bf16[16,72,128]{2,1,0:T(8,128)(2,1)S(1)}, u32[]{:S(2)}, u32[]{:S(2)}) async-start(bf16[16,72,128]{2,1,0:T(8,128)(2,1)} %pad_maximum_fusion.1), calls=%async_computation.3 | async-start | bytes 589824 | tf_op jit(solution)/shard_map/all_to_all | solution.py:342
  133.3 12.0 %collective-permute-start.11 = (bf16[2,2,2,2,32,128]{5,4,3,2,1,0:T(8,128)(2,1)S(1)}, bf16[2,2,2,2,32,128]{5,4,3,2,1,0:T(8,128)(2,1)S(1)}, u32[]{:S(2)}, u32[]{:S(2)}) collective-permute-start(bf16[2,2,2,2,32,128]{5,4,3,2,1,0:T(8,128)(2,1)S(1)} %fusion), channel_id=1, source_target_pairs={{0,2},{1,3},{2,0},{3,1},{4,6},{5,7},{6,4},{7,5},{8,10},{9,11},{10,... | collective-permute-start | bytes 393224 | tf_op jit(solution)/shard_map/ppermute | solution.py:424
  145.4 4.6 %all-to-all-done.3 = bf16[16,72,128]{2,1,0:T(8,128)(2,1)S(1)} async-done(((bf16[16,72,128]{2,1,0:T(8,128)(2,1)}), bf16[16,72,128]{2,1,0:T(8,128)(2,1)S(1)}, u32[]{:S(2)}, u32[]{:S(2)}) %all-to-all-start.3) | async-done | bytes 294944 | tf_op jit(solution)/shard_map/all_to_all | solution.py:342
  150.1 0.8 broadcast_in_dim.8
  150.8 14.6 %all-to-all-start.4 = ((bf16[32,40,128]{2,1,0:T(8,128)(2,1)}), bf16[32,40,128]{2,1,0:T(8,128)(2,1)S(1)}, u32[]{:S(2)}, u32[]{:S(2)}) async-start(bf16[32,40,128]{2,1,0:T(8,128)(2,1)} %broadcast_in_dim.8), calls=%async_computation.4 | async-start | bytes 655360 | tf_op jit(solution)/shard_map/all_to_all | solution.py:342
  165.6 9.4 %all-to-all-done.4 = bf16[32,40,128]{2,1,0:T(8,128)(2,1)S(1)} async-done(((bf16[32,40,128]{2,1,0:T(8,128)(2,1)}), bf16[32,40,128]{2,1,0:T(8,128)(2,1)S(1)}, u32[]{:S(2)}, u32[]{:S(2)}) %all-to-all-start.4) | async-done | bytes 327712 | tf_op jit(solution)/shard_map/all_to_all | solution.py:342
  175.0 0.8 copy.58
  175.9 3.8 %all-to-all-start.5 = ((bf16[4,2,2,2,32,128]{5,4,3,2,1,0:T(8,128)(2,1)}), bf16[4,2,2,2,32,128]{5,4,3,2,1,0:T(8,128)(2,1)S(1)}, u32[]{:S(2)}, u32[]{:S(2)}) async-start(bf16[4,2,2,2,32,128]{5,4,3,2,1,0:T(8,128)(2,1)} %bitcast.45), calls=%async_computation.5 | async-start | bytes 524288 | tf_op jit(solution)/shard_map/all_to_all | solution.py:342
  179.7 0.6 slice_select_fusion.2
  180.3 1.7 shard_map.116
  182.0 2.3 %shard_map.117 = (f32[27,32,32]{2,1,0:T(8,128)}, f32[8,32,64]{2,1,0:T(8,128)}, f32[27,64,64]{2,1,0:T(8,128)}) custom-call(bf16[1280,128]{1,0:T(8,128)(2,1)} %bitcast.107), custom_call_target="tpu_custom_call" | custom-call | tf_op jit(solution)/shard_map/pallas_call | solution.py:557
  184.3 0.5 all-to-all-done.5
  184.9 0.9 copy.60
  (62 shorter events, 1.8 us)
Async XLA Ops:
  0.6 31.3 %copy-start.2 = (bf16[27,64,64]{2,1,0:T(8,128)(2,1)S(1)}, bf16[27,64,64]{2,1,0:T(8,128)(2,1)}, u32[]{:S(2)}) copy-start(bf16[27,64,64]{2,1,0:T(8,128)(2,1)} %param.10) | copy-start | bytes 663556
  0.6 35.0 %all-to-all-start = ((bf16[8,2,2,32,128]{4,2,1,3,0:T(2,128)(2,1)}), bf16[8,2,2,32,128]{4,2,1,3,0:T(2,128)(2,1)S(1)}, u32[]{:S(2)}, u32[]{:S(2)}) async-start(bf16[8,2,2,32,128]{4,2,1,3,0:T(2,128)(2,1)} %bitcast.121), calls=%async_computation | async-start | bytes 524288 | tf_op jit(solution)/shard_map/all_to_all | solution.py:342
  18.3 13.6 %copy-start.6 = (bf16[8,64,32]{1,2,0:T(8,128)(2,1)S(1)}, bf16[8,64,32]{1,2,0:T(8,128)(2,1)}, u32[]{:S(2)}) copy-start(bf16[8,64,32]{1,2,0:T(8,128)(2,1)} %param.9) | copy-start | bytes 98308
  19.9 21.7 %collective-permute-start = (bf16[256,128]{1,0:T(8,128)(2,1)}, bf16[256,128]{1,0:T(8,128)(2,1)}, u32[]{:S(2)}, u32[]{:S(2)}) collective-permute-start(bf16[256,128]{1,0:T(8,128)(2,1)} %shard_map.110), channel_id=1, source_target_pairs={{0,71},{1,135},{2,199},{3,263},{4,327},{5,391},{6,455},{7,7},{8,79... | collective-permute-start | bytes 196616 | tf_op jit(solution)/shard_map/ppermute | solution.py:361
  34.0 0.9 copy-start.5
  41.6 14.5 %collective-permute-start.1 = (bf16[8,2,32,128]{3,2,1,0:T(8,128)(2,1)S(1)}, bf16[8,2,32,128]{3,2,1,0:T(8,128)(2,1)S(1)}, u32[]{:S(2)}, u32[]{:S(2)}) collective-permute-start(bf16[8,2,32,128]{3,2,1,0:T(8,128)(2,1)S(1)} %slice_select_fusion.1), channel_id=1, source_target_pairs={{8,0},{9,1},{10,2},{11,3},{12,4},{13,5},{14,6},{15,7},{0,8},{1,9},... | collective-permute-start | bytes 393224 | tf_op jit(solution)/shard_map/ppermute | solution.py:39
  46.0 21.4 %all-to-all-start.1 = ((bf16[32,8,128]{2,1,0:T(8,128)(2,1)}), bf16[32,8,128]{2,1,0:T(8,128)(2,1)S(1)}, u32[]{:S(2)}, u32[]{:S(2)}) async-start(bf16[32,8,128]{2,1,0:T(8,128)(2,1)} %bitcast.4), calls=%async_computation.1 | async-start | bytes 131072 | tf_op jit(solution)/shard_map/all_to_all | solution.py:342
  56.2 13.8 %collective-permute-start.2 = (bf16[24,1,32,128]{3,2,1,0:T(8,128)(2,1)S(1)}, bf16[24,1,32,128]{3,2,1,0:T(8,128)(2,1)S(1)}, u32[]{:S(2)}, u32[]{:S(2)}) collective-permute-start(bf16[24,1,32,128]{3,2,1,0:T(8,128)(2,1)S(1)} %get-tuple-element.67), channel_id=1, source_target_pairs={{0,16},{1,17},{2,18},{3,19},{4,20},{5,21},{6,22},{7,23},{8,24},{9,... | collective-permute-start | bytes 589832 | tf_op jit(solution)/shard_map/ppermute | solution.py:39
  59.4 10.6 %collective-permute-start.3 = (bf16[24,1,32,128]{3,2,1,0:T(8,128)(2,1)S(1)}, bf16[24,1,32,128]{3,2,1,0:T(8,128)(2,1)S(1)}, u32[]{:S(2)}, u32[]{:S(2)}) collective-permute-start(bf16[24,1,32,128]{3,2,1,0:T(8,128)(2,1)S(1)} %get-tuple-element.66), channel_id=1, source_target_pairs={{16,0},{17,1},{18,2},{19,3},{20,4},{21,5},{22,6},{23,7},{24,8},{25... | collective-permute-start | bytes 589832 | tf_op jit(solution)/shard_map/ppermute | solution.py:39
  67.4 2.6 %copy-start.1 = (bf16[256,256]{1,0:T(8,128)(2,1)S(1)}, bf16[256,256]{1,0:T(8,128)(2,1)}, u32[]{:S(2)}) copy-start(bf16[256,256]{1,0:T(8,128)(2,1)} %constant.116.clone.refs_5_) | copy-start | bytes 393220
  67.4 9.1 %collective-permute-start.6 = (bf16[128,128]{1,0:T(8,128)(2,1)S(1)}, bf16[128,128]{1,0:T(8,128)(2,1)S(1)}, u32[]{:S(2)}, u32[]{:S(2)}) collective-permute-start(bf16[128,128]{1,0:T(8,128)(2,1)S(1)} %fusion.7), channel_id=1, source_target_pairs={{8,0},{9,1},{10,2},{11,3},{12,4},{13,5},{14,6},{15,7},{0,8},{1,9},... | collective-permute-start | bytes 98312 | tf_op jit(solution)/shard_map/ppermute | solution.py:39
  73.1 3.8 %collective-permute-start.4 = (bf16[64,768]{1,0:T(8,128)(2,1)S(1)}, bf16[64,768]{1,0:T(8,128)(2,1)S(1)}, u32[]{:S(2)}, u32[]{:S(2)}) collective-permute-start(bf16[64,768]{1,0:T(8,128)(2,1)S(1)} %get-tuple-element.35.refs_0_), channel_id=1, source_target_pairs={{0,16},{1,17},{2,18},{3,19},{4,20},{5,21},{6,22},{7,23},{8,24},{9,... | collective-permute-start | bytes 294920 | tf_op jit(solution)/shard_map/ppermute | solution.py:39
  75.3 5.4 %collective-permute-start.5 = (bf16[64,768]{1,0:T(8,128)(2,1)S(1)}, bf16[64,768]{1,0:T(8,128)(2,1)S(1)}, u32[]{:S(2)}, u32[]{:S(2)}) collective-permute-start(bf16[64,768]{1,0:T(8,128)(2,1)S(1)} %get-tuple-element.35.refs_0_), channel_id=1, source_target_pairs={{16,0},{17,1},{18,2},{19,3},{20,4},{21,5},{22,6},{23,7},{24,8},{25... | collective-permute-start | bytes 294920 | tf_op jit(solution)/shard_map/ppermute | solution.py:39
  81.3 4.4 %collective-permute-start.7 = (bf16[64,768]{1,0:T(8,128)(2,1)S(1)}, bf16[64,768]{1,0:T(8,128)(2,1)S(1)}, u32[]{:S(2)}, u32[]{:S(2)}) collective-permute-start(bf16[64,768]{1,0:T(8,128)(2,1)S(1)} %get-tuple-element.39.refs_3_.refs_0_), channel_id=1, source_target_pairs={{0,16},{1,17},{2,18},{3,19},{4,20},{5,21},{6,22},{7,23},{8,24},{9,... | collective-permute-start | bytes 294920 | tf_op jit(solution)/shard_map/ppermute | solution.py:39
  83.6 5.4 %collective-permute-start.8 = (bf16[64,768]{1,0:T(8,128)(2,1)S(1)}, bf16[64,768]{1,0:T(8,128)(2,1)S(1)}, u32[]{:S(2)}, u32[]{:S(2)}) collective-permute-start(bf16[64,768]{1,0:T(8,128)(2,1)S(1)} %get-tuple-element.39.refs_3_.refs_0_), channel_id=1, source_target_pairs={{16,0},{17,1},{18,2},{19,3},{20,4},{21,5},{22,6},{23,7},{24,8},{25... | collective-permute-start | bytes 294920 | tf_op jit(solution)/shard_map/ppermute | solution.py:39
  85.1 4.0 %copy-start = (bf16[256,256]{1,0:T(8,128)(2,1)S(1)}, bf16[256,256]{1,0:T(8,128)(2,1)}, u32[]{:S(2)}) copy-start(bf16[256,256]{1,0:T(8,128)(2,1)} %constant.117.clone.refs_8_) | copy-start | bytes 393220
  92.2 28.1 %all-to-all-start.2 = ((bf16[32,56,128]{2,1,0:T(8,128)(2,1)}), bf16[32,56,128]{2,1,0:T(8,128)(2,1)S(1)}, u32[]{:S(2)}, u32[]{:S(2)}) async-start(bf16[32,56,128]{2,1,0:T(8,128)(2,1)} %pad_maximum_fusion), calls=%async_computation.2 | async-start | bytes 917504 | tf_op jit(solution)/shard_map/all_to_all | solution.py:342
  108.6 10.9 %collective-permute-start.10 = (bf16[17,1,32,128]{3,2,1,0:T(8,128)(2,1)S(1)}, bf16[17,1,32,128]{3,2,1,0:T(8,128)(2,1)S(1)}, u32[]{:S(2)}, u32[]{:S(2)}) collective-permute-start(bf16[17,1,32,128]{3,2,1,0:T(8,128)(2,1)S(1)} %get-tuple-element.68), channel_id=1, source_target_pairs={{16,0},{17,1},{18,2},{19,3},{20,4},{21,5},{22,6},{23,7},{24,8},{25... | collective-permute-start | bytes 417800 | tf_op jit(solution)/shard_map/ppermute | solution.py:39
  109.9 9.6 %collective-permute-start.9 = (bf16[17,1,32,128]{3,2,1,0:T(8,128)(2,1)S(1)}, bf16[17,1,32,128]{3,2,1,0:T(8,128)(2,1)S(1)}, u32[]{:S(2)}, u32[]{:S(2)}) collective-permute-start(bf16[17,1,32,128]{3,2,1,0:T(8,128)(2,1)S(1)} %get-tuple-element.69), channel_id=1, source_target_pairs={{0,16},{1,17},{2,18},{3,19},{4,20},{5,21},{6,22},{7,23},{8,24},{9,... | collective-permute-start | bytes 417800 | tf_op jit(solution)/shard_map/ppermute | solution.py:39
  121.3 28.8 %all-to-all-start.3 = ((bf16[16,72,128]{2,1,0:T(8,128)(2,1)}), bf16[16,72,128]{2,1,0:T(8,128)(2,1)S(1)}, u32[]{:S(2)}, u32[]{:S(2)}) async-start(bf16[16,72,128]{2,1,0:T(8,128)(2,1)} %pad_maximum_fusion.1), calls=%async_computation.3 | async-start | bytes 589824 | tf_op jit(solution)/shard_map/all_to_all | solution.py:342
  133.3 32.1 %collective-permute-start.11 = (bf16[2,2,2,2,32,128]{5,4,3,2,1,0:T(8,128)(2,1)S(1)}, bf16[2,2,2,2,32,128]{5,4,3,2,1,0:T(8,128)(2,1)S(1)}, u32[]{:S(2)}, u32[]{:S(2)}) collective-permute-start(bf16[2,2,2,2,32,128]{5,4,3,2,1,0:T(8,128)(2,1)S(1)} %fusion), channel_id=1, source_target_pairs={{0,2},{1,3},{2,0},{3,1},{4,6},{5,7},{6,4},{7,5},{8,10},{9,11},{10,... | collective-permute-start | bytes 393224 | tf_op jit(solution)/shard_map/ppermute | solution.py:424
  150.0 15.5 %copy-start.4 = (bf16[16,72,128]{2,1,0:T(8,128)(2,1)}, bf16[16,72,128]{2,1,0:T(8,128)(2,1)S(1)}, u32[]{:S(2)}) copy-start(bf16[16,72,128]{2,1,0:T(8,128)(2,1)S(1)} %all-to-all-done.3) | copy-start | bytes 884740
  150.8 24.2 %all-to-all-start.4 = ((bf16[32,40,128]{2,1,0:T(8,128)(2,1)}), bf16[32,40,128]{2,1,0:T(8,128)(2,1)S(1)}, u32[]{:S(2)}, u32[]{:S(2)}) async-start(bf16[32,40,128]{2,1,0:T(8,128)(2,1)} %broadcast_in_dim.8), calls=%async_computation.4 | async-start | bytes 655360 | tf_op jit(solution)/shard_map/all_to_all | solution.py:342
  175.0 0.8 copy-start.3
  175.8 3.9 %slice-start = ((bf16[16,72,128]{2,1,0:T(8,128)(2,1)}), bf16[16,32,128]{2,1,0:T(8,128)(2,1)S(1)}, s32[]{:S(2)}) async-start(bf16[16,72,128]{2,1,0:T(8,128)(2,1)} %copy-done.4), calls=%async_computation.6 | async-start | bytes 262144 | tf_op jit(solution)/shard_map/slice | solution.py:546
  175.9 9.0 %all-to-all-start.5 = ((bf16[4,2,2,2,32,128]{5,4,3,2,1,0:T(8,128)(2,1)}), bf16[4,2,2,2,32,128]{5,4,3,2,1,0:T(8,128)(2,1)S(1)}, u32[]{:S(2)}, u32[]{:S(2)}) async-start(bf16[4,2,2,2,32,128]{5,4,3,2,1,0:T(8,128)(2,1)} %bitcast.45), calls=%async_computation.5 | async-start | bytes 524288 | tf_op jit(solution)/shard_map/all_to_all | solution.py:342

commit v10 on v9

--- a/solution.py
+++ b/solution.py
@@ -531,14 +531,15 @@
     mixed = trade(jnp.concatenate([grads, coarse], axis=1), ("grp", "sp"), near)
     part = jnp.sum(mixed[:, :kept].astype(F32), axis=0).astype(BF16)
     coarse = for_column(mixed[:, kept:])
+    spread = last_pieces(dpre2, batch * x_cells)
+    part, coarse, *spread[1:] = lax.optimization_barrier((part, coarse, *spread[1:]))
     gradient = call(
         input_kernel,
         shape((batch * x_cells, *own.shape[1:]), BF16),
         half,
-        *last_pieces(dpre2, batch * x_cells),
+        *spread,
         fine_back,
     )
-    part, gradient, coarse = lax.optimization_barrier((part, gradient, coarse))
     gradient = far_exchange(gradient.reshape(batch // 4, 2, 2, x_cells, y_cells, chans, LANES))
     part = jnp.broadcast_to(part[None], (coarse.shape[0], *part.shape))
     mixed = trade(jnp.concatenate([part, coarse], axis=1), ("grp", "sp"), columns())

time: 187 us -> 185 us (0.989)
    ppermute x10, waiting for transfers between devices: 12.8 us -> 7.37 us  [arrival(): return lax.ppermute(block, ('grp', 'sp'), pairs)]
    all_to_all x6, waiting for transfers between devices: 21.2 us -> 25.6 us  [trade(): lax.all_to_all(parts, axis, split_axis=0, concat_axis=0, axis_index_group...]
  transfers between devices with their start and end apart: 18 -> 18, of which waited for: 9 -> 10; matrix products, arithmetic and copies ran while one was open for 3% -> 3% of each run, Pallas kernels for 5% -> 5%
where the time goes in v10:
time: 185 us; the launch traced here: 184 us
  starting transfers between devices  121 us (65%)
  waiting for transfers between devices  39.1 us (21%)
  Pallas kernels  13.1 us (7%)
  local copies, waits for them, and re-layouts  7.07 us (4%)
  other arithmetic  2.62 us (1%)
    all_to_all x6, starting transfers between devices, trade(): lax.all_to_all(parts, axis, split_axis=0, concat_axis=0, axis_index_group...  72.8 us
    all_to_all x6, waiting for transfers between devices, trade(): lax.all_to_all(parts, axis, split_axis=0, concat_axis=0, axis_index_group...  25.6 us
    ppermute x10, starting transfers between devices, arrival(): return lax.ppermute(block, ('grp', 'sp'), pairs)  23.8 us
    ppermute x1, starting transfers between devices, turned(): return lax.ppermute(block, ('grp', 'sp'), pairs)  12 us
    ppermute x1, starting transfers between devices, far_exchange(): lax.ppermute(sent, 'sp', [(col, col ^ 2) for col in range(lax.axis_size('...  12 us
    pallas_call x5, Pallas kernels, call(): pl.pallas_call(kernel, out_shape=outs, in_specs=[pl.BlockSpec(memory_spac...  7.45 us
    ppermute x10, waiting for transfers between devices, arrival(): return lax.ppermute(block, ('grp', 'sp'), pairs)  7.37 us
    ppermute x1, waiting for transfers between devices, turned(): return lax.ppermute(block, ('grp', 'sp'), pairs)  5.86 us
  transfers between devices with their start and end apart: 18, of which 10 were waited for; matrix products, arithmetic and copies ran while one was open for 3% of the time, Pallas kernels for 5%

profile of v10, /device:TPU:1, one launch (start us, length us, event | category | flops | bytes accessed | tf_op | source)
XLA Modules:
  0.0 183.7 jit_solution(13990697454041529151)
XLA Ops:
  0.6 17.7 %all-to-all-start = ((bf16[8,2,2,32,128]{4,2,1,3,0:T(2,128)(2,1)}), bf16[8,2,2,32,128]{4,2,1,3,0:T(2,128)(2,1)S(1)}, u32[]{:S(2)}, u32[]{:S(2)}) async-start(bf16[8,2,2,32,128]{4,2,1,3,0:T(2,128)(2,1)} %bitcast.121), calls=%async_computation | async-start | bytes 524288 | tf_op jit(solution)/shard_map/all_to_all | solution.py:342
  18.3 1.6 shard_map.110
  19.9 12.0 %collective-permute-start = (bf16[256,128]{1,0:T(8,128)(2,1)}, bf16[256,128]{1,0:T(8,128)(2,1)}, u32[]{:S(2)}, u32[]{:S(2)}) collective-permute-start(bf16[256,128]{1,0:T(8,128)(2,1)} %shard_map.110), channel_id=1, source_target_pairs={{0,71},{1,135},{2,199},{3,263},{4,327},{5,391},{6,455},{7,7},{8,79... | collective-permute-start | bytes 196616 | tf_op jit(solution)/shard_map/ppermute | solution.py:361
  32.0 0.4 copy.65
  32.4 0.4 reshape.119
  32.8 1.2 copy.44
  34.0 0.4 reshape.117
  34.4 0.6 copy-done.5
  35.3 0.2 copy.42
  35.7 5.9 %collective-permute-done = bf16[256,128]{1,0:T(8,128)(2,1)} collective-permute-done((bf16[256,128]{1,0:T(8,128)(2,1)}, bf16[256,128]{1,0:T(8,128)(2,1)}, u32[]{:S(2)}, u32[]{:S(2)}) %collective-permute-start) | collective-permute-done | bytes 65568 | tf_op jit(solution)/shard_map/ppermute | solution.py:361
  41.6 4.4 %collective-permute-start.1 = (bf16[8,2,32,128]{3,2,1,0:T(8,128)(2,1)S(1)}, bf16[8,2,32,128]{3,2,1,0:T(8,128)(2,1)S(1)}, u32[]{:S(2)}, u32[]{:S(2)}) collective-permute-start(bf16[8,2,32,128]{3,2,1,0:T(8,128)(2,1)S(1)} %slice_select_fusion.1), channel_id=1, source_target_pairs={{8,0},{9,1},{10,2},{11,3},{12,4},{13,5},{14,6},{15,7},{0,8},{1,9},... | collective-permute-start | bytes 393224 | tf_op jit(solution)/shard_map/ppermute | solution.py:39
  46.0 9.6 %all-to-all-start.1 = ((bf16[32,8,128]{2,1,0:T(8,128)(2,1)}), bf16[32,8,128]{2,1,0:T(8,128)(2,1)S(1)}, u32[]{:S(2)}, u32[]{:S(2)}) async-start(bf16[32,8,128]{2,1,0:T(8,128)(2,1)} %bitcast.4), calls=%async_computation.1 | async-start | bytes 131072 | tf_op jit(solution)/shard_map/all_to_all | solution.py:342
  56.3 3.1 %collective-permute-start.2 = (bf16[24,1,32,128]{3,2,1,0:T(8,128)(2,1)S(1)}, bf16[24,1,32,128]{3,2,1,0:T(8,128)(2,1)S(1)}, u32[]{:S(2)}, u32[]{:S(2)}) collective-permute-start(bf16[24,1,32,128]{3,2,1,0:T(8,128)(2,1)S(1)} %get-tuple-element.69), channel_id=1, source_target_pairs={{0,16},{1,17},{2,18},{3,19},{4,20},{5,21},{6,22},{7,23},{8,24},{9,... | collective-permute-start | bytes 589832 | tf_op jit(solution)/shard_map/ppermute | solution.py:39
  59.4 1.3 collective-permute-start.3
  60.7 6.7 %all-to-all-done.1 = bf16[32,8,128]{2,1,0:T(8,128)(2,1)S(1)} async-done(((bf16[32,8,128]{2,1,0:T(8,128)(2,1)}), bf16[32,8,128]{2,1,0:T(8,128)(2,1)S(1)}, u32[]{:S(2)}, u32[]{:S(2)}) %all-to-all-start.1) | async-done | bytes 65568 | tf_op jit(solution)/shard_map/all_to_all | solution.py:342
  67.5 2.6 %collective-permute-start.6 = (bf16[128,128]{1,0:T(8,128)(2,1)S(1)}, bf16[128,128]{1,0:T(8,128)(2,1)S(1)}, u32[]{:S(2)}, u32[]{:S(2)}) collective-permute-start(bf16[128,128]{1,0:T(8,128)(2,1)S(1)} %fusion.7), channel_id=1, source_target_pairs={{8,0},{9,1},{10,2},{11,3},{12,4},{13,5},{14,6},{15,7},{0,8},{1,9},... | collective-permute-start | bytes 98312 | tf_op jit(solution)/shard_map/ppermute | solution.py:39
  70.1 3.0 %shard_map.111 = (bf16[64,768]{1,0:T(8,128)(2,1)S(1)}, bf16[256,768]{1,0:T(8,128)(2,1)S(1)}, f32[12,128,128]{2,1,0:T(8,128)S(1)}) custom-call(s32[1]{0:T(128)} %bitcast.half, bf16[24,2,32,128]{3,2,1,0:T(8,128)(2,1)S(1)} %maximum_select_fusion.refs_0_.refs_3_, bf16[24,1,32,128]{3,2,1,0:T(8,128)(2,1)S(1)} %collective-permute-done.2.refs_1_.refs_4_, ...), custom_call_target="tpu_custom_call" | custom-call | tf_op jit(solution)/shard_map/pallas_call | solution.py:22
  73.1 2.2 %collective-permute-start.4 = (bf16[64,768]{1,0:T(8,128)(2,1)S(1)}, bf16[64,768]{1,0:T(8,128)(2,1)S(1)}, u32[]{:S(2)}, u32[]{:S(2)}) collective-permute-start(bf16[64,768]{1,0:T(8,128)(2,1)S(1)} %get-tuple-element.36.refs_0_), channel_id=1, source_target_pairs={{0,16},{1,17},{2,18},{3,19},{4,20},{5,21},{6,22},{7,23},{8,24},{9,... | collective-permute-start | bytes 294920 | tf_op jit(solution)/shard_map/ppermute | solution.py:39
  75.3 1.3 collective-permute-start.5
  76.7 0.3 collective-permute-done.4.refs_1_
  76.9 3.7 %collective-permute-done.5.refs_2_ = bf16[64,768]{1,0:T(8,128)(2,1)S(1)} collective-permute-done((bf16[64,768]{1,0:T(8,128)(2,1)S(1)}, bf16[64,768]{1,0:T(8,128)(2,1)S(1)}, u32[]{:S(2)}, u32[]{:S(2)}) %collective-permute-start.5) | collective-permute-done | bytes 98336 | tf_op jit(solution)/shard_map/ppermute | solution.py:39
  80.7 0.7 shard_map.112
  81.3 2.3 %collective-permute-start.7 = (bf16[64,768]{1,0:T(8,128)(2,1)S(1)}, bf16[64,768]{1,0:T(8,128)(2,1)S(1)}, u32[]{:S(2)}, u32[]{:S(2)}) collective-permute-start(bf16[64,768]{1,0:T(8,128)(2,1)S(1)} %get-tuple-element.40.refs_3_.refs_0_), channel_id=1, source_target_pairs={{0,16},{1,17},{2,18},{3,19},{4,20},{5,21},{6,22},{7,23},{8,24},{9,... | collective-permute-start | bytes 294920 | tf_op jit(solution)/shard_map/ppermute | solution.py:39
  83.7 1.3 collective-permute-start.8
  85.1 0.6 shard_map.113.refs_11_
  85.7 3.3 %collective-permute-done.8.refs_2_ = bf16[64,768]{1,0:T(8,128)(2,1)S(1)} collective-permute-done((bf16[64,768]{1,0:T(8,128)(2,1)S(1)}, bf16[64,768]{1,0:T(8,128)(2,1)S(1)}, u32[]{:S(2)}, u32[]{:S(2)}) %collective-permute-start.8) | collective-permute-done | bytes 98336 | tf_op jit(solution)/shard_map/ppermute | solution.py:39
  89.1 2.4 %shard_map.114 = (bf16[24,2,32,128]{3,2,1,0:T(8,128)(2,1)S(1)}, bf16[1280,128]{1,0:T(8,128)(2,1)S(1)}) custom-call(s32[1]{0:T(128)} %bitcast.half, bf16[64,768]{1,0:T(8,128)(2,1)S(1)} %get-tuple-element.40.refs_3_.refs_0_, bf16[64,768]{1,0:T(8,128)(2,1)S(1)} %collective-permute-done.7.refs_1_, bf16[64,768]{1,0:T(8,128)(2,1)S(1)} %collective-permute-done.8.refs_2_, ...), custom_call_target="tpu_custom_call" | custom-call | tf_op jit(solution)/shard_map/pallas_call | solution.py:22
  91.4 0.8 pad_maximum_fusion
  92.2 16.4 %all-to-all-start.2 = ((bf16[32,56,128]{2,1,0:T(8,128)(2,1)}), bf16[32,56,128]{2,1,0:T(8,128)(2,1)S(1)}, u32[]{:S(2)}, u32[]{:S(2)}) async-start(bf16[32,56,128]{2,1,0:T(8,128)(2,1)} %pad_maximum_fusion), calls=%async_computation.2 | async-start | bytes 917504 | tf_op jit(solution)/shard_map/all_to_all | solution.py:342
  108.7 1.3 collective-permute-start.10
  110.0 4.0 %collective-permute-start.9 = (bf16[17,1,32,128]{3,2,1,0:T(8,128)(2,1)S(1)}, bf16[17,1,32,128]{3,2,1,0:T(8,128)(2,1)S(1)}, u32[]{:S(2)}, u32[]{:S(2)}) collective-permute-start(bf16[17,1,32,128]{3,2,1,0:T(8,128)(2,1)S(1)} %get-tuple-element.71), channel_id=1, source_target_pairs={{0,16},{1,17},{2,18},{3,19},{4,20},{5,21},{6,22},{7,23},{8,24},{9,... | collective-permute-start | bytes 417800 | tf_op jit(solution)/shard_map/ppermute | solution.py:39
  114.0 5.5 %all-to-all-done.2 = bf16[32,56,128]{2,1,0:T(8,128)(2,1)S(1)} async-done(((bf16[32,56,128]{2,1,0:T(8,128)(2,1)}), bf16[32,56,128]{2,1,0:T(8,128)(2,1)S(1)}, u32[]{:S(2)}, u32[]{:S(2)}) %all-to-all-start.2) | async-done | bytes 458784 | tf_op jit(solution)/shard_map/all_to_all | solution.py:342
  119.7 0.7 pad_maximum_fusion.1
  120.5 11.8 %all-to-all-start.3 = ((bf16[16,72,128]{2,1,0:T(8,128)(2,1)}), bf16[16,72,128]{2,1,0:T(8,128)(2,1)S(1)}, u32[]{:S(2)}, u32[]{:S(2)}) async-start(bf16[16,72,128]{2,1,0:T(8,128)(2,1)} %pad_maximum_fusion.1), calls=%async_computation.3 | async-start | bytes 589824 | tf_op jit(solution)/shard_map/all_to_all | solution.py:342
  132.4 0.8 shard_map.116
  133.3 12.0 %collective-permute-start.11 = (bf16[2,2,2,2,32,128]{5,4,3,2,1,0:T(8,128)(2,1)S(1)}, bf16[2,2,2,2,32,128]{5,4,3,2,1,0:T(8,128)(2,1)S(1)}, u32[]{:S(2)}, u32[]{:S(2)}) collective-permute-start(bf16[2,2,2,2,32,128]{5,4,3,2,1,0:T(8,128)(2,1)S(1)} %fusion), channel_id=1, source_target_pairs={{0,2},{1,3},{2,0},{3,1},{4,6},{5,7},{6,4},{7,5},{8,10},{9,11},{10,... | collective-permute-start | bytes 393224 | tf_op jit(solution)/shard_map/ppermute | solution.py:424
  145.3 3.7 %all-to-all-done.3 = bf16[16,72,128]{2,1,0:T(8,128)(2,1)S(1)} async-done(((bf16[16,72,128]{2,1,0:T(8,128)(2,1)}), bf16[16,72,128]{2,1,0:T(8,128)(2,1)S(1)}, u32[]{:S(2)}, u32[]{:S(2)}) %all-to-all-start.3) | async-done | bytes 294944 | tf_op jit(solution)/shard_map/all_to_all | solution.py:342
  149.1 0.8 broadcast_in_dim.8
  149.8 13.6 %all-to-all-start.4 = ((bf16[32,40,128]{2,1,0:T(8,128)(2,1)}), bf16[32,40,128]{2,1,0:T(8,128)(2,1)S(1)}, u32[]{:S(2)}, u32[]{:S(2)}) async-start(bf16[32,40,128]{2,1,0:T(8,128)(2,1)} %broadcast_in_dim.8), calls=%async_computation.4 | async-start | bytes 655360 | tf_op jit(solution)/shard_map/all_to_all | solution.py:342
  163.5 0.2 collective-permute-done.11
  163.8 9.2 %all-to-all-done.4 = bf16[32,40,128]{2,1,0:T(8,128)(2,1)S(1)} async-done(((bf16[32,40,128]{2,1,0:T(8,128)(2,1)}), bf16[32,40,128]{2,1,0:T(8,128)(2,1)S(1)}, u32[]{:S(2)}, u32[]{:S(2)}) %all-to-all-start.4) | async-done | bytes 327712 | tf_op jit(solution)/shard_map/all_to_all | solution.py:342
  173.0 0.8 copy.58
  173.8 3.8 %all-to-all-start.5 = ((bf16[4,2,2,2,32,128]{5,4,3,2,1,0:T(8,128)(2,1)}), bf16[4,2,2,2,32,128]{5,4,3,2,1,0:T(8,128)(2,1)S(1)}, u32[]{:S(2)}, u32[]{:S(2)}) async-start(bf16[4,2,2,2,32,128]{5,4,3,2,1,0:T(8,128)(2,1)} %bitcast.45), calls=%async_computation.5 | async-start | bytes 524288 | tf_op jit(solution)/shard_map/all_to_all | solution.py:342
  177.6 0.6 slice_select_fusion.2
  178.3 1.7 shard_map.115
  180.0 2.3 %shard_map.117 = (f32[27,32,32]{2,1,0:T(8,128)}, f32[8,32,64]{2,1,0:T(8,128)}, f32[27,64,64]{2,1,0:T(8,128)}) custom-call(bf16[1280,128]{1,0:T(8,128)(2,1)} %bitcast.107), custom_call_target="tpu_custom_call" | custom-call | tf_op jit(solution)/shard_map/pallas_call | solution.py:558
  182.3 0.5 all-to-all-done.5
  182.8 0.9 copy.60
  (62 shorter events, 2.0 us)
Async XLA Ops:
  0.6 31.3 %copy-start.2 = (bf16[27,64,64]{2,1,0:T(8,128)(2,1)S(1)}, bf16[27,64,64]{2,1,0:T(8,128)(2,1)}, u32[]{:S(2)}) copy-start(bf16[27,64,64]{2,1,0:T(8,128)(2,1)} %param.10) | copy-start | bytes 663556
  0.6 35.0 %all-to-all-start = ((bf16[8,2,2,32,128]{4,2,1,3,0:T(2,128)(2,1)}), bf16[8,2,2,32,128]{4,2,1,3,0:T(2,128)(2,1)S(1)}, u32[]{:S(2)}, u32[]{:S(2)}) async-start(bf16[8,2,2,32,128]{4,2,1,3,0:T(2,128)(2,1)} %bitcast.121), calls=%async_computation | async-start | bytes 524288 | tf_op jit(solution)/shard_map/all_to_all | solution.py:342
  18.3 13.6 %copy-start.6 = (bf16[8,64,32]{1,2,0:T(8,128)(2,1)S(1)}, bf16[8,64,32]{1,2,0:T(8,128)(2,1)}, u32[]{:S(2)}) copy-start(bf16[8,64,32]{1,2,0:T(8,128)(2,1)} %param.9) | copy-start | bytes 98308
  19.9 21.7 %collective-permute-start = (bf16[256,128]{1,0:T(8,128)(2,1)}, bf16[256,128]{1,0:T(8,128)(2,1)}, u32[]{:S(2)}, u32[]{:S(2)}) collective-permute-start(bf16[256,128]{1,0:T(8,128)(2,1)} %shard_map.110), channel_id=1, source_target_pairs={{0,71},{1,135},{2,199},{3,263},{4,327},{5,391},{6,455},{7,7},{8,79... | collective-permute-start | bytes 196616 | tf_op jit(solution)/shard_map/ppermute | solution.py:361
  34.0 0.9 copy-start.5
  41.6 14.6 %collective-permute-start.1 = (bf16[8,2,32,128]{3,2,1,0:T(8,128)(2,1)S(1)}, bf16[8,2,32,128]{3,2,1,0:T(8,128)(2,1)S(1)}, u32[]{:S(2)}, u32[]{:S(2)}) collective-permute-start(bf16[8,2,32,128]{3,2,1,0:T(8,128)(2,1)S(1)} %slice_select_fusion.1), channel_id=1, source_target_pairs={{8,0},{9,1},{10,2},{11,3},{12,4},{13,5},{14,6},{15,7},{0,8},{1,9},... | collective-permute-start | bytes 393224 | tf_op jit(solution)/shard_map/ppermute | solution.py:39
  46.0 21.4 %all-to-all-start.1 = ((bf16[32,8,128]{2,1,0:T(8,128)(2,1)}), bf16[32,8,128]{2,1,0:T(8,128)(2,1)S(1)}, u32[]{:S(2)}, u32[]{:S(2)}) async-start(bf16[32,8,128]{2,1,0:T(8,128)(2,1)} %bitcast.4), calls=%async_computation.1 | async-start | bytes 131072 | tf_op jit(solution)/shard_map/all_to_all | solution.py:342
  56.3 13.8 %collective-permute-start.2 = (bf16[24,1,32,128]{3,2,1,0:T(8,128)(2,1)S(1)}, bf16[24,1,32,128]{3,2,1,0:T(8,128)(2,1)S(1)}, u32[]{:S(2)}, u32[]{:S(2)}) collective-permute-start(bf16[24,1,32,128]{3,2,1,0:T(8,128)(2,1)S(1)} %get-tuple-element.69), channel_id=1, source_target_pairs={{0,16},{1,17},{2,18},{3,19},{4,20},{5,21},{6,22},{7,23},{8,24},{9,... | collective-permute-start | bytes 589832 | tf_op jit(solution)/shard_map/ppermute | solution.py:39
  59.4 10.6 %collective-permute-start.3 = (bf16[24,1,32,128]{3,2,1,0:T(8,128)(2,1)S(1)}, bf16[24,1,32,128]{3,2,1,0:T(8,128)(2,1)S(1)}, u32[]{:S(2)}, u32[]{:S(2)}) collective-permute-start(bf16[24,1,32,128]{3,2,1,0:T(8,128)(2,1)S(1)} %get-tuple-element.68), channel_id=1, source_target_pairs={{16,0},{17,1},{18,2},{19,3},{20,4},{21,5},{22,6},{23,7},{24,8},{25... | collective-permute-start | bytes 589832 | tf_op jit(solution)/shard_map/ppermute | solution.py:39
  67.4 2.6 %copy-start.1 = (bf16[256,256]{1,0:T(8,128)(2,1)S(1)}, bf16[256,256]{1,0:T(8,128)(2,1)}, u32[]{:S(2)}) copy-start(bf16[256,256]{1,0:T(8,128)(2,1)} %constant.116.clone.refs_5_) | copy-start | bytes 393220
  67.5 9.2 %collective-permute-start.6 = (bf16[128,128]{1,0:T(8,128)(2,1)S(1)}, bf16[128,128]{1,0:T(8,128)(2,1)S(1)}, u32[]{:S(2)}, u32[]{:S(2)}) collective-permute-start(bf16[128,128]{1,0:T(8,128)(2,1)S(1)} %fusion.7), channel_id=1, source_target_pairs={{8,0},{9,1},{10,2},{11,3},{12,4},{13,5},{14,6},{15,7},{0,8},{1,9},... | collective-permute-start | bytes 98312 | tf_op jit(solution)/shard_map/ppermute | solution.py:39
  73.1 3.8 %collective-permute-start.4 = (bf16[64,768]{1,0:T(8,128)(2,1)S(1)}, bf16[64,768]{1,0:T(8,128)(2,1)S(1)}, u32[]{:S(2)}, u32[]{:S(2)}) collective-permute-start(bf16[64,768]{1,0:T(8,128)(2,1)S(1)} %get-tuple-element.36.refs_0_), channel_id=1, source_target_pairs={{0,16},{1,17},{2,18},{3,19},{4,20},{5,21},{6,22},{7,23},{8,24},{9,... | collective-permute-start | bytes 294920 | tf_op jit(solution)/shard_map/ppermute | solution.py:39
  75.3 5.4 %collective-permute-start.5 = (bf16[64,768]{1,0:T(8,128)(2,1)S(1)}, bf16[64,768]{1,0:T(8,128)(2,1)S(1)}, u32[]{:S(2)}, u32[]{:S(2)}) collective-permute-start(bf16[64,768]{1,0:T(8,128)(2,1)S(1)} %get-tuple-element.36.refs_0_), channel_id=1, source_target_pairs={{16,0},{17,1},{18,2},{19,3},{20,4},{21,5},{22,6},{23,7},{24,8},{25... | collective-permute-start | bytes 294920 | tf_op jit(solution)/shard_map/ppermute | solution.py:39
  81.3 4.4 %collective-permute-start.7 = (bf16[64,768]{1,0:T(8,128)(2,1)S(1)}, bf16[64,768]{1,0:T(8,128)(2,1)S(1)}, u32[]{:S(2)}, u32[]{:S(2)}) collective-permute-start(bf16[64,768]{1,0:T(8,128)(2,1)S(1)} %get-tuple-element.40.refs_3_.refs_0_), channel_id=1, source_target_pairs={{0,16},{1,17},{2,18},{3,19},{4,20},{5,21},{6,22},{7,23},{8,24},{9,... | collective-permute-start | bytes 294920 | tf_op jit(solution)/shard_map/ppermute | solution.py:39
  83.7 5.4 %collective-permute-start.8 = (bf16[64,768]{1,0:T(8,128)(2,1)S(1)}, bf16[64,768]{1,0:T(8,128)(2,1)S(1)}, u32[]{:S(2)}, u32[]{:S(2)}) collective-permute-start(bf16[64,768]{1,0:T(8,128)(2,1)S(1)} %get-tuple-element.40.refs_3_.refs_0_), channel_id=1, source_target_pairs={{16,0},{17,1},{18,2},{19,3},{20,4},{21,5},{22,6},{23,7},{24,8},{25... | collective-permute-start | bytes 294920 | tf_op jit(solution)/shard_map/ppermute | solution.py:39
  85.1 4.0 %copy-start = (bf16[256,256]{1,0:T(8,128)(2,1)S(1)}, bf16[256,256]{1,0:T(8,128)(2,1)}, u32[]{:S(2)}) copy-start(bf16[256,256]{1,0:T(8,128)(2,1)} %constant.117.clone.refs_8_) | copy-start | bytes 393220
  92.2 27.2 %all-to-all-start.2 = ((bf16[32,56,128]{2,1,0:T(8,128)(2,1)}), bf16[32,56,128]{2,1,0:T(8,128)(2,1)S(1)}, u32[]{:S(2)}, u32[]{:S(2)}) async-start(bf16[32,56,128]{2,1,0:T(8,128)(2,1)} %pad_maximum_fusion), calls=%async_computation.2 | async-start | bytes 917504 | tf_op jit(solution)/shard_map/all_to_all | solution.py:342
  108.7 11.0 %collective-permute-start.10 = (bf16[17,1,32,128]{3,2,1,0:T(8,128)(2,1)S(1)}, bf16[17,1,32,128]{3,2,1,0:T(8,128)(2,1)S(1)}, u32[]{:S(2)}, u32[]{:S(2)}) collective-permute-start(bf16[17,1,32,128]{3,2,1,0:T(8,128)(2,1)S(1)} %get-tuple-element.70), channel_id=1, source_target_pairs={{16,0},{17,1},{18,2},{19,3},{20,4},{21,5},{22,6},{23,7},{24,8},{25... | collective-permute-start | bytes 417800 | tf_op jit(solution)/shard_map/ppermute | solution.py:39
  110.0 9.7 %collective-permute-start.9 = (bf16[17,1,32,128]{3,2,1,0:T(8,128)(2,1)S(1)}, bf16[17,1,32,128]{3,2,1,0:T(8,128)(2,1)S(1)}, u32[]{:S(2)}, u32[]{:S(2)}) collective-permute-start(bf16[17,1,32,128]{3,2,1,0:T(8,128)(2,1)S(1)} %get-tuple-element.71), channel_id=1, source_target_pairs={{0,16},{1,17},{2,18},{3,19},{4,20},{5,21},{6,22},{7,23},{8,24},{9,... | collective-permute-start | bytes 417800 | tf_op jit(solution)/shard_map/ppermute | solution.py:39
  120.5 28.6 %all-to-all-start.3 = ((bf16[16,72,128]{2,1,0:T(8,128)(2,1)}), bf16[16,72,128]{2,1,0:T(8,128)(2,1)S(1)}, u32[]{:S(2)}, u32[]{:S(2)}) async-start(bf16[16,72,128]{2,1,0:T(8,128)(2,1)} %pad_maximum_fusion.1), calls=%async_computation.3 | async-start | bytes 589824 | tf_op jit(solution)/shard_map/all_to_all | solution.py:342
  133.3 30.5 %collective-permute-start.11 = (bf16[2,2,2,2,32,128]{5,4,3,2,1,0:T(8,128)(2,1)S(1)}, bf16[2,2,2,2,32,128]{5,4,3,2,1,0:T(8,128)(2,1)S(1)}, u32[]{:S(2)}, u32[]{:S(2)}) collective-permute-start(bf16[2,2,2,2,32,128]{5,4,3,2,1,0:T(8,128)(2,1)S(1)} %fusion), channel_id=1, source_target_pairs={{0,2},{1,3},{2,0},{3,1},{4,6},{5,7},{6,4},{7,5},{8,10},{9,11},{10,... | collective-permute-start | bytes 393224 | tf_op jit(solution)/shard_map/ppermute | solution.py:424
  149.0 14.8 %copy-start.4 = (bf16[16,72,128]{2,1,0:T(8,128)(2,1)}, bf16[16,72,128]{2,1,0:T(8,128)(2,1)S(1)}, u32[]{:S(2)}) copy-start(bf16[16,72,128]{2,1,0:T(8,128)(2,1)S(1)} %all-to-all-done.3) | copy-start | bytes 884740
  149.8 23.2 %all-to-all-start.4 = ((bf16[32,40,128]{2,1,0:T(8,128)(2,1)}), bf16[32,40,128]{2,1,0:T(8,128)(2,1)S(1)}, u32[]{:S(2)}, u32[]{:S(2)}) async-start(bf16[32,40,128]{2,1,0:T(8,128)(2,1)} %broadcast_in_dim.8), calls=%async_computation.4 | async-start | bytes 655360 | tf_op jit(solution)/shard_map/all_to_all | solution.py:342
  173.0 0.8 copy-start.3
  173.8 3.9 %slice-start = ((bf16[16,72,128]{2,1,0:T(8,128)(2,1)}), bf16[16,32,128]{2,1,0:T(8,128)(2,1)S(1)}, s32[]{:S(2)}) async-start(bf16[16,72,128]{2,1,0:T(8,128)(2,1)} %copy-done.4), calls=%async_computation.6 | async-start | bytes 262144 | tf_op jit(solution)/shard_map/slice | solution.py:547
  173.8 9.0 %all-to-all-start.5 = ((bf16[4,2,2,2,32,128]{5,4,3,2,1,0:T(8,128)(2,1)}), bf16[4,2,2,2,32,128]{5,4,3,2,1,0:T(8,128)(2,1)S(1)}, u32[]{:S(2)}, u32[]{:S(2)}) async-start(bf16[4,2,2,2,32,128]{5,4,3,2,1,0:T(8,128)(2,1)} %bitcast.45), calls=%async_computation.5 | async-start | bytes 524288 | tf_op jit(solution)/shard_map/all_to_all | solution.py:342

commit v11 on v10

--- a/solution.py
+++ b/solution.py
@@ -546,13 +546,13 @@
     part = jnp.sum(mixed[:, :kept].astype(F32), axis=0).astype(BF16)
     coarse = from_column(mixed[:, kept:])
     grads = share(part, ("grp", "sp"), near).reshape(grad_rows, LANES)
-    grads, gradient = lax.optimization_barrier((grads, gradient))
-    gradient = near_exchange(gradient)
-    grad_input = jnp.transpose(gradient, (0, 2, 1, 5, 3, 4, 6)).reshape(features.shape)
-
     result = pl.pallas_call(
         unpack_kernel, out_shape=shape((chans3, width), BF16), interpret=INTERPRET
     )(coarse)
+    grads, gradient, result = lax.optimization_barrier((grads, gradient, result))
+    gradient = near_exchange(gradient)
+    grad_input = jnp.transpose(gradient, (0, 2, 1, 5, 3, 4, 6)).reshape(features.shape)
+
     result = result.reshape(cotangent.shape)
 
     grad_fine, grad_down, grad_coarse = pl.pallas_call(

time: 185 us -> 195 us (1.054)
  waiting for transfers between devices: 39.1 us -> 53.8 us
  starting transfers between devices: 121 us -> 116 us
    ppermute x1, waiting for transfers between devices: 0.25 us -> 18.4 us  [far_exchange(): lax.ppermute(sent, 'sp', [(col, col ^ 2) for col in range(lax.axis_size('...]
    all_to_all x6, starting transfers between devices: 72.8 us -> 67.9 us  [trade(): lax.all_to_all(parts, axis, split_axis=0, concat_axis=0, axis_index_group...]
    all_to_all x6, waiting for transfers between devices: 25.6 us -> 22.1 us  [trade(): lax.all_to_all(parts, axis, split_axis=0, concat_axis=0, axis_index_group...]
  transfers between devices with their start and end apart: 18 -> 18, of which waited for: 10 -> 9; matrix products, arithmetic and copies ran while one was open for 3% -> 3% of each run, Pallas kernels for 5% -> 5%
where the time goes in v11:
time: 195 us; the launch traced here: 194 us
  starting transfers between devices  116 us (59%)
  waiting for transfers between devices  53.8 us (28%)
  Pallas kernels  13.1 us (7%)
  local copies, waits for them, and re-layouts  7.03 us (4%)
  other arithmetic  2.62 us (1%)
    all_to_all x6, starting transfers between devices, trade(): lax.all_to_all(parts, axis, split_axis=0, concat_axis=0, axis_index_group...  67.9 us
    ppermute x10, starting transfers between devices, arrival(): return lax.ppermute(block, ('grp', 'sp'), pairs)  23.8 us
    all_to_all x6, waiting for transfers between devices, trade(): lax.all_to_all(parts, axis, split_axis=0, concat_axis=0, axis_index_group...  22.1 us
    ppermute x1, waiting for transfers between devices, far_exchange(): lax.ppermute(sent, 'sp', [(col, col ^ 2) for col in range(lax.axis_size('...  18.4 us
    ppermute x1, starting transfers between devices, turned(): return lax.ppermute(block, ('grp', 'sp'), pairs)  12 us
    ppermute x1, starting transfers between devices, far_exchange(): lax.ppermute(sent, 'sp', [(col, col ^ 2) for col in range(lax.axis_size('...  12 us
    pallas_call x5, Pallas kernels, call(): pl.pallas_call(kernel, out_shape=outs, in_specs=[pl.BlockSpec(memory_spac...  7.46 us
    ppermute x10, waiting for transfers between devices, arrival(): return lax.ppermute(block, ('grp', 'sp'), pairs)  7.36 us
  transfers between devices with their start and end apart: 18, of which 9 were waited for; matrix products, arithmetic and copies ran while one was open for 3% of the time, Pallas kernels for 5%

profile of v11, /device:TPU:1, one launch (start us, length us, event | category | flops | bytes accessed | tf_op | source)
XLA Modules:
  0.0 193.5 jit_solution(8335958651416102556)
XLA Ops:
  0.6 17.7 %all-to-all-start = ((bf16[8,2,2,32,128]{4,2,1,3,0:T(2,128)(2,1)}), bf16[8,2,2,32,128]{4,2,1,3,0:T(2,128)(2,1)S(1)}, u32[]{:S(2)}, u32[]{:S(2)}) async-start(bf16[8,2,2,32,128]{4,2,1,3,0:T(2,128)(2,1)} %bitcast.121), calls=%async_computation | async-start | bytes 524288 | tf_op jit(solution)/shard_map/all_to_all | solution.py:342
  18.3 1.6 shard_map.110
  19.9 12.0 %collective-permute-start = (bf16[256,128]{1,0:T(8,128)(2,1)}, bf16[256,128]{1,0:T(8,128)(2,1)}, u32[]{:S(2)}, u32[]{:S(2)}) collective-permute-start(bf16[256,128]{1,0:T(8,128)(2,1)} %shard_map.110), channel_id=1, source_target_pairs={{0,71},{1,135},{2,199},{3,263},{4,327},{5,391},{6,455},{7,7},{8,79... | collective-permute-start | bytes 196616 | tf_op jit(solution)/shard_map/ppermute | solution.py:361
  32.0 0.4 copy.65
  32.4 0.4 reshape.119
  32.8 1.2 copy.44
  34.0 0.4 reshape.117
  34.4 0.6 copy-done.4
  35.3 0.2 copy.42
  35.7 5.9 %collective-permute-done = bf16[256,128]{1,0:T(8,128)(2,1)} collective-permute-done((bf16[256,128]{1,0:T(8,128)(2,1)}, bf16[256,128]{1,0:T(8,128)(2,1)}, u32[]{:S(2)}, u32[]{:S(2)}) %collective-permute-start) | collective-permute-done | bytes 65568 | tf_op jit(solution)/shard_map/ppermute | solution.py:361
  41.6 4.4 %collective-permute-start.1 = (bf16[8,2,32,128]{3,2,1,0:T(8,128)(2,1)S(1)}, bf16[8,2,32,128]{3,2,1,0:T(8,128)(2,1)S(1)}, u32[]{:S(2)}, u32[]{:S(2)}) collective-permute-start(bf16[8,2,32,128]{3,2,1,0:T(8,128)(2,1)S(1)} %slice_select_fusion.1), channel_id=1, source_target_pairs={{8,0},{9,1},{10,2},{11,3},{12,4},{13,5},{14,6},{15,7},{0,8},{1,9},... | collective-permute-start | bytes 393224 | tf_op jit(solution)/shard_map/ppermute | solution.py:39
  46.0 9.6 %all-to-all-start.1 = ((bf16[32,8,128]{2,1,0:T(8,128)(2,1)}), bf16[32,8,128]{2,1,0:T(8,128)(2,1)S(1)}, u32[]{:S(2)}, u32[]{:S(2)}) async-start(bf16[32,8,128]{2,1,0:T(8,128)(2,1)} %bitcast.4), calls=%async_computation.1 | async-start | bytes 131072 | tf_op jit(solution)/shard_map/all_to_all | solution.py:342
  56.0 0.2 copy.50.refs_6_
  56.3 3.1 %collective-permute-start.2 = (bf16[24,1,32,128]{3,2,1,0:T(8,128)(2,1)S(1)}, bf16[24,1,32,128]{3,2,1,0:T(8,128)(2,1)S(1)}, u32[]{:S(2)}, u32[]{:S(2)}) collective-permute-start(bf16[24,1,32,128]{3,2,1,0:T(8,128)(2,1)S(1)} %get-tuple-element.71), channel_id=1, source_target_pairs={{0,16},{1,17},{2,18},{3,19},{4,20},{5,21},{6,22},{7,23},{8,24},{9,... | collective-permute-start | bytes 589832 | tf_op jit(solution)/shard_map/ppermute | solution.py:39
  59.4 1.3 collective-permute-start.3
  60.7 6.7 %all-to-all-done.1 = bf16[32,8,128]{2,1,0:T(8,128)(2,1)S(1)} async-done(((bf16[32,8,128]{2,1,0:T(8,128)(2,1)}), bf16[32,8,128]{2,1,0:T(8,128)(2,1)S(1)}, u32[]{:S(2)}, u32[]{:S(2)}) %all-to-all-start.1) | async-done | bytes 65568 | tf_op jit(solution)/shard_map/all_to_all | solution.py:342
  67.5 2.6 %collective-permute-start.6 = (bf16[128,128]{1,0:T(8,128)(2,1)S(1)}, bf16[128,128]{1,0:T(8,128)(2,1)S(1)}, u32[]{:S(2)}, u32[]{:S(2)}) collective-permute-start(bf16[128,128]{1,0:T(8,128)(2,1)S(1)} %fusion.7), channel_id=1, source_target_pairs={{8,0},{9,1},{10,2},{11,3},{12,4},{13,5},{14,6},{15,7},{0,8},{1,9},... | collective-permute-start | bytes 98312 | tf_op jit(solution)/shard_map/ppermute | solution.py:39
  70.1 3.0 %shard_map.111 = (bf16[64,768]{1,0:T(8,128)(2,1)S(1)}, bf16[256,768]{1,0:T(8,128)(2,1)S(1)}, f32[12,128,128]{2,1,0:T(8,128)S(1)}) custom-call(s32[1]{0:T(128)} %bitcast.half, bf16[24,2,32,128]{3,2,1,0:T(8,128)(2,1)S(1)} %maximum_select_fusion.refs_0_.refs_3_, bf16[24,1,32,128]{3,2,1,0:T(8,128)(2,1)S(1)} %collective-permute-done.2.refs_1_.refs_4_, ...), custom_call_target="tpu_custom_call" | custom-call | tf_op jit(solution)/shard_map/pallas_call | solution.py:22
  73.1 2.2 %collective-permute-start.4 = (bf16[64,768]{1,0:T(8,128)(2,1)S(1)}, bf16[64,768]{1,0:T(8,128)(2,1)S(1)}, u32[]{:S(2)}, u32[]{:S(2)}) collective-permute-start(bf16[64,768]{1,0:T(8,128)(2,1)S(1)} %get-tuple-element.37.refs_0_), channel_id=1, source_target_pairs={{0,16},{1,17},{2,18},{3,19},{4,20},{5,21},{6,22},{7,23},{8,24},{9,... | collective-permute-start | bytes 294920 | tf_op jit(solution)/shard_map/ppermute | solution.py:39
  75.3 1.3 collective-permute-start.5
  76.7 0.3 collective-permute-done.4.refs_1_
  76.9 3.7 %collective-permute-done.5.refs_2_ = bf16[64,768]{1,0:T(8,128)(2,1)S(1)} collective-permute-done((bf16[64,768]{1,0:T(8,128)(2,1)S(1)}, bf16[64,768]{1,0:T(8,128)(2,1)S(1)}, u32[]{:S(2)}, u32[]{:S(2)}) %collective-permute-start.5) | collective-permute-done | bytes 98336 | tf_op jit(solution)/shard_map/ppermute | solution.py:39
  80.7 0.7 shard_map.112
  81.3 2.4 %collective-permute-start.7 = (bf16[64,768]{1,0:T(8,128)(2,1)S(1)}, bf16[64,768]{1,0:T(8,128)(2,1)S(1)}, u32[]{:S(2)}, u32[]{:S(2)}) collective-permute-start(bf16[64,768]{1,0:T(8,128)(2,1)S(1)} %get-tuple-element.41.refs_3_.refs_0_), channel_id=1, source_target_pairs={{0,16},{1,17},{2,18},{3,19},{4,20},{5,21},{6,22},{7,23},{8,24},{9,... | collective-permute-start | bytes 294920 | tf_op jit(solution)/shard_map/ppermute | solution.py:39
  83.7 1.3 collective-permute-start.8
  85.1 0.6 shard_map.113.refs_11_
  85.7 3.3 %collective-permute-done.8.refs_2_ = bf16[64,768]{1,0:T(8,128)(2,1)S(1)} collective-permute-done((bf16[64,768]{1,0:T(8,128)(2,1)S(1)}, bf16[64,768]{1,0:T(8,128)(2,1)S(1)}, u32[]{:S(2)}, u32[]{:S(2)}) %collective-permute-start.8) | collective-permute-done | bytes 98336 | tf_op jit(solution)/shard_map/ppermute | solution.py:39
  89.1 2.4 %shard_map.114 = (bf16[24,2,32,128]{3,2,1,0:T(8,128)(2,1)S(1)}, bf16[1280,128]{1,0:T(8,128)(2,1)S(1)}) custom-call(s32[1]{0:T(128)} %bitcast.half, bf16[64,768]{1,0:T(8,128)(2,1)S(1)} %get-tuple-element.41.refs_3_.refs_0_, bf16[64,768]{1,0:T(8,128)(2,1)S(1)} %collective-permute-done.7.refs_1_, bf16[64,768]{1,0:T(8,128)(2,1)S(1)} %collective-permute-done.8.refs_2_, ...), custom_call_target="tpu_custom_call" | custom-call | tf_op jit(solution)/shard_map/pallas_call | solution.py:22
  91.4 0.8 pad_maximum_fusion
  92.2 16.4 %all-to-all-start.2 = ((bf16[32,56,128]{2,1,0:T(8,128)(2,1)}), bf16[32,56,128]{2,1,0:T(8,128)(2,1)S(1)}, u32[]{:S(2)}, u32[]{:S(2)}) async-start(bf16[32,56,128]{2,1,0:T(8,128)(2,1)} %pad_maximum_fusion), calls=%async_computation.2 | async-start | bytes 917504 | tf_op jit(solution)/shard_map/all_to_all | solution.py:342
  108.7 1.3 collective-permute-start.10
  110.0 4.0 %collective-permute-start.9 = (bf16[17,1,32,128]{3,2,1,0:T(8,128)(2,1)S(1)}, bf16[17,1,32,128]{3,2,1,0:T(8,128)(2,1)S(1)}, u32[]{:S(2)}, u32[]{:S(2)}) collective-permute-start(bf16[17,1,32,128]{3,2,1,0:T(8,128)(2,1)S(1)} %get-tuple-element.73), channel_id=1, source_target_pairs={{0,16},{1,17},{2,18},{3,19},{4,20},{5,21},{6,22},{7,23},{8,24},{9,... | collective-permute-start | bytes 417800 | tf_op jit(solution)/shard_map/ppermute | solution.py:39
  114.0 5.5 %all-to-all-done.2 = bf16[32,56,128]{2,1,0:T(8,128)(2,1)S(1)} async-done(((bf16[32,56,128]{2,1,0:T(8,128)(2,1)}), bf16[32,56,128]{2,1,0:T(8,128)(2,1)S(1)}, u32[]{:S(2)}, u32[]{:S(2)}) %all-to-all-start.2) | async-done | bytes 458784 | tf_op jit(solution)/shard_map/all_to_all | solution.py:342
  119.7 0.7 pad_maximum_fusion.1
  120.5 11.9 %all-to-all-start.3 = ((bf16[16,72,128]{2,1,0:T(8,128)(2,1)}), bf16[16,72,128]{2,1,0:T(8,128)(2,1)S(1)}, u32[]{:S(2)}, u32[]{:S(2)}) async-start(bf16[16,72,128]{2,1,0:T(8,128)(2,1)} %pad_maximum_fusion.1), calls=%async_computation.3 | async-start | bytes 589824 | tf_op jit(solution)/shard_map/all_to_all | solution.py:342
  132.4 0.8 shard_map.115
  133.3 12.0 %collective-permute-start.11 = (bf16[2,2,2,2,32,128]{5,4,3,2,1,0:T(8,128)(2,1)S(1)}, bf16[2,2,2,2,32,128]{5,4,3,2,1,0:T(8,128)(2,1)S(1)}, u32[]{:S(2)}, u32[]{:S(2)}) collective-permute-start(bf16[2,2,2,2,32,128]{5,4,3,2,1,0:T(8,128)(2,1)S(1)} %fusion), channel_id=1, source_target_pairs={{0,2},{1,3},{2,0},{3,1},{4,6},{5,7},{6,4},{7,5},{8,10},{9,11},{10,... | collective-permute-start | bytes 393224 | tf_op jit(solution)/shard_map/ppermute | solution.py:424
  145.3 18.4 %collective-permute-done.11 = bf16[2,2,2,2,32,128]{5,4,3,2,1,0:T(8,128)(2,1)S(1)} collective-permute-done((bf16[2,2,2,2,32,128]{5,4,3,2,1,0:T(8,128)(2,1)S(1)}, bf16[2,2,2,2,32,128]{5,4,3,2,1,0:T(8,128)(2,1)S(1)}, u32[]{:S(2)}, u32[]{:S(2)}) %collective-permute-start.11) | collective-permute-done | bytes 131104 | tf_op jit(solution)/shard_map/ppermute | solution.py:424
  163.8 0.8 broadcast_in_dim.8
  164.6 8.8 %all-to-all-start.4 = ((bf16[32,40,128]{2,1,0:T(8,128)(2,1)}), bf16[32,40,128]{2,1,0:T(8,128)(2,1)S(1)}, u32[]{:S(2)}, u32[]{:S(2)}) async-start(bf16[32,40,128]{2,1,0:T(8,128)(2,1)} %broadcast_in_dim.8), calls=%async_computation.4 | async-start | bytes 655360 | tf_op jit(solution)/shard_map/all_to_all | solution.py:342
  173.4 0.6 slice_select_fusion.2
  174.1 1.7 shard_map.116
  175.8 7.1 %all-to-all-done.4 = bf16[32,40,128]{2,1,0:T(8,128)(2,1)S(1)} async-done(((bf16[32,40,128]{2,1,0:T(8,128)(2,1)}), bf16[32,40,128]{2,1,0:T(8,128)(2,1)S(1)}, u32[]{:S(2)}, u32[]{:S(2)}) %all-to-all-start.4) | async-done | bytes 327712 | tf_op jit(solution)/shard_map/all_to_all | solution.py:342
  182.9 0.8 copy.58
  183.7 3.7 %all-to-all-start.5 = ((bf16[4,2,2,2,32,128]{5,4,3,2,1,0:T(8,128)(2,1)}), bf16[4,2,2,2,32,128]{5,4,3,2,1,0:T(8,128)(2,1)S(1)}, u32[]{:S(2)}, u32[]{:S(2)}) async-start(bf16[4,2,2,2,32,128]{5,4,3,2,1,0:T(8,128)(2,1)} %bitcast.45), calls=%async_computation.5 | async-start | bytes 524288 | tf_op jit(solution)/shard_map/all_to_all | solution.py:342
  187.4 2.3 %shard_map.117 = (f32[27,32,32]{2,1,0:T(8,128)}, f32[8,32,64]{2,1,0:T(8,128)}, f32[27,64,64]{2,1,0:T(8,128)}) custom-call(bf16[1280,128]{1,0:T(8,128)(2,1)} %bitcast.107), custom_call_target="tpu_custom_call" | custom-call | tf_op jit(solution)/shard_map/pallas_call | solution.py:558
  189.7 2.8 %all-to-all-done.5 = bf16[4,2,2,2,32,128]{5,4,3,2,1,0:T(8,128)(2,1)S(1)} async-done(((bf16[4,2,2,2,32,128]{5,4,3,2,1,0:T(8,128)(2,1)}), bf16[4,2,2,2,32,128]{5,4,3,2,1,0:T(8,128)(2,1)S(1)}, u32[]{:S(2)}, u32[]{:S(2)}) %all-to-all-start.5) | async-done | bytes 262176 | tf_op jit(solution)/shard_map/all_to_all | solution.py:342
  192.6 0.9 copy.60
  (59 shorter events, 1.8 us)
Async XLA Ops:
  0.6 31.3 %copy-start.2 = (bf16[27,64,64]{2,1,0:T(8,128)(2,1)S(1)}, bf16[27,64,64]{2,1,0:T(8,128)(2,1)}, u32[]{:S(2)}) copy-start(bf16[27,64,64]{2,1,0:T(8,128)(2,1)} %param.10) | copy-start | bytes 663556
  0.6 35.0 %all-to-all-start = ((bf16[8,2,2,32,128]{4,2,1,3,0:T(2,128)(2,1)}), bf16[8,2,2,32,128]{4,2,1,3,0:T(2,128)(2,1)S(1)}, u32[]{:S(2)}, u32[]{:S(2)}) async-start(bf16[8,2,2,32,128]{4,2,1,3,0:T(2,128)(2,1)} %bitcast.121), calls=%async_computation | async-start | bytes 524288 | tf_op jit(solution)/shard_map/all_to_all | solution.py:342
  18.3 13.6 %copy-start.5 = (bf16[8,64,32]{1,2,0:T(8,128)(2,1)S(1)}, bf16[8,64,32]{1,2,0:T(8,128)(2,1)}, u32[]{:S(2)}) copy-start(bf16[8,64,32]{1,2,0:T(8,128)(2,1)} %param.9) | copy-start | bytes 98308
  19.9 21.7 %collective-permute-start = (bf16[256,128]{1,0:T(8,128)(2,1)}, bf16[256,128]{1,0:T(8,128)(2,1)}, u32[]{:S(2)}, u32[]{:S(2)}) collective-permute-start(bf16[256,128]{1,0:T(8,128)(2,1)} %shard_map.110), channel_id=1, source_target_pairs={{0,71},{1,135},{2,199},{3,263},{4,327},{5,391},{6,455},{7,7},{8,79... | collective-permute-start | bytes 196616 | tf_op jit(solution)/shard_map/ppermute | solution.py:361
  34.0 0.9 copy-start.4
  41.6 14.6 %collective-permute-start.1 = (bf16[8,2,32,128]{3,2,1,0:T(8,128)(2,1)S(1)}, bf16[8,2,32,128]{3,2,1,0:T(8,128)(2,1)S(1)}, u32[]{:S(2)}, u32[]{:S(2)}) collective-permute-start(bf16[8,2,32,128]{3,2,1,0:T(8,128)(2,1)S(1)} %slice_select_fusion.1), channel_id=1, source_target_pairs={{8,0},{9,1},{10,2},{11,3},{12,4},{13,5},{14,6},{15,7},{0,8},{1,9},... | collective-permute-start | bytes 393224 | tf_op jit(solution)/shard_map/ppermute | solution.py:39
  46.0 21.4 %all-to-all-start.1 = ((bf16[32,8,128]{2,1,0:T(8,128)(2,1)}), bf16[32,8,128]{2,1,0:T(8,128)(2,1)S(1)}, u32[]{:S(2)}, u32[]{:S(2)}) async-start(bf16[32,8,128]{2,1,0:T(8,128)(2,1)} %bitcast.4), calls=%async_computation.1 | async-start | bytes 131072 | tf_op jit(solution)/shard_map/all_to_all | solution.py:342
  56.3 13.8 %collective-permute-start.2 = (bf16[24,1,32,128]{3,2,1,0:T(8,128)(2,1)S(1)}, bf16[24,1,32,128]{3,2,1,0:T(8,128)(2,1)S(1)}, u32[]{:S(2)}, u32[]{:S(2)}) collective-permute-start(bf16[24,1,32,128]{3,2,1,0:T(8,128)(2,1)S(1)} %get-tuple-element.71), channel_id=1, source_target_pairs={{0,16},{1,17},{2,18},{3,19},{4,20},{5,21},{6,22},{7,23},{8,24},{9,... | collective-permute-start | bytes 589832 | tf_op jit(solution)/shard_map/ppermute | solution.py:39
  59.4 10.6 %collective-permute-start.3 = (bf16[24,1,32,128]{3,2,1,0:T(8,128)(2,1)S(1)}, bf16[24,1,32,128]{3,2,1,0:T(8,128)(2,1)S(1)}, u32[]{:S(2)}, u32[]{:S(2)}) collective-permute-start(bf16[24,1,32,128]{3,2,1,0:T(8,128)(2,1)S(1)} %get-tuple-element.70), channel_id=1, source_target_pairs={{16,0},{17,1},{18,2},{19,3},{20,4},{21,5},{22,6},{23,7},{24,8},{25... | collective-permute-start | bytes 589832 | tf_op jit(solution)/shard_map/ppermute | solution.py:39
  67.4 2.6 %copy-start.1 = (bf16[256,256]{1,0:T(8,128)(2,1)S(1)}, bf16[256,256]{1,0:T(8,128)(2,1)}, u32[]{:S(2)}) copy-start(bf16[256,256]{1,0:T(8,128)(2,1)} %constant.116.clone.refs_5_) | copy-start | bytes 393220
  67.5 9.2 %collective-permute-start.6 = (bf16[128,128]{1,0:T(8,128)(2,1)S(1)}, bf16[128,128]{1,0:T(8,128)(2,1)S(1)}, u32[]{:S(2)}, u32[]{:S(2)}) collective-permute-start(bf16[128,128]{1,0:T(8,128)(2,1)S(1)} %fusion.7), channel_id=1, source_target_pairs={{8,0},{9,1},{10,2},{11,3},{12,4},{13,5},{14,6},{15,7},{0,8},{1,9},... | collective-permute-start | bytes 98312 | tf_op jit(solution)/shard_map/ppermute | solution.py:39
  73.1 3.8 %collective-permute-start.4 = (bf16[64,768]{1,0:T(8,128)(2,1)S(1)}, bf16[64,768]{1,0:T(8,128)(2,1)S(1)}, u32[]{:S(2)}, u32[]{:S(2)}) collective-permute-start(bf16[64,768]{1,0:T(8,128)(2,1)S(1)} %get-tuple-element.37.refs_0_), channel_id=1, source_target_pairs={{0,16},{1,17},{2,18},{3,19},{4,20},{5,21},{6,22},{7,23},{8,24},{9,... | collective-permute-start | bytes 294920 | tf_op jit(solution)/shard_map/ppermute | solution.py:39
  75.3 5.4 %collective-permute-start.5 = (bf16[64,768]{1,0:T(8,128)(2,1)S(1)}, bf16[64,768]{1,0:T(8,128)(2,1)S(1)}, u32[]{:S(2)}, u32[]{:S(2)}) collective-permute-start(bf16[64,768]{1,0:T(8,128)(2,1)S(1)} %get-tuple-element.37.refs_0_), channel_id=1, source_target_pairs={{16,0},{17,1},{18,2},{19,3},{20,4},{21,5},{22,6},{23,7},{24,8},{25... | collective-permute-start | bytes 294920 | tf_op jit(solution)/shard_map/ppermute | solution.py:39
  81.3 4.4 %collective-permute-start.7 = (bf16[64,768]{1,0:T(8,128)(2,1)S(1)}, bf16[64,768]{1,0:T(8,128)(2,1)S(1)}, u32[]{:S(2)}, u32[]{:S(2)}) collective-permute-start(bf16[64,768]{1,0:T(8,128)(2,1)S(1)} %get-tuple-element.41.refs_3_.refs_0_), channel_id=1, source_target_pairs={{0,16},{1,17},{2,18},{3,19},{4,20},{5,21},{6,22},{7,23},{8,24},{9,... | collective-permute-start | bytes 294920 | tf_op jit(solution)/shard_map/ppermute | solution.py:39
  83.7 5.4 %collective-permute-start.8 = (bf16[64,768]{1,0:T(8,128)(2,1)S(1)}, bf16[64,768]{1,0:T(8,128)(2,1)S(1)}, u32[]{:S(2)}, u32[]{:S(2)}) collective-permute-start(bf16[64,768]{1,0:T(8,128)(2,1)S(1)} %get-tuple-element.41.refs_3_.refs_0_), channel_id=1, source_target_pairs={{16,0},{17,1},{18,2},{19,3},{20,4},{21,5},{22,6},{23,7},{24,8},{25... | collective-permute-start | bytes 294920 | tf_op jit(solution)/shard_map/ppermute | solution.py:39
  85.1 4.0 %copy-start = (bf16[256,256]{1,0:T(8,128)(2,1)S(1)}, bf16[256,256]{1,0:T(8,128)(2,1)}, u32[]{:S(2)}) copy-start(bf16[256,256]{1,0:T(8,128)(2,1)} %constant.117.clone.refs_8_) | copy-start | bytes 393220
  92.2 27.2 %all-to-all-start.2 = ((bf16[32,56,128]{2,1,0:T(8,128)(2,1)}), bf16[32,56,128]{2,1,0:T(8,128)(2,1)S(1)}, u32[]{:S(2)}, u32[]{:S(2)}) async-start(bf16[32,56,128]{2,1,0:T(8,128)(2,1)} %pad_maximum_fusion), calls=%async_computation.2 | async-start | bytes 917504 | tf_op jit(solution)/shard_map/all_to_all | solution.py:342
  108.7 11.0 %collective-permute-start.10 = (bf16[17,1,32,128]{3,2,1,0:T(8,128)(2,1)S(1)}, bf16[17,1,32,128]{3,2,1,0:T(8,128)(2,1)S(1)}, u32[]{:S(2)}, u32[]{:S(2)}) collective-permute-start(bf16[17,1,32,128]{3,2,1,0:T(8,128)(2,1)S(1)} %get-tuple-element.72), channel_id=1, source_target_pairs={{16,0},{17,1},{18,2},{19,3},{20,4},{21,5},{22,6},{23,7},{24,8},{25... | collective-permute-start | bytes 417800 | tf_op jit(solution)/shard_map/ppermute | solution.py:39
  110.0 9.7 %collective-permute-start.9 = (bf16[17,1,32,128]{3,2,1,0:T(8,128)(2,1)S(1)}, bf16[17,1,32,128]{3,2,1,0:T(8,128)(2,1)S(1)}, u32[]{:S(2)}, u32[]{:S(2)}) collective-permute-start(bf16[17,1,32,128]{3,2,1,0:T(8,128)(2,1)S(1)} %get-tuple-element.73), channel_id=1, source_target_pairs={{0,16},{1,17},{2,18},{3,19},{4,20},{5,21},{6,22},{7,23},{8,24},{9,... | collective-permute-start | bytes 417800 | tf_op jit(solution)/shard_map/ppermute | solution.py:39
  120.5 43.3 %all-to-all-start.3 = ((bf16[16,72,128]{2,1,0:T(8,128)(2,1)}), bf16[16,72,128]{2,1,0:T(8,128)(2,1)S(1)}, u32[]{:S(2)}, u32[]{:S(2)}) async-start(bf16[16,72,128]{2,1,0:T(8,128)(2,1)} %pad_maximum_fusion.1), calls=%async_computation.3 | async-start | bytes 589824 | tf_op jit(solution)/shard_map/all_to_all | solution.py:342
  133.3 30.4 %collective-permute-start.11 = (bf16[2,2,2,2,32,128]{5,4,3,2,1,0:T(8,128)(2,1)S(1)}, bf16[2,2,2,2,32,128]{5,4,3,2,1,0:T(8,128)(2,1)S(1)}, u32[]{:S(2)}, u32[]{:S(2)}) collective-permute-start(bf16[2,2,2,2,32,128]{5,4,3,2,1,0:T(8,128)(2,1)S(1)} %fusion), channel_id=1, source_target_pairs={{0,2},{1,3},{2,0},{3,1},{4,6},{5,7},{6,4},{7,5},{8,10},{9,11},{10,... | collective-permute-start | bytes 393224 | tf_op jit(solution)/shard_map/ppermute | solution.py:424
  164.6 18.4 %all-to-all-start.4 = ((bf16[32,40,128]{2,1,0:T(8,128)(2,1)}), bf16[32,40,128]{2,1,0:T(8,128)(2,1)S(1)}, u32[]{:S(2)}, u32[]{:S(2)}) async-start(bf16[32,40,128]{2,1,0:T(8,128)(2,1)} %broadcast_in_dim.8), calls=%async_computation.4 | async-start | bytes 655360 | tf_op jit(solution)/shard_map/all_to_all | solution.py:342
  182.9 0.8 copy-start.3
  183.7 8.8 %all-to-all-start.5 = ((bf16[4,2,2,2,32,128]{5,4,3,2,1,0:T(8,128)(2,1)}), bf16[4,2,2,2,32,128]{5,4,3,2,1,0:T(8,128)(2,1)S(1)}, u32[]{:S(2)}, u32[]{:S(2)}) async-start(bf16[4,2,2,2,32,128]{5,4,3,2,1,0:T(8,128)(2,1)} %bitcast.45), calls=%async_computation.5 | async-start | bytes 524288 | tf_op jit(solution)/shard_map/all_to_all | solution.py:342
